TPU v7x, 32 devices: a whole 2x2x4 slice. The times are simulated.
32 devices in a mesh: opt: 8 (over z, y), layer: 4 (over x, core).
Axes of the slice: x: 2, y: 2, z: 4, core: 2. Of those that a mesh axis runs over, the one named last changes fastest.
Arguments:
- momentum: bfloat16 [4, 8, 1024, 512], P('layer', None, 'opt'), may hold values from -4000 to 4000
- weights: bfloat16 [4, 8, 1024, 512], P('layer', None, 'opt'), may hold values from -6 to 6
Outputs:
- new_weights: bfloat16 [4, 8, 1024, 512], P('layer', None, 'opt')
All inputs are finite; a program needn't handle non-finite values.
Results may differ from a plain program's by a relative error of at most 0.0041.
Values may be sent and summed in bfloat16 or wider, within the bound.
No kernel may reach another device: no remote copies, remote signals or barrier semaphores. Data moves between devices by JAX's collectives and lax.ppermute only.
A program may use at most 64 MiB of HBM per device.

v0:
```python
import jax
import jax.numpy as jnp
from jax import lax
from jax.sharding import PartitionSpec as P

ITERS = 3


first_coef = 3.4445
second_coef = -4.775
third_coef = 2.0315
epsilon = 1e-06
step_rate = 0.5
decay_rate = 0.1


def batched(first_matrix, second_matrix):
    return jnp.einsum("erk,ekc->erc", first_matrix, second_matrix, precision=lax.Precision.HIGHEST)


def square_total(regrouped):
    squares = jnp.sum(jnp.square(regrouped.astype(jnp.float32)), axis=(1, 2))
    return lax.psum(squares, "layer")


def identity_rows(row_count, gram_order):
    column_ids = lax.broadcasted_iota(jnp.int32, (row_count, gram_order), 1)
    row_ids = lax.broadcasted_iota(jnp.int32, (row_count, gram_order), 0)
    return (column_ids == row_ids).astype(jnp.float32)[None]


def newton_whole(gram_sum, trace_sum):
    identity_matrix = identity_rows(gram_sum.shape[1], gram_sum.shape[2])
    current = gram_sum / (trace_sum + epsilon)[:, None, None]
    accum = identity_matrix
    for iteration in range(ITERS):
        squared = batched(current, current)
        polynomial = first_coef * identity_matrix + second_coef * current + third_coef * squared
        accum = batched(accum, polynomial)
        if iteration + 1 < ITERS:
            current = batched(batched(current, polynomial), polynomial)
    return accum


def on_device(momentum, weights):
    regrouped = lax.all_to_all(momentum, "opt", split_axis=1, concat_axis=2, tiled=True)[0]
    layers = lax.axis_size("layer")
    matrix_rows = regrouped.shape[1]
    gram_local = lax.dot_general(
        regrouped, regrouped, (((1,), (1,)), ((0,), (0,))), preferred_element_type=jnp.float32
    )
    gram_sum = lax.psum(gram_local, "layer")
    trace_sum = square_total(regrouped)
    accum = newton_whole(gram_sum, trace_sum)
    factor = (accum * jnp.sqrt(layers * matrix_rows / (trace_sum + epsilon))[:, None, None]).astype(
        jnp.bfloat16
    )
    update = lax.dot_general(
        regrouped, factor, (((2,), (1,)), ((0,), (0,))), preferred_element_type=jnp.float32
    )
    update = update.astype(jnp.bfloat16)[None]
    returned = lax.all_to_all(update, "opt", split_axis=2, concat_axis=1, tiled=True)
    shrink = 1.0 - step_rate * decay_rate
    return (shrink * weights.astype(jnp.float32) - step_rate * returned.astype(jnp.float32)).astype(
        jnp.bfloat16
    )


def solution(mesh):
    in_specs = (P("layer", None, "opt", None), P("layer", None, "opt", None))
    out_specs = P("layer", None, "opt", None)
    return jax.shard_map(
        on_device, mesh=mesh, in_specs=in_specs, out_specs=out_specs, check_vma=False
    )
```

profile of v0, /device:TPU:0, one launch (start us, length us, event | category | flops | bytes accessed | tf_op | source)
XLA Modules:
  0.0 150.1 jit_solution(18168067993652703602)
XLA Ops:
  6.5 0.0 all-reduce.2.cloned.1.call-start
  6.5 33.0 %all_to_all.8 = bf16[1,8,128,512]{3,2,0,1:T(8,128)(2,1)S(1)} all-to-all(bf16[1,8,128,512]{3,2,0,1:T(8,128)(2,1)} %bitcast.53), channel_id=1, replica_groups=mesh['opt'=8,'layer'=4] {'opt'}, dimensions={1} | all-to-all | bytes 2097152 | tf_op jit(solution)/shard_map/all_to_all | solution.py:46
  39.6 1.7 %convolution_bitcast_fusion = f32[1,512,512]{2,1,0:T(8,128)} fusion(bf16[1,8,128,512]{3,2,0,1:T(8,128)(2,1)S(1)} %all_to_all.8), kind=kOutput, calls=%fused_computation.14 | convolution fusion | flops 536870912 | bytes 2097152 | tf_op jit(solution)/shard_map/dot_general | solution.py:49
  41.3 0.0 all-reduce.2.cloned.1.call-update
  41.3 1.2 multiply_reduce_fusion
  42.5 6.3 %psum.15 = f32[1]{0:T(128)} all-reduce(f32[1]{0:T(128)} %bitcast.4), channel_id=1, replica_groups=mesh['opt'=8,'layer'=4] {'layer'}, use_global_device_ids=true, to_apply=%region_2.0 | all-reduce | flops 1 | bytes 8 | tf_op jit(solution)/shard_map/psum | solution.py:23
  49.5 27.1 %all-reduce.2.cloned.1.call-done = f32[1,512,512]{2,1,0:T(8,128)} async-done(((f32[1,512,512]{2,1,0:T(8,128)}), f32[1,512,512]{2,1,0:T(8,128)}) %all-reduce.2.cloned.1.call-update) | async-done | bytes 1048592 | tf_op jit(solution)/shard_map/psum | solution.py:52
  76.6 4.0 %fusion.6 = f32[512,512]{1,0:T(8,128)S(1)} fusion(f32[1,512,512]{2,1,0:T(8,128)} %all-reduce.2.cloned.1.call-done, f32[]{:T(128)} %bitcast.5), kind=kOutput, calls=%fused_computation.17 | convolution fusion | flops 1612709888 | bytes 2097156 | tf_op jit(solution)/shard_map/erk,ekc->erc/dot_general | solution.py:18
  80.6 0.0 copy-start.1
  80.6 1.1 fusion.12
  81.6 0.2 copy-done.1
  81.8 1.9 %fusion.8 = f32[512,512]{1,0:T(8,128)S(1)} fusion(f32[512,512]{1,0:T(8,128)S(1)} %fusion.6, f32[1,512,512]{2,1,0:T(8,128)S(1)} %copy-done.1, f32[]{:T(128)} %bitcast.5), kind=kOutput, calls=%fused_computation.19 | convolution fusion | flops 1610874880 | bytes 3145732 | tf_op jit(solution)/shard_map/erk,ekc->erc/dot_general | solution.py:18
  83.7 1.8 %fusion.13 = f32[512,512]{1,0:T(8,128)S(1)} fusion(f32[512,512]{1,0:T(8,128)S(1)} %fusion.8, f32[512,512]{1,0:T(8,128)S(1)} %fusion.6), kind=kOutput, calls=%fused_computation.27 | convolution fusion | flops 1610612736 | bytes 3145728 | tf_op jit(solution)/shard_map/erk,ekc->erc/dot_general | solution.py:18
  85.5 1.9 %fusion.2 = f32[512,512]{1,0:T(8,128)S(1)} fusion(f32[512,512]{1,0:T(8,128)S(1)} %fusion.13), kind=kOutput, calls=%fused_computation.11 | convolution fusion | flops 1612185600 | bytes 2097152 | tf_op jit(solution)/shard_map/erk,ekc->erc/dot_general | solution.py:18
  87.4 1.8 %fusion.15 = f32[512,512]{1,0:T(8,128)S(1)} fusion(f32[512,512]{1,0:T(8,128)S(1)} %fusion.13, f32[512,512]{1,0:T(8,128)S(1)} %fusion.2), kind=kOutput, calls=%fused_computation.29 | convolution fusion | flops 1610612736 | bytes 3145728 | tf_op jit(solution)/shard_map/erk,ekc->erc/dot_general | solution.py:18
  89.3 1.8 %fusion.16 = f32[512,512]{1,0:T(8,128)S(1)} fusion(f32[512,512]{1,0:T(8,128)S(1)} %fusion.15, f32[512,512]{1,0:T(8,128)S(1)} %fusion.2), kind=kOutput, calls=%fused_computation.30 | convolution fusion | flops 1610612736 | bytes 3145728 | tf_op jit(solution)/shard_map/erk,ekc->erc/dot_general | solution.py:18
  91.1 2.1 %fusion.1 = f32[512,512]{1,0:T(8,128)S(1)} fusion(f32[512,512]{1,0:T(8,128)S(1)} %fusion.16), kind=kOutput, calls=%fused_computation.9 | convolution fusion | flops 1612185600 | bytes 2097152 | tf_op jit(solution)/shard_map/erk,ekc->erc/dot_general | solution.py:18
  93.2 1.8 %fusion.14 = f32[512,512]{1,0:T(8,128)S(1)} fusion(f32[512,512]{1,0:T(8,128)S(1)} %fusion.12, f32[512,512]{1,0:T(8,128)S(1)} %fusion.2), kind=kOutput, calls=%fused_computation.28 | convolution fusion | flops 1610612736 | bytes 3145728 | tf_op jit(solution)/shard_map/erk,ekc->erc/dot_general | solution.py:18
  95.1 1.8 %fusion.7 = bf16[512,512]{1,0:T(8,128)(2,1)S(1)} fusion(f32[512,512]{1,0:T(8,128)S(1)} %fusion.14, f32[512,512]{1,0:T(8,128)S(1)} %fusion.1, f32[]{:T(128)} %bitcast.9), kind=kOutput, calls=%fused_computation.18 | convolution fusion | flops 1611137024 | bytes 2621444 | tf_op jit(solution)/shard_map/erk,ekc->erc/dot_general | solution.py:18
  97.0 0.8 fusion.4
  97.7 1.8 %copy.7 = bf16[1,1,1024,512]{3,1,0,2:T(2,128)(2,1)S(1)} copy(bf16[1,1,1024,512]{2,3,1,0:T(8,128)(2,1)S(1)} %fusion.4) | data formatting | bytes 2097152 | tf_op jit(solution)/shard_map/broadcast_in_dim | solution.py:61
  99.6 0.5 broadcast.70
  100.1 7.0 %reduce.2 = bf16[1024,512]{1,0:T(8,128)(2,1)S(1)} reduce(bf16[1024,1,1,512]{3,2,1,0:T(2,128)(2,1)S(1)} %bitcast.50, bf16[]{:T(256)} %broadcast.70), dimensions={1,2}, to_apply=%bitcast.29.reduce_sub_computation | reduce | bytes 2097154
  107.1 0.8 reshape.135
  107.9 30.7 %all_to_all.9 = bf16[8,2,32768]{2,1,0:T(2,128)(2,1)S(1)} all-to-all(bf16[8,2,32768]{2,1,0:T(2,128)(2,1)S(1)} %reshape.135), channel_id=1, replica_groups=mesh['opt'=8,'layer'=4] {'opt'}, dimensions={0} | all-to-all | bytes 2097152 | tf_op jit(solution)/shard_map/all_to_all | solution.py:62
  138.6 1.0 reshape.136
  139.6 0.0 copy-start
  139.7 2.2 %convert_multiply_fusion = f32[1,1,1024,512]{3,1,0,2:T(1,128)S(1)} fusion(bf16[1024,1,1,512]{3,2,1,0:T(2,128)(2,1)S(1)} %reshape.136), kind=kLoop, calls=%fused_computation.2 | loop fusion | flops 1048576 | bytes 3145728 | tf_op jit(solution)/shard_map/mul | solution.py:64
  141.8 0.0 copy-done
  141.8 1.4 fusion
Async XLA Ops:
  6.5 70.0 %all-reduce.2.cloned.1.call-start = ((), (), s32[]{:S(2)}) async-start(), calls=%async_computation.2 | async-start | bytes 2097152 | tf_op jit(solution)/shard_map/psum | solution.py:52
  80.6 1.2 copy-start.1
  139.6 2.2 %copy-start = (bf16[1,8,128,512]{3,2,1,0:T(8,128)(2,1)S(1)}, bf16[1,8,128,512]{3,2,1,0:T(8,128)(2,1)}, u32[]{:S(2)}) copy-start(bf16[1,8,128,512]{3,2,1,0:T(8,128)(2,1)} %param.3) | copy-start | bytes 3145732
Sparse Core Ops, SparseCore 0:
  41.4 35.0 all-reduce.1
where the time goes:
time: 150 us
  blocking collectives  70 us (47%)
  waiting for transfers between devices  27.1 us (18%)
  matrix products  22.6 us (15%)
  between operations  14.2 us (9%)
  other arithmetic  11.8 us (8%)
  local copies, waits for them, and re-layouts  4.33 us (3%)
    all_to_all x1, blocking collectives, on_device(): lax.all_to_all(momentum, 'opt', split_axis=1, concat_axis=2, tiled=True)[0]  33 us
    all_to_all x1, blocking collectives, on_device(): lax.all_to_all(update, 'opt', split_axis=2, concat_axis=1, tiled=True)  30.7 us
    psum x1, waiting for transfers between devices, on_device(): gram_sum = lax.psum(gram_local, 'layer')  27.1 us
    dot_general x10, matrix products, batched(): jnp.einsum('erk,ekc->erc', first_matrix, second_matrix, precision=lax.Pre...  20.2 us
    unnamed x1, other arithmetic  7.04 us
    psum x1, blocking collectives, square_total(): return lax.psum(squares, 'layer')  6.31 us
  transfers between devices with their start and end apart: 1, of which 1 were waited for; matrix products, arithmetic and copies ran while one was open for 1% of the time, Pallas kernels for 0%

commit v1 on v0

v1 whole, which is shorter than its diff:
```python
import functools

import jax
import jax.numpy as jnp
from jax import lax
from jax.experimental import pallas as pl
from jax.experimental.pallas import tpu as pltpu
from jax.sharding import PartitionSpec as P

ITERS = 3
BLOCK = 128
VMEM_BYTES = 48 << 20

first_coef = 3.4445
second_coef = -4.775
third_coef = 2.0315
epsilon = 1e-06
step_rate = 0.5
decay_rate = 0.1

AXES = ("opt", "layer")


def layout(opt, layer):
    lows, highs, shift = opt // 2, layer // 2, opt // 4

    def device(half, low, high, pair):
        low = (low + half * shift) % lows
        return (half * lows + low) * layer + high * 2 + pair

    places = [(low, high) for low in range(lows) for high in range(highs)]
    groups = [[device(half, *place, pair) for place in places] for half in range(2) for pair in range(2)]
    pair_swap = [
        (device(half, *place, pair), device(half, *place, 1 - pair))
        for half in range(2)
        for pair in range(2)
        for place in places
    ]
    half_swap = [
        (device(half, *place, pair), device(1 - half, *place, pair))
        for half in range(2)
        for pair in range(2)
        for place in places
    ]
    return groups, pair_swap, half_swap


def block_pairs(order):
    count = order // BLOCK
    upper = [(i, j) for i in range(count) for j in range(i, count)]
    first = [pair for pair in upper if pair[0] < count // 4 or pair[0] == pair[1] and pair[0] < count // 2]
    return first + [pair for pair in upper if pair not in first]


def call(kernel, out_shape, grid, in_specs, out_specs, *operands):
    return pl.pallas_call(
        kernel,
        out_shape=out_shape,
        grid=grid,
        in_specs=in_specs,
        out_specs=out_specs,
        compiler_params=pltpu.CompilerParams(vmem_limit_bytes=VMEM_BYTES),
    )(*operands)


def whole(array):
    rest = array.shape[1:]
    return pl.BlockSpec((None,) + rest, lambda expert: (expert,) + (0,) * len(rest))


SCALAR = pl.BlockSpec(memory_space=pltpu.SMEM)


def product(first, second):
    return jnp.dot(first, second, preferred_element_type=jnp.float32)


def gram_kernel(pairs, rows_ref, gram_ref):
    wide = 2 * BLOCK
    order = rows_ref.shape[1]
    place = {pair: index for index, pair in enumerate(pairs)}
    for row in range(0, order, wide):
        for column in range(row, order, wide):
            tile = lax.dot_general(
                rows_ref[:, row : row + wide],
                rows_ref[:, column : column + wide],
                (((0,), (0,)), ((), ())),
                preferred_element_type=jnp.float32,
            )
            for i in range(2):
                for j in range(2):
                    index = place.get((row // BLOCK + i, column // BLOCK + j))
                    if index is not None:
                        gram_ref[pl.ds(index * BLOCK, BLOCK), :] = tile[
                            i * BLOCK : (i + 1) * BLOCK, j * BLOCK : (j + 1) * BLOCK
                        ]


def pair_sum_kernel(pair_ref, own_ref, other_ref, total_ref, half_ref):
    total_ref[...] = own_ref[...] + other_ref[...]
    length = half_ref.shape[0]
    start = pl.multiple_of(pair_ref[0] * length, length)
    half_ref[...] = total_ref[pl.ds(start, length), :].astype(half_ref.dtype)


def split(matrix):
    high = matrix.astype(jnp.bfloat16)
    return high, (matrix - high.astype(jnp.float32)).astype(jnp.bfloat16)


def product_of_split(first, second):
    return product(first[0], second[0]) + (product(first[0], second[1]) + product(first[1], second[0]))


def newton(current, identity):
    accum = None
    for iteration in range(ITERS):
        halves = split(current)
        squared = product_of_split(halves, halves)
        polynomial = jnp.where(identity, first_coef, 0.0) + second_coef * current + third_coef * squared
        poly_halves = split(polynomial)
        accum = polynomial if accum is None else product_of_split(split(accum), poly_halves)
        if iteration + 1 < ITERS:
            current = product_of_split(split(product_of_split(halves, poly_halves)), poly_halves)
    return accum


def update_kernel(pairs, scale, pair_ref, total_ref, near_ref, far_ref, rows_ref, update_ref):
    order = rows_ref.shape[1]
    length = near_ref.shape[0]
    first_pair = pair_ref[0] == 0
    near, far = near_ref[...].astype(jnp.float32), far_ref[...].astype(jnp.float32)
    total = (
        total_ref[:length, :] + jnp.where(first_pair, near, far),
        total_ref[length:, :] + jnp.where(first_pair, far, near),
    )
    blocks = {}
    for index, (i, j) in enumerate(pairs):
        place = index * BLOCK % length
        tile = total[index * BLOCK // length][place : place + BLOCK]
        blocks[i, j] = tile
        if i != j:
            blocks[j, i] = tile.T
    count = order // BLOCK
    gram = jnp.concatenate(
        [jnp.concatenate([blocks[i, j] for j in range(count)], axis=1) for i in range(count)], axis=0
    )
    identity = lax.broadcasted_iota(jnp.int32, gram.shape, 0) == lax.broadcasted_iota(jnp.int32, gram.shape, 1)
    trace_sum = jnp.sum(jnp.where(identity, gram, 0.0))
    accum = newton(gram / (trace_sum + epsilon), identity)
    factor = (accum * jnp.sqrt(scale / (trace_sum + epsilon))).astype(jnp.bfloat16)
    update_ref[...] = product(rows_ref[...], factor).astype(update_ref.dtype)


def on_device(momentum, weights):
    _, experts, row_count, order = momentum.shape
    opt, layer = lax.axis_size("opt"), lax.axis_size("layer")
    groups, pair_swap, half_swap = layout(opt, layer)
    members = len(groups[0])
    owned = experts // members
    pairs = block_pairs(order)
    packed_rows = len(pairs) * BLOCK
    pair = (lax.axis_index("layer") % 2).astype(jnp.int32).reshape(1)
    exchange = functools.partial(
        lax.all_to_all, axis_name=AXES, split_axis=0, concat_axis=0, axis_index_groups=groups, tiled=True
    )

    arrived = exchange(momentum[0])
    rows = arrived.reshape(members, owned, row_count, order).swapaxes(0, 1)
    rows = rows.reshape(owned, members * row_count, order)

    packed = jax.ShapeDtypeStruct((owned, packed_rows, BLOCK), jnp.float32)
    half_shape = jax.ShapeDtypeStruct((owned, packed_rows // 2, BLOCK), jnp.bfloat16)
    own = call(
        functools.partial(gram_kernel, pairs), packed, (owned,), [whole(rows)], whole(packed), rows
    )
    other = lax.ppermute(own, AXES, pair_swap)
    total, half = call(
        pair_sum_kernel,
        (packed, half_shape),
        (owned,),
        [SCALAR, whole(packed), whole(packed)],
        (whole(packed), whole(half_shape)),
        pair,
        own,
        other,
    )
    near = lax.ppermute(half, AXES, half_swap)
    far = lax.ppermute(near, AXES, pair_swap)
    scale = float(layer * opt * row_count)
    update = call(
        functools.partial(update_kernel, pairs, scale),
        jax.ShapeDtypeStruct(rows.shape, jnp.bfloat16),
        (owned,),
        [SCALAR, whole(packed), whole(half_shape), whole(half_shape), whole(rows)],
        whole(rows),
        pair,
        total,
        near,
        far,
        rows,
    )
    update = update.reshape(owned, members, row_count, order).swapaxes(0, 1)
    returned = exchange(update.reshape(experts, row_count, order))[None]
    shrink = 1.0 - step_rate * decay_rate
    return (shrink * weights.astype(jnp.float32) - step_rate * returned.astype(jnp.float32)).astype(
        jnp.bfloat16
    )


def solution(mesh):
    in_specs = (P("layer", None, "opt", None), P("layer", None, "opt", None))
    out_specs = P("layer", None, "opt", None)
    return jax.shard_map(
        on_device, mesh=mesh, in_specs=in_specs, out_specs=out_specs, check_vma=False
    )
```

time: 150 us -> 63.4 us (0.42)
  blocking collectives: 70 us -> 40.3 us
  matrix products: 22.6 us -> 0 us
  waiting for transfers between devices: 27.1 us -> 9 us
  between operations: 14.2 us -> 0.05 us
  other arithmetic: 11.8 us -> 1.43 us
  Pallas kernels: 0 us -> 9.63 us
  local copies, waits for them, and re-layouts: 4.33 us -> 0.01 us
  starting transfers between devices: 0.01 us -> 2.76 us
    psum x1 -> x0, waiting for transfers between devices: 27.1 us -> none  [on_device(): gram_sum = lax.psum(gram_local, 'layer')]
    all_to_all x2, blocking collectives: 63.7 us -> 40.3 us  [the longest x1 21.2 us: on_device(): arrived = exchange(momentum[0])]
    dot_general x12 -> x0, matrix products: 22.6 us -> none  [the longest x10 20.2 us: batched(): jnp.einsum('erk,ekc->erc', first_matrix, second_matrix, precision=lax.Pre...]
    pallas_call x0 -> x3, Pallas kernels: none -> 9.63 us  [call(): pl.pallas_call(kernel, out_shape=out_shape, grid=grid, in_specs=in_specs,...]
    ppermute x0 -> x3, waiting for transfers between devices: none -> 9 us  [the longest x1 5.53 us: on_device(): near = lax.ppermute(half, AXES, half_swap)]
    unnamed x1 -> x0, other arithmetic: 7.04 us -> none
    psum x1 -> x0, blocking collectives: 6.31 us -> none  [square_total(): return lax.psum(squares, 'layer')]
    ppermute x0 -> x3, starting transfers between devices: none -> 2.76 us  [the longest x1 2.68 us: on_device(): near = lax.ppermute(half, AXES, half_swap)]
  transfers between devices with their start and end apart: 1 -> 3, of which waited for: 1 -> 3; matrix products, arithmetic and copies ran while one was open for 1% -> 0% of each run, Pallas kernels for 0% -> 0%
where the time goes in v1:
time: 63.4 us; the launch traced here: 63.2 us
  blocking collectives  40.3 us (64%)
  Pallas kernels  9.63 us (15%)
  waiting for transfers between devices  9 us (14%)
  starting transfers between devices  2.76 us (4%)
  other arithmetic  1.43 us (2%)
    all_to_all x1, blocking collectives, on_device(): arrived = exchange(momentum[0])  21.2 us
    all_to_all x1, blocking collectives, on_device(): returned = exchange(update.reshape(experts, row_count, order))[None]  19.1 us
    pallas_call x3, Pallas kernels, call(): pl.pallas_call(kernel, out_shape=out_shape, grid=grid, in_specs=in_specs,...  9.63 us
    ppermute x1, waiting for transfers between devices, on_device(): near = lax.ppermute(half, AXES, half_swap)  5.53 us
    ppermute x1, starting transfers between devices, on_device(): near = lax.ppermute(half, AXES, half_swap)  2.68 us
    ppermute x1, waiting for transfers between devices, on_device(): other = lax.ppermute(own, AXES, pair_swap)  2.07 us
    convert_element_type x1, other arithmetic, on_device(): (shrink * weights.astype(jnp.float32) - step_rate * returned.astype(jnp.f...  1.43 us
    ppermute x1, waiting for transfers between devices, on_device(): far = lax.ppermute(near, AXES, pair_swap)  1.39 us
  transfers between devices with their start and end apart: 3, of which 3 were waited for; matrix products, arithmetic and copies ran while one was open for 0% of the time, Pallas kernels for 0%

profile of v1, /device:TPU:0, one launch (start us, length us, event | category | flops | bytes accessed | tf_op | source)
XLA Modules:
  0.0 63.2 jit_solution(5891992532049634187)
XLA Ops:
  0.0 21.2 %all_to_all.10 = bf16[8,128,512]{2,1,0:T(8,128)(2,1)S(1)} all-to-all(bf16[8,128,512]{2,1,0:T(8,128)(2,1)} %bitcast.11), channel_id=1, replica_groups={{0,2,4,6,8,10,12,14},{1,3,5,7,9,11,13,15},{24,26,28,30,16,18,20,22},{25..., dimensions={0} | all-to-all | bytes 2097152 | tf_op jit(solution)/shard_map/all_to_all | solution.py:168
  21.2 0.6 shard_map.28.own_ref
  21.8 0.1 collective-permute-start
  21.9 2.1 %collective-permute-done.other_ref = f32[1,1280,128]{2,1,0:T(8,128)S(1)} collective-permute-done((f32[1,1280,128]{2,1,0:T(8,128)S(1)}, f32[1,1280,128]{2,1,0:T(8,128)S(1)}, u32[]{:S(2)}, u32[]{:S(2)}) %collective-permute-start) | collective-permute-done | bytes 655392 | tf_op jit(solution)/shard_map/ppermute | solution.py:177
  24.0 0.1 shard_map.29
  24.1 2.7 %collective-permute-start.1 = (bf16[1,640,128]{2,1,0:T(8,128)(2,1)S(1)}, bf16[1,640,128]{2,1,0:T(8,128)(2,1)S(1)}, u32[]{:S(2)}, u32[]{:S(2)}) collective-permute-start(bf16[1,640,128]{2,1,0:T(8,128)(2,1)S(1)} %get-tuple-element.8), channel_id=1, source_target_pairs={{0,24},{2,26},{4,28},{6,30},{8,16},{10,18},{12,20},{14,22},{1,25},... | collective-permute-start | bytes 491528 | tf_op jit(solution)/shard_map/ppermute | solution.py:188
  26.8 5.5 %collective-permute-done.1.near_ref = bf16[1,640,128]{2,1,0:T(8,128)(2,1)S(1)} collective-permute-done((bf16[1,640,128]{2,1,0:T(8,128)(2,1)S(1)}, bf16[1,640,128]{2,1,0:T(8,128)(2,1)S(1)}, u32[]{:S(2)}, u32[]{:S(2)}) %collective-permute-start.1) | collective-permute-done | bytes 163872 | tf_op jit(solution)/shard_map/ppermute | solution.py:188
  32.3 0.0 collective-permute-start.2
  32.3 1.4 %collective-permute-done.2.far_ref = bf16[1,640,128]{2,1,0:T(8,128)(2,1)S(1)} collective-permute-done((bf16[1,640,128]{2,1,0:T(8,128)(2,1)S(1)}, bf16[1,640,128]{2,1,0:T(8,128)(2,1)S(1)}, u32[]{:S(2)}, u32[]{:S(2)}) %collective-permute-start.2) | collective-permute-done | bytes 163872 | tf_op jit(solution)/shard_map/ppermute | solution.py:189
  33.7 8.9 %shard_map.30 = bf16[1,1024,512]{2,1,0:T(8,128)(2,1)S(1)} custom-call(s32[1]{0:T(128)} %bitcast.pair_ref, f32[1,1280,128]{2,1,0:T(8,128)S(1)} %get-tuple-element.7.total_ref, bf16[1,640,128]{2,1,0:T(8,128)(2,1)S(1)} %collective-permute-done.1.near_ref, bf16[1,640,128]{2,1,0:T(8,128)(2,1)S(1)} %collective-permute-done.2.far_ref, bf16[1,1024,512]{2,1,0:T(8,128)(2,1)S(1)} %bitcast.9), custom_call_target="tpu_custom_call" | custom-call | tf_op jit(solution)/shard_map/pallas_call | solution.py:56
  42.6 0.0 copy-start
  42.7 19.1 %all_to_all.11 = bf16[8,128,512]{2,1,0:T(8,128)(2,1)S(1)} all-to-all(bf16[8,128,512]{2,1,0:T(8,128)(2,1)S(1)} %bitcast.10), channel_id=1, replica_groups={{0,2,4,6,8,10,12,14},{1,3,5,7,9,11,13,15},{24,26,28,30,16,18,20,22},{25..., dimensions={0} | all-to-all | bytes 2097152 | tf_op jit(solution)/shard_map/all_to_all | solution.py:204
  61.7 0.0 copy-done
  61.7 1.4 %fusion = bf16[1,8,128,512]{3,2,1,0:T(8,128)(2,1)} fusion(bf16[8,128,512]{2,1,0:T(8,128)(2,1)S(1)} %all_to_all.11, bf16[1,8,128,512]{3,2,1,0:T(8,128)(2,1)S(1)} %copy-done), kind=kLoop, calls=%fused_computation.1 | loop fusion | flops 3145728 | bytes 3145728 | tf_op jit(solution)/shard_map/convert_element_type | solution.py:206
Async XLA Ops:
  21.8 2.2 %collective-permute-start = (f32[1,1280,128]{2,1,0:T(8,128)S(1)}, f32[1,1280,128]{2,1,0:T(8,128)S(1)}, u32[]{:S(2)}, u32[]{:S(2)}) collective-permute-start(f32[1,1280,128]{2,1,0:T(8,128)S(1)} %shard_map.28.own_ref), channel_id=1, source_target_pairs={{0,1},{2,3},{4,5},{6,7},{8,9},{10,11},{12,13},{14,15},{1,0},{3,2},... | collective-permute-start | bytes 1966088 | tf_op jit(solution)/shard_map/ppermute | solution.py:177
  24.1 8.2 %collective-permute-start.1 = (bf16[1,640,128]{2,1,0:T(8,128)(2,1)S(1)}, bf16[1,640,128]{2,1,0:T(8,128)(2,1)S(1)}, u32[]{:S(2)}, u32[]{:S(2)}) collective-permute-start(bf16[1,640,128]{2,1,0:T(8,128)(2,1)S(1)} %get-tuple-element.8), channel_id=1, source_target_pairs={{0,24},{2,26},{4,28},{6,30},{8,16},{10,18},{12,20},{14,22},{1,25},... | collective-permute-start | bytes 491528 | tf_op jit(solution)/shard_map/ppermute | solution.py:188
  32.3 1.4 %collective-permute-start.2 = (bf16[1,640,128]{2,1,0:T(8,128)(2,1)S(1)}, bf16[1,640,128]{2,1,0:T(8,128)(2,1)S(1)}, u32[]{:S(2)}, u32[]{:S(2)}) collective-permute-start(bf16[1,640,128]{2,1,0:T(8,128)(2,1)S(1)} %collective-permute-done.1.near_ref), channel_id=1, source_target_pairs={{0,1},{2,3},{4,5},{6,7},{8,9},{10,11},{12,13},{14,15},{1,0},{3,2},... | collective-permute-start | bytes 491528 | tf_op jit(solution)/shard_map/ppermute | solution.py:189
  42.6 19.1 %copy-start = (bf16[1,8,128,512]{3,2,1,0:T(8,128)(2,1)S(1)}, bf16[1,8,128,512]{3,2,1,0:T(8,128)(2,1)}, u32[]{:S(2)}) copy-start(bf16[1,8,128,512]{3,2,1,0:T(8,128)(2,1)} %param.3) | copy-start | bytes 3145732

commit v2 on v0

v2 whole, which is shorter than its diff:
```python
import functools

import jax
import jax.numpy as jnp
from jax import lax
from jax.experimental import pallas as pl
from jax.experimental.pallas import tpu as pltpu
from jax.sharding import PartitionSpec as P

ITERS = 3
BLOCK = 128
WIDE = 256
F32_TILE = 8
BF16_TILE = 16
VMEM_BYTES = 48 << 20

first_coef = 3.4445
second_coef = -4.775
third_coef = 2.0315
epsilon = 1e-06
step_rate = 0.5
decay_rate = 0.1

AXES = ("opt", "layer")


def positions(opt, layer):
    rest_count = opt // 8
    spots = [
        (half, z, y, rest, x, pair)
        for half in range(2)
        for z in range(2)
        for y in range(2)
        for rest in range(rest_count)
        for x in range(2)
        for pair in range(2)
    ]

    def device(half, z, y, rest, x, pair):
        return (((half * 2 + z) * 2 + y) * rest_count + rest) * layer + x * 2 + pair

    def swap(flips):
        return [(device(*spot), device(*(value ^ flip for value, flip in zip(spot, flips)))) for spot in spots]

    return {
        "x": swap((0, 0, 0, 0, 1, 0)),
        "y": swap((0, 0, 1, 0, 0, 0)),
        "z": swap((0, 1, 0, 0, 0, 0)),
        "antipode": swap((0, 1, 1, 0, 1, 0)),
        "mirror": swap((1, 1, 0, 0, 0, 0)),
        "pair": swap((0, 0, 0, 0, 0, 1)),
    }


def own_place(rest_count):
    place = lax.axis_index("opt") // rest_count
    across, pair = lax.axis_index("layer") // 2, lax.axis_index("layer") % 2
    half, z, y = place // 4, place // 2 % 2, place % 2
    colour = across ^ (2 * y) ^ (3 * (z ^ half))
    return jnp.stack([colour, pair, across]).astype(jnp.int32)


def call(kernel, out_shape, place, *operands, scratch=()):
    vmem = pl.BlockSpec(memory_space=pltpu.VMEM)
    return pl.pallas_call(
        kernel,
        out_shape=out_shape,
        in_specs=[pl.BlockSpec(memory_space=pltpu.SMEM)] + [vmem] * len(operands),
        out_specs=jax.tree.map(lambda _: vmem, out_shape),
        scratch_shapes=list(scratch),
        compiler_params=pltpu.CompilerParams(vmem_limit_bytes=VMEM_BYTES),
    )(place, *operands)


def product(first, second):
    return jnp.dot(first, second, preferred_element_type=jnp.float32)


def halves_of(order):
    count = order // BLOCK
    folds = [(i, i + 1) for i in range(0, count, 2)]
    others = [(i, j) for i in range(count) for j in range(i + 1, count)]
    middle_fold, middle = len(folds) // 2, len(others) // 2
    return [(folds[:middle_fold], others[:middle]), (folds[middle_fold:], others[middle:])]


def half_blocks(order):
    folds, others = halves_of(order)[0]
    return len(folds), len(folds) + len(others)


def packed_shape(order):
    return jax.ShapeDtypeStruct((2, half_blocks(order)[1] * BLOCK + F32_TILE, BLOCK), jnp.float32)


def message_shape(order):
    return jax.ShapeDtypeStruct((half_blocks(order)[1] * BLOCK + BF16_TILE, BLOCK), jnp.bfloat16)


def grid_ids():
    shape = (BLOCK, BLOCK)
    return lax.broadcasted_iota(jnp.int32, shape, 0), lax.broadcasted_iota(jnp.int32, shape, 1)


def diagonal(block):
    row_ids, column_ids = grid_ids()
    return jnp.sum(jnp.where(row_ids == column_ids, block, 0.0), axis=0, keepdims=True)


def padded(rows, height):
    missing = height - sum(row.shape[0] for row in rows)
    return jnp.concatenate(rows + [jnp.zeros((missing, BLOCK), rows[0].dtype)], axis=0)


def pack(block, order):
    row_ids, column_ids = grid_ids()
    result = []
    for folds, others in halves_of(order):
        tiles, rows = [], []
        for i, j in folds:
            second = block(j, j)
            tiles.append(jnp.where(row_ids <= column_ids, block(i, i), second))
            rows.append(diagonal(second))
        tiles += [block(i, j) for i, j in others]
        result.append(jnp.concatenate(tiles + [padded(rows, F32_TILE)], axis=0))
    return result


def unpack(halves, order):
    row_ids, column_ids = grid_ids()
    blocks = {}
    for (folds, others), half in zip(halves_of(order), halves):
        tiles = [half[k * BLOCK : (k + 1) * BLOCK] for k in range(len(folds) + len(others))]
        tail = half[len(tiles) * BLOCK :]
        for k, (i, j) in enumerate(folds):
            mirrored = tiles[k].T
            blocks[i, i] = jnp.where(row_ids <= column_ids, tiles[k], mirrored)
            second = jnp.where(row_ids > column_ids, tiles[k], mirrored)
            blocks[j, j] = jnp.where(row_ids == column_ids, tail[k : k + 1], second)
        for k, (i, j) in enumerate(others):
            blocks[i, j] = tiles[len(folds) + k]
    return blocks


def to_message(half, order):
    fold_count, block_count = half_blocks(order)
    length = block_count * BLOCK
    body, tail = half[:length], half[length : length + fold_count]
    rounded = body.astype(jnp.bfloat16)
    rows = [
        diagonal(
            body[k * BLOCK : (k + 1) * BLOCK] - rounded[k * BLOCK : (k + 1) * BLOCK].astype(jnp.float32)
        )
        for k in range(fold_count)
    ]
    high = tail.astype(jnp.bfloat16).astype(jnp.float32)
    extra = padded(rows + [high, tail - high], BF16_TILE)
    return jnp.concatenate([rounded, extra.astype(jnp.bfloat16)], axis=0)


def from_message(message, order):
    fold_count, block_count = half_blocks(order)
    length = block_count * BLOCK
    row_ids, column_ids = grid_ids()
    values = message.astype(jnp.float32)
    body, extra = values[:length], values[length:]
    tiles = [
        body[k * BLOCK : (k + 1) * BLOCK] + jnp.where(row_ids == column_ids, extra[k : k + 1], 0.0)
        for k in range(fold_count)
    ]
    tail = extra[fold_count : 2 * fold_count] + extra[2 * fold_count : 3 * fold_count]
    return jnp.concatenate(tiles + [body[fold_count * BLOCK :], padded([tail], F32_TILE)], axis=0)


def deal_kernel(place_ref, momentum_ref, *piece_refs):
    for step, piece_ref in enumerate(piece_refs):
        piece_ref[...] = momentum_ref[place_ref[0] ^ (step + 1)]


def expert_rows(place_ref, momentum_ref, piece_refs, expert):
    count = momentum_ref.shape[1] // 2
    span = pl.ds(pl.multiple_of(expert * count, count), count)
    return [momentum_ref[place_ref[0], span, :]] + [piece_ref[span, :] for piece_ref in piece_refs]


def gram_kernel(place_ref, momentum_ref, x_ref, y_ref, z_ref, kept_ref, sent_ref):
    order = momentum_ref.shape[2]
    pair = place_ref[1]
    for expert, out_ref in ((1 - pair, sent_ref), (pair, kept_ref)):
        rows = jnp.concatenate(expert_rows(place_ref, momentum_ref, (x_ref, y_ref, z_ref), expert), axis=0)
        tiles = {}
        for row in range(0, order, WIDE):
            for column in range(row, order, WIDE):
                tiles[row, column] = lax.dot_general(
                    rows[:, row : row + WIDE],
                    rows[:, column : column + WIDE],
                    (((0,), (0,)), ((), ())),
                    preferred_element_type=jnp.float32,
                )

        def block(i, j):
            row, column = i * BLOCK, j * BLOCK
            tile = tiles[row // WIDE * WIDE, column // WIDE * WIDE]
            return tile[row % WIDE :, column % WIDE :][:BLOCK, :BLOCK]

        for half, value in enumerate(pack(block, order)):
            out_ref[half] = value


def place_sum_kernel(order, place_ref, own_ref, other_ref, sum_ref, message_ref):
    sum_ref[...] = own_ref[...] + other_ref[...]
    message_ref[...] = to_message(sum_ref[1 - place_ref[2]], order)


def cube_sum_kernel(order, place_ref, sum_ref, arrived_ref, half_ref, message_ref):
    half = sum_ref[place_ref[2]] + from_message(arrived_ref[...], order)
    half_ref[...] = half
    message_ref[...] = to_message(half, order)


def total_kernel(order, place_ref, half_ref, arrived_ref, far_ref, total_ref, message_ref):
    total = half_ref[...] + from_message(far_ref[...], order)
    total_ref[...] = total
    message_ref[...] = to_message(total - from_message(arrived_ref[...], order), order)


def split(matrix):
    high = matrix.astype(jnp.bfloat16)
    return high, (matrix - high.astype(jnp.float32)).astype(jnp.bfloat16)


def product_of_split(first, second):
    return product(first[0], second[0]) + (product(first[0], second[1]) + product(first[1], second[0]))


def assemble(upper, count):
    return jnp.concatenate(
        [
            jnp.concatenate([upper[i, j] if i <= j else upper[j, i].T for j in range(count)], axis=1)
            for i in range(count)
        ],
        axis=0,
    )


def split_whole(upper, count):
    parts = {key: split(value) for key, value in upper.items()}
    return tuple(assemble({key: value[part] for key, value in parts.items()}, count) for part in range(2))


def symmetric_product(first, second, count):
    size = first[0].shape[0] // count
    return {
        (i, j): product_of_split(
            tuple(part[i * size : (i + 1) * size, :] for part in first),
            tuple(part[:, j * size : (j + 1) * size] for part in second),
        )
        for i in range(count)
        for j in range(i, count)
    }


def newton(current, count):
    size = current[0, 0].shape[0]
    shape = (size, size)
    identity = lax.broadcasted_iota(jnp.int32, shape, 0) == lax.broadcasted_iota(jnp.int32, shape, 1)
    accum = None
    for iteration in range(ITERS):
        halves = split_whole(current, count)
        squared = symmetric_product(halves, halves, count)
        polynomial = {
            (i, j): (jnp.where(identity, first_coef, 0.0) if i == j else 0.0)
            + second_coef * current[i, j]
            + third_coef * squared[i, j]
            for i, j in current
        }
        poly_halves = split_whole(polynomial, count)
        if accum is None:
            accum = polynomial
        else:
            accum = symmetric_product(split_whole(accum, count), poly_halves, count)
        if iteration + 1 < ITERS:
            inner = symmetric_product(halves, poly_halves, count)
            current = symmetric_product(split_whole(inner, count), poly_halves, count)
    return accum


def factor_kernel(order, scale, place_ref, sum_ref, total_ref, rest_ref, factor_ref):
    kept = place_ref[2]
    total = total_ref[...]
    other = sum_ref[1 - kept] + from_message(rest_ref[...], order)
    halves = [jnp.where(kept == 0, total, other), jnp.where(kept == 0, other, total)]
    blocks = unpack(halves, order)
    trace_row = sum(diagonal(blocks[i, i]) for i in range(order // BLOCK))
    trace_sum = jnp.sum(trace_row)
    count, ratio = order // WIDE, WIDE // BLOCK
    current = {}
    for i in range(count):
        for j in range(i, count):
            tile = jnp.concatenate(
                [
                    jnp.concatenate(
                        [
                            blocks[row, column] if row <= column else blocks[column, row].T
                            for column in range(j * ratio, (j + 1) * ratio)
                        ],
                        axis=1,
                    )
                    for row in range(i * ratio, (i + 1) * ratio)
                ],
                axis=0,
            )
            current[i, j] = tile / (trace_sum + epsilon)
    accum = newton(current, count)
    growth = jnp.sqrt(scale / (trace_sum + epsilon))
    factor_ref[...] = assemble(
        {key: (value * growth).astype(jnp.bfloat16) for key, value in accum.items()}, count
    )


def update_kernel(place_ref, own_ref, other_ref, momentum_ref, x_ref, y_ref, z_ref, *update_refs):
    pair = place_ref[1]
    count = momentum_ref.shape[1] // 2
    for expert, factor_ref in ((pair, own_ref), (1 - pair, other_ref)):
        rows = jnp.concatenate(expert_rows(place_ref, momentum_ref, (x_ref, y_ref, z_ref), expert), axis=0)
        update = product(rows, factor_ref[...]).astype(jnp.bfloat16)
        span = pl.ds(pl.multiple_of(expert * count, count), count)
        for step, update_ref in enumerate(update_refs):
            update_ref[span, :] = update[step * count : (step + 1) * count]


def weights_kernel(place_ref, weights_ref, *refs):
    update_refs, out_ref = refs[:-1], refs[-1]
    shrink = 1.0 - step_rate * decay_rate
    for step, update_ref in enumerate(update_refs):
        colour = place_ref[0] ^ step
        out_ref[colour] = (
            shrink * weights_ref[colour].astype(jnp.float32) - step_rate * update_ref[...].astype(jnp.float32)
        ).astype(out_ref.dtype)


def on_device(momentum, weights):
    order = momentum.shape[3]
    opt, layer = lax.axis_size("opt"), lax.axis_size("layer")
    rest_count = opt // 8
    swaps = positions(opt, layer)
    place = own_place(rest_count)
    rest_groups = [[group * rest_count + rest for rest in range(rest_count)] for group in range(8)]

    def regroup(array, split_axis, concat_axis):
        if rest_count == 1:
            return array
        return lax.all_to_all(
            array,
            "opt",
            split_axis=split_axis,
            concat_axis=concat_axis,
            axis_index_groups=rest_groups,
            tiled=True,
        )

    def move(array, way):
        return lax.ppermute(array, AXES, swaps[way])

    spread = regroup(momentum[0], 0, 1)
    experts, row_count, _ = spread.shape
    by_colour = (experts // 2, 2 * row_count, order)
    spread = spread.reshape(by_colour)
    piece = jax.ShapeDtypeStruct(by_colour[1:], spread.dtype)
    packed, message = packed_shape(order), message_shape(order)
    half = jax.ShapeDtypeStruct(packed.shape[1:], packed.dtype)

    dealt = call(deal_kernel, (piece,) * 3, place, spread)
    arrived = [move(array, way) for array, way in zip(dealt, "xyz")]
    kept, sent = call(gram_kernel, (packed, packed), place, spread, *arrived)
    place_sum, first = call(
        functools.partial(place_sum_kernel, order), (packed, message), place, kept, move(sent, "pair")
    )
    near = move(first, "antipode")
    cube_half, second = call(
        functools.partial(cube_sum_kernel, order), (half, message), place, place_sum, near
    )
    total, third = call(
        functools.partial(total_kernel, order),
        (half, message),
        place,
        cube_half,
        near,
        move(second, "mirror"),
    )
    factor = call(
        functools.partial(factor_kernel, order, float(layer * opt * momentum.shape[2])),
        jax.ShapeDtypeStruct((order, order), jnp.bfloat16),
        place,
        place_sum,
        total,
        move(third, "antipode"),
    )
    updates = call(
        update_kernel, (piece,) * 4, place, factor, move(factor, "pair"), spread, *arrived
    )
    returned = [move(array, way) for array, way in zip(updates[1:], "xyz")]
    fresh = call(
        weights_kernel,
        jax.ShapeDtypeStruct(by_colour, weights.dtype),
        place,
        regroup(weights[0], 0, 1).reshape(by_colour),
        updates[0],
        *returned,
    )
    return regroup(fresh.reshape(experts, row_count, order), 1, 0)[None]


def solution(mesh):
    in_specs = (P("layer", None, "opt", None), P("layer", None, "opt", None))
    out_specs = P("layer", None, "opt", None)
    return jax.shard_map(
        on_device, mesh=mesh, in_specs=in_specs, out_specs=out_specs, check_vma=False
    )
```

time: 150 us -> 62.2 us (0.41)
  blocking collectives: 70 us -> 0 us
  matrix products: 22.6 us -> 0 us
  starting transfers between devices: 0.01 us -> 17.3 us
  between operations: 14.2 us -> 0.07 us
  Pallas kernels: 0 us -> 13.9 us
  other arithmetic: 11.8 us -> 0.08 us
  local copies, waits for them, and re-layouts: 4.33 us -> 1.24 us
  waiting for transfers between devices: 27.1 us -> 29.5 us
    all_to_all x2 -> x0, blocking collectives: 63.7 us -> none  [the longest x1 33 us: on_device(): lax.all_to_all(momentum, 'opt', split_axis=1, concat_axis=2, tiled=True)[0]]
    ppermute x0 -> x11, waiting for transfers between devices: none -> 29.5 us  [move(): return lax.ppermute(array, AXES, swaps[way])]
    psum x1 -> x0, waiting for transfers between devices: 27.1 us -> none  [on_device(): gram_sum = lax.psum(gram_local, 'layer')]
    dot_general x12 -> x0, matrix products: 22.6 us -> none  [the longest x10 20.2 us: batched(): jnp.einsum('erk,ekc->erc', first_matrix, second_matrix, precision=lax.Pre...]
    ppermute x0 -> x11, starting transfers between devices: none -> 17.3 us  [move(): return lax.ppermute(array, AXES, swaps[way])]
    pallas_call x0 -> x8, Pallas kernels: none -> 13.9 us  [call(): pl.pallas_call(kernel, out_shape=out_shape, in_specs=[pl.BlockSpec(memory...]
    unnamed x1 -> x0, other arithmetic: 7.04 us -> none
    psum x1 -> x0, blocking collectives: 6.31 us -> none  [square_total(): return lax.psum(squares, 'layer')]
  transfers between devices with their start and end apart: 1 -> 11, of which waited for: 1 -> 11; matrix products, arithmetic and copies ran while one was open for 1% -> 0% of each run, Pallas kernels for 0% -> 0%
where the time goes in v2:
time: 62.2 us; the launch traced here: 62.1 us
  waiting for transfers between devices  29.5 us (47%)
  starting transfers between devices  17.3 us (28%)
  Pallas kernels  13.9 us (22%)
  local copies, waits for them, and re-layouts  1.24 us (2%)
    ppermute x11, waiting for transfers between devices, move(): return lax.ppermute(array, AXES, swaps[way])  29.5 us
    ppermute x11, starting transfers between devices, move(): return lax.ppermute(array, AXES, swaps[way])  17.3 us
    pallas_call x8, Pallas kernels, call(): pl.pallas_call(kernel, out_shape=out_shape, in_specs=[pl.BlockSpec(memory...  13.9 us
  transfers between devices with their start and end apart: 11, of which 11 were waited for; matrix products, arithmetic and copies ran while one was open for 0% of the time, Pallas kernels for 0%

profile of v2, /device:TPU:0, one launch (start us, length us, event | category | flops | bytes accessed | tf_op | source)
XLA Modules:
  0.0 62.1 jit_solution(18436628973566838047)
XLA Ops:
  0.0 0.1 pad_add_fusion.place_ref
  0.1 1.2 %copy-done = bf16[1,8,128,512]{3,2,1,0:T(8,128)(2,1)S(1)} copy-done((bf16[1,8,128,512]{3,2,1,0:T(8,128)(2,1)S(1)}, bf16[1,8,128,512]{3,2,1,0:T(8,128)(2,1)}, u32[]{:S(2)}) %copy-start) | copy-done | bytes 1048600
  1.3 0.6 shard_map.28
  1.9 3.0 %collective-permute-start = (bf16[256,512]{1,0:T(8,128)(2,1)S(1)}, bf16[256,512]{1,0:T(8,128)(2,1)S(1)}, u32[]{:S(2)}, u32[]{:S(2)}) collective-permute-start(bf16[256,512]{1,0:T(8,128)(2,1)S(1)} %get-tuple-element.20), channel_id=1, source_target_pairs={{0,2},{1,3},{2,0},{3,1},{4,6},{5,7},{6,4},{7,5},{8,10},{9,11},{10,... | collective-permute-start | bytes 786440 | tf_op jit(solution)/shard_map/ppermute | solution.py:363
  4.9 1.5 %collective-permute-start.1 = (bf16[256,512]{1,0:T(8,128)(2,1)S(1)}, bf16[256,512]{1,0:T(8,128)(2,1)S(1)}, u32[]{:S(2)}, u32[]{:S(2)}) collective-permute-start(bf16[256,512]{1,0:T(8,128)(2,1)S(1)} %get-tuple-element.21), channel_id=1, source_target_pairs={{0,4},{1,5},{2,6},{3,7},{4,0},{5,1},{6,2},{7,3},{8,12},{9,13},{10,... | collective-permute-start | bytes 786440 | tf_op jit(solution)/shard_map/ppermute | solution.py:363
  6.4 1.6 %collective-permute-start.2 = (bf16[256,512]{1,0:T(8,128)(2,1)S(1)}, bf16[256,512]{1,0:T(8,128)(2,1)S(1)}, u32[]{:S(2)}, u32[]{:S(2)}) collective-permute-start(bf16[256,512]{1,0:T(8,128)(2,1)S(1)} %get-tuple-element.22), channel_id=1, source_target_pairs={{0,8},{1,9},{2,10},{3,11},{4,12},{5,13},{6,14},{7,15},{8,0},{9,1},... | collective-permute-start | bytes 786440 | tf_op jit(solution)/shard_map/ppermute | solution.py:363
  8.0 3.2 %collective-permute-done.x_ref = bf16[256,512]{1,0:T(8,128)(2,1)S(1)} collective-permute-done((bf16[256,512]{1,0:T(8,128)(2,1)S(1)}, bf16[256,512]{1,0:T(8,128)(2,1)S(1)}, u32[]{:S(2)}, u32[]{:S(2)}) %collective-permute-start) | collective-permute-done | bytes 262176 | tf_op jit(solution)/shard_map/ppermute | solution.py:363
  11.2 1.5 %collective-permute-done.1.y_ref = bf16[256,512]{1,0:T(8,128)(2,1)S(1)} collective-permute-done((bf16[256,512]{1,0:T(8,128)(2,1)S(1)}, bf16[256,512]{1,0:T(8,128)(2,1)S(1)}, u32[]{:S(2)}, u32[]{:S(2)}) %collective-permute-start.1) | collective-permute-done | bytes 262176 | tf_op jit(solution)/shard_map/ppermute | solution.py:363
  12.7 1.2 %collective-permute-done.2.z_ref = bf16[256,512]{1,0:T(8,128)(2,1)S(1)} collective-permute-done((bf16[256,512]{1,0:T(8,128)(2,1)S(1)}, bf16[256,512]{1,0:T(8,128)(2,1)S(1)}, u32[]{:S(2)}, u32[]{:S(2)}) %collective-permute-start.2) | collective-permute-done | bytes 262176 | tf_op jit(solution)/shard_map/ppermute | solution.py:363
  13.9 1.2 %shard_map.29 = (f32[2,520,128]{2,1,0:T(8,128)S(1)}, f32[2,520,128]{2,1,0:T(8,128)S(1)}) custom-call(s32[3]{0:T(128)S(1)} %pad_add_fusion.place_ref, bf16[4,256,512]{2,1,0:T(8,128)(2,1)S(1)} %bitcast.7, bf16[256,512]{1,0:T(8,128)(2,1)S(1)} %collective-permute-done.x_ref, bf16[256,512]{1,0:T(8,128)(2,1)S(1)} %collective-permute-done.1.y_ref, ...), custom_call_target="tpu_custom_call" | custom-call | tf_op jit(solution)/shard_map/pallas_call | solution.py:65
  15.1 0.1 collective-permute-start.3
  15.2 1.9 %collective-permute-done.3.other_ref = f32[2,520,128]{2,1,0:T(8,128)S(1)} collective-permute-done((f32[2,520,128]{2,1,0:T(8,128)S(1)}, f32[2,520,128]{2,1,0:T(8,128)S(1)}, u32[]{:S(2)}, u32[]{:S(2)}) %collective-permute-start.3) | collective-permute-done | bytes 532512 | tf_op jit(solution)/shard_map/ppermute | solution.py:363
  17.1 0.6 %shard_map.30 = (f32[2,520,128]{2,1,0:T(8,128)S(1)}, bf16[528,128]{1,0:T(8,128)(2,1)S(1)}) custom-call(s32[3]{0:T(128)S(1)} %pad_add_fusion.place_ref, f32[2,520,128]{2,1,0:T(8,128)S(1)} %get-tuple-element.23.own_ref, f32[2,520,128]{2,1,0:T(8,128)S(1)} %collective-permute-done.3.other_ref), custom_call_target="tpu_custom_call" | custom-call | tf_op jit(solution)/shard_map/pallas_call | solution.py:65
  17.7 1.6 %collective-permute-start.4 = (bf16[528,128]{1,0:T(8,128)(2,1)S(1)}, bf16[528,128]{1,0:T(8,128)(2,1)S(1)}, u32[]{:S(2)}, u32[]{:S(2)}) collective-permute-start(bf16[528,128]{1,0:T(8,128)(2,1)S(1)} %get-tuple-element.26), channel_id=1, source_target_pairs={{0,14},{1,15},{2,12},{3,13},{4,10},{5,11},{6,8},{7,9},{8,6},{9,7},... | collective-permute-start | bytes 405512 | tf_op jit(solution)/shard_map/ppermute | solution.py:363
  19.2 5.9 %collective-permute-done.4.arrived_ref = bf16[528,128]{1,0:T(8,128)(2,1)S(1)} collective-permute-done((bf16[528,128]{1,0:T(8,128)(2,1)S(1)}, bf16[528,128]{1,0:T(8,128)(2,1)S(1)}, u32[]{:S(2)}, u32[]{:S(2)}) %collective-permute-start.4) | collective-permute-done | bytes 135200 | tf_op jit(solution)/shard_map/ppermute | solution.py:363
  25.2 0.6 shard_map.31
  25.8 3.7 %collective-permute-start.5 = (bf16[528,128]{1,0:T(8,128)(2,1)S(1)}, bf16[528,128]{1,0:T(8,128)(2,1)S(1)}, u32[]{:S(2)}, u32[]{:S(2)}) collective-permute-start(bf16[528,128]{1,0:T(8,128)(2,1)S(1)} %get-tuple-element.28), channel_id=1, source_target_pairs={{0,24},{1,25},{2,26},{3,27},{4,28},{5,29},{6,30},{7,31},{8,16},{9,... | collective-permute-start | bytes 405512 | tf_op jit(solution)/shard_map/ppermute | solution.py:363
  29.5 3.3 %collective-permute-done.5.far_ref = bf16[528,128]{1,0:T(8,128)(2,1)S(1)} collective-permute-done((bf16[528,128]{1,0:T(8,128)(2,1)S(1)}, bf16[528,128]{1,0:T(8,128)(2,1)S(1)}, u32[]{:S(2)}, u32[]{:S(2)}) %collective-permute-start.5) | collective-permute-done | bytes 135200 | tf_op jit(solution)/shard_map/ppermute | solution.py:363
  32.7 0.6 %shard_map.32 = (f32[520,128]{1,0:T(8,128)S(1)}, bf16[528,128]{1,0:T(8,128)(2,1)S(1)}) custom-call(s32[3]{0:T(128)S(1)} %pad_add_fusion.place_ref, f32[520,128]{1,0:T(8,128)S(1)} %get-tuple-element.27.half_ref, bf16[528,128]{1,0:T(8,128)(2,1)S(1)} %collective-permute-done.4.arrived_ref, bf16[528,128]{1,0:T(8,128)(2,1)S(1)} %collective-permute-done.5.far_ref), custom_call_target="tpu_custom_call" | custom-call | tf_op jit(solution)/shard_map/pallas_call | solution.py:65
  33.4 2.4 %collective-permute-start.6 = (bf16[528,128]{1,0:T(8,128)(2,1)S(1)}, bf16[528,128]{1,0:T(8,128)(2,1)S(1)}, u32[]{:S(2)}, u32[]{:S(2)}) collective-permute-start(bf16[528,128]{1,0:T(8,128)(2,1)S(1)} %get-tuple-element.30), channel_id=1, source_target_pairs={{0,14},{1,15},{2,12},{3,13},{4,10},{5,11},{6,8},{7,9},{8,6},{9,7},... | collective-permute-start | bytes 405512 | tf_op jit(solution)/shard_map/ppermute | solution.py:363
  35.7 4.5 %collective-permute-done.6.rest_ref = bf16[528,128]{1,0:T(8,128)(2,1)S(1)} collective-permute-done((bf16[528,128]{1,0:T(8,128)(2,1)S(1)}, bf16[528,128]{1,0:T(8,128)(2,1)S(1)}, u32[]{:S(2)}, u32[]{:S(2)}) %collective-permute-start.6) | collective-permute-done | bytes 135200 | tf_op jit(solution)/shard_map/ppermute | solution.py:363
  40.2 7.2 %shard_map.33.own_ref = bf16[512,512]{1,0:T(8,128)(2,1)S(1)} custom-call(s32[3]{0:T(128)S(1)} %pad_add_fusion.place_ref, f32[2,520,128]{2,1,0:T(8,128)S(1)} %get-tuple-element.25.sum_ref, f32[520,128]{1,0:T(8,128)S(1)} %get-tuple-element.29.total_ref, bf16[528,128]{1,0:T(8,128)(2,1)S(1)} %collective-permute-done.6.rest_ref), custom_call_target="tpu_custom_call" | custom-call | tf_op jit(solution)/shard_map/pallas_call | solution.py:65
  47.4 0.1 collective-permute-start.7
  47.5 1.9 %collective-permute-done.7.other_ref = bf16[512,512]{1,0:T(8,128)(2,1)S(1)} collective-permute-done((bf16[512,512]{1,0:T(8,128)(2,1)S(1)}, bf16[512,512]{1,0:T(8,128)(2,1)S(1)}, u32[]{:S(2)}, u32[]{:S(2)}) %collective-permute-start.7) | collective-permute-done | bytes 524320 | tf_op jit(solution)/shard_map/ppermute | solution.py:363
  49.4 1.2 %shard_map.34 = (bf16[256,512]{1,0:T(8,128)(2,1)S(1)}, bf16[256,512]{1,0:T(8,128)(2,1)S(1)}, bf16[256,512]{1,0:T(8,128)(2,1)S(1)}, bf16[256,512]{1,0:T(8,128)(2,1)S(1)}) custom-call(s32[3]{0:T(128)S(1)} %pad_add_fusion.place_ref, bf16[512,512]{1,0:T(8,128)(2,1)S(1)} %shard_map.33.own_ref, bf16[512,512]{1,0:T(8,128)(2,1)S(1)} %collective-permute-done.7.other_ref, ...), custom_call_target="tpu_custom_call" | custom-call | tf_op jit(solution)/shard_map/pallas_call | solution.py:65
  50.6 0.6 collective-permute-start.8
  51.2 1.0 %collective-permute-start.9 = (bf16[256,512]{1,0:T(8,128)(2,1)S(1)}, bf16[256,512]{1,0:T(8,128)(2,1)S(1)}, u32[]{:S(2)}, u32[]{:S(2)}) collective-permute-start(bf16[256,512]{1,0:T(8,128)(2,1)S(1)} %get-tuple-element.33), channel_id=1, source_target_pairs={{0,4},{1,5},{2,6},{3,7},{4,0},{5,1},{6,2},{7,3},{8,12},{9,13},{10,... | collective-permute-start | bytes 786440 | tf_op jit(solution)/shard_map/ppermute | solution.py:363
  52.2 1.9 %collective-permute-start.10 = (bf16[256,512]{1,0:T(8,128)(2,1)S(1)}, bf16[256,512]{1,0:T(8,128)(2,1)S(1)}, u32[]{:S(2)}, u32[]{:S(2)}) collective-permute-start(bf16[256,512]{1,0:T(8,128)(2,1)S(1)} %get-tuple-element.34), channel_id=1, source_target_pairs={{0,8},{1,9},{2,10},{3,11},{4,12},{5,13},{6,14},{7,15},{8,0},{9,1},... | collective-permute-start | bytes 786440 | tf_op jit(solution)/shard_map/ppermute | solution.py:363
  54.1 4.9 %collective-permute-done.8.refs_1_ = bf16[256,512]{1,0:T(8,128)(2,1)S(1)} collective-permute-done((bf16[256,512]{1,0:T(8,128)(2,1)S(1)}, bf16[256,512]{1,0:T(8,128)(2,1)S(1)}, u32[]{:S(2)}, u32[]{:S(2)}) %collective-permute-start.8) | collective-permute-done | bytes 262176 | tf_op jit(solution)/shard_map/ppermute | solution.py:363
  59.0 0.3 collective-permute-done.9.refs_2_
  59.3 0.9 %collective-permute-done.10.refs_3_ = bf16[256,512]{1,0:T(8,128)(2,1)S(1)} collective-permute-done((bf16[256,512]{1,0:T(8,128)(2,1)S(1)}, bf16[256,512]{1,0:T(8,128)(2,1)S(1)}, u32[]{:S(2)}, u32[]{:S(2)}) %collective-permute-start.10) | collective-permute-done | bytes 262176 | tf_op jit(solution)/shard_map/ppermute | solution.py:363
  60.2 1.9 %shard_map.35 = bf16[4,256,512]{2,1,0:T(8,128)(2,1)} custom-call(s32[3]{0:T(128)S(1)} %pad_add_fusion.place_ref, bf16[4,256,512]{2,1,0:T(8,128)(2,1)S(1)} %bitcast.9, bf16[256,512]{1,0:T(8,128)(2,1)S(1)} %get-tuple-element.31.refs_0_, bf16[256,512]{1,0:T(8,128)(2,1)S(1)} %collective-permute-done.8.refs_1_, ...), custom_call_target="tpu_custom_call" | custom-call | tf_op jit(solution)/shard_map/pallas_call | solution.py:65
  (5 shorter events, 0.0 us)
Async XLA Ops:
  0.1 1.2 %copy-start = (bf16[1,8,128,512]{3,2,1,0:T(8,128)(2,1)S(1)}, bf16[1,8,128,512]{3,2,1,0:T(8,128)(2,1)}, u32[]{:S(2)}) copy-start(bf16[1,8,128,512]{3,2,1,0:T(8,128)(2,1)} %param.2) | copy-start | bytes 3145732
  1.9 9.3 %collective-permute-start = (bf16[256,512]{1,0:T(8,128)(2,1)S(1)}, bf16[256,512]{1,0:T(8,128)(2,1)S(1)}, u32[]{:S(2)}, u32[]{:S(2)}) collective-permute-start(bf16[256,512]{1,0:T(8,128)(2,1)S(1)} %get-tuple-element.20), channel_id=1, source_target_pairs={{0,2},{1,3},{2,0},{3,1},{4,6},{5,7},{6,4},{7,5},{8,10},{9,11},{10,... | collective-permute-start | bytes 786440 | tf_op jit(solution)/shard_map/ppermute | solution.py:363
  4.9 7.8 %collective-permute-start.1 = (bf16[256,512]{1,0:T(8,128)(2,1)S(1)}, bf16[256,512]{1,0:T(8,128)(2,1)S(1)}, u32[]{:S(2)}, u32[]{:S(2)}) collective-permute-start(bf16[256,512]{1,0:T(8,128)(2,1)S(1)} %get-tuple-element.21), channel_id=1, source_target_pairs={{0,4},{1,5},{2,6},{3,7},{4,0},{5,1},{6,2},{7,3},{8,12},{9,13},{10,... | collective-permute-start | bytes 786440 | tf_op jit(solution)/shard_map/ppermute | solution.py:363
  6.4 7.5 %collective-permute-start.2 = (bf16[256,512]{1,0:T(8,128)(2,1)S(1)}, bf16[256,512]{1,0:T(8,128)(2,1)S(1)}, u32[]{:S(2)}, u32[]{:S(2)}) collective-permute-start(bf16[256,512]{1,0:T(8,128)(2,1)S(1)} %get-tuple-element.22), channel_id=1, source_target_pairs={{0,8},{1,9},{2,10},{3,11},{4,12},{5,13},{6,14},{7,15},{8,0},{9,1},... | collective-permute-start | bytes 786440 | tf_op jit(solution)/shard_map/ppermute | solution.py:363
  15.1 2.0 %collective-permute-start.3 = (f32[2,520,128]{2,1,0:T(8,128)S(1)}, f32[2,520,128]{2,1,0:T(8,128)S(1)}, u32[]{:S(2)}, u32[]{:S(2)}) collective-permute-start(f32[2,520,128]{2,1,0:T(8,128)S(1)} %get-tuple-element.24), channel_id=1, source_target_pairs={{0,1},{1,0},{2,3},{3,2},{4,5},{5,4},{6,7},{7,6},{8,9},{9,8},{10,11... | collective-permute-start | bytes 1597448 | tf_op jit(solution)/shard_map/ppermute | solution.py:363
  17.7 7.5 %collective-permute-start.4 = (bf16[528,128]{1,0:T(8,128)(2,1)S(1)}, bf16[528,128]{1,0:T(8,128)(2,1)S(1)}, u32[]{:S(2)}, u32[]{:S(2)}) collective-permute-start(bf16[528,128]{1,0:T(8,128)(2,1)S(1)} %get-tuple-element.26), channel_id=1, source_target_pairs={{0,14},{1,15},{2,12},{3,13},{4,10},{5,11},{6,8},{7,9},{8,6},{9,7},... | collective-permute-start | bytes 405512 | tf_op jit(solution)/shard_map/ppermute | solution.py:363
  25.8 23.6 %copy-start.1 = (bf16[1,8,128,512]{3,2,1,0:T(8,128)(2,1)S(1)}, bf16[1,8,128,512]{3,2,1,0:T(8,128)(2,1)}, u32[]{:S(2)}) copy-start(bf16[1,8,128,512]{3,2,1,0:T(8,128)(2,1)} %param.2) | copy-start | bytes 3145732
  25.8 6.9 %collective-permute-start.5 = (bf16[528,128]{1,0:T(8,128)(2,1)S(1)}, bf16[528,128]{1,0:T(8,128)(2,1)S(1)}, u32[]{:S(2)}, u32[]{:S(2)}) collective-permute-start(bf16[528,128]{1,0:T(8,128)(2,1)S(1)} %get-tuple-element.28), channel_id=1, source_target_pairs={{0,24},{1,25},{2,26},{3,27},{4,28},{5,29},{6,30},{7,31},{8,16},{9,... | collective-permute-start | bytes 405512 | tf_op jit(solution)/shard_map/ppermute | solution.py:363
  33.4 6.9 %collective-permute-start.6 = (bf16[528,128]{1,0:T(8,128)(2,1)S(1)}, bf16[528,128]{1,0:T(8,128)(2,1)S(1)}, u32[]{:S(2)}, u32[]{:S(2)}) collective-permute-start(bf16[528,128]{1,0:T(8,128)(2,1)S(1)} %get-tuple-element.30), channel_id=1, source_target_pairs={{0,14},{1,15},{2,12},{3,13},{4,10},{5,11},{6,8},{7,9},{8,6},{9,7},... | collective-permute-start | bytes 405512 | tf_op jit(solution)/shard_map/ppermute | solution.py:363
  47.4 12.8 %copy-start.2 = (bf16[1,8,128,512]{3,2,1,0:T(8,128)(2,1)S(1)}, bf16[1,8,128,512]{3,2,1,0:T(8,128)(2,1)}, u32[]{:S(2)}) copy-start(bf16[1,8,128,512]{3,2,1,0:T(8,128)(2,1)} %param.3) | copy-start | bytes 3145732
  47.4 2.0 %collective-permute-start.7 = (bf16[512,512]{1,0:T(8,128)(2,1)S(1)}, bf16[512,512]{1,0:T(8,128)(2,1)S(1)}, u32[]{:S(2)}, u32[]{:S(2)}) collective-permute-start(bf16[512,512]{1,0:T(8,128)(2,1)S(1)} %shard_map.33.own_ref), channel_id=1, source_target_pairs={{0,1},{1,0},{2,3},{3,2},{4,5},{5,4},{6,7},{7,6},{8,9},{9,8},{10,11... | collective-permute-start | bytes 1572872 | tf_op jit(solution)/shard_map/ppermute | solution.py:363
  50.6 8.4 %collective-permute-start.8 = (bf16[256,512]{1,0:T(8,128)(2,1)S(1)}, bf16[256,512]{1,0:T(8,128)(2,1)S(1)}, u32[]{:S(2)}, u32[]{:S(2)}) collective-permute-start(bf16[256,512]{1,0:T(8,128)(2,1)S(1)} %get-tuple-element.32), channel_id=1, source_target_pairs={{0,2},{1,3},{2,0},{3,1},{4,6},{5,7},{6,4},{7,5},{8,10},{9,11},{10,... | collective-permute-start | bytes 786440 | tf_op jit(solution)/shard_map/ppermute | solution.py:363
  51.2 8.1 %collective-permute-start.9 = (bf16[256,512]{1,0:T(8,128)(2,1)S(1)}, bf16[256,512]{1,0:T(8,128)(2,1)S(1)}, u32[]{:S(2)}, u32[]{:S(2)}) collective-permute-start(bf16[256,512]{1,0:T(8,128)(2,1)S(1)} %get-tuple-element.33), channel_id=1, source_target_pairs={{0,4},{1,5},{2,6},{3,7},{4,0},{5,1},{6,2},{7,3},{8,12},{9,13},{10,... | collective-permute-start | bytes 786440 | tf_op jit(solution)/shard_map/ppermute | solution.py:363
  52.2 8.0 %collective-permute-start.10 = (bf16[256,512]{1,0:T(8,128)(2,1)S(1)}, bf16[256,512]{1,0:T(8,128)(2,1)S(1)}, u32[]{:S(2)}, u32[]{:S(2)}) collective-permute-start(bf16[256,512]{1,0:T(8,128)(2,1)S(1)} %get-tuple-element.34), channel_id=1, source_target_pairs={{0,8},{1,9},{2,10},{3,11},{4,12},{5,13},{6,14},{7,15},{8,0},{9,1},... | collective-permute-start | bytes 786440 | tf_op jit(solution)/shard_map/ppermute | solution.py:363

commit v3 on v2

v3 whole, which is shorter than its diff:
```python
import functools
import itertools

import jax
import jax.numpy as jnp
from jax import lax
from jax.experimental import pallas as pl
from jax.experimental.pallas import tpu as pltpu
from jax.sharding import PartitionSpec as P

ITERS = 3
BLOCK = 128
WIDE = 256
F32_TILE = 8
BF16_TILE = 16
VMEM_BYTES = 48 << 20

first_coef = 3.4445
second_coef = -4.775
third_coef = 2.0315
epsilon = 1e-06
step_rate = 0.5
decay_rate = 0.1

AXES = ("opt", "layer")


X, Y, Z = (0, 0, 0, 0, 1, 0), (0, 0, 1, 0, 0, 0), (0, 1, 0, 0, 0, 0)
MIRROR, ANTIPODE, BOTH = (1, 1, 0, 0, 0, 0), (0, 1, 1, 0, 1, 0), (1, 0, 1, 0, 1, 0)
NEIGHBOURS = ((X, Y), (Z, X), (Y, Z))
OWNERS = ((MIRROR, BOTH), (BOTH, MIRROR), (ANTIPODE, ANTIPODE))
PAIR = (((0, 0, 0, 0, 0, 1),) * 2,)


def colour_step(flips):
    return flips[4] ^ 2 * flips[2] ^ 3 * (flips[1] ^ flips[0])


def quarter_step(flips):
    return flips[4] + 2 * flips[0]


def swaps(opt, layer, partners):
    rest_count = opt // 8
    sizes = (2, 2, 2, rest_count, 2, 2)

    def device(half, z, y, rest, x, pair):
        return (((half * 2 + z) * 2 + y) * rest_count + rest) * layer + x * 2 + pair

    return [
        [
            (device(*spot), device(*(value ^ flip for value, flip in zip(spot, flips[spot[5]]))))
            for spot in itertools.product(*map(range, sizes))
        ]
        for flips in partners
    ]


def by_pair(pair, values):
    return values[0] + pair * (values[1] - values[0])


class Place:
    def __init__(self, rest_count):
        index = lax.axis_index("opt") // rest_count
        x, self.pair = lax.axis_index("layer") // 2, lax.axis_index("layer") % 2
        half, z, y = index // 4, index // 2 % 2, index % 2
        self.colour = x ^ (2 * y) ^ (3 * (z ^ half))
        self.quarter = x + 2 * half

    def colour_at(self, step):
        return self.colour ^ by_pair(self.pair, [colour_step(flips) for flips in NEIGHBOURS[step]])

    def quarter_at(self, step):
        return self.quarter ^ by_pair(self.pair, [quarter_step(flips) for flips in OWNERS[step]])


def call(kernel, out_shape, *operands, spaces=None, scratch=()):
    vmem = pl.BlockSpec(memory_space=pltpu.VMEM)
    return pl.pallas_call(
        kernel,
        out_shape=out_shape,
        in_specs=[vmem] * len(operands) if spaces is None else [pl.BlockSpec(memory_space=space) for space in spaces],
        out_specs=jax.tree.map(lambda _: vmem, out_shape),
        scratch_shapes=list(scratch),
        compiler_params=pltpu.CompilerParams(vmem_limit_bytes=VMEM_BYTES),
    )(*operands)


def product(first, second):
    return jnp.dot(first, second, preferred_element_type=jnp.float32)


def quarters_of(order):
    count = order // BLOCK
    folds = [("fold", i, i + 1) for i in range(0, count, 2)]
    others = [("plain", i, j) for i in range(count) for j in range(i + 1, count)]
    length = (len(folds) + len(others)) // 4
    quarters = []
    for quarter in range(4):
        blocks = folds[quarter::4]
        missing = length - len(blocks)
        quarters.append(blocks + others[:missing])
        others = others[missing:]
    return quarters


def quarter_blocks(order):
    quarters = quarters_of(order)
    return max(sum(kind == "fold" for kind, _, _ in blocks) for blocks in quarters), len(quarters[0])


def packed_shape(order):
    return jax.ShapeDtypeStruct((4, quarter_blocks(order)[1] * BLOCK + F32_TILE, BLOCK), jnp.float32)


def message_shape(order):
    return jax.ShapeDtypeStruct((quarter_blocks(order)[1] * BLOCK + BF16_TILE, BLOCK), jnp.bfloat16)


def grid_ids():
    shape = (BLOCK, BLOCK)
    return lax.broadcasted_iota(jnp.int32, shape, 0), lax.broadcasted_iota(jnp.int32, shape, 1)


def diagonal(block):
    row_ids, column_ids = grid_ids()
    return jnp.sum(jnp.where(row_ids == column_ids, block, 0.0), axis=0, keepdims=True)


def padded(rows, height):
    missing = height - sum(row.shape[0] for row in rows)
    return jnp.concatenate(rows + [jnp.zeros((missing, BLOCK), jnp.float32)], axis=0)


def pack(block, order):
    row_ids, column_ids = grid_ids()
    result = []
    for blocks in quarters_of(order):
        tiles, rows = [], []
        for kind, i, j in blocks:
            if kind == "fold":
                second = block(j, j)
                tiles.append(jnp.where(row_ids <= column_ids, block(i, i), second))
                rows.append(diagonal(second))
            else:
                tiles.append(block(i, j))
        result.append(jnp.concatenate(tiles + [padded(rows, F32_TILE)], axis=0))
    return result


def unpack(quarters, order):
    row_ids, column_ids = grid_ids()
    result = {}
    for blocks, quarter in zip(quarters_of(order), quarters):
        tail = quarter[len(blocks) * BLOCK :]
        for k, (kind, i, j) in enumerate(blocks):
            tile = quarter[k * BLOCK : (k + 1) * BLOCK]
            if kind == "fold":
                mirrored = tile.T
                result[i, i] = jnp.where(row_ids <= column_ids, tile, mirrored)
                second = jnp.where(row_ids > column_ids, tile, mirrored)
                result[j, j] = jnp.where(row_ids == column_ids, tail[k : k + 1], second)
            else:
                result[i, j] = tile
    return result


def to_message(quarter, order):
    fold_count, block_count = quarter_blocks(order)
    length = block_count * BLOCK
    body, tail = quarter[:length], quarter[length : length + fold_count]
    rounded = body.astype(jnp.bfloat16)
    rows = [
        diagonal(
            body[k * BLOCK : (k + 1) * BLOCK] - rounded[k * BLOCK : (k + 1) * BLOCK].astype(jnp.float32)
        )
        for k in range(fold_count)
    ]
    high = tail.astype(jnp.bfloat16).astype(jnp.float32)
    extra = padded(rows + [high, tail - high], BF16_TILE)
    return jnp.concatenate([rounded, extra.astype(jnp.bfloat16)], axis=0)


def from_message(message, order):
    fold_count, block_count = quarter_blocks(order)
    length = block_count * BLOCK
    row_ids, column_ids = grid_ids()
    values = message.astype(jnp.float32)
    body, extra = values[:length], values[length:]
    tiles = [
        body[k * BLOCK : (k + 1) * BLOCK] + jnp.where(row_ids == column_ids, extra[k : k + 1], 0.0)
        for k in range(fold_count)
    ]
    tail = extra[fold_count : 2 * fold_count] + extra[2 * fold_count : 3 * fold_count]
    return jnp.concatenate(tiles + [body[fold_count * BLOCK :], padded([tail], F32_TILE)], axis=0)


def deal_kernel(rest_count, momentum_ref, *refs):
    piece_refs, semaphores = refs[:-1], refs[-1]
    place = Place(rest_count)
    copies = []
    for number, piece_ref in enumerate(piece_refs):
        colour = place.colour if number == 0 else place.colour_at(number - 1)
        copies.append(pltpu.make_async_copy(momentum_ref.at[colour], piece_ref, semaphores.at[number]))
    for copy in copies[1:] + copies[:1]:
        copy.start()
    for copy in copies:
        copy.wait()


def expert_rows(piece_refs, expert):
    count = piece_refs[0].shape[0] // 2
    span = pl.ds(pl.multiple_of(expert * count, count), count)
    return jnp.concatenate([piece_ref[span, :] for piece_ref in piece_refs], axis=0)


def gram_kernel(rest_count, *refs):
    piece_refs, (kept_ref, sent_ref) = refs[:4], refs[4:]
    order = piece_refs[0].shape[1]
    pair = Place(rest_count).pair
    for expert, out_ref in ((1 - pair, sent_ref), (pair, kept_ref)):
        rows = expert_rows(piece_refs, expert)
        tiles = {}
        for row in range(0, order, WIDE):
            for column in range(row, order, WIDE):
                tiles[row, column] = lax.dot_general(
                    rows[:, row : row + WIDE],
                    rows[:, column : column + WIDE],
                    (((0,), (0,)), ((), ())),
                    preferred_element_type=jnp.float32,
                )

        def block(i, j):
            row, column = i * BLOCK, j * BLOCK
            tile = tiles[row // WIDE * WIDE, column // WIDE * WIDE]
            return tile[row % WIDE :, column % WIDE :][:BLOCK, :BLOCK]

        for quarter, value in enumerate(pack(block, order)):
            out_ref[quarter] = value


def reduce_kernel(rest_count, order, own_ref, other_ref, sum_ref, *message_refs):
    place = Place(rest_count)
    sum_ref[...] = own_ref[...] + other_ref[...]
    for step, message_ref in enumerate(message_refs):
        message_ref[...] = to_message(sum_ref[place.quarter_at(step)], order)


def gather_kernel(rest_count, order, sum_ref, *refs):
    arrived_refs, total_ref, message_refs = refs[:3], refs[3], refs[4:]
    arrived = [from_message(arrived_ref[...], order) for arrived_ref in arrived_refs]
    total = sum_ref[Place(rest_count).quarter] + (arrived[0] + (arrived[1] + arrived[2]))
    total_ref[...] = total
    for value, message_ref in zip(arrived, message_refs):
        message_ref[...] = to_message(total - value, order)


def split(matrix):
    high = matrix.astype(jnp.bfloat16)
    return high, (matrix - high.astype(jnp.float32)).astype(jnp.bfloat16)


def product_of_split(first, second):
    return product(first[0], second[0]) + (product(first[0], second[1]) + product(first[1], second[0]))


def assemble(upper, count):
    return jnp.concatenate(
        [
            jnp.concatenate([upper[i, j] if i <= j else upper[j, i].T for j in range(count)], axis=1)
            for i in range(count)
        ],
        axis=0,
    )


def split_whole(upper, count):
    parts = {key: split(value) for key, value in upper.items()}
    return tuple(assemble({key: value[part] for key, value in parts.items()}, count) for part in range(2))


def symmetric_product(first, second, count):
    size = first[0].shape[0] // count
    return {
        (i, j): product_of_split(
            tuple(part[i * size : (i + 1) * size, :] for part in first),
            tuple(part[:, j * size : (j + 1) * size] for part in second),
        )
        for i in range(count)
        for j in range(i, count)
    }


def newton(current, count):
    size = current[0, 0].shape[0]
    shape = (size, size)
    identity = lax.broadcasted_iota(jnp.int32, shape, 0) == lax.broadcasted_iota(jnp.int32, shape, 1)
    accum = None
    for iteration in range(ITERS):
        halves = split_whole(current, count)
        squared = symmetric_product(halves, halves, count)
        polynomial = {
            (i, j): (jnp.where(identity, first_coef, 0.0) if i == j else 0.0)
            + second_coef * current[i, j]
            + third_coef * squared[i, j]
            for i, j in current
        }
        poly_halves = split_whole(polynomial, count)
        if accum is None:
            accum = polynomial
        else:
            accum = symmetric_product(split_whole(accum, count), poly_halves, count)
        if iteration + 1 < ITERS:
            inner = symmetric_product(halves, poly_halves, count)
            current = symmetric_product(split_whole(inner, count), poly_halves, count)
    return accum


def factor_kernel(rest_count, order, scale, sum_ref, total_ref, *refs):
    rest_refs, factor_ref, quarters_ref = refs[:3], refs[3], refs[4]
    place = Place(rest_count)
    quarters_ref[place.quarter] = total_ref[...]
    for step, rest_ref in enumerate(rest_refs):
        quarter = place.quarter_at(step)
        quarters_ref[quarter] = sum_ref[quarter] + from_message(rest_ref[...], order)
    blocks = unpack([quarters_ref[quarter] for quarter in range(4)], order)
    trace_sum = jnp.sum(sum(diagonal(blocks[i, i]) for i in range(order // BLOCK)))
    count, ratio = order // WIDE, WIDE // BLOCK
    current = {}
    for i in range(count):
        for j in range(i, count):
            tile = jnp.concatenate(
                [
                    jnp.concatenate(
                        [
                            blocks[row, column] if row <= column else blocks[column, row].T
                            for column in range(j * ratio, (j + 1) * ratio)
                        ],
                        axis=1,
                    )
                    for row in range(i * ratio, (i + 1) * ratio)
                ],
                axis=0,
            )
            current[i, j] = tile / (trace_sum + epsilon)
    accum = newton(current, count)
    growth = jnp.sqrt(scale / (trace_sum + epsilon))
    factor_ref[...] = assemble(
        {key: (value * growth).astype(jnp.bfloat16) for key, value in accum.items()}, count
    )


def update_kernel(rest_count, own_ref, other_ref, *refs):
    piece_refs, update_refs = refs[:4], refs[4:]
    pair = Place(rest_count).pair
    count = piece_refs[0].shape[0] // 2
    for expert, factor_ref in ((pair, own_ref), (1 - pair, other_ref)):
        update = product(expert_rows(piece_refs, expert), factor_ref[...]).astype(jnp.bfloat16)
        span = pl.ds(pl.multiple_of(expert * count, count), count)
        for number, update_ref in enumerate(update_refs):
            update_ref[span, :] = update[number * count : (number + 1) * count]


def weights_kernel(rest_count, weights_ref, *refs):
    update_refs, out_ref = refs[:4], refs[4]
    place = Place(rest_count)
    shrink = 1.0 - step_rate * decay_rate
    for number, update_ref in enumerate(update_refs):
        colour = place.colour if number == 0 else place.colour_at(number - 1)
        out_ref[colour] = (
            shrink * weights_ref[colour].astype(jnp.float32) - step_rate * update_ref[...].astype(jnp.float32)
        ).astype(out_ref.dtype)


def on_device(momentum, weights):
    order = momentum.shape[3]
    opt, layer = lax.axis_size("opt"), lax.axis_size("layer")
    rest_count = opt // 8
    rest_groups = [[group * rest_count + rest for rest in range(rest_count)] for group in range(8)]
    scale = float(layer * opt * momentum.shape[2])

    def regroup(array, split_axis, concat_axis):
        if rest_count == 1:
            return array
        return lax.all_to_all(
            array,
            "opt",
            split_axis=split_axis,
            concat_axis=concat_axis,
            axis_index_groups=rest_groups,
            tiled=True,
        )

    def swap(arrays, partners):
        return [lax.ppermute(array, AXES, perm) for array, perm in zip(arrays, swaps(opt, layer, partners))]

    spread = regroup(momentum[0], 0, 1)
    experts, row_count, _ = spread.shape
    by_colour = (experts // 2, 2 * row_count, order)
    piece = jax.ShapeDtypeStruct(by_colour[1:], spread.dtype)
    packed, message = packed_shape(order), message_shape(order)
    quarter = jax.ShapeDtypeStruct(packed.shape[1:], packed.dtype)

    own, *dealt = call(
        functools.partial(deal_kernel, rest_count),
        (piece,) * 4,
        spread.reshape(by_colour),
        spaces=[pltpu.HBM],
        scratch=[pltpu.SemaphoreType.DMA((4,))],
    )
    pieces = [own] + swap(dealt, NEIGHBOURS)
    kept, sent = call(functools.partial(gram_kernel, rest_count), (packed, packed), *pieces)
    place_sum, *parts = call(
        functools.partial(reduce_kernel, rest_count, order),
        (packed,) + (message,) * 3,
        kept,
        *swap([sent], PAIR),
    )
    total, *rests = call(
        functools.partial(gather_kernel, rest_count, order),
        (quarter,) + (message,) * 3,
        place_sum,
        *swap(parts, OWNERS),
    )
    factor = call(
        functools.partial(factor_kernel, rest_count, order, scale),
        jax.ShapeDtypeStruct((order, order), jnp.bfloat16),
        place_sum,
        total,
        *swap(rests, OWNERS),
        scratch=[pltpu.VMEM(packed.shape, packed.dtype)],
    )
    own_update, *updates = call(
        functools.partial(update_kernel, rest_count),
        (piece,) * 4,
        factor,
        *swap([factor], PAIR),
        *pieces,
    )
    fresh = call(
        functools.partial(weights_kernel, rest_count),
        jax.ShapeDtypeStruct(by_colour, weights.dtype),
        regroup(weights[0], 0, 1).reshape(by_colour),
        own_update,
        *swap(updates, NEIGHBOURS),
    )
    return regroup(fresh.reshape(experts, row_count, order), 1, 0)[None]


def solution(mesh):
    in_specs = (P("layer", None, "opt", None), P("layer", None, "opt", None))
    out_specs = P("layer", None, "opt", None)
    return jax.shard_map(
        on_device, mesh=mesh, in_specs=in_specs, out_specs=out_specs, check_vma=False
    )
```

time: 62.2 us -> 58.6 us (0.942)
  starting transfers between devices: 17.3 us -> 22 us
  Pallas kernels: 13.9 us -> 9.66 us
  waiting for transfers between devices: 29.5 us -> 25.5 us
    ppermute x11 -> x14, starting transfers between devices: 17.3 us -> 22 us  [swap(): lax.ppermute(array, AXES, perm)]
    pallas_call x8 -> x7, Pallas kernels: 13.9 us -> 9.66 us  [call(): pl.pallas_call(kernel, out_shape=out_shape, in_specs=[vmem] * len(operand...]
    ppermute x11 -> x14, waiting for transfers between devices: 29.5 us -> 25.5 us  [swap(): lax.ppermute(array, AXES, perm)]
  transfers between devices with their start and end apart: 11 -> 14, of which waited for: 11 -> 10; matrix products, arithmetic and copies ran while one was open for 0% -> 0% of each run, Pallas kernels for 0% -> 0%
where the time goes in v3:
time: 58.6 us; the launch traced here: 58.5 us
  waiting for transfers between devices  25.5 us (44%)
  starting transfers between devices  22 us (38%)
  Pallas kernels  9.66 us (16%)
  local copies, waits for them, and re-layouts  1.23 us (2%)
    ppermute x14, waiting for transfers between devices, swap(): lax.ppermute(array, AXES, perm)  25.5 us
    ppermute x14, starting transfers between devices, swap(): lax.ppermute(array, AXES, perm)  22 us
    pallas_call x7, Pallas kernels, call(): pl.pallas_call(kernel, out_shape=out_shape, in_specs=[vmem] * len(operand...  9.66 us
    unnamed x4, local copies, waits for them, and re-layouts  1.23 us
  transfers between devices with their start and end apart: 14, of which 10 were waited for; matrix products, arithmetic and copies ran while one was open for 0% of the time, Pallas kernels for 0%

profile of v3, /device:TPU:0, one launch (start us, length us, event | category | flops | bytes accessed | tf_op | source)
XLA Modules:
  0.0 58.5 jit_solution(4771635486515358080)
XLA Ops:
  0.0 1.2 %copy-done.1 = bf16[1,8,128,512]{3,2,1,0:T(8,128)(2,1)S(1)} copy-done((bf16[1,8,128,512]{3,2,1,0:T(8,128)(2,1)S(1)}, bf16[1,8,128,512]{3,2,1,0:T(8,128)(2,1)}, u32[]{:S(2)}) %copy-start.1) | copy-done | bytes 1048600
  1.2 0.1 shard_map.28
  1.3 3.0 %collective-permute-start = (bf16[256,512]{1,0:T(8,128)(2,1)S(1)}, bf16[256,512]{1,0:T(8,128)(2,1)S(1)}, u32[]{:S(2)}, u32[]{:S(2)}) collective-permute-start(bf16[256,512]{1,0:T(8,128)(2,1)S(1)} %get-tuple-element.24), channel_id=1, source_target_pairs={{0,2},{1,5},{2,0},{3,7},{4,6},{5,1},{6,4},{7,3},{8,10},{9,13},{10,... | collective-permute-start | bytes 786440 | tf_op jit(solution)/shard_map/ppermute | solution.py:396
  4.4 1.6 %collective-permute-start.1 = (bf16[256,512]{1,0:T(8,128)(2,1)S(1)}, bf16[256,512]{1,0:T(8,128)(2,1)S(1)}, u32[]{:S(2)}, u32[]{:S(2)}) collective-permute-start(bf16[256,512]{1,0:T(8,128)(2,1)S(1)} %get-tuple-element.25), channel_id=1, source_target_pairs={{0,8},{1,3},{2,10},{3,1},{4,12},{5,7},{6,14},{7,5},{8,0},{9,11},{1... | collective-permute-start | bytes 786440 | tf_op jit(solution)/shard_map/ppermute | solution.py:396
  5.9 1.5 %collective-permute-start.2 = (bf16[256,512]{1,0:T(8,128)(2,1)S(1)}, bf16[256,512]{1,0:T(8,128)(2,1)S(1)}, u32[]{:S(2)}, u32[]{:S(2)}) collective-permute-start(bf16[256,512]{1,0:T(8,128)(2,1)S(1)} %get-tuple-element.26), channel_id=1, source_target_pairs={{0,4},{1,9},{2,6},{3,11},{4,0},{5,13},{6,2},{7,15},{8,12},{9,1},{1... | collective-permute-start | bytes 786440 | tf_op jit(solution)/shard_map/ppermute | solution.py:396
  7.4 3.5 %collective-permute-done.refs_1_ = bf16[256,512]{1,0:T(8,128)(2,1)S(1)} collective-permute-done((bf16[256,512]{1,0:T(8,128)(2,1)S(1)}, bf16[256,512]{1,0:T(8,128)(2,1)S(1)}, u32[]{:S(2)}, u32[]{:S(2)}) %collective-permute-start) | collective-permute-done | bytes 262176 | tf_op jit(solution)/shard_map/ppermute | solution.py:396
  10.9 2.4 %collective-permute-done.1.refs_2_ = bf16[256,512]{1,0:T(8,128)(2,1)S(1)} collective-permute-done((bf16[256,512]{1,0:T(8,128)(2,1)S(1)}, bf16[256,512]{1,0:T(8,128)(2,1)S(1)}, u32[]{:S(2)}, u32[]{:S(2)}) %collective-permute-start.1) | collective-permute-done | bytes 262176 | tf_op jit(solution)/shard_map/ppermute | solution.py:396
  13.4 0.6 %shard_map.29 = (f32[4,264,128]{2,1,0:T(8,128)S(1)}, f32[4,264,128]{2,1,0:T(8,128)S(1)}) custom-call(bf16[256,512]{1,0:T(8,128)(2,1)S(1)} %get-tuple-element.23.refs_0_, bf16[256,512]{1,0:T(8,128)(2,1)S(1)} %collective-permute-done.refs_1_, bf16[256,512]{1,0:T(8,128)(2,1)S(1)} %collective-permute-done.1.refs_2_, ...), custom_call_target="tpu_custom_call" | custom-call | tf_op jit(solution)/shard_map/pallas_call | solution.py:80
  14.0 0.1 collective-permute-start.3
  14.1 1.9 %collective-permute-done.3.other_ref = f32[4,264,128]{2,1,0:T(8,128)S(1)} collective-permute-done((f32[4,264,128]{2,1,0:T(8,128)S(1)}, f32[4,264,128]{2,1,0:T(8,128)S(1)}, u32[]{:S(2)}, u32[]{:S(2)}) %collective-permute-start.3) | collective-permute-done | bytes 540704 | tf_op jit(solution)/shard_map/ppermute | solution.py:396
  16.0 0.1 shard_map.30
  16.1 3.7 %collective-permute-start.4 = (bf16[272,128]{1,0:T(8,128)(2,1)S(1)}, bf16[272,128]{1,0:T(8,128)(2,1)S(1)}, u32[]{:S(2)}, u32[]{:S(2)}) collective-permute-start(bf16[272,128]{1,0:T(8,128)(2,1)S(1)} %get-tuple-element.30), channel_id=1, source_target_pairs={{0,24},{1,23},{2,26},{3,21},{4,28},{5,19},{6,30},{7,17},{8,16},{9,... | collective-permute-start | bytes 208904 | tf_op jit(solution)/shard_map/ppermute | solution.py:396
  19.8 2.6 %collective-permute-start.6 = (bf16[272,128]{1,0:T(8,128)(2,1)S(1)}, bf16[272,128]{1,0:T(8,128)(2,1)S(1)}, u32[]{:S(2)}, u32[]{:S(2)}) collective-permute-start(bf16[272,128]{1,0:T(8,128)(2,1)S(1)} %get-tuple-element.32), channel_id=1, source_target_pairs={{0,14},{1,15},{2,12},{3,13},{4,10},{5,11},{6,8},{7,9},{8,6},{9,7},... | collective-permute-start | bytes 208904 | tf_op jit(solution)/shard_map/ppermute | solution.py:396
  22.3 4.7 %collective-permute-done.5.refs_1_ = bf16[272,128]{1,0:T(8,128)(2,1)S(1)} collective-permute-done((bf16[272,128]{1,0:T(8,128)(2,1)S(1)}, bf16[272,128]{1,0:T(8,128)(2,1)S(1)}, u32[]{:S(2)}, u32[]{:S(2)}) %collective-permute-start.5) | collective-permute-done | bytes 69664 | tf_op jit(solution)/shard_map/ppermute | solution.py:396
  27.0 0.1 collective-permute-done.6.refs_2_
  27.1 0.1 shard_map.31
  27.2 3.1 %collective-permute-start.7 = (bf16[272,128]{1,0:T(8,128)(2,1)S(1)}, bf16[272,128]{1,0:T(8,128)(2,1)S(1)}, u32[]{:S(2)}, u32[]{:S(2)}) collective-permute-start(bf16[272,128]{1,0:T(8,128)(2,1)S(1)} %get-tuple-element.34), channel_id=1, source_target_pairs={{0,24},{1,23},{2,26},{3,21},{4,28},{5,19},{6,30},{7,17},{8,16},{9,... | collective-permute-start | bytes 208904 | tf_op jit(solution)/shard_map/ppermute | solution.py:396
  30.3 0.5 collective-permute-start.8
  30.8 2.6 %collective-permute-start.9 = (bf16[272,128]{1,0:T(8,128)(2,1)S(1)}, bf16[272,128]{1,0:T(8,128)(2,1)S(1)}, u32[]{:S(2)}, u32[]{:S(2)}) collective-permute-start(bf16[272,128]{1,0:T(8,128)(2,1)S(1)} %get-tuple-element.36), channel_id=1, source_target_pairs={{0,14},{1,15},{2,12},{3,13},{4,10},{5,11},{6,8},{7,9},{8,6},{9,7},... | collective-permute-start | bytes 208904 | tf_op jit(solution)/shard_map/ppermute | solution.py:396
  33.5 0.0 collective-permute-done.7.refs_0_
  33.5 4.2 %collective-permute-done.8.refs_1_ = bf16[272,128]{1,0:T(8,128)(2,1)S(1)} collective-permute-done((bf16[272,128]{1,0:T(8,128)(2,1)S(1)}, bf16[272,128]{1,0:T(8,128)(2,1)S(1)}, u32[]{:S(2)}, u32[]{:S(2)}) %collective-permute-start.8) | collective-permute-done | bytes 69664 | tf_op jit(solution)/shard_map/ppermute | solution.py:396
  37.6 0.1 collective-permute-done.9.refs_2_
  37.7 6.7 %shard_map.32.own_ref = bf16[512,512]{1,0:T(8,128)(2,1)S(1)} custom-call(f32[4,264,128]{2,1,0:T(8,128)S(1)} %get-tuple-element.29.sum_ref, f32[264,128]{1,0:T(8,128)S(1)} %get-tuple-element.33.total_ref, bf16[272,128]{1,0:T(8,128)(2,1)S(1)} %collective-permute-done.7.refs_0_, bf16[272,128]{1,0:T(8,128)(2,1)S(1)} %collective-permute-done.8.refs_1_, ...), custom_call_target="tpu_custom_call" | custom-call | tf_op jit(solution)/shard_map/pallas_call | solution.py:80
  44.4 0.1 collective-permute-start.10
  44.5 1.9 %collective-permute-done.10.other_ref = bf16[512,512]{1,0:T(8,128)(2,1)S(1)} collective-permute-done((bf16[512,512]{1,0:T(8,128)(2,1)S(1)}, bf16[512,512]{1,0:T(8,128)(2,1)S(1)}, u32[]{:S(2)}, u32[]{:S(2)}) %collective-permute-start.10) | collective-permute-done | bytes 524320 | tf_op jit(solution)/shard_map/ppermute | solution.py:396
  46.4 0.7 %shard_map.33 = (bf16[256,512]{1,0:T(8,128)(2,1)S(1)}, bf16[256,512]{1,0:T(8,128)(2,1)S(1)}, bf16[256,512]{1,0:T(8,128)(2,1)S(1)}, bf16[256,512]{1,0:T(8,128)(2,1)S(1)}) custom-call(bf16[512,512]{1,0:T(8,128)(2,1)S(1)} %shard_map.32.own_ref, bf16[512,512]{1,0:T(8,128)(2,1)S(1)} %collective-permute-done.10.other_ref, ...), custom_call_target="tpu_custom_call" | custom-call | tf_op jit(solution)/shard_map/pallas_call | solution.py:80
  47.1 1.2 %collective-permute-start.11 = (bf16[256,512]{1,0:T(8,128)(2,1)S(1)}, bf16[256,512]{1,0:T(8,128)(2,1)S(1)}, u32[]{:S(2)}, u32[]{:S(2)}) collective-permute-start(bf16[256,512]{1,0:T(8,128)(2,1)S(1)} %get-tuple-element.38), channel_id=1, source_target_pairs={{0,2},{1,5},{2,0},{3,7},{4,6},{5,1},{6,4},{7,3},{8,10},{9,13},{10,... | collective-permute-start | bytes 786440 | tf_op jit(solution)/shard_map/ppermute | solution.py:396
  48.2 1.1 %collective-permute-start.12 = (bf16[256,512]{1,0:T(8,128)(2,1)S(1)}, bf16[256,512]{1,0:T(8,128)(2,1)S(1)}, u32[]{:S(2)}, u32[]{:S(2)}) collective-permute-start(bf16[256,512]{1,0:T(8,128)(2,1)S(1)} %get-tuple-element.39), channel_id=1, source_target_pairs={{0,8},{1,3},{2,10},{3,1},{4,12},{5,7},{6,14},{7,5},{8,0},{9,11},{1... | collective-permute-start | bytes 786440 | tf_op jit(solution)/shard_map/ppermute | solution.py:396
  49.4 0.9 %collective-permute-start.13 = (bf16[256,512]{1,0:T(8,128)(2,1)S(1)}, bf16[256,512]{1,0:T(8,128)(2,1)S(1)}, u32[]{:S(2)}, u32[]{:S(2)}) collective-permute-start(bf16[256,512]{1,0:T(8,128)(2,1)S(1)} %get-tuple-element.40), channel_id=1, source_target_pairs={{0,4},{1,9},{2,6},{3,11},{4,0},{5,13},{6,2},{7,15},{8,12},{9,1},{1... | collective-permute-start | bytes 786440 | tf_op jit(solution)/shard_map/ppermute | solution.py:396
  50.3 6.0 %collective-permute-done.11.refs_1_ = bf16[256,512]{1,0:T(8,128)(2,1)S(1)} collective-permute-done((bf16[256,512]{1,0:T(8,128)(2,1)S(1)}, bf16[256,512]{1,0:T(8,128)(2,1)S(1)}, u32[]{:S(2)}, u32[]{:S(2)}) %collective-permute-start.11) | collective-permute-done | bytes 262176 | tf_op jit(solution)/shard_map/ppermute | solution.py:396
  56.3 0.8 %collective-permute-done.12.refs_2_ = bf16[256,512]{1,0:T(8,128)(2,1)S(1)} collective-permute-done((bf16[256,512]{1,0:T(8,128)(2,1)S(1)}, bf16[256,512]{1,0:T(8,128)(2,1)S(1)}, u32[]{:S(2)}, u32[]{:S(2)}) %collective-permute-start.12) | collective-permute-done | bytes 262176 | tf_op jit(solution)/shard_map/ppermute | solution.py:396
  57.1 1.3 %shard_map.34 = bf16[4,256,512]{2,1,0:T(8,128)(2,1)} custom-call(bf16[4,256,512]{2,1,0:T(8,128)(2,1)S(1)} %bitcast.3, bf16[256,512]{1,0:T(8,128)(2,1)S(1)} %get-tuple-element.37.refs_0_, bf16[256,512]{1,0:T(8,128)(2,1)S(1)} %collective-permute-done.11.refs_1_, bf16[256,512]{1,0:T(8,128)(2,1)S(1)} %collective-permute-done.12.refs_2_, ...), custom_call_target="tpu_custom_call" | custom-call | tf_op jit(solution)/shard_map/pallas_call | solution.py:80
  (7 shorter events, 0.0 us)
Async XLA Ops:
  0.0 1.2 %copy-start.1 = (bf16[1,8,128,512]{3,2,1,0:T(8,128)(2,1)S(1)}, bf16[1,8,128,512]{3,2,1,0:T(8,128)(2,1)}, u32[]{:S(2)}) copy-start(bf16[1,8,128,512]{3,2,1,0:T(8,128)(2,1)} %param.2) | copy-start | bytes 3145732
  1.3 9.6 %collective-permute-start = (bf16[256,512]{1,0:T(8,128)(2,1)S(1)}, bf16[256,512]{1,0:T(8,128)(2,1)S(1)}, u32[]{:S(2)}, u32[]{:S(2)}) collective-permute-start(bf16[256,512]{1,0:T(8,128)(2,1)S(1)} %get-tuple-element.24), channel_id=1, source_target_pairs={{0,2},{1,5},{2,0},{3,7},{4,6},{5,1},{6,4},{7,3},{8,10},{9,13},{10,... | collective-permute-start | bytes 786440 | tf_op jit(solution)/shard_map/ppermute | solution.py:396
  4.4 9.0 %collective-permute-start.1 = (bf16[256,512]{1,0:T(8,128)(2,1)S(1)}, bf16[256,512]{1,0:T(8,128)(2,1)S(1)}, u32[]{:S(2)}, u32[]{:S(2)}) collective-permute-start(bf16[256,512]{1,0:T(8,128)(2,1)S(1)} %get-tuple-element.25), channel_id=1, source_target_pairs={{0,8},{1,3},{2,10},{3,1},{4,12},{5,7},{6,14},{7,5},{8,0},{9,11},{1... | collective-permute-start | bytes 786440 | tf_op jit(solution)/shard_map/ppermute | solution.py:396
  5.9 7.4 %collective-permute-start.2 = (bf16[256,512]{1,0:T(8,128)(2,1)S(1)}, bf16[256,512]{1,0:T(8,128)(2,1)S(1)}, u32[]{:S(2)}, u32[]{:S(2)}) collective-permute-start(bf16[256,512]{1,0:T(8,128)(2,1)S(1)} %get-tuple-element.26), channel_id=1, source_target_pairs={{0,4},{1,9},{2,6},{3,11},{4,0},{5,13},{6,2},{7,15},{8,12},{9,1},{1... | collective-permute-start | bytes 786440 | tf_op jit(solution)/shard_map/ppermute | solution.py:396
  14.0 2.0 %collective-permute-start.3 = (f32[4,264,128]{2,1,0:T(8,128)S(1)}, f32[4,264,128]{2,1,0:T(8,128)S(1)}, u32[]{:S(2)}, u32[]{:S(2)}) collective-permute-start(f32[4,264,128]{2,1,0:T(8,128)S(1)} %get-tuple-element.28), channel_id=1, source_target_pairs={{0,1},{1,0},{2,3},{3,2},{4,5},{5,4},{6,7},{7,6},{8,9},{9,8},{10,11... | collective-permute-start | bytes 1622024 | tf_op jit(solution)/shard_map/ppermute | solution.py:396
  16.1 6.3 %collective-permute-start.4 = (bf16[272,128]{1,0:T(8,128)(2,1)S(1)}, bf16[272,128]{1,0:T(8,128)(2,1)S(1)}, u32[]{:S(2)}, u32[]{:S(2)}) collective-permute-start(bf16[272,128]{1,0:T(8,128)(2,1)S(1)} %get-tuple-element.30), channel_id=1, source_target_pairs={{0,24},{1,23},{2,26},{3,21},{4,28},{5,19},{6,30},{7,17},{8,16},{9,... | collective-permute-start | bytes 208904 | tf_op jit(solution)/shard_map/ppermute | solution.py:396
  19.8 7.3 %collective-permute-start.5 = (bf16[272,128]{1,0:T(8,128)(2,1)S(1)}, bf16[272,128]{1,0:T(8,128)(2,1)S(1)}, u32[]{:S(2)}, u32[]{:S(2)}) collective-permute-start(bf16[272,128]{1,0:T(8,128)(2,1)S(1)} %get-tuple-element.31), channel_id=1, source_target_pairs={{0,22},{1,25},{2,20},{3,27},{4,18},{5,29},{6,16},{7,31},{8,30},{9,... | collective-permute-start | bytes 208904 | tf_op jit(solution)/shard_map/ppermute | solution.py:396
  19.8 7.3 %collective-permute-start.6 = (bf16[272,128]{1,0:T(8,128)(2,1)S(1)}, bf16[272,128]{1,0:T(8,128)(2,1)S(1)}, u32[]{:S(2)}, u32[]{:S(2)}) collective-permute-start(bf16[272,128]{1,0:T(8,128)(2,1)S(1)} %get-tuple-element.32), channel_id=1, source_target_pairs={{0,14},{1,15},{2,12},{3,13},{4,10},{5,11},{6,8},{7,9},{8,6},{9,7},... | collective-permute-start | bytes 208904 | tf_op jit(solution)/shard_map/ppermute | solution.py:396
  27.2 6.3 %collective-permute-start.7 = (bf16[272,128]{1,0:T(8,128)(2,1)S(1)}, bf16[272,128]{1,0:T(8,128)(2,1)S(1)}, u32[]{:S(2)}, u32[]{:S(2)}) collective-permute-start(bf16[272,128]{1,0:T(8,128)(2,1)S(1)} %get-tuple-element.34), channel_id=1, source_target_pairs={{0,24},{1,23},{2,26},{3,21},{4,28},{5,19},{6,30},{7,17},{8,16},{9,... | collective-permute-start | bytes 208904 | tf_op jit(solution)/shard_map/ppermute | solution.py:396
  30.3 7.3 %collective-permute-start.8 = (bf16[272,128]{1,0:T(8,128)(2,1)S(1)}, bf16[272,128]{1,0:T(8,128)(2,1)S(1)}, u32[]{:S(2)}, u32[]{:S(2)}) collective-permute-start(bf16[272,128]{1,0:T(8,128)(2,1)S(1)} %get-tuple-element.35), channel_id=1, source_target_pairs={{0,22},{1,25},{2,20},{3,27},{4,18},{5,29},{6,16},{7,31},{8,30},{9,... | collective-permute-start | bytes 208904 | tf_op jit(solution)/shard_map/ppermute | solution.py:396
  30.8 6.9 %collective-permute-start.9 = (bf16[272,128]{1,0:T(8,128)(2,1)S(1)}, bf16[272,128]{1,0:T(8,128)(2,1)S(1)}, u32[]{:S(2)}, u32[]{:S(2)}) collective-permute-start(bf16[272,128]{1,0:T(8,128)(2,1)S(1)} %get-tuple-element.36), channel_id=1, source_target_pairs={{0,14},{1,15},{2,12},{3,13},{4,10},{5,11},{6,8},{7,9},{8,6},{9,7},... | collective-permute-start | bytes 208904 | tf_op jit(solution)/shard_map/ppermute | solution.py:396
  44.4 12.8 %copy-start = (bf16[1,8,128,512]{3,2,1,0:T(8,128)(2,1)S(1)}, bf16[1,8,128,512]{3,2,1,0:T(8,128)(2,1)}, u32[]{:S(2)}) copy-start(bf16[1,8,128,512]{3,2,1,0:T(8,128)(2,1)} %param.3) | copy-start | bytes 3145732
  44.4 2.0 %collective-permute-start.10 = (bf16[512,512]{1,0:T(8,128)(2,1)S(1)}, bf16[512,512]{1,0:T(8,128)(2,1)S(1)}, u32[]{:S(2)}, u32[]{:S(2)}) collective-permute-start(bf16[512,512]{1,0:T(8,128)(2,1)S(1)} %shard_map.32.own_ref), channel_id=1, source_target_pairs={{0,1},{1,0},{2,3},{3,2},{4,5},{5,4},{6,7},{7,6},{8,9},{9,8},{10,11... | collective-permute-start | bytes 1572872 | tf_op jit(solution)/shard_map/ppermute | solution.py:396
  47.1 9.2 %collective-permute-start.11 = (bf16[256,512]{1,0:T(8,128)(2,1)S(1)}, bf16[256,512]{1,0:T(8,128)(2,1)S(1)}, u32[]{:S(2)}, u32[]{:S(2)}) collective-permute-start(bf16[256,512]{1,0:T(8,128)(2,1)S(1)} %get-tuple-element.38), channel_id=1, source_target_pairs={{0,2},{1,5},{2,0},{3,7},{4,6},{5,1},{6,4},{7,3},{8,10},{9,13},{10,... | collective-permute-start | bytes 786440 | tf_op jit(solution)/shard_map/ppermute | solution.py:396
  48.2 8.9 %collective-permute-start.12 = (bf16[256,512]{1,0:T(8,128)(2,1)S(1)}, bf16[256,512]{1,0:T(8,128)(2,1)S(1)}, u32[]{:S(2)}, u32[]{:S(2)}) collective-permute-start(bf16[256,512]{1,0:T(8,128)(2,1)S(1)} %get-tuple-element.39), channel_id=1, source_target_pairs={{0,8},{1,3},{2,10},{3,1},{4,12},{5,7},{6,14},{7,5},{8,0},{9,11},{1... | collective-permute-start | bytes 786440 | tf_op jit(solution)/shard_map/ppermute | solution.py:396
  49.4 7.7 %collective-permute-start.13 = (bf16[256,512]{1,0:T(8,128)(2,1)S(1)}, bf16[256,512]{1,0:T(8,128)(2,1)S(1)}, u32[]{:S(2)}, u32[]{:S(2)}) collective-permute-start(bf16[256,512]{1,0:T(8,128)(2,1)S(1)} %get-tuple-element.40), channel_id=1, source_target_pairs={{0,4},{1,9},{2,6},{3,11},{4,0},{5,13},{6,2},{7,15},{8,12},{9,1},{1... | collective-permute-start | bytes 786440 | tf_op jit(solution)/shard_map/ppermute | solution.py:396

commit v4 on v3

--- a/solution.py
+++ b/solution.py
@@ -25,11 +25,18 @@
 AXES = ("opt", "layer")
 
 
-X, Y, Z = (0, 0, 0, 0, 1, 0), (0, 0, 1, 0, 0, 0), (0, 1, 0, 0, 0, 0)
-MIRROR, ANTIPODE, BOTH = (1, 1, 0, 0, 0, 0), (0, 1, 1, 0, 1, 0), (1, 0, 1, 0, 1, 0)
-NEIGHBOURS = ((X, Y), (Z, X), (Y, Z))
-OWNERS = ((MIRROR, BOTH), (BOTH, MIRROR), (ANTIPODE, ANTIPODE))
-PAIR = (((0, 0, 0, 0, 0, 1),) * 2,)
+def flips_of(z, y, x, pair=0, half=0):
+    return (half, z, y, 0, x, pair)
+
+
+def neighbour_steps():
+    ways = [(0, 0, 1), (0, 1, 0), (1, 0, 0)]
+    order = [(ways[step], ways[(step + 1) % 3]) for step in range(3)]
+    return [tuple(flips_of(*way, pair=cross) for way in step) for cross in range(2) for step in order]
+
+
+ROWS = neighbour_steps() + [(flips_of(0, 0, 0, pair=1),) * 2]
+OWNERS = [(flips,) * 2 for flips in (flips_of(1, 0, 0, half=1), flips_of(0, 1, 1, half=1), flips_of(1, 1, 1))]
 
 
 def colour_step(flips):
@@ -68,8 +75,11 @@
         self.colour = x ^ (2 * y) ^ (3 * (z ^ half))
         self.quarter = x + 2 * half
 
-    def colour_at(self, step):
-        return self.colour ^ by_pair(self.pair, [colour_step(flips) for flips in NEIGHBOURS[step]])
+    def block(self, number):
+        if number == 0:
+            return self.colour, self.pair
+        flips = ROWS[number - 1]
+        return self.colour ^ by_pair(self.pair, [colour_step(way) for way in flips]), self.pair ^ flips[0][5]
 
     def quarter_at(self, step):
         return self.quarter ^ by_pair(self.pair, [quarter_step(flips) for flips in OWNERS[step]])
@@ -197,52 +207,36 @@
 
 
 def deal_kernel(rest_count, momentum_ref, *refs):
-    piece_refs, semaphores = refs[:-1], refs[-1]
     place = Place(rest_count)
-    copies = []
-    for number, piece_ref in enumerate(piece_refs):
-        colour = place.colour if number == 0 else place.colour_at(number - 1)
-        copies.append(pltpu.make_async_copy(momentum_ref.at[colour], piece_ref, semaphores.at[number]))
-    for copy in copies[1:] + copies[:1]:
-        copy.start()
-    for copy in copies:
-        copy.wait()
-
-
-def expert_rows(piece_refs, expert):
-    count = piece_refs[0].shape[0] // 2
-    span = pl.ds(pl.multiple_of(expert * count, count), count)
-    return jnp.concatenate([piece_ref[span, :] for piece_ref in piece_refs], axis=0)
-
-
-def gram_kernel(rest_count, *refs):
-    piece_refs, (kept_ref, sent_ref) = refs[:4], refs[4:]
-    order = piece_refs[0].shape[1]
-    pair = Place(rest_count).pair
-    for expert, out_ref in ((1 - pair, sent_ref), (pair, kept_ref)):
-        rows = expert_rows(piece_refs, expert)
-        tiles = {}
-        for row in range(0, order, WIDE):
-            for column in range(row, order, WIDE):
-                tiles[row, column] = lax.dot_general(
-                    rows[:, row : row + WIDE],
-                    rows[:, column : column + WIDE],
-                    (((0,), (0,)), ((), ())),
-                    preferred_element_type=jnp.float32,
-                )
-
-        def block(i, j):
-            row, column = i * BLOCK, j * BLOCK
-            tile = tiles[row // WIDE * WIDE, column // WIDE * WIDE]
-            return tile[row % WIDE :, column % WIDE :][:BLOCK, :BLOCK]
-
-        for quarter, value in enumerate(pack(block, order)):
-            out_ref[quarter] = value
-
-
-def reduce_kernel(rest_count, order, own_ref, other_ref, sum_ref, *message_refs):
+    for number, block_ref in enumerate(refs):
+        block_ref[...] = momentum_ref[place.block(number)]
+
+
+def gram_kernel(*refs):
+    rows = jnp.concatenate([block_ref[...] for block_ref in refs[:-1]], axis=0)
+    packed_ref = refs[-1]
+    order = rows.shape[1]
+    tiles = {}
+    for row in range(0, order, WIDE):
+        for column in range(row, order, WIDE):
+            tiles[row, column] = lax.dot_general(
+                rows[:, row : row + WIDE],
+                rows[:, column : column + WIDE],
+                (((0,), (0,)), ((), ())),
+                preferred_element_type=jnp.float32,
+            )
+
+    def block(i, j):
+        row, column = i * BLOCK, j * BLOCK
+        tile = tiles[row // WIDE * WIDE, column // WIDE * WIDE]
+        return tile[row % WIDE :, column % WIDE :][:BLOCK, :BLOCK]
+
+    for quarter, value in enumerate(pack(block, order)):
+        packed_ref[quarter] = value
+
+
+def reduce_kernel(rest_count, order, sum_ref, *message_refs):
     place = Place(rest_count)
-    sum_ref[...] = own_ref[...] + other_ref[...]
     for step, message_ref in enumerate(message_refs):
         message_ref[...] = to_message(sum_ref[place.quarter_at(step)], order)
 
@@ -351,25 +345,22 @@
     )
 
 
-def update_kernel(rest_count, own_ref, other_ref, *refs):
-    piece_refs, update_refs = refs[:4], refs[4:]
-    pair = Place(rest_count).pair
-    count = piece_refs[0].shape[0] // 2
-    for expert, factor_ref in ((pair, own_ref), (1 - pair, other_ref)):
-        update = product(expert_rows(piece_refs, expert), factor_ref[...]).astype(jnp.bfloat16)
-        span = pl.ds(pl.multiple_of(expert * count, count), count)
-        for number, update_ref in enumerate(update_refs):
-            update_ref[span, :] = update[number * count : (number + 1) * count]
+def update_kernel(factor_ref, *refs):
+    block_refs, update_refs = refs[: len(refs) // 2], refs[len(refs) // 2 :]
+    update = product(jnp.concatenate([block_ref[...] for block_ref in block_refs], axis=0), factor_ref[...])
+    count = block_refs[0].shape[0]
+    for number, update_ref in enumerate(update_refs):
+        update_ref[...] = update[number * count : (number + 1) * count].astype(update_ref.dtype)
 
 
 def weights_kernel(rest_count, weights_ref, *refs):
-    update_refs, out_ref = refs[:4], refs[4]
+    update_refs, out_ref = refs[:-1], refs[-1]
     place = Place(rest_count)
     shrink = 1.0 - step_rate * decay_rate
     for number, update_ref in enumerate(update_refs):
-        colour = place.colour if number == 0 else place.colour_at(number - 1)
-        out_ref[colour] = (
-            shrink * weights_ref[colour].astype(jnp.float32) - step_rate * update_ref[...].astype(jnp.float32)
+        block = place.block(number)
+        out_ref[block] = (
+            shrink * weights_ref[block].astype(jnp.float32) - step_rate * update_ref[...].astype(jnp.float32)
         ).astype(out_ref.dtype)
 
 
@@ -392,31 +383,27 @@
             tiled=True,
         )
 
-    def swap(arrays, partners):
-        return [lax.ppermute(array, AXES, perm) for array, perm in zip(arrays, swaps(opt, layer, partners))]
+    def swap(arrays, partners, back=False):
+        permutes = swaps(opt, layer, partners)
+        if back:
+            permutes = [[(target, source) for source, target in permute] for permute in permutes]
+        return [lax.ppermute(array, AXES, permute) for array, permute in zip(arrays, permutes)]
 
     spread = regroup(momentum[0], 0, 1)
     experts, row_count, _ = spread.shape
-    by_colour = (experts // 2, 2 * row_count, order)
-    piece = jax.ShapeDtypeStruct(by_colour[1:], spread.dtype)
+    by_block = (experts // 2, 2, row_count, order)
+    blocks = (jax.ShapeDtypeStruct(by_block[2:], spread.dtype),) * (1 + len(ROWS))
     packed, message = packed_shape(order), message_shape(order)
     quarter = jax.ShapeDtypeStruct(packed.shape[1:], packed.dtype)
 
     own, *dealt = call(
         functools.partial(deal_kernel, rest_count),
-        (piece,) * 4,
-        spread.reshape(by_colour),
-        spaces=[pltpu.HBM],
-        scratch=[pltpu.SemaphoreType.DMA((4,))],
-    )
-    pieces = [own] + swap(dealt, NEIGHBOURS)
-    kept, sent = call(functools.partial(gram_kernel, rest_count), (packed, packed), *pieces)
-    place_sum, *parts = call(
-        functools.partial(reduce_kernel, rest_count, order),
-        (packed,) + (message,) * 3,
-        kept,
-        *swap([sent], PAIR),
-    )
+        blocks,
+        spread.reshape(by_block),
+    )
+    rows = [own] + swap(dealt, ROWS)
+    place_sum = call(gram_kernel, packed, *rows)
+    parts = call(functools.partial(reduce_kernel, rest_count, order), (message,) * 3, place_sum)
     total, *rests = call(
         functools.partial(gather_kernel, rest_count, order),
         (quarter,) + (message,) * 3,
@@ -431,19 +418,13 @@
         *swap(rests, OWNERS),
         scratch=[pltpu.VMEM(packed.shape, packed.dtype)],
     )
-    own_update, *updates = call(
-        functools.partial(update_kernel, rest_count),
-        (piece,) * 4,
-        factor,
-        *swap([factor], PAIR),
-        *pieces,
-    )
+    own_update, *updates = call(update_kernel, blocks, factor, *rows)
     fresh = call(
         functools.partial(weights_kernel, rest_count),
-        jax.ShapeDtypeStruct(by_colour, weights.dtype),
-        regroup(weights[0], 0, 1).reshape(by_colour),
+        jax.ShapeDtypeStruct(by_block, weights.dtype),
+        regroup(weights[0], 0, 1).reshape(by_block),
         own_update,
-        *swap(updates, NEIGHBOURS),
+        *swap(updates, ROWS, back=True),
     )
     return regroup(fresh.reshape(experts, row_count, order), 1, 0)[None]
 

time: 58.6 us -> 55.4 us (0.945)
  waiting for transfers between devices: 25.5 us -> 17.8 us
  starting transfers between devices: 22 us -> 26.6 us
    ppermute x14 -> x20, waiting for transfers between devices: 25.5 us -> 17.8 us  [swap(): lax.ppermute(array, AXES, permute)]
    ppermute x14 -> x20, starting transfers between devices: 22 us -> 26.6 us  [swap(): lax.ppermute(array, AXES, permute)]
  transfers between devices with their start and end apart: 14 -> 20, of which waited for: 10 -> 13; matrix products, arithmetic and copies ran while one was open for 0% -> 0% of each run, Pallas kernels for 0% -> 0%
where the time goes in v4:
time: 55.4 us; the launch traced here: 55.3 us
  starting transfers between devices  26.6 us (48%)
  waiting for transfers between devices  17.8 us (32%)
  Pallas kernels  9.59 us (17%)
  local copies, waits for them, and re-layouts  1.23 us (2%)
    ppermute x20, starting transfers between devices, swap(): lax.ppermute(array, AXES, permute)  26.6 us
    ppermute x20, waiting for transfers between devices, swap(): lax.ppermute(array, AXES, permute)  17.8 us
    pallas_call x7, Pallas kernels, call(): pl.pallas_call(kernel, out_shape=out_shape, in_specs=[vmem] * len(operand...  9.59 us
    unnamed x4, local copies, waits for them, and re-layouts  1.23 us
  transfers between devices with their start and end apart: 20, of which 13 were waited for; matrix products, arithmetic and copies ran while one was open for 0% of the time, Pallas kernels for 0%

profile of v4, /device:TPU:0, one launch (start us, length us, event | category | flops | bytes accessed | tf_op | source)
XLA Modules:
  0.0 55.3 jit_solution(1260648880909277085)
XLA Ops:
  0.0 1.2 %copy-done.1 = bf16[1,8,128,512]{3,2,1,0:T(8,128)(2,1)S(1)} copy-done((bf16[1,8,128,512]{3,2,1,0:T(8,128)(2,1)S(1)}, bf16[1,8,128,512]{3,2,1,0:T(8,128)(2,1)}, u32[]{:S(2)}) %copy-start.1) | copy-done | bytes 1048600
  1.3 3.0 %collective-permute-start = (bf16[128,512]{1,0:T(8,128)(2,1)S(1)}, bf16[128,512]{1,0:T(8,128)(2,1)S(1)}, u32[]{:S(2)}, u32[]{:S(2)}) collective-permute-start(bf16[128,512]{1,0:T(8,128)(2,1)S(1)} %get-tuple-element.29), channel_id=1, source_target_pairs={{0,2},{1,5},{2,0},{3,7},{4,6},{5,1},{6,4},{7,3},{8,10},{9,13},{10,... | collective-permute-start | bytes 393224 | tf_op jit(solution)/shard_map/ppermute | solution.py:390
  4.3 1.5 %collective-permute-start.1 = (bf16[128,512]{1,0:T(8,128)(2,1)S(1)}, bf16[128,512]{1,0:T(8,128)(2,1)S(1)}, u32[]{:S(2)}, u32[]{:S(2)}) collective-permute-start(bf16[128,512]{1,0:T(8,128)(2,1)S(1)} %get-tuple-element.30), channel_id=1, source_target_pairs={{0,4},{1,9},{2,6},{3,11},{4,0},{5,13},{6,2},{7,15},{8,12},{9,1},{1... | collective-permute-start | bytes 393224 | tf_op jit(solution)/shard_map/ppermute | solution.py:390
  5.8 1.6 %collective-permute-start.2 = (bf16[128,512]{1,0:T(8,128)(2,1)S(1)}, bf16[128,512]{1,0:T(8,128)(2,1)S(1)}, u32[]{:S(2)}, u32[]{:S(2)}) collective-permute-start(bf16[128,512]{1,0:T(8,128)(2,1)S(1)} %get-tuple-element.31), channel_id=1, source_target_pairs={{0,8},{1,3},{2,10},{3,1},{4,12},{5,7},{6,14},{7,5},{8,0},{9,11},{1... | collective-permute-start | bytes 393224 | tf_op jit(solution)/shard_map/ppermute | solution.py:390
  7.4 1.7 %collective-permute-start.4 = (bf16[128,512]{1,0:T(8,128)(2,1)S(1)}, bf16[128,512]{1,0:T(8,128)(2,1)S(1)}, u32[]{:S(2)}, u32[]{:S(2)}) collective-permute-start(bf16[128,512]{1,0:T(8,128)(2,1)S(1)} %get-tuple-element.33), channel_id=1, source_target_pairs={{0,5},{1,8},{2,7},{3,10},{4,1},{5,12},{6,3},{7,14},{8,13},{9,0},{1... | collective-permute-start | bytes 393224 | tf_op jit(solution)/shard_map/ppermute | solution.py:390
  9.3 0.5 collective-permute-start.6
  9.8 1.4 %collective-permute-done.2.refs_3_ = bf16[128,512]{1,0:T(8,128)(2,1)S(1)} collective-permute-done((bf16[128,512]{1,0:T(8,128)(2,1)S(1)}, bf16[128,512]{1,0:T(8,128)(2,1)S(1)}, u32[]{:S(2)}, u32[]{:S(2)}) %collective-permute-start.2) | collective-permute-done | bytes 131104 | tf_op jit(solution)/shard_map/ppermute | solution.py:390
  11.2 1.2 %collective-permute-done.3.refs_4_ = bf16[128,512]{1,0:T(8,128)(2,1)S(1)} collective-permute-done((bf16[128,512]{1,0:T(8,128)(2,1)S(1)}, bf16[128,512]{1,0:T(8,128)(2,1)S(1)}, u32[]{:S(2)}, u32[]{:S(2)}) %collective-permute-start.3) | collective-permute-done | bytes 131104 | tf_op jit(solution)/shard_map/ppermute | solution.py:390
  12.4 1.1 %collective-permute-done.5.refs_6_ = bf16[128,512]{1,0:T(8,128)(2,1)S(1)} collective-permute-done((bf16[128,512]{1,0:T(8,128)(2,1)S(1)}, bf16[128,512]{1,0:T(8,128)(2,1)S(1)}, u32[]{:S(2)}, u32[]{:S(2)}) %collective-permute-start.5) | collective-permute-done | bytes 131104 | tf_op jit(solution)/shard_map/ppermute | solution.py:390
  13.5 0.6 %shard_map.29.sum_ref = f32[4,264,128]{2,1,0:T(8,128)S(1)} custom-call(bf16[128,512]{1,0:T(8,128)(2,1)S(1)} %get-tuple-element.28.refs_0_, bf16[128,512]{1,0:T(8,128)(2,1)S(1)} %collective-permute-done.refs_1_, bf16[128,512]{1,0:T(8,128)(2,1)S(1)} %collective-permute-done.1.refs_2_, bf16[128,512]{1,0:T(8,128)(2,1)S(1)} %collective-permute-done.2.refs_3_, ...), custom_call_target="tpu_custom_call" | custom-call | tf_op jit(solution)/shard_map/pallas_call | solution.py:90
  14.2 3.4 %collective-permute-start.7 = (bf16[272,128]{1,0:T(8,128)(2,1)S(1)}, bf16[272,128]{1,0:T(8,128)(2,1)S(1)}, u32[]{:S(2)}, u32[]{:S(2)}) collective-permute-start(bf16[272,128]{1,0:T(8,128)(2,1)S(1)} %get-tuple-element.36), channel_id=1, source_target_pairs={{0,24},{1,25},{2,26},{3,27},{4,28},{5,29},{6,30},{7,31},{8,16},{9,... | collective-permute-start | bytes 208904 | tf_op jit(solution)/shard_map/ppermute | solution.py:390
  17.7 0.9 %collective-permute-start.8 = (bf16[272,128]{1,0:T(8,128)(2,1)S(1)}, bf16[272,128]{1,0:T(8,128)(2,1)S(1)}, u32[]{:S(2)}, u32[]{:S(2)}) collective-permute-start(bf16[272,128]{1,0:T(8,128)(2,1)S(1)} %get-tuple-element.37), channel_id=1, source_target_pairs={{0,22},{1,23},{2,20},{3,21},{4,18},{5,19},{6,16},{7,17},{8,30},{9,... | collective-permute-start | bytes 208904 | tf_op jit(solution)/shard_map/ppermute | solution.py:390
  18.6 1.9 %collective-permute-start.9 = (bf16[272,128]{1,0:T(8,128)(2,1)S(1)}, bf16[272,128]{1,0:T(8,128)(2,1)S(1)}, u32[]{:S(2)}, u32[]{:S(2)}) collective-permute-start(bf16[272,128]{1,0:T(8,128)(2,1)S(1)} %get-tuple-element.38), channel_id=1, source_target_pairs={{0,14},{1,15},{2,12},{3,13},{4,10},{5,11},{6,8},{7,9},{8,6},{9,7},... | collective-permute-start | bytes 208904 | tf_op jit(solution)/shard_map/ppermute | solution.py:390
  20.5 4.9 %collective-permute-done.8.refs_1_ = bf16[272,128]{1,0:T(8,128)(2,1)S(1)} collective-permute-done((bf16[272,128]{1,0:T(8,128)(2,1)S(1)}, bf16[272,128]{1,0:T(8,128)(2,1)S(1)}, u32[]{:S(2)}, u32[]{:S(2)}) %collective-permute-start.8) | collective-permute-done | bytes 69664 | tf_op jit(solution)/shard_map/ppermute | solution.py:390
  25.4 0.6 %collective-permute-done.9.refs_2_ = bf16[272,128]{1,0:T(8,128)(2,1)S(1)} collective-permute-done((bf16[272,128]{1,0:T(8,128)(2,1)S(1)}, bf16[272,128]{1,0:T(8,128)(2,1)S(1)}, u32[]{:S(2)}, u32[]{:S(2)}) %collective-permute-start.9) | collective-permute-done | bytes 69664 | tf_op jit(solution)/shard_map/ppermute | solution.py:390
  26.2 2.7 %collective-permute-start.10 = (bf16[272,128]{1,0:T(8,128)(2,1)S(1)}, bf16[272,128]{1,0:T(8,128)(2,1)S(1)}, u32[]{:S(2)}, u32[]{:S(2)}) collective-permute-start(bf16[272,128]{1,0:T(8,128)(2,1)S(1)} %get-tuple-element.40), channel_id=1, source_target_pairs={{0,24},{1,25},{2,26},{3,27},{4,28},{5,29},{6,30},{7,31},{8,16},{9,... | collective-permute-start | bytes 208904 | tf_op jit(solution)/shard_map/ppermute | solution.py:390
  28.9 3.5 %collective-permute-start.12 = (bf16[272,128]{1,0:T(8,128)(2,1)S(1)}, bf16[272,128]{1,0:T(8,128)(2,1)S(1)}, u32[]{:S(2)}, u32[]{:S(2)}) collective-permute-start(bf16[272,128]{1,0:T(8,128)(2,1)S(1)} %get-tuple-element.42), channel_id=1, source_target_pairs={{0,14},{1,15},{2,12},{3,13},{4,10},{5,11},{6,8},{7,9},{8,6},{9,7},... | collective-permute-start | bytes 208904 | tf_op jit(solution)/shard_map/ppermute | solution.py:390
  32.4 3.8 %collective-permute-done.11.refs_1_ = bf16[272,128]{1,0:T(8,128)(2,1)S(1)} collective-permute-done((bf16[272,128]{1,0:T(8,128)(2,1)S(1)}, bf16[272,128]{1,0:T(8,128)(2,1)S(1)}, u32[]{:S(2)}, u32[]{:S(2)}) %collective-permute-start.11) | collective-permute-done | bytes 69664 | tf_op jit(solution)/shard_map/ppermute | solution.py:390
  36.2 6.7 %shard_map.32.factor_ref = bf16[512,512]{1,0:T(8,128)(2,1)S(1)} custom-call(f32[4,264,128]{2,1,0:T(8,128)S(1)} %shard_map.29.sum_ref, f32[264,128]{1,0:T(8,128)S(1)} %get-tuple-element.39.total_ref, bf16[272,128]{1,0:T(8,128)(2,1)S(1)} %collective-permute-done.10.refs_0_, bf16[272,128]{1,0:T(8,128)(2,1)S(1)} %collective-permute-done.11.refs_1_, ...), custom_call_target="tpu_custom_call" | custom-call | tf_op jit(solution)/shard_map/pallas_call | solution.py:90
  42.9 0.7 %shard_map.33 = (bf16[128,512]{1,0:T(8,128)(2,1)S(1)}, bf16[128,512]{1,0:T(8,128)(2,1)S(1)}, bf16[128,512]{1,0:T(8,128)(2,1)S(1)}, bf16[128,512]{1,0:T(8,128)(2,...) custom-call(bf16[512,512]{1,0:T(8,128)(2,1)S(1)} %shard_map.32.facto, ...), custom_call_target="tpu_custom_call" | custom-call | tf_op jit(solution)/shard_map/pallas_call | solution.py:90
  43.6 1.0 %collective-permute-start.13 = (bf16[128,512]{1,0:T(8,128)(2,1)S(1)}, bf16[128,512]{1,0:T(8,128)(2,1)S(1)}, u32[]{:S(2)}, u32[]{:S(2)}) collective-permute-start(bf16[128,512]{1,0:T(8,128)(2,1)S(1)} %get-tuple-element.44), channel_id=1, source_target_pairs={{2,0},{5,1},{0,2},{7,3},{6,4},{1,5},{4,6},{3,7},{10,8},{13,9},{8,1... | collective-permute-start | bytes 393224 | tf_op jit(solution)/shard_map/ppermute | solution.py:390
  44.6 1.4 %collective-permute-start.14 = (bf16[128,512]{1,0:T(8,128)(2,1)S(1)}, bf16[128,512]{1,0:T(8,128)(2,1)S(1)}, u32[]{:S(2)}, u32[]{:S(2)}) collective-permute-start(bf16[128,512]{1,0:T(8,128)(2,1)S(1)} %get-tuple-element.45), channel_id=1, source_target_pairs={{4,0},{9,1},{6,2},{11,3},{0,4},{13,5},{2,6},{15,7},{12,8},{1,9},{1... | collective-permute-start | bytes 393224 | tf_op jit(solution)/shard_map/ppermute | solution.py:390
  45.9 1.2 %collective-permute-start.15 = (bf16[128,512]{1,0:T(8,128)(2,1)S(1)}, bf16[128,512]{1,0:T(8,128)(2,1)S(1)}, u32[]{:S(2)}, u32[]{:S(2)}) collective-permute-start(bf16[128,512]{1,0:T(8,128)(2,1)S(1)} %get-tuple-element.46), channel_id=1, source_target_pairs={{8,0},{3,1},{10,2},{1,3},{12,4},{7,5},{14,6},{5,7},{0,8},{11,9},{2... | collective-permute-start | bytes 393224 | tf_op jit(solution)/shard_map/ppermute | solution.py:390
  47.1 1.2 %collective-permute-start.17 = (bf16[128,512]{1,0:T(8,128)(2,1)S(1)}, bf16[128,512]{1,0:T(8,128)(2,1)S(1)}, u32[]{:S(2)}, u32[]{:S(2)}) collective-permute-start(bf16[128,512]{1,0:T(8,128)(2,1)S(1)} %get-tuple-element.48), channel_id=1, source_target_pairs={{5,0},{8,1},{7,2},{10,3},{1,4},{12,5},{3,6},{14,7},{13,8},{0,9},{1... | collective-permute-start | bytes 393224 | tf_op jit(solution)/shard_map/ppermute | solution.py:390
  48.3 0.4 collective-permute-done.13.refs_1_
  48.8 0.7 %collective-permute-done.14.refs_2_ = bf16[128,512]{1,0:T(8,128)(2,1)S(1)} collective-permute-done((bf16[128,512]{1,0:T(8,128)(2,1)S(1)}, bf16[128,512]{1,0:T(8,128)(2,1)S(1)}, u32[]{:S(2)}, u32[]{:S(2)}) %collective-permute-start.14) | collective-permute-done | bytes 131104 | tf_op jit(solution)/shard_map/ppermute | solution.py:390
  49.5 0.8 %collective-permute-start.19 = (bf16[128,512]{1,0:T(8,128)(2,1)S(1)}, bf16[128,512]{1,0:T(8,128)(2,1)S(1)}, u32[]{:S(2)}, u32[]{:S(2)}) collective-permute-start(bf16[128,512]{1,0:T(8,128)(2,1)S(1)} %get-tuple-element.50), channel_id=1, source_target_pairs={{1,0},{0,1},{3,2},{2,3},{5,4},{4,5},{7,6},{6,7},{9,8},{8,9},{11,10... | collective-permute-start | bytes 393224 | tf_op jit(solution)/shard_map/ppermute | solution.py:390
  50.3 0.6 collective-permute-done.15.refs_3_
  50.9 0.6 %collective-permute-done.16.refs_4_ = bf16[128,512]{1,0:T(8,128)(2,1)S(1)} collective-permute-done((bf16[128,512]{1,0:T(8,128)(2,1)S(1)}, bf16[128,512]{1,0:T(8,128)(2,1)S(1)}, u32[]{:S(2)}, u32[]{:S(2)}) %collective-permute-start.16) | collective-permute-done | bytes 131104 | tf_op jit(solution)/shard_map/ppermute | solution.py:390
  51.5 0.9 %collective-permute-done.17.refs_5_ = bf16[128,512]{1,0:T(8,128)(2,1)S(1)} collective-permute-done((bf16[128,512]{1,0:T(8,128)(2,1)S(1)}, bf16[128,512]{1,0:T(8,128)(2,1)S(1)}, u32[]{:S(2)}, u32[]{:S(2)}) %collective-permute-start.17) | collective-permute-done | bytes 131104 | tf_op jit(solution)/shard_map/ppermute | solution.py:390
  52.3 1.6 %collective-permute-done.18.refs_6_ = bf16[128,512]{1,0:T(8,128)(2,1)S(1)} collective-permute-done((bf16[128,512]{1,0:T(8,128)(2,1)S(1)}, bf16[128,512]{1,0:T(8,128)(2,1)S(1)}, u32[]{:S(2)}, u32[]{:S(2)}) %collective-permute-start.18) | collective-permute-done | bytes 131104 | tf_op jit(solution)/shard_map/ppermute | solution.py:390
  53.9 1.3 %shard_map.34 = bf16[4,2,128,512]{3,2,1,0:T(8,128)(2,1)} custom-call(bf16[4,2,128,512]{3,2,1,0:T(8,128)(2,1)S(1)} %bitcast.3, bf16[128,512]{1,0:T(8,128)(2,1)S(1)} %get-tuple-element.43.refs_0_, bf16[128,512]{1,0:T(8,128)(2,1)S(1)} %collective-permute-done.13.refs_1_, bf16[128,512]{1,0:T(8,128)(2,1)S(1)} %collective-permute-done.14.refs_2_, ...), custom_call_target="tpu_custom_call" | custom-call | tf_op jit(solution)/shard_map/pallas_call | solution.py:90
  (19 shorter events, 0.7 us)
Async XLA Ops:
  0.0 1.2 %copy-start.1 = (bf16[1,8,128,512]{3,2,1,0:T(8,128)(2,1)S(1)}, bf16[1,8,128,512]{3,2,1,0:T(8,128)(2,1)}, u32[]{:S(2)}) copy-start(bf16[1,8,128,512]{3,2,1,0:T(8,128)(2,1)} %param.2) | copy-start | bytes 3145732
  1.3 7.9 %collective-permute-start = (bf16[128,512]{1,0:T(8,128)(2,1)S(1)}, bf16[128,512]{1,0:T(8,128)(2,1)S(1)}, u32[]{:S(2)}, u32[]{:S(2)}) collective-permute-start(bf16[128,512]{1,0:T(8,128)(2,1)S(1)} %get-tuple-element.29), channel_id=1, source_target_pairs={{0,2},{1,5},{2,0},{3,7},{4,6},{5,1},{6,4},{7,3},{8,10},{9,13},{10,... | collective-permute-start | bytes 393224 | tf_op jit(solution)/shard_map/ppermute | solution.py:390
  4.3 5.0 %collective-permute-start.1 = (bf16[128,512]{1,0:T(8,128)(2,1)S(1)}, bf16[128,512]{1,0:T(8,128)(2,1)S(1)}, u32[]{:S(2)}, u32[]{:S(2)}) collective-permute-start(bf16[128,512]{1,0:T(8,128)(2,1)S(1)} %get-tuple-element.30), channel_id=1, source_target_pairs={{0,4},{1,9},{2,6},{3,11},{4,0},{5,13},{6,2},{7,15},{8,12},{9,1},{1... | collective-permute-start | bytes 393224 | tf_op jit(solution)/shard_map/ppermute | solution.py:390
  5.8 5.4 %collective-permute-start.2 = (bf16[128,512]{1,0:T(8,128)(2,1)S(1)}, bf16[128,512]{1,0:T(8,128)(2,1)S(1)}, u32[]{:S(2)}, u32[]{:S(2)}) collective-permute-start(bf16[128,512]{1,0:T(8,128)(2,1)S(1)} %get-tuple-element.31), channel_id=1, source_target_pairs={{0,8},{1,3},{2,10},{3,1},{4,12},{5,7},{6,14},{7,5},{8,0},{9,11},{1... | collective-permute-start | bytes 393224 | tf_op jit(solution)/shard_map/ppermute | solution.py:390
  7.4 5.0 %collective-permute-start.3 = (bf16[128,512]{1,0:T(8,128)(2,1)S(1)}, bf16[128,512]{1,0:T(8,128)(2,1)S(1)}, u32[]{:S(2)}, u32[]{:S(2)}) collective-permute-start(bf16[128,512]{1,0:T(8,128)(2,1)S(1)} %get-tuple-element.32), channel_id=1, source_target_pairs={{0,3},{1,4},{2,1},{3,6},{4,7},{5,0},{6,5},{7,2},{8,11},{9,12},{10,... | collective-permute-start | bytes 393224 | tf_op jit(solution)/shard_map/ppermute | solution.py:390
  7.4 5.0 %collective-permute-start.4 = (bf16[128,512]{1,0:T(8,128)(2,1)S(1)}, bf16[128,512]{1,0:T(8,128)(2,1)S(1)}, u32[]{:S(2)}, u32[]{:S(2)}) collective-permute-start(bf16[128,512]{1,0:T(8,128)(2,1)S(1)} %get-tuple-element.33), channel_id=1, source_target_pairs={{0,5},{1,8},{2,7},{3,10},{4,1},{5,12},{6,3},{7,14},{8,13},{9,0},{1... | collective-permute-start | bytes 393224 | tf_op jit(solution)/shard_map/ppermute | solution.py:390
  9.1 4.4 %collective-permute-start.5 = (bf16[128,512]{1,0:T(8,128)(2,1)S(1)}, bf16[128,512]{1,0:T(8,128)(2,1)S(1)}, u32[]{:S(2)}, u32[]{:S(2)}) collective-permute-start(bf16[128,512]{1,0:T(8,128)(2,1)S(1)} %get-tuple-element.34), channel_id=1, source_target_pairs={{0,9},{1,2},{2,11},{3,0},{4,13},{5,6},{6,15},{7,4},{8,1},{9,10},{1... | collective-permute-start | bytes 393224 | tf_op jit(solution)/shard_map/ppermute | solution.py:390
  9.3 4.3 %collective-permute-start.6 = (bf16[128,512]{1,0:T(8,128)(2,1)S(1)}, bf16[128,512]{1,0:T(8,128)(2,1)S(1)}, u32[]{:S(2)}, u32[]{:S(2)}) collective-permute-start(bf16[128,512]{1,0:T(8,128)(2,1)S(1)} %get-tuple-element.35), channel_id=1, source_target_pairs={{0,1},{1,0},{2,3},{3,2},{4,5},{5,4},{6,7},{7,6},{8,9},{9,8},{10,11... | collective-permute-start | bytes 393224 | tf_op jit(solution)/shard_map/ppermute | solution.py:390
  14.2 6.3 %collective-permute-start.7 = (bf16[272,128]{1,0:T(8,128)(2,1)S(1)}, bf16[272,128]{1,0:T(8,128)(2,1)S(1)}, u32[]{:S(2)}, u32[]{:S(2)}) collective-permute-start(bf16[272,128]{1,0:T(8,128)(2,1)S(1)} %get-tuple-element.36), channel_id=1, source_target_pairs={{0,24},{1,25},{2,26},{3,27},{4,28},{5,29},{6,30},{7,31},{8,16},{9,... | collective-permute-start | bytes 208904 | tf_op jit(solution)/shard_map/ppermute | solution.py:390
  17.7 7.7 %collective-permute-start.8 = (bf16[272,128]{1,0:T(8,128)(2,1)S(1)}, bf16[272,128]{1,0:T(8,128)(2,1)S(1)}, u32[]{:S(2)}, u32[]{:S(2)}) collective-permute-start(bf16[272,128]{1,0:T(8,128)(2,1)S(1)} %get-tuple-element.37), channel_id=1, source_target_pairs={{0,22},{1,23},{2,20},{3,21},{4,18},{5,19},{6,16},{7,17},{8,30},{9,... | collective-permute-start | bytes 208904 | tf_op jit(solution)/shard_map/ppermute | solution.py:390
  18.6 7.4 %collective-permute-start.9 = (bf16[272,128]{1,0:T(8,128)(2,1)S(1)}, bf16[272,128]{1,0:T(8,128)(2,1)S(1)}, u32[]{:S(2)}, u32[]{:S(2)}) collective-permute-start(bf16[272,128]{1,0:T(8,128)(2,1)S(1)} %get-tuple-element.38), channel_id=1, source_target_pairs={{0,14},{1,15},{2,12},{3,13},{4,10},{5,11},{6,8},{7,9},{8,6},{9,7},... | collective-permute-start | bytes 208904 | tf_op jit(solution)/shard_map/ppermute | solution.py:390
  26.2 6.3 %collective-permute-start.10 = (bf16[272,128]{1,0:T(8,128)(2,1)S(1)}, bf16[272,128]{1,0:T(8,128)(2,1)S(1)}, u32[]{:S(2)}, u32[]{:S(2)}) collective-permute-start(bf16[272,128]{1,0:T(8,128)(2,1)S(1)} %get-tuple-element.40), channel_id=1, source_target_pairs={{0,24},{1,25},{2,26},{3,27},{4,28},{5,29},{6,30},{7,31},{8,16},{9,... | collective-permute-start | bytes 208904 | tf_op jit(solution)/shard_map/ppermute | solution.py:390
  28.9 7.3 %collective-permute-start.11 = (bf16[272,128]{1,0:T(8,128)(2,1)S(1)}, bf16[272,128]{1,0:T(8,128)(2,1)S(1)}, u32[]{:S(2)}, u32[]{:S(2)}) collective-permute-start(bf16[272,128]{1,0:T(8,128)(2,1)S(1)} %get-tuple-element.41), channel_id=1, source_target_pairs={{0,22},{1,23},{2,20},{3,21},{4,18},{5,19},{6,16},{7,17},{8,30},{9,... | collective-permute-start | bytes 208904 | tf_op jit(solution)/shard_map/ppermute | solution.py:390
  28.9 7.3 %collective-permute-start.12 = (bf16[272,128]{1,0:T(8,128)(2,1)S(1)}, bf16[272,128]{1,0:T(8,128)(2,1)S(1)}, u32[]{:S(2)}, u32[]{:S(2)}) collective-permute-start(bf16[272,128]{1,0:T(8,128)(2,1)S(1)} %get-tuple-element.42), channel_id=1, source_target_pairs={{0,14},{1,15},{2,12},{3,13},{4,10},{5,11},{6,8},{7,9},{8,6},{9,7},... | collective-permute-start | bytes 208904 | tf_op jit(solution)/shard_map/ppermute | solution.py:390
  42.9 11.1 %copy-start = (bf16[1,8,128,512]{3,2,1,0:T(8,128)(2,1)S(1)}, bf16[1,8,128,512]{3,2,1,0:T(8,128)(2,1)}, u32[]{:S(2)}) copy-start(bf16[1,8,128,512]{3,2,1,0:T(8,128)(2,1)} %param.3) | copy-start | bytes 3145732
  43.6 5.0 %collective-permute-start.13 = (bf16[128,512]{1,0:T(8,128)(2,1)S(1)}, bf16[128,512]{1,0:T(8,128)(2,1)S(1)}, u32[]{:S(2)}, u32[]{:S(2)}) collective-permute-start(bf16[128,512]{1,0:T(8,128)(2,1)S(1)} %get-tuple-element.44), channel_id=1, source_target_pairs={{2,0},{5,1},{0,2},{7,3},{6,4},{1,5},{4,6},{3,7},{10,8},{13,9},{8,1... | collective-permute-start | bytes 393224 | tf_op jit(solution)/shard_map/ppermute | solution.py:390
  44.6 5.0 %collective-permute-start.14 = (bf16[128,512]{1,0:T(8,128)(2,1)S(1)}, bf16[128,512]{1,0:T(8,128)(2,1)S(1)}, u32[]{:S(2)}, u32[]{:S(2)}) collective-permute-start(bf16[128,512]{1,0:T(8,128)(2,1)S(1)} %get-tuple-element.45), channel_id=1, source_target_pairs={{4,0},{9,1},{6,2},{11,3},{0,4},{13,5},{2,6},{15,7},{12,8},{1,9},{1... | collective-permute-start | bytes 393224 | tf_op jit(solution)/shard_map/ppermute | solution.py:390
  45.9 5.0 %collective-permute-start.15 = (bf16[128,512]{1,0:T(8,128)(2,1)S(1)}, bf16[128,512]{1,0:T(8,128)(2,1)S(1)}, u32[]{:S(2)}, u32[]{:S(2)}) collective-permute-start(bf16[128,512]{1,0:T(8,128)(2,1)S(1)} %get-tuple-element.46), channel_id=1, source_target_pairs={{8,0},{3,1},{10,2},{1,3},{12,4},{7,5},{14,6},{5,7},{0,8},{11,9},{2... | collective-permute-start | bytes 393224 | tf_op jit(solution)/shard_map/ppermute | solution.py:390
  47.1 4.4 %collective-permute-start.16 = (bf16[128,512]{1,0:T(8,128)(2,1)S(1)}, bf16[128,512]{1,0:T(8,128)(2,1)S(1)}, u32[]{:S(2)}, u32[]{:S(2)}) collective-permute-start(bf16[128,512]{1,0:T(8,128)(2,1)S(1)} %get-tuple-element.47), channel_id=1, source_target_pairs={{3,0},{4,1},{1,2},{6,3},{7,4},{0,5},{5,6},{2,7},{11,8},{12,9},{9,1... | collective-permute-start | bytes 393224 | tf_op jit(solution)/shard_map/ppermute | solution.py:390
  47.1 5.2 %collective-permute-start.17 = (bf16[128,512]{1,0:T(8,128)(2,1)S(1)}, bf16[128,512]{1,0:T(8,128)(2,1)S(1)}, u32[]{:S(2)}, u32[]{:S(2)}) collective-permute-start(bf16[128,512]{1,0:T(8,128)(2,1)S(1)} %get-tuple-element.48), channel_id=1, source_target_pairs={{5,0},{8,1},{7,2},{10,3},{1,4},{12,5},{3,6},{14,7},{13,8},{0,9},{1... | collective-permute-start | bytes 393224 | tf_op jit(solution)/shard_map/ppermute | solution.py:390
  48.6 5.3 %collective-permute-start.18 = (bf16[128,512]{1,0:T(8,128)(2,1)S(1)}, bf16[128,512]{1,0:T(8,128)(2,1)S(1)}, u32[]{:S(2)}, u32[]{:S(2)}) collective-permute-start(bf16[128,512]{1,0:T(8,128)(2,1)S(1)} %get-tuple-element.49), channel_id=1, source_target_pairs={{9,0},{2,1},{11,2},{0,3},{13,4},{6,5},{15,6},{4,7},{1,8},{10,9},{3... | collective-permute-start | bytes 393224 | tf_op jit(solution)/shard_map/ppermute | solution.py:390
  49.5 4.4 %collective-permute-start.19 = (bf16[128,512]{1,0:T(8,128)(2,1)S(1)}, bf16[128,512]{1,0:T(8,128)(2,1)S(1)}, u32[]{:S(2)}, u32[]{:S(2)}) collective-permute-start(bf16[128,512]{1,0:T(8,128)(2,1)S(1)} %get-tuple-element.50), channel_id=1, source_target_pairs={{1,0},{0,1},{3,2},{2,3},{5,4},{4,5},{7,6},{6,7},{9,8},{8,9},{11,10... | collective-permute-start | bytes 393224 | tf_op jit(solution)/shard_map/ppermute | solution.py:390

commit v5 on v4

--- a/solution.py
+++ b/solution.py
@@ -14,6 +14,7 @@
 F32_TILE = 8
 BF16_TILE = 16
 VMEM_BYTES = 48 << 20
+EARLY = 5
 
 first_coef = 3.4445
 second_coef = -4.775
@@ -32,7 +33,7 @@
 def neighbour_steps():
     ways = [(0, 0, 1), (0, 1, 0), (1, 0, 0)]
     order = [(ways[step], ways[(step + 1) % 3]) for step in range(3)]
-    return [tuple(flips_of(*way, pair=cross) for way in step) for cross in range(2) for step in order]
+    return [tuple(flips_of(*way, pair=cross) for way in step) for cross in (1, 0) for step in order]
 
 
 ROWS = neighbour_steps() + [(flips_of(0, 0, 0, pair=1),) * 2]
@@ -85,12 +86,12 @@
         return self.quarter ^ by_pair(self.pair, [quarter_step(flips) for flips in OWNERS[step]])
 
 
-def call(kernel, out_shape, *operands, spaces=None, scratch=()):
+def call(kernel, out_shape, *operands, scratch=()):
     vmem = pl.BlockSpec(memory_space=pltpu.VMEM)
     return pl.pallas_call(
         kernel,
         out_shape=out_shape,
-        in_specs=[vmem] * len(operands) if spaces is None else [pl.BlockSpec(memory_space=space) for space in spaces],
+        in_specs=[vmem] * len(operands),
         out_specs=jax.tree.map(lambda _: vmem, out_shape),
         scratch_shapes=list(scratch),
         compiler_params=pltpu.CompilerParams(vmem_limit_bytes=VMEM_BYTES),
@@ -212,9 +213,8 @@
         block_ref[...] = momentum_ref[place.block(number)]
 
 
-def gram_kernel(*refs):
-    rows = jnp.concatenate([block_ref[...] for block_ref in refs[:-1]], axis=0)
-    packed_ref = refs[-1]
+def packed_gram(block_refs):
+    rows = jnp.concatenate([block_ref[...] for block_ref in block_refs], axis=0)
     order = rows.shape[1]
     tiles = {}
     for row in range(0, order, WIDE):
@@ -231,8 +231,17 @@
         tile = tiles[row // WIDE * WIDE, column // WIDE * WIDE]
         return tile[row % WIDE :, column % WIDE :][:BLOCK, :BLOCK]
 
-    for quarter, value in enumerate(pack(block, order)):
-        packed_ref[quarter] = value
+    return pack(block, order)
+
+
+def early_gram_kernel(*refs):
+    for quarter, value in enumerate(packed_gram(refs[:-1])):
+        refs[-1][quarter] = value
+
+
+def gram_kernel(early_ref, *refs):
+    for quarter, value in enumerate(packed_gram(refs[:-1])):
+        refs[-1][quarter] = early_ref[quarter] + value
 
 
 def reduce_kernel(rest_count, order, sum_ref, *message_refs):
@@ -353,15 +362,37 @@
         update_ref[...] = update[number * count : (number + 1) * count].astype(update_ref.dtype)
 
 
-def weights_kernel(rest_count, weights_ref, *refs):
-    update_refs, out_ref = refs[:-1], refs[-1]
+def weights_kernel(rest_count, numbers, weights_ref, *refs):
+    out_ref, fresh_ref, semaphores = refs[-3:]
     place = Place(rest_count)
     shrink = 1.0 - step_rate * decay_rate
-    for number, update_ref in enumerate(update_refs):
+    copies = []
+    for slot, (number, update_ref) in enumerate(zip(numbers, refs)):
         block = place.block(number)
-        out_ref[block] = (
+        fresh_ref[slot] = (
             shrink * weights_ref[block].astype(jnp.float32) - step_rate * update_ref[...].astype(jnp.float32)
-        ).astype(out_ref.dtype)
+        ).astype(fresh_ref.dtype)
+        copies.append(pltpu.make_async_copy(fresh_ref.at[slot], out_ref.at[block], semaphores.at[slot]))
+        copies[-1].start()
+    for copy in copies:
+        copy.wait()
+
+
+def new_weights(rest_count, numbers, weights, updates, so_far=None):
+    vmem, whole = pl.BlockSpec(memory_space=pltpu.VMEM), pl.BlockSpec(memory_space=pltpu.HBM)
+    operands = [weights, *updates] + ([] if so_far is None else [so_far])
+    return pl.pallas_call(
+        functools.partial(weights_kernel, rest_count, numbers),
+        out_shape=jax.ShapeDtypeStruct(weights.shape, weights.dtype),
+        in_specs=[vmem] * (1 + len(updates)) + ([] if so_far is None else [whole]),
+        out_specs=whole,
+        scratch_shapes=[
+            pltpu.VMEM((len(numbers),) + weights.shape[2:], weights.dtype),
+            pltpu.SemaphoreType.DMA((len(numbers),)),
+        ],
+        input_output_aliases={} if so_far is None else {len(operands) - 1: 0},
+        compiler_params=pltpu.CompilerParams(vmem_limit_bytes=VMEM_BYTES),
+    )(*operands)
 
 
 def on_device(momentum, weights):
@@ -402,7 +433,8 @@
         spread.reshape(by_block),
     )
     rows = [own] + swap(dealt, ROWS)
-    place_sum = call(gram_kernel, packed, *rows)
+    early_gram = call(early_gram_kernel, packed, *rows[:EARLY])
+    place_sum = call(gram_kernel, packed, early_gram, *rows[EARLY:])
     parts = call(functools.partial(reduce_kernel, rest_count, order), (message,) * 3, place_sum)
     total, *rests = call(
         functools.partial(gather_kernel, rest_count, order),
@@ -419,13 +451,11 @@
         scratch=[pltpu.VMEM(packed.shape, packed.dtype)],
     )
     own_update, *updates = call(update_kernel, blocks, factor, *rows)
-    fresh = call(
-        functools.partial(weights_kernel, rest_count),
-        jax.ShapeDtypeStruct(by_block, weights.dtype),
-        regroup(weights[0], 0, 1).reshape(by_block),
-        own_update,
-        *swap(updates, ROWS, back=True),
-    )
+    held = regroup(weights[0], 0, 1).reshape(by_block)
+    returned = [own_update] + swap(updates, ROWS, back=True)
+    numbers = range(len(blocks))
+    fresh = new_weights(rest_count, numbers[:EARLY], held, returned[:EARLY])
+    fresh = new_weights(rest_count, numbers[EARLY:], held, returned[EARLY:], fresh)
     return regroup(fresh.reshape(experts, row_count, order), 1, 0)[None]
 
 

time: 55.4 us -> 53.7 us (0.969)
  waiting for transfers between devices: 17.8 us -> 15.2 us
  Pallas kernels: 9.59 us -> 10.3 us
    ppermute x20, waiting for transfers between devices: 17.8 us -> 15.2 us  [swap(): lax.ppermute(array, AXES, permute)]
    pallas_call x0 -> x2, Pallas kernels: none -> 1.77 us  [new_weights(): pl.pallas_call(functools.partial(weights_kernel, rest_count, numbers), ou...]
    pallas_call x7, Pallas kernels: 9.59 us -> 8.55 us  [call(): pl.pallas_call(kernel, out_shape=out_shape, in_specs=[vmem] * len(operand...]
  transfers between devices with their start and end apart: 20 -> 20, of which waited for: 13 -> 10; matrix products, arithmetic and copies ran while one was open for 0% -> 0% of each run, Pallas kernels for 0% -> 3%
where the time goes in v5:
time: 53.7 us; the launch traced here: 53.5 us
  starting transfers between devices  26.7 us (50%)
  waiting for transfers between devices  15.2 us (28%)
  Pallas kernels  10.3 us (19%)
  local copies, waits for them, and re-layouts  1.23 us (2%)
    ppermute x20, starting transfers between devices, swap(): lax.ppermute(array, AXES, permute)  26.7 us
    ppermute x20, waiting for transfers between devices, swap(): lax.ppermute(array, AXES, permute)  15.2 us
    pallas_call x7, Pallas kernels, call(): pl.pallas_call(kernel, out_shape=out_shape, in_specs=[vmem] * len(operand...  8.55 us
    pallas_call x2, Pallas kernels, new_weights(): pl.pallas_call(functools.partial(weights_kernel, rest_count, numbers), ou...  1.77 us
    unnamed x4, local copies, waits for them, and re-layouts  1.23 us
  transfers between devices with their start and end apart: 20, of which 10 were waited for; matrix products, arithmetic and copies ran while one was open for 0% of the time, Pallas kernels for 3%

profile of v5, /device:TPU:0, one launch (start us, length us, event | category | flops | bytes accessed | tf_op | source)
XLA Modules:
  0.0 53.5 jit_solution(11322352344419477794)
XLA Ops:
  0.0 1.2 %copy-done.1 = bf16[1,8,128,512]{3,2,1,0:T(8,128)(2,1)S(1)} copy-done((bf16[1,8,128,512]{3,2,1,0:T(8,128)(2,1)S(1)}, bf16[1,8,128,512]{3,2,1,0:T(8,128)(2,1)}, u32[]{:S(2)}) %copy-start.1) | copy-done | bytes 1048600
  1.3 2.4 %collective-permute-start = (bf16[128,512]{1,0:T(8,128)(2,1)S(1)}, bf16[128,512]{1,0:T(8,128)(2,1)S(1)}, u32[]{:S(2)}, u32[]{:S(2)}) collective-permute-start(bf16[128,512]{1,0:T(8,128)(2,1)S(1)} %get-tuple-element.29), channel_id=1, source_target_pairs={{0,3},{1,4},{2,1},{3,6},{4,7},{5,0},{6,5},{7,2},{8,11},{9,12},{10,... | collective-permute-start | bytes 393224 | tf_op jit(solution)/shard_map/ppermute | solution.py:421
  3.8 1.8 %collective-permute-start.2 = (bf16[128,512]{1,0:T(8,128)(2,1)S(1)}, bf16[128,512]{1,0:T(8,128)(2,1)S(1)}, u32[]{:S(2)}, u32[]{:S(2)}) collective-permute-start(bf16[128,512]{1,0:T(8,128)(2,1)S(1)} %get-tuple-element.31), channel_id=1, source_target_pairs={{0,9},{1,2},{2,11},{3,0},{4,13},{5,6},{6,15},{7,4},{8,1},{9,10},{1... | collective-permute-start | bytes 393224 | tf_op jit(solution)/shard_map/ppermute | solution.py:421
  5.6 1.5 %collective-permute-start.3 = (bf16[128,512]{1,0:T(8,128)(2,1)S(1)}, bf16[128,512]{1,0:T(8,128)(2,1)S(1)}, u32[]{:S(2)}, u32[]{:S(2)}) collective-permute-start(bf16[128,512]{1,0:T(8,128)(2,1)S(1)} %get-tuple-element.32), channel_id=1, source_target_pairs={{0,2},{1,5},{2,0},{3,7},{4,6},{5,1},{6,4},{7,3},{8,10},{9,13},{10,... | collective-permute-start | bytes 393224 | tf_op jit(solution)/shard_map/ppermute | solution.py:421
  7.1 0.5 collective-permute-start.4
  7.6 1.6 %collective-permute-start.5 = (bf16[128,512]{1,0:T(8,128)(2,1)S(1)}, bf16[128,512]{1,0:T(8,128)(2,1)S(1)}, u32[]{:S(2)}, u32[]{:S(2)}) collective-permute-start(bf16[128,512]{1,0:T(8,128)(2,1)S(1)} %get-tuple-element.34), channel_id=1, source_target_pairs={{0,8},{1,3},{2,10},{3,1},{4,12},{5,7},{6,14},{7,5},{8,0},{9,11},{1... | collective-permute-start | bytes 393224 | tf_op jit(solution)/shard_map/ppermute | solution.py:421
  9.4 1.2 %collective-permute-done.3.refs_4_ = bf16[128,512]{1,0:T(8,128)(2,1)S(1)} collective-permute-done((bf16[128,512]{1,0:T(8,128)(2,1)S(1)}, bf16[128,512]{1,0:T(8,128)(2,1)S(1)}, u32[]{:S(2)}, u32[]{:S(2)}) %collective-permute-start.3) | collective-permute-done | bytes 131104 | tf_op jit(solution)/shard_map/ppermute | solution.py:421
  10.6 0.5 shard_map.29.early_ref
  11.1 1.0 %collective-permute-done.4.refs_0_.refs_5_ = bf16[128,512]{1,0:T(8,128)(2,1)S(1)} collective-permute-done((bf16[128,512]{1,0:T(8,128)(2,1)S(1)}, bf16[128,512]{1,0:T(8,128)(2,1)S(1)}, u32[]{:S(2)}, u32[]{:S(2)}) %collective-permute-start.4) | collective-permute-done | bytes 131104 | tf_op jit(solution)/shard_map/ppermute | solution.py:421
  12.1 0.7 %collective-permute-done.5.refs_1_.refs_6_ = bf16[128,512]{1,0:T(8,128)(2,1)S(1)} collective-permute-done((bf16[128,512]{1,0:T(8,128)(2,1)S(1)}, bf16[128,512]{1,0:T(8,128)(2,1)S(1)}, u32[]{:S(2)}, u32[]{:S(2)}) %collective-permute-start.5) | collective-permute-done | bytes 131104 | tf_op jit(solution)/shard_map/ppermute | solution.py:421
  12.8 0.4 shard_map.30.sum_ref
  13.3 3.7 %collective-permute-start.7 = (bf16[272,128]{1,0:T(8,128)(2,1)S(1)}, bf16[272,128]{1,0:T(8,128)(2,1)S(1)}, u32[]{:S(2)}, u32[]{:S(2)}) collective-permute-start(bf16[272,128]{1,0:T(8,128)(2,1)S(1)} %get-tuple-element.36), channel_id=1, source_target_pairs={{0,24},{1,25},{2,26},{3,27},{4,28},{5,29},{6,30},{7,31},{8,16},{9,... | collective-permute-start | bytes 208904 | tf_op jit(solution)/shard_map/ppermute | solution.py:421
  17.0 1.3 %collective-permute-start.8 = (bf16[272,128]{1,0:T(8,128)(2,1)S(1)}, bf16[272,128]{1,0:T(8,128)(2,1)S(1)}, u32[]{:S(2)}, u32[]{:S(2)}) collective-permute-start(bf16[272,128]{1,0:T(8,128)(2,1)S(1)} %get-tuple-element.37), channel_id=1, source_target_pairs={{0,22},{1,23},{2,20},{3,21},{4,18},{5,19},{6,16},{7,17},{8,30},{9,... | collective-permute-start | bytes 208904 | tf_op jit(solution)/shard_map/ppermute | solution.py:421
  18.3 1.3 %collective-permute-start.9 = (bf16[272,128]{1,0:T(8,128)(2,1)S(1)}, bf16[272,128]{1,0:T(8,128)(2,1)S(1)}, u32[]{:S(2)}, u32[]{:S(2)}) collective-permute-start(bf16[272,128]{1,0:T(8,128)(2,1)S(1)} %get-tuple-element.38), channel_id=1, source_target_pairs={{0,14},{1,15},{2,12},{3,13},{4,10},{5,11},{6,8},{7,9},{8,6},{9,7},... | collective-permute-start | bytes 208904 | tf_op jit(solution)/shard_map/ppermute | solution.py:421
  19.6 4.8 %collective-permute-done.8.refs_1_ = bf16[272,128]{1,0:T(8,128)(2,1)S(1)} collective-permute-done((bf16[272,128]{1,0:T(8,128)(2,1)S(1)}, bf16[272,128]{1,0:T(8,128)(2,1)S(1)}, u32[]{:S(2)}, u32[]{:S(2)}) %collective-permute-start.8) | collective-permute-done | bytes 69664 | tf_op jit(solution)/shard_map/ppermute | solution.py:421
  24.4 0.7 %collective-permute-done.9.refs_2_ = bf16[272,128]{1,0:T(8,128)(2,1)S(1)} collective-permute-done((bf16[272,128]{1,0:T(8,128)(2,1)S(1)}, bf16[272,128]{1,0:T(8,128)(2,1)S(1)}, u32[]{:S(2)}, u32[]{:S(2)}) %collective-permute-start.9) | collective-permute-done | bytes 69664 | tf_op jit(solution)/shard_map/ppermute | solution.py:421
  25.2 2.7 %collective-permute-start.10 = (bf16[272,128]{1,0:T(8,128)(2,1)S(1)}, bf16[272,128]{1,0:T(8,128)(2,1)S(1)}, u32[]{:S(2)}, u32[]{:S(2)}) collective-permute-start(bf16[272,128]{1,0:T(8,128)(2,1)S(1)} %get-tuple-element.40), channel_id=1, source_target_pairs={{0,24},{1,25},{2,26},{3,27},{4,28},{5,29},{6,30},{7,31},{8,16},{9,... | collective-permute-start | bytes 208904 | tf_op jit(solution)/shard_map/ppermute | solution.py:421
  28.1 3.4 %collective-permute-start.12 = (bf16[272,128]{1,0:T(8,128)(2,1)S(1)}, bf16[272,128]{1,0:T(8,128)(2,1)S(1)}, u32[]{:S(2)}, u32[]{:S(2)}) collective-permute-start(bf16[272,128]{1,0:T(8,128)(2,1)S(1)} %get-tuple-element.42), channel_id=1, source_target_pairs={{0,14},{1,15},{2,12},{3,13},{4,10},{5,11},{6,8},{7,9},{8,6},{9,7},... | collective-permute-start | bytes 208904 | tf_op jit(solution)/shard_map/ppermute | solution.py:421
  31.5 4.2 %collective-permute-done.11.refs_1_ = bf16[272,128]{1,0:T(8,128)(2,1)S(1)} collective-permute-done((bf16[272,128]{1,0:T(8,128)(2,1)S(1)}, bf16[272,128]{1,0:T(8,128)(2,1)S(1)}, u32[]{:S(2)}, u32[]{:S(2)}) %collective-permute-start.11) | collective-permute-done | bytes 69664 | tf_op jit(solution)/shard_map/ppermute | solution.py:421
  35.6 6.7 %shard_map.33.factor_ref = bf16[512,512]{1,0:T(8,128)(2,1)S(1)} custom-call(f32[4,264,128]{2,1,0:T(8,128)S(1)} %shard_map.30.sum_ref, f32[264,128]{1,0:T(8,128)S(1)} %get-tuple-element.39.total_ref, bf16[272,128]{1,0:T(8,128)(2,1)S(1)} %collective-permute-done.10.refs_0_, bf16[272,128]{1,0:T(8,128)(2,1)S(1)} %collective-permute-done.11.refs_1_, ...), custom_call_target="tpu_custom_call" | custom-call | tf_op jit(solution)/shard_map/pallas_call | solution.py:91
  42.3 0.7 %shard_map.34 = (bf16[128,512]{1,0:T(8,128)(2,1)S(1)}, bf16[128,512]{1,0:T(8,128)(2,1)S(1)}, bf16[128,512]{1,0:T(8,128)(2,1)S(1)}, bf16[128,512]{1,0:T(8,128)(2,...) custom-call(bf16[512,512]{1,0:T(8,128)(2,1)S(1)} %shard_map.33.facto, ...), custom_call_target="tpu_custom_call" | custom-call | tf_op jit(solution)/shard_map/pallas_call | solution.py:91
  43.1 1.4 %collective-permute-start.17 = (bf16[128,512]{1,0:T(8,128)(2,1)S(1)}, bf16[128,512]{1,0:T(8,128)(2,1)S(1)}, u32[]{:S(2)}, u32[]{:S(2)}) collective-permute-start(bf16[128,512]{1,0:T(8,128)(2,1)S(1)} %get-tuple-element.48), channel_id=1, source_target_pairs={{5,0},{8,1},{7,2},{10,3},{1,4},{12,5},{3,6},{14,7},{13,8},{0,9},{1... | collective-permute-start | bytes 393224 | tf_op jit(solution)/shard_map/ppermute | solution.py:421
  44.5 0.3 collective-permute-start.18
  44.8 1.1 %collective-permute-start.19 = (bf16[128,512]{1,0:T(8,128)(2,1)S(1)}, bf16[128,512]{1,0:T(8,128)(2,1)S(1)}, u32[]{:S(2)}, u32[]{:S(2)}) collective-permute-start(bf16[128,512]{1,0:T(8,128)(2,1)S(1)} %get-tuple-element.50), channel_id=1, source_target_pairs={{2,0},{5,1},{0,2},{7,3},{6,4},{1,5},{4,6},{3,7},{10,8},{13,9},{8,1... | collective-permute-start | bytes 393224 | tf_op jit(solution)/shard_map/ppermute | solution.py:421
  45.9 1.1 %collective-permute-start.13 = (bf16[128,512]{1,0:T(8,128)(2,1)S(1)}, bf16[128,512]{1,0:T(8,128)(2,1)S(1)}, u32[]{:S(2)}, u32[]{:S(2)}) collective-permute-start(bf16[128,512]{1,0:T(8,128)(2,1)S(1)} %get-tuple-element.43), channel_id=1, source_target_pairs={{4,0},{9,1},{6,2},{11,3},{0,4},{13,5},{2,6},{15,7},{12,8},{1,9},{1... | collective-permute-start | bytes 393224 | tf_op jit(solution)/shard_map/ppermute | solution.py:421
  47.0 0.4 collective-permute-done.16.refs_1_
  47.5 1.1 %collective-permute-start.14 = (bf16[128,512]{1,0:T(8,128)(2,1)S(1)}, bf16[128,512]{1,0:T(8,128)(2,1)S(1)}, u32[]{:S(2)}, u32[]{:S(2)}) collective-permute-start(bf16[128,512]{1,0:T(8,128)(2,1)S(1)} %get-tuple-element.44), channel_id=1, source_target_pairs={{8,0},{3,1},{10,2},{1,3},{12,4},{7,5},{14,6},{5,7},{0,8},{11,9},{2... | collective-permute-start | bytes 393224 | tf_op jit(solution)/shard_map/ppermute | solution.py:421
  48.6 1.0 %collective-permute-start.15 = (bf16[128,512]{1,0:T(8,128)(2,1)S(1)}, bf16[128,512]{1,0:T(8,128)(2,1)S(1)}, u32[]{:S(2)}, u32[]{:S(2)}) collective-permute-start(bf16[128,512]{1,0:T(8,128)(2,1)S(1)} %get-tuple-element.45), channel_id=1, source_target_pairs={{1,0},{0,1},{3,2},{2,3},{5,4},{4,5},{7,6},{6,7},{9,8},{8,9},{11,10... | collective-permute-start | bytes 393224 | tf_op jit(solution)/shard_map/ppermute | solution.py:421
  49.9 0.5 collective-permute-done.19.refs_4_
  50.3 0.9 %shard_map.35.refs_3_ = bf16[4,2,128,512]{3,2,1,0:T(8,128)(2,1)} custom-call(bf16[4,2,128,512]{3,2,1,0:T(8,128)(2,1)S(1)} %bitcast.3, bf16[128,512]{1,0:T(8,128)(2,1)S(1)} %get-tuple-element.46.refs_0_, bf16[128,512]{1,0:T(8,128)(2,1)S(1)} %collective-permute-done.16.refs_1_, bf16[128,512]{1,0:T(8,128)(2,1)S(1)} %collective-permute-done.17.refs_2_, ...), custom_call_target="tpu_custom_call" | custom-call | tf_op jit(solution)/shard_map/pallas_call | solution.py:384
  51.3 1.4 %collective-permute-done.14.refs_1_ = bf16[128,512]{1,0:T(8,128)(2,1)S(1)} collective-permute-done((bf16[128,512]{1,0:T(8,128)(2,1)S(1)}, bf16[128,512]{1,0:T(8,128)(2,1)S(1)}, u32[]{:S(2)}, u32[]{:S(2)}) %collective-permute-start.14) | collective-permute-done | bytes 131104 | tf_op jit(solution)/shard_map/ppermute | solution.py:421
  52.7 0.8 %shard_map.36 = bf16[4,2,128,512]{3,2,1,0:T(8,128)(2,1)} custom-call(bf16[4,2,128,512]{3,2,1,0:T(8,128)(2,1)S(1)} %bitcast.4, bf16[128,512]{1,0:T(8,128)(2,1)S(1)} %collective-permute-done.13.refs_0_, bf16[128,512]{1,0:T(8,128)(2,1)S(1)} %collective-permute-done.14.refs_1_, ...), custom_call_target="tpu_custom_call", output_to_operand_aliasing={{}: (4, {})} | custom-call | tf_op jit(solution)/shard_map/pallas_call | solution.py:384
  (21 shorter events, 1.1 us)
Async XLA Ops:
  0.0 1.2 %copy-start.1 = (bf16[1,8,128,512]{3,2,1,0:T(8,128)(2,1)S(1)}, bf16[1,8,128,512]{3,2,1,0:T(8,128)(2,1)}, u32[]{:S(2)}) copy-start(bf16[1,8,128,512]{3,2,1,0:T(8,128)(2,1)} %param.2) | copy-start | bytes 3145732
  1.3 6.3 %collective-permute-start = (bf16[128,512]{1,0:T(8,128)(2,1)S(1)}, bf16[128,512]{1,0:T(8,128)(2,1)S(1)}, u32[]{:S(2)}, u32[]{:S(2)}) collective-permute-start(bf16[128,512]{1,0:T(8,128)(2,1)S(1)} %get-tuple-element.29), channel_id=1, source_target_pairs={{0,3},{1,4},{2,1},{3,6},{4,7},{5,0},{6,5},{7,2},{8,11},{9,12},{10,... | collective-permute-start | bytes 393224 | tf_op jit(solution)/shard_map/ppermute | solution.py:421
  3.7 5.5 %collective-permute-start.1 = (bf16[128,512]{1,0:T(8,128)(2,1)S(1)}, bf16[128,512]{1,0:T(8,128)(2,1)S(1)}, u32[]{:S(2)}, u32[]{:S(2)}) collective-permute-start(bf16[128,512]{1,0:T(8,128)(2,1)S(1)} %get-tuple-element.30), channel_id=1, source_target_pairs={{0,5},{1,8},{2,7},{3,10},{4,1},{5,12},{6,3},{7,14},{8,13},{9,0},{1... | collective-permute-start | bytes 393224 | tf_op jit(solution)/shard_map/ppermute | solution.py:421
  3.8 5.5 %collective-permute-start.2 = (bf16[128,512]{1,0:T(8,128)(2,1)S(1)}, bf16[128,512]{1,0:T(8,128)(2,1)S(1)}, u32[]{:S(2)}, u32[]{:S(2)}) collective-permute-start(bf16[128,512]{1,0:T(8,128)(2,1)S(1)} %get-tuple-element.31), channel_id=1, source_target_pairs={{0,9},{1,2},{2,11},{3,0},{4,13},{5,6},{6,15},{7,4},{8,1},{9,10},{1... | collective-permute-start | bytes 393224 | tf_op jit(solution)/shard_map/ppermute | solution.py:421
  5.6 5.0 %collective-permute-start.3 = (bf16[128,512]{1,0:T(8,128)(2,1)S(1)}, bf16[128,512]{1,0:T(8,128)(2,1)S(1)}, u32[]{:S(2)}, u32[]{:S(2)}) collective-permute-start(bf16[128,512]{1,0:T(8,128)(2,1)S(1)} %get-tuple-element.32), channel_id=1, source_target_pairs={{0,2},{1,5},{2,0},{3,7},{4,6},{5,1},{6,4},{7,3},{8,10},{9,13},{10,... | collective-permute-start | bytes 393224 | tf_op jit(solution)/shard_map/ppermute | solution.py:421
  7.1 5.0 %collective-permute-start.4 = (bf16[128,512]{1,0:T(8,128)(2,1)S(1)}, bf16[128,512]{1,0:T(8,128)(2,1)S(1)}, u32[]{:S(2)}, u32[]{:S(2)}) collective-permute-start(bf16[128,512]{1,0:T(8,128)(2,1)S(1)} %get-tuple-element.33), channel_id=1, source_target_pairs={{0,4},{1,9},{2,6},{3,11},{4,0},{5,13},{6,2},{7,15},{8,12},{9,1},{1... | collective-permute-start | bytes 393224 | tf_op jit(solution)/shard_map/ppermute | solution.py:421
  7.6 5.2 %collective-permute-start.5 = (bf16[128,512]{1,0:T(8,128)(2,1)S(1)}, bf16[128,512]{1,0:T(8,128)(2,1)S(1)}, u32[]{:S(2)}, u32[]{:S(2)}) collective-permute-start(bf16[128,512]{1,0:T(8,128)(2,1)S(1)} %get-tuple-element.34), channel_id=1, source_target_pairs={{0,8},{1,3},{2,10},{3,1},{4,12},{5,7},{6,14},{7,5},{8,0},{9,11},{1... | collective-permute-start | bytes 393224 | tf_op jit(solution)/shard_map/ppermute | solution.py:421
  9.2 3.6 %collective-permute-start.6 = (bf16[128,512]{1,0:T(8,128)(2,1)S(1)}, bf16[128,512]{1,0:T(8,128)(2,1)S(1)}, u32[]{:S(2)}, u32[]{:S(2)}) collective-permute-start(bf16[128,512]{1,0:T(8,128)(2,1)S(1)} %get-tuple-element.35), channel_id=1, source_target_pairs={{0,1},{1,0},{2,3},{3,2},{4,5},{5,4},{6,7},{7,6},{8,9},{9,8},{10,11... | collective-permute-start | bytes 393224 | tf_op jit(solution)/shard_map/ppermute | solution.py:421
  13.3 6.3 %collective-permute-start.7 = (bf16[272,128]{1,0:T(8,128)(2,1)S(1)}, bf16[272,128]{1,0:T(8,128)(2,1)S(1)}, u32[]{:S(2)}, u32[]{:S(2)}) collective-permute-start(bf16[272,128]{1,0:T(8,128)(2,1)S(1)} %get-tuple-element.36), channel_id=1, source_target_pairs={{0,24},{1,25},{2,26},{3,27},{4,28},{5,29},{6,30},{7,31},{8,16},{9,... | collective-permute-start | bytes 208904 | tf_op jit(solution)/shard_map/ppermute | solution.py:421
  17.0 7.4 %collective-permute-start.8 = (bf16[272,128]{1,0:T(8,128)(2,1)S(1)}, bf16[272,128]{1,0:T(8,128)(2,1)S(1)}, u32[]{:S(2)}, u32[]{:S(2)}) collective-permute-start(bf16[272,128]{1,0:T(8,128)(2,1)S(1)} %get-tuple-element.37), channel_id=1, source_target_pairs={{0,22},{1,23},{2,20},{3,21},{4,18},{5,19},{6,16},{7,17},{8,30},{9,... | collective-permute-start | bytes 208904 | tf_op jit(solution)/shard_map/ppermute | solution.py:421
  18.3 6.8 %collective-permute-start.9 = (bf16[272,128]{1,0:T(8,128)(2,1)S(1)}, bf16[272,128]{1,0:T(8,128)(2,1)S(1)}, u32[]{:S(2)}, u32[]{:S(2)}) collective-permute-start(bf16[272,128]{1,0:T(8,128)(2,1)S(1)} %get-tuple-element.38), channel_id=1, source_target_pairs={{0,14},{1,15},{2,12},{3,13},{4,10},{5,11},{6,8},{7,9},{8,6},{9,7},... | collective-permute-start | bytes 208904 | tf_op jit(solution)/shard_map/ppermute | solution.py:421
  25.2 6.3 %collective-permute-start.10 = (bf16[272,128]{1,0:T(8,128)(2,1)S(1)}, bf16[272,128]{1,0:T(8,128)(2,1)S(1)}, u32[]{:S(2)}, u32[]{:S(2)}) collective-permute-start(bf16[272,128]{1,0:T(8,128)(2,1)S(1)} %get-tuple-element.40), channel_id=1, source_target_pairs={{0,24},{1,25},{2,26},{3,27},{4,28},{5,29},{6,30},{7,31},{8,16},{9,... | collective-permute-start | bytes 208904 | tf_op jit(solution)/shard_map/ppermute | solution.py:421
  27.9 7.8 %collective-permute-start.11 = (bf16[272,128]{1,0:T(8,128)(2,1)S(1)}, bf16[272,128]{1,0:T(8,128)(2,1)S(1)}, u32[]{:S(2)}, u32[]{:S(2)}) collective-permute-start(bf16[272,128]{1,0:T(8,128)(2,1)S(1)} %get-tuple-element.41), channel_id=1, source_target_pairs={{0,22},{1,23},{2,20},{3,21},{4,18},{5,19},{6,16},{7,17},{8,30},{9,... | collective-permute-start | bytes 208904 | tf_op jit(solution)/shard_map/ppermute | solution.py:421
  28.1 7.6 %collective-permute-start.12 = (bf16[272,128]{1,0:T(8,128)(2,1)S(1)}, bf16[272,128]{1,0:T(8,128)(2,1)S(1)}, u32[]{:S(2)}, u32[]{:S(2)}) collective-permute-start(bf16[272,128]{1,0:T(8,128)(2,1)S(1)} %get-tuple-element.42), channel_id=1, source_target_pairs={{0,14},{1,15},{2,12},{3,13},{4,10},{5,11},{6,8},{7,9},{8,6},{9,7},... | collective-permute-start | bytes 208904 | tf_op jit(solution)/shard_map/ppermute | solution.py:421
  42.3 8.1 %copy-start = (bf16[1,8,128,512]{3,2,1,0:T(8,128)(2,1)S(1)}, bf16[1,8,128,512]{3,2,1,0:T(8,128)(2,1)}, u32[]{:S(2)}) copy-start(bf16[1,8,128,512]{3,2,1,0:T(8,128)(2,1)} %param.3) | copy-start | bytes 3145732
  43.0 4.4 %collective-permute-start.16 = (bf16[128,512]{1,0:T(8,128)(2,1)S(1)}, bf16[128,512]{1,0:T(8,128)(2,1)S(1)}, u32[]{:S(2)}, u32[]{:S(2)}) collective-permute-start(bf16[128,512]{1,0:T(8,128)(2,1)S(1)} %get-tuple-element.47), channel_id=1, source_target_pairs={{3,0},{4,1},{1,2},{6,3},{7,4},{0,5},{5,6},{2,7},{11,8},{12,9},{9,1... | collective-permute-start | bytes 393224 | tf_op jit(solution)/shard_map/ppermute | solution.py:421
  43.1 5.5 %collective-permute-start.17 = (bf16[128,512]{1,0:T(8,128)(2,1)S(1)}, bf16[128,512]{1,0:T(8,128)(2,1)S(1)}, u32[]{:S(2)}, u32[]{:S(2)}) collective-permute-start(bf16[128,512]{1,0:T(8,128)(2,1)S(1)} %get-tuple-element.48), channel_id=1, source_target_pairs={{5,0},{8,1},{7,2},{10,3},{1,4},{12,5},{3,6},{14,7},{13,8},{0,9},{1... | collective-permute-start | bytes 393224 | tf_op jit(solution)/shard_map/ppermute | solution.py:421
  44.5 5.3 %collective-permute-start.18 = (bf16[128,512]{1,0:T(8,128)(2,1)S(1)}, bf16[128,512]{1,0:T(8,128)(2,1)S(1)}, u32[]{:S(2)}, u32[]{:S(2)}) collective-permute-start(bf16[128,512]{1,0:T(8,128)(2,1)S(1)} %get-tuple-element.49), channel_id=1, source_target_pairs={{9,0},{2,1},{11,2},{0,3},{13,4},{6,5},{15,6},{4,7},{1,8},{10,9},{3... | collective-permute-start | bytes 393224 | tf_op jit(solution)/shard_map/ppermute | solution.py:421
  44.8 5.5 %collective-permute-start.19 = (bf16[128,512]{1,0:T(8,128)(2,1)S(1)}, bf16[128,512]{1,0:T(8,128)(2,1)S(1)}, u32[]{:S(2)}, u32[]{:S(2)}) collective-permute-start(bf16[128,512]{1,0:T(8,128)(2,1)S(1)} %get-tuple-element.50), channel_id=1, source_target_pairs={{2,0},{5,1},{0,2},{7,3},{6,4},{1,5},{4,6},{3,7},{10,8},{13,9},{8,1... | collective-permute-start | bytes 393224 | tf_op jit(solution)/shard_map/ppermute | solution.py:421
  45.9 5.3 %collective-permute-start.13 = (bf16[128,512]{1,0:T(8,128)(2,1)S(1)}, bf16[128,512]{1,0:T(8,128)(2,1)S(1)}, u32[]{:S(2)}, u32[]{:S(2)}) collective-permute-start(bf16[128,512]{1,0:T(8,128)(2,1)S(1)} %get-tuple-element.43), channel_id=1, source_target_pairs={{4,0},{9,1},{6,2},{11,3},{0,4},{13,5},{2,6},{15,7},{12,8},{1,9},{1... | collective-permute-start | bytes 393224 | tf_op jit(solution)/shard_map/ppermute | solution.py:421
  47.5 5.2 %collective-permute-start.14 = (bf16[128,512]{1,0:T(8,128)(2,1)S(1)}, bf16[128,512]{1,0:T(8,128)(2,1)S(1)}, u32[]{:S(2)}, u32[]{:S(2)}) collective-permute-start(bf16[128,512]{1,0:T(8,128)(2,1)S(1)} %get-tuple-element.44), channel_id=1, source_target_pairs={{8,0},{3,1},{10,2},{1,3},{12,4},{7,5},{14,6},{5,7},{0,8},{11,9},{2... | collective-permute-start | bytes 393224 | tf_op jit(solution)/shard_map/ppermute | solution.py:421
  48.6 4.1 %collective-permute-start.15 = (bf16[128,512]{1,0:T(8,128)(2,1)S(1)}, bf16[128,512]{1,0:T(8,128)(2,1)S(1)}, u32[]{:S(2)}, u32[]{:S(2)}) collective-permute-start(bf16[128,512]{1,0:T(8,128)(2,1)S(1)} %get-tuple-element.45), channel_id=1, source_target_pairs={{1,0},{0,1},{3,2},{2,3},{5,4},{4,5},{7,6},{6,7},{9,8},{8,9},{11,10... | collective-permute-start | bytes 393224 | tf_op jit(solution)/shard_map/ppermute | solution.py:421

commit v6 on v5

--- a/solution.py
+++ b/solution.py
@@ -259,15 +259,6 @@
         message_ref[...] = to_message(total - value, order)
 
 
-def split(matrix):
-    high = matrix.astype(jnp.bfloat16)
-    return high, (matrix - high.astype(jnp.float32)).astype(jnp.bfloat16)
-
-
-def product_of_split(first, second):
-    return product(first[0], second[0]) + (product(first[0], second[1]) + product(first[1], second[0]))
-
-
 def assemble(upper, count):
     return jnp.concatenate(
         [
@@ -278,46 +269,60 @@
     )
 
 
-def split_whole(upper, count):
-    parts = {key: split(value) for key, value in upper.items()}
-    return tuple(assemble({key: value[part] for key, value in parts.items()}, count) for part in range(2))
+def rounded(upper, count):
+    return assemble({key: value.astype(jnp.bfloat16) for key, value in upper.items()}, count)
 
 
 def symmetric_product(first, second, count):
-    size = first[0].shape[0] // count
+    size = first.shape[0] // count
     return {
-        (i, j): product_of_split(
-            tuple(part[i * size : (i + 1) * size, :] for part in first),
-            tuple(part[:, j * size : (j + 1) * size] for part in second),
-        )
+        (i, j): product(first[i * size : (i + 1) * size, :], second[:, j * size : (j + 1) * size])
         for i in range(count)
         for j in range(i, count)
     }
 
 
+def exact_square(upper, count):
+    high = rounded(upper, count)
+    low = rounded(
+        {key: value - value.astype(jnp.bfloat16).astype(jnp.float32) for key, value in upper.items()}, count
+    )
+    return combine(
+        (1.0, symmetric_product(high, high, count)),
+        (1.0, combine((1.0, symmetric_product(high, low, count)), (1.0, symmetric_product(low, high, count)))),
+    )
+
+
+def combine(*terms):
+    return {
+        key: functools.reduce(jnp.add, [value[key] if factor == 1.0 else factor * value[key] for factor, value in terms])
+        for key in terms[0][1]
+    }
+
+
 def newton(current, count):
-    size = current[0, 0].shape[0]
-    shape = (size, size)
-    identity = lax.broadcasted_iota(jnp.int32, shape, 0) == lax.broadcasted_iota(jnp.int32, shape, 1)
-    accum = None
+    accum_identity, accum = 1.0, None
     for iteration in range(ITERS):
-        halves = split_whole(current, count)
-        squared = symmetric_product(halves, halves, count)
-        polynomial = {
-            (i, j): (jnp.where(identity, first_coef, 0.0) if i == j else 0.0)
-            + second_coef * current[i, j]
-            + third_coef * squared[i, j]
-            for i, j in current
-        }
-        poly_halves = split_whole(polynomial, count)
+        last = iteration + 1 == ITERS
+        current_high = None if last else rounded(current, count)
+        squared = exact_square(current, count) if last else symmetric_product(current_high, current_high, count)
+        rest = combine((second_coef, current), (third_coef, squared))
+        rest_high = rounded(rest, count)
         if accum is None:
-            accum = polynomial
+            accum = rest
         else:
-            accum = symmetric_product(split_whole(accum, count), poly_halves, count)
-        if iteration + 1 < ITERS:
-            inner = symmetric_product(halves, poly_halves, count)
-            current = symmetric_product(split_whole(inner, count), poly_halves, count)
-    return accum
+            accum = combine(
+                (accum_identity, rest),
+                (first_coef, accum),
+                (1.0, symmetric_product(rounded(accum, count), rest_high, count)),
+            )
+        accum_identity *= first_coef
+        if not last:
+            inner = combine((first_coef, current), (1.0, symmetric_product(current_high, rest_high, count)))
+            current = combine(
+                (first_coef, inner), (1.0, symmetric_product(rounded(inner, count), rest_high, count))
+            )
+    return accum_identity, accum
 
 
 def factor_kernel(rest_count, order, scale, sum_ref, total_ref, *refs):
@@ -329,6 +334,7 @@
         quarters_ref[quarter] = sum_ref[quarter] + from_message(rest_ref[...], order)
     blocks = unpack([quarters_ref[quarter] for quarter in range(4)], order)
     trace_sum = jnp.sum(sum(diagonal(blocks[i, i]) for i in range(order // BLOCK)))
+    shrink = 1.0 / (trace_sum + epsilon)
     count, ratio = order // WIDE, WIDE // BLOCK
     current = {}
     for i in range(count):
@@ -346,11 +352,17 @@
                 ],
                 axis=0,
             )
-            current[i, j] = tile / (trace_sum + epsilon)
-    accum = newton(current, count)
+            current[i, j] = tile * shrink
+    accum_identity, accum = newton(current, count)
     growth = jnp.sqrt(scale / (trace_sum + epsilon))
-    factor_ref[...] = assemble(
-        {key: (value * growth).astype(jnp.bfloat16) for key, value in accum.items()}, count
+    shape = (WIDE, WIDE)
+    identity = lax.broadcasted_iota(jnp.int32, shape, 0) == lax.broadcasted_iota(jnp.int32, shape, 1)
+    factor_ref[...] = rounded(
+        {
+            (i, j): (value + jnp.where(identity, accum_identity, 0.0) if i == j else value) * growth
+            for (i, j), value in accum.items()
+        },
+        count,
     )
 
 

time: 53.7 us -> 50.7 us (0.944)
  Pallas kernels: 10.3 us -> 7.37 us
    pallas_call x7, Pallas kernels: 8.55 us -> 5.6 us  [call(): pl.pallas_call(kernel, out_shape=out_shape, in_specs=[vmem] * len(operand...]
where the time goes in v6:
time: 50.7 us; the launch traced here: 50.6 us
  starting transfers between devices  26.7 us (53%)
  waiting for transfers between devices  15.2 us (30%)
  Pallas kernels  7.37 us (15%)
  local copies, waits for them, and re-layouts  1.23 us (2%)
    ppermute x20, starting transfers between devices, swap(): lax.ppermute(array, AXES, permute)  26.7 us
    ppermute x20, waiting for transfers between devices, swap(): lax.ppermute(array, AXES, permute)  15.2 us
    pallas_call x7, Pallas kernels, call(): pl.pallas_call(kernel, out_shape=out_shape, in_specs=[vmem] * len(operand...  5.6 us
    pallas_call x2, Pallas kernels, new_weights(): pl.pallas_call(functools.partial(weights_kernel, rest_count, numbers), ou...  1.77 us
    unnamed x4, local copies, waits for them, and re-layouts  1.23 us
  transfers between devices with their start and end apart: 20, of which 10 were waited for; matrix products, arithmetic and copies ran while one was open for 0% of the time, Pallas kernels for 3%

profile of v6, /device:TPU:0, one launch (start us, length us, event | category | flops | bytes accessed | tf_op | source)
XLA Modules:
  0.0 50.6 jit_solution(18101776733461940765)
XLA Ops:
  0.0 1.2 %copy-done.1 = bf16[1,8,128,512]{3,2,1,0:T(8,128)(2,1)S(1)} copy-done((bf16[1,8,128,512]{3,2,1,0:T(8,128)(2,1)S(1)}, bf16[1,8,128,512]{3,2,1,0:T(8,128)(2,1)}, u32[]{:S(2)}) %copy-start.1) | copy-done | bytes 1048600
  1.3 2.4 %collective-permute-start = (bf16[128,512]{1,0:T(8,128)(2,1)S(1)}, bf16[128,512]{1,0:T(8,128)(2,1)S(1)}, u32[]{:S(2)}, u32[]{:S(2)}) collective-permute-start(bf16[128,512]{1,0:T(8,128)(2,1)S(1)} %get-tuple-element.29), channel_id=1, source_target_pairs={{0,3},{1,4},{2,1},{3,6},{4,7},{5,0},{6,5},{7,2},{8,11},{9,12},{10,... | collective-permute-start | bytes 393224 | tf_op jit(solution)/shard_map/ppermute | solution.py:433
  3.8 1.8 %collective-permute-start.2 = (bf16[128,512]{1,0:T(8,128)(2,1)S(1)}, bf16[128,512]{1,0:T(8,128)(2,1)S(1)}, u32[]{:S(2)}, u32[]{:S(2)}) collective-permute-start(bf16[128,512]{1,0:T(8,128)(2,1)S(1)} %get-tuple-element.31), channel_id=1, source_target_pairs={{0,9},{1,2},{2,11},{3,0},{4,13},{5,6},{6,15},{7,4},{8,1},{9,10},{1... | collective-permute-start | bytes 393224 | tf_op jit(solution)/shard_map/ppermute | solution.py:433
  5.6 1.5 %collective-permute-start.3 = (bf16[128,512]{1,0:T(8,128)(2,1)S(1)}, bf16[128,512]{1,0:T(8,128)(2,1)S(1)}, u32[]{:S(2)}, u32[]{:S(2)}) collective-permute-start(bf16[128,512]{1,0:T(8,128)(2,1)S(1)} %get-tuple-element.32), channel_id=1, source_target_pairs={{0,2},{1,5},{2,0},{3,7},{4,6},{5,1},{6,4},{7,3},{8,10},{9,13},{10,... | collective-permute-start | bytes 393224 | tf_op jit(solution)/shard_map/ppermute | solution.py:433
  7.1 0.5 %collective-permute-start.4 = (bf16[128,512]{1,0:T(8,128)(2,1)S(1)}, bf16[128,512]{1,0:T(8,128)(2,1)S(1)}, u32[]{:S(2)}, u32[]{:S(2)}) collective-permute-start(bf16[128,512]{1,0:T(8,128)(2,1)S(1)} %get-tuple-element.33), channel_id=1, source_target_pairs={{0,4},{1,9},{2,6},{3,11},{4,0},{5,13},{6,2},{7,15},{8,12},{9,1},{1... | collective-permute-start | bytes 393224 | tf_op jit(solution)/shard_map/ppermute | solution.py:433
  7.6 1.6 %collective-permute-start.5 = (bf16[128,512]{1,0:T(8,128)(2,1)S(1)}, bf16[128,512]{1,0:T(8,128)(2,1)S(1)}, u32[]{:S(2)}, u32[]{:S(2)}) collective-permute-start(bf16[128,512]{1,0:T(8,128)(2,1)S(1)} %get-tuple-element.34), channel_id=1, source_target_pairs={{0,8},{1,3},{2,10},{3,1},{4,12},{5,7},{6,14},{7,5},{8,0},{9,11},{1... | collective-permute-start | bytes 393224 | tf_op jit(solution)/shard_map/ppermute | solution.py:433
  9.4 1.2 %collective-permute-done.3.refs_4_ = bf16[128,512]{1,0:T(8,128)(2,1)S(1)} collective-permute-done((bf16[128,512]{1,0:T(8,128)(2,1)S(1)}, bf16[128,512]{1,0:T(8,128)(2,1)S(1)}, u32[]{:S(2)}, u32[]{:S(2)}) %collective-permute-start.3) | collective-permute-done | bytes 131104 | tf_op jit(solution)/shard_map/ppermute | solution.py:433
  10.6 0.5 %shard_map.29.early_ref = f32[4,264,128]{2,1,0:T(8,128)S(1)} custom-call(bf16[128,512]{1,0:T(8,128)(2,1)S(1)} %get-tuple-element.28.refs_0_, bf16[128,512]{1,0:T(8,128)(2,1)S(1)} %collective-permute-done.refs_1_, bf16[128,512]{1,0:T(8,128)(2,1)S(1)} %collective-permute-done.1.refs_2_, bf16[128,512]{1,0:T(8,128)(2,1)S(1)} %collective-permute-done.2.refs_3_, ...), custom_call_target="tpu_custom_call" | custom-call | tf_op jit(solution)/shard_map/pallas_call | solution.py:91
  11.1 1.0 %collective-permute-done.4.refs_0_.refs_5_ = bf16[128,512]{1,0:T(8,128)(2,1)S(1)} collective-permute-done((bf16[128,512]{1,0:T(8,128)(2,1)S(1)}, bf16[128,512]{1,0:T(8,128)(2,1)S(1)}, u32[]{:S(2)}, u32[]{:S(2)}) %collective-permute-start.4) | collective-permute-done | bytes 131104 | tf_op jit(solution)/shard_map/ppermute | solution.py:433
  12.1 0.7 %collective-permute-done.5.refs_1_.refs_6_ = bf16[128,512]{1,0:T(8,128)(2,1)S(1)} collective-permute-done((bf16[128,512]{1,0:T(8,128)(2,1)S(1)}, bf16[128,512]{1,0:T(8,128)(2,1)S(1)}, u32[]{:S(2)}, u32[]{:S(2)}) %collective-permute-start.5) | collective-permute-done | bytes 131104 | tf_op jit(solution)/shard_map/ppermute | solution.py:433
  12.8 0.4 shard_map.30.sum_ref
  13.3 3.7 %collective-permute-start.7 = (bf16[272,128]{1,0:T(8,128)(2,1)S(1)}, bf16[272,128]{1,0:T(8,128)(2,1)S(1)}, u32[]{:S(2)}, u32[]{:S(2)}) collective-permute-start(bf16[272,128]{1,0:T(8,128)(2,1)S(1)} %get-tuple-element.36), channel_id=1, source_target_pairs={{0,24},{1,25},{2,26},{3,27},{4,28},{5,29},{6,30},{7,31},{8,16},{9,... | collective-permute-start | bytes 208904 | tf_op jit(solution)/shard_map/ppermute | solution.py:433
  17.0 1.3 %collective-permute-start.8 = (bf16[272,128]{1,0:T(8,128)(2,1)S(1)}, bf16[272,128]{1,0:T(8,128)(2,1)S(1)}, u32[]{:S(2)}, u32[]{:S(2)}) collective-permute-start(bf16[272,128]{1,0:T(8,128)(2,1)S(1)} %get-tuple-element.37), channel_id=1, source_target_pairs={{0,22},{1,23},{2,20},{3,21},{4,18},{5,19},{6,16},{7,17},{8,30},{9,... | collective-permute-start | bytes 208904 | tf_op jit(solution)/shard_map/ppermute | solution.py:433
  18.3 1.3 %collective-permute-start.9 = (bf16[272,128]{1,0:T(8,128)(2,1)S(1)}, bf16[272,128]{1,0:T(8,128)(2,1)S(1)}, u32[]{:S(2)}, u32[]{:S(2)}) collective-permute-start(bf16[272,128]{1,0:T(8,128)(2,1)S(1)} %get-tuple-element.38), channel_id=1, source_target_pairs={{0,14},{1,15},{2,12},{3,13},{4,10},{5,11},{6,8},{7,9},{8,6},{9,7},... | collective-permute-start | bytes 208904 | tf_op jit(solution)/shard_map/ppermute | solution.py:433
  19.6 4.8 %collective-permute-done.8.refs_1_ = bf16[272,128]{1,0:T(8,128)(2,1)S(1)} collective-permute-done((bf16[272,128]{1,0:T(8,128)(2,1)S(1)}, bf16[272,128]{1,0:T(8,128)(2,1)S(1)}, u32[]{:S(2)}, u32[]{:S(2)}) %collective-permute-start.8) | collective-permute-done | bytes 69664 | tf_op jit(solution)/shard_map/ppermute | solution.py:433
  24.4 0.7 %collective-permute-done.9.refs_2_ = bf16[272,128]{1,0:T(8,128)(2,1)S(1)} collective-permute-done((bf16[272,128]{1,0:T(8,128)(2,1)S(1)}, bf16[272,128]{1,0:T(8,128)(2,1)S(1)}, u32[]{:S(2)}, u32[]{:S(2)}) %collective-permute-start.9) | collective-permute-done | bytes 69664 | tf_op jit(solution)/shard_map/ppermute | solution.py:433
  25.2 2.7 %collective-permute-start.10 = (bf16[272,128]{1,0:T(8,128)(2,1)S(1)}, bf16[272,128]{1,0:T(8,128)(2,1)S(1)}, u32[]{:S(2)}, u32[]{:S(2)}) collective-permute-start(bf16[272,128]{1,0:T(8,128)(2,1)S(1)} %get-tuple-element.40), channel_id=1, source_target_pairs={{0,24},{1,25},{2,26},{3,27},{4,28},{5,29},{6,30},{7,31},{8,16},{9,... | collective-permute-start | bytes 208904 | tf_op jit(solution)/shard_map/ppermute | solution.py:433
  28.1 3.4 %collective-permute-start.12 = (bf16[272,128]{1,0:T(8,128)(2,1)S(1)}, bf16[272,128]{1,0:T(8,128)(2,1)S(1)}, u32[]{:S(2)}, u32[]{:S(2)}) collective-permute-start(bf16[272,128]{1,0:T(8,128)(2,1)S(1)} %get-tuple-element.42), channel_id=1, source_target_pairs={{0,14},{1,15},{2,12},{3,13},{4,10},{5,11},{6,8},{7,9},{8,6},{9,7},... | collective-permute-start | bytes 208904 | tf_op jit(solution)/shard_map/ppermute | solution.py:433
  31.5 4.2 %collective-permute-done.11.refs_1_ = bf16[272,128]{1,0:T(8,128)(2,1)S(1)} collective-permute-done((bf16[272,128]{1,0:T(8,128)(2,1)S(1)}, bf16[272,128]{1,0:T(8,128)(2,1)S(1)}, u32[]{:S(2)}, u32[]{:S(2)}) %collective-permute-start.11) | collective-permute-done | bytes 69664 | tf_op jit(solution)/shard_map/ppermute | solution.py:433
  35.6 3.7 %shard_map.33.factor_ref = bf16[512,512]{1,0:T(8,128)(2,1)S(1)} custom-call(f32[4,264,128]{2,1,0:T(8,128)S(1)} %shard_map.30.sum_ref, f32[264,128]{1,0:T(8,128)S(1)} %get-tuple-element.39.total_ref, bf16[272,128]{1,0:T(8,128)(2,1)S(1)} %collective-permute-done.10.refs_0_, bf16[272,128]{1,0:T(8,128)(2,1)S(1)} %collective-permute-done.11.refs_1_, ...), custom_call_target="tpu_custom_call" | custom-call | tf_op jit(solution)/shard_map/pallas_call | solution.py:91
  39.3 0.7 %shard_map.34 = (bf16[128,512]{1,0:T(8,128)(2,1)S(1)}, bf16[128,512]{1,0:T(8,128)(2,1)S(1)}, bf16[128,512]{1,0:T(8,128)(2,1)S(1)}, bf16[128,512]{1,0:T(8,128)(2,...) custom-call(bf16[512,512]{1,0:T(8,128)(2,1)S(1)} %shard_map.33.facto, ...), custom_call_target="tpu_custom_call" | custom-call | tf_op jit(solution)/shard_map/pallas_call | solution.py:91
  40.1 1.4 %collective-permute-start.17 = (bf16[128,512]{1,0:T(8,128)(2,1)S(1)}, bf16[128,512]{1,0:T(8,128)(2,1)S(1)}, u32[]{:S(2)}, u32[]{:S(2)}) collective-permute-start(bf16[128,512]{1,0:T(8,128)(2,1)S(1)} %get-tuple-element.48), channel_id=1, source_target_pairs={{5,0},{8,1},{7,2},{10,3},{1,4},{12,5},{3,6},{14,7},{13,8},{0,9},{1... | collective-permute-start | bytes 393224 | tf_op jit(solution)/shard_map/ppermute | solution.py:433
  41.6 0.3 collective-permute-start.18
  41.9 1.1 %collective-permute-start.19 = (bf16[128,512]{1,0:T(8,128)(2,1)S(1)}, bf16[128,512]{1,0:T(8,128)(2,1)S(1)}, u32[]{:S(2)}, u32[]{:S(2)}) collective-permute-start(bf16[128,512]{1,0:T(8,128)(2,1)S(1)} %get-tuple-element.50), channel_id=1, source_target_pairs={{2,0},{5,1},{0,2},{7,3},{6,4},{1,5},{4,6},{3,7},{10,8},{13,9},{8,1... | collective-permute-start | bytes 393224 | tf_op jit(solution)/shard_map/ppermute | solution.py:433
  43.0 1.1 %collective-permute-start.13 = (bf16[128,512]{1,0:T(8,128)(2,1)S(1)}, bf16[128,512]{1,0:T(8,128)(2,1)S(1)}, u32[]{:S(2)}, u32[]{:S(2)}) collective-permute-start(bf16[128,512]{1,0:T(8,128)(2,1)S(1)} %get-tuple-element.43), channel_id=1, source_target_pairs={{4,0},{9,1},{6,2},{11,3},{0,4},{13,5},{2,6},{15,7},{12,8},{1,9},{1... | collective-permute-start | bytes 393224 | tf_op jit(solution)/shard_map/ppermute | solution.py:433
  44.1 0.4 collective-permute-done.16.refs_1_
  44.5 1.1 %collective-permute-start.14 = (bf16[128,512]{1,0:T(8,128)(2,1)S(1)}, bf16[128,512]{1,0:T(8,128)(2,1)S(1)}, u32[]{:S(2)}, u32[]{:S(2)}) collective-permute-start(bf16[128,512]{1,0:T(8,128)(2,1)S(1)} %get-tuple-element.44), channel_id=1, source_target_pairs={{8,0},{3,1},{10,2},{1,3},{12,4},{7,5},{14,6},{5,7},{0,8},{11,9},{2... | collective-permute-start | bytes 393224 | tf_op jit(solution)/shard_map/ppermute | solution.py:433
  45.6 1.0 %collective-permute-start.15 = (bf16[128,512]{1,0:T(8,128)(2,1)S(1)}, bf16[128,512]{1,0:T(8,128)(2,1)S(1)}, u32[]{:S(2)}, u32[]{:S(2)}) collective-permute-start(bf16[128,512]{1,0:T(8,128)(2,1)S(1)} %get-tuple-element.45), channel_id=1, source_target_pairs={{1,0},{0,1},{3,2},{2,3},{5,4},{4,5},{7,6},{6,7},{9,8},{8,9},{11,10... | collective-permute-start | bytes 393224 | tf_op jit(solution)/shard_map/ppermute | solution.py:433
  46.9 0.5 collective-permute-done.19.refs_4_
  47.4 0.9 %shard_map.35.refs_3_ = bf16[4,2,128,512]{3,2,1,0:T(8,128)(2,1)} custom-call(bf16[4,2,128,512]{3,2,1,0:T(8,128)(2,1)S(1)} %bitcast.3, bf16[128,512]{1,0:T(8,128)(2,1)S(1)} %get-tuple-element.46.refs_0_, bf16[128,512]{1,0:T(8,128)(2,1)S(1)} %collective-permute-done.16.refs_1_, bf16[128,512]{1,0:T(8,128)(2,1)S(1)} %collective-permute-done.17.refs_2_, ...), custom_call_target="tpu_custom_call" | custom-call | tf_op jit(solution)/shard_map/pallas_call | solution.py:396
  48.3 1.4 %collective-permute-done.14.refs_1_ = bf16[128,512]{1,0:T(8,128)(2,1)S(1)} collective-permute-done((bf16[128,512]{1,0:T(8,128)(2,1)S(1)}, bf16[128,512]{1,0:T(8,128)(2,1)S(1)}, u32[]{:S(2)}, u32[]{:S(2)}) %collective-permute-start.14) | collective-permute-done | bytes 131104 | tf_op jit(solution)/shard_map/ppermute | solution.py:433
  49.7 0.8 %shard_map.36 = bf16[4,2,128,512]{3,2,1,0:T(8,128)(2,1)} custom-call(bf16[4,2,128,512]{3,2,1,0:T(8,128)(2,1)S(1)} %bitcast.4, bf16[128,512]{1,0:T(8,128)(2,1)S(1)} %collective-permute-done.13.refs_0_, bf16[128,512]{1,0:T(8,128)(2,1)S(1)} %collective-permute-done.14.refs_1_, ...), custom_call_target="tpu_custom_call", output_to_operand_aliasing={{}: (4, {})} | custom-call | tf_op jit(solution)/shard_map/pallas_call | solution.py:396
  (21 shorter events, 1.1 us)
Async XLA Ops:
  0.0 1.2 %copy-start.1 = (bf16[1,8,128,512]{3,2,1,0:T(8,128)(2,1)S(1)}, bf16[1,8,128,512]{3,2,1,0:T(8,128)(2,1)}, u32[]{:S(2)}) copy-start(bf16[1,8,128,512]{3,2,1,0:T(8,128)(2,1)} %param.2) | copy-start | bytes 3145732
  1.3 6.3 %collective-permute-start = (bf16[128,512]{1,0:T(8,128)(2,1)S(1)}, bf16[128,512]{1,0:T(8,128)(2,1)S(1)}, u32[]{:S(2)}, u32[]{:S(2)}) collective-permute-start(bf16[128,512]{1,0:T(8,128)(2,1)S(1)} %get-tuple-element.29), channel_id=1, source_target_pairs={{0,3},{1,4},{2,1},{3,6},{4,7},{5,0},{6,5},{7,2},{8,11},{9,12},{10,... | collective-permute-start | bytes 393224 | tf_op jit(solution)/shard_map/ppermute | solution.py:433
  3.7 5.5 %collective-permute-start.1 = (bf16[128,512]{1,0:T(8,128)(2,1)S(1)}, bf16[128,512]{1,0:T(8,128)(2,1)S(1)}, u32[]{:S(2)}, u32[]{:S(2)}) collective-permute-start(bf16[128,512]{1,0:T(8,128)(2,1)S(1)} %get-tuple-element.30), channel_id=1, source_target_pairs={{0,5},{1,8},{2,7},{3,10},{4,1},{5,12},{6,3},{7,14},{8,13},{9,0},{1... | collective-permute-start | bytes 393224 | tf_op jit(solution)/shard_map/ppermute | solution.py:433
  3.8 5.5 %collective-permute-start.2 = (bf16[128,512]{1,0:T(8,128)(2,1)S(1)}, bf16[128,512]{1,0:T(8,128)(2,1)S(1)}, u32[]{:S(2)}, u32[]{:S(2)}) collective-permute-start(bf16[128,512]{1,0:T(8,128)(2,1)S(1)} %get-tuple-element.31), channel_id=1, source_target_pairs={{0,9},{1,2},{2,11},{3,0},{4,13},{5,6},{6,15},{7,4},{8,1},{9,10},{1... | collective-permute-start | bytes 393224 | tf_op jit(solution)/shard_map/ppermute | solution.py:433
  5.6 5.0 %collective-permute-start.3 = (bf16[128,512]{1,0:T(8,128)(2,1)S(1)}, bf16[128,512]{1,0:T(8,128)(2,1)S(1)}, u32[]{:S(2)}, u32[]{:S(2)}) collective-permute-start(bf16[128,512]{1,0:T(8,128)(2,1)S(1)} %get-tuple-element.32), channel_id=1, source_target_pairs={{0,2},{1,5},{2,0},{3,7},{4,6},{5,1},{6,4},{7,3},{8,10},{9,13},{10,... | collective-permute-start | bytes 393224 | tf_op jit(solution)/shard_map/ppermute | solution.py:433
  7.1 5.0 %collective-permute-start.4 = (bf16[128,512]{1,0:T(8,128)(2,1)S(1)}, bf16[128,512]{1,0:T(8,128)(2,1)S(1)}, u32[]{:S(2)}, u32[]{:S(2)}) collective-permute-start(bf16[128,512]{1,0:T(8,128)(2,1)S(1)} %get-tuple-element.33), channel_id=1, source_target_pairs={{0,4},{1,9},{2,6},{3,11},{4,0},{5,13},{6,2},{7,15},{8,12},{9,1},{1... | collective-permute-start | bytes 393224 | tf_op jit(solution)/shard_map/ppermute | solution.py:433
  7.6 5.2 %collective-permute-start.5 = (bf16[128,512]{1,0:T(8,128)(2,1)S(1)}, bf16[128,512]{1,0:T(8,128)(2,1)S(1)}, u32[]{:S(2)}, u32[]{:S(2)}) collective-permute-start(bf16[128,512]{1,0:T(8,128)(2,1)S(1)} %get-tuple-element.34), channel_id=1, source_target_pairs={{0,8},{1,3},{2,10},{3,1},{4,12},{5,7},{6,14},{7,5},{8,0},{9,11},{1... | collective-permute-start | bytes 393224 | tf_op jit(solution)/shard_map/ppermute | solution.py:433
  9.2 3.6 %collective-permute-start.6 = (bf16[128,512]{1,0:T(8,128)(2,1)S(1)}, bf16[128,512]{1,0:T(8,128)(2,1)S(1)}, u32[]{:S(2)}, u32[]{:S(2)}) collective-permute-start(bf16[128,512]{1,0:T(8,128)(2,1)S(1)} %get-tuple-element.35), channel_id=1, source_target_pairs={{0,1},{1,0},{2,3},{3,2},{4,5},{5,4},{6,7},{7,6},{8,9},{9,8},{10,11... | collective-permute-start | bytes 393224 | tf_op jit(solution)/shard_map/ppermute | solution.py:433
  13.3 6.3 %collective-permute-start.7 = (bf16[272,128]{1,0:T(8,128)(2,1)S(1)}, bf16[272,128]{1,0:T(8,128)(2,1)S(1)}, u32[]{:S(2)}, u32[]{:S(2)}) collective-permute-start(bf16[272,128]{1,0:T(8,128)(2,1)S(1)} %get-tuple-element.36), channel_id=1, source_target_pairs={{0,24},{1,25},{2,26},{3,27},{4,28},{5,29},{6,30},{7,31},{8,16},{9,... | collective-permute-start | bytes 208904 | tf_op jit(solution)/shard_map/ppermute | solution.py:433
  17.0 7.4 %collective-permute-start.8 = (bf16[272,128]{1,0:T(8,128)(2,1)S(1)}, bf16[272,128]{1,0:T(8,128)(2,1)S(1)}, u32[]{:S(2)}, u32[]{:S(2)}) collective-permute-start(bf16[272,128]{1,0:T(8,128)(2,1)S(1)} %get-tuple-element.37), channel_id=1, source_target_pairs={{0,22},{1,23},{2,20},{3,21},{4,18},{5,19},{6,16},{7,17},{8,30},{9,... | collective-permute-start | bytes 208904 | tf_op jit(solution)/shard_map/ppermute | solution.py:433
  18.3 6.8 %collective-permute-start.9 = (bf16[272,128]{1,0:T(8,128)(2,1)S(1)}, bf16[272,128]{1,0:T(8,128)(2,1)S(1)}, u32[]{:S(2)}, u32[]{:S(2)}) collective-permute-start(bf16[272,128]{1,0:T(8,128)(2,1)S(1)} %get-tuple-element.38), channel_id=1, source_target_pairs={{0,14},{1,15},{2,12},{3,13},{4,10},{5,11},{6,8},{7,9},{8,6},{9,7},... | collective-permute-start | bytes 208904 | tf_op jit(solution)/shard_map/ppermute | solution.py:433
  25.2 6.3 %collective-permute-start.10 = (bf16[272,128]{1,0:T(8,128)(2,1)S(1)}, bf16[272,128]{1,0:T(8,128)(2,1)S(1)}, u32[]{:S(2)}, u32[]{:S(2)}) collective-permute-start(bf16[272,128]{1,0:T(8,128)(2,1)S(1)} %get-tuple-element.40), channel_id=1, source_target_pairs={{0,24},{1,25},{2,26},{3,27},{4,28},{5,29},{6,30},{7,31},{8,16},{9,... | collective-permute-start | bytes 208904 | tf_op jit(solution)/shard_map/ppermute | solution.py:433
  27.9 7.8 %collective-permute-start.11 = (bf16[272,128]{1,0:T(8,128)(2,1)S(1)}, bf16[272,128]{1,0:T(8,128)(2,1)S(1)}, u32[]{:S(2)}, u32[]{:S(2)}) collective-permute-start(bf16[272,128]{1,0:T(8,128)(2,1)S(1)} %get-tuple-element.41), channel_id=1, source_target_pairs={{0,22},{1,23},{2,20},{3,21},{4,18},{5,19},{6,16},{7,17},{8,30},{9,... | collective-permute-start | bytes 208904 | tf_op jit(solution)/shard_map/ppermute | solution.py:433
  28.1 7.6 %collective-permute-start.12 = (bf16[272,128]{1,0:T(8,128)(2,1)S(1)}, bf16[272,128]{1,0:T(8,128)(2,1)S(1)}, u32[]{:S(2)}, u32[]{:S(2)}) collective-permute-start(bf16[272,128]{1,0:T(8,128)(2,1)S(1)} %get-tuple-element.42), channel_id=1, source_target_pairs={{0,14},{1,15},{2,12},{3,13},{4,10},{5,11},{6,8},{7,9},{8,6},{9,7},... | collective-permute-start | bytes 208904 | tf_op jit(solution)/shard_map/ppermute | solution.py:433
  39.3 8.0 %copy-start = (bf16[1,8,128,512]{3,2,1,0:T(8,128)(2,1)S(1)}, bf16[1,8,128,512]{3,2,1,0:T(8,128)(2,1)}, u32[]{:S(2)}) copy-start(bf16[1,8,128,512]{3,2,1,0:T(8,128)(2,1)} %param.3) | copy-start | bytes 3145732
  40.1 4.4 %collective-permute-start.16 = (bf16[128,512]{1,0:T(8,128)(2,1)S(1)}, bf16[128,512]{1,0:T(8,128)(2,1)S(1)}, u32[]{:S(2)}, u32[]{:S(2)}) collective-permute-start(bf16[128,512]{1,0:T(8,128)(2,1)S(1)} %get-tuple-element.47), channel_id=1, source_target_pairs={{3,0},{4,1},{1,2},{6,3},{7,4},{0,5},{5,6},{2,7},{11,8},{12,9},{9,1... | collective-permute-start | bytes 393224 | tf_op jit(solution)/shard_map/ppermute | solution.py:433
  40.1 5.5 %collective-permute-start.17 = (bf16[128,512]{1,0:T(8,128)(2,1)S(1)}, bf16[128,512]{1,0:T(8,128)(2,1)S(1)}, u32[]{:S(2)}, u32[]{:S(2)}) collective-permute-start(bf16[128,512]{1,0:T(8,128)(2,1)S(1)} %get-tuple-element.48), channel_id=1, source_target_pairs={{5,0},{8,1},{7,2},{10,3},{1,4},{12,5},{3,6},{14,7},{13,8},{0,9},{1... | collective-permute-start | bytes 393224 | tf_op jit(solution)/shard_map/ppermute | solution.py:433
  41.6 5.3 %collective-permute-start.18 = (bf16[128,512]{1,0:T(8,128)(2,1)S(1)}, bf16[128,512]{1,0:T(8,128)(2,1)S(1)}, u32[]{:S(2)}, u32[]{:S(2)}) collective-permute-start(bf16[128,512]{1,0:T(8,128)(2,1)S(1)} %get-tuple-element.49), channel_id=1, source_target_pairs={{9,0},{2,1},{11,2},{0,3},{13,4},{6,5},{15,6},{4,7},{1,8},{10,9},{3... | collective-permute-start | bytes 393224 | tf_op jit(solution)/shard_map/ppermute | solution.py:433
  41.9 5.5 %collective-permute-start.19 = (bf16[128,512]{1,0:T(8,128)(2,1)S(1)}, bf16[128,512]{1,0:T(8,128)(2,1)S(1)}, u32[]{:S(2)}, u32[]{:S(2)}) collective-permute-start(bf16[128,512]{1,0:T(8,128)(2,1)S(1)} %get-tuple-element.50), channel_id=1, source_target_pairs={{2,0},{5,1},{0,2},{7,3},{6,4},{1,5},{4,6},{3,7},{10,8},{13,9},{8,1... | collective-permute-start | bytes 393224 | tf_op jit(solution)/shard_map/ppermute | solution.py:433
  43.0 5.3 %collective-permute-start.13 = (bf16[128,512]{1,0:T(8,128)(2,1)S(1)}, bf16[128,512]{1,0:T(8,128)(2,1)S(1)}, u32[]{:S(2)}, u32[]{:S(2)}) collective-permute-start(bf16[128,512]{1,0:T(8,128)(2,1)S(1)} %get-tuple-element.43), channel_id=1, source_target_pairs={{4,0},{9,1},{6,2},{11,3},{0,4},{13,5},{2,6},{15,7},{12,8},{1,9},{1... | collective-permute-start | bytes 393224 | tf_op jit(solution)/shard_map/ppermute | solution.py:433
  44.5 5.2 %collective-permute-start.14 = (bf16[128,512]{1,0:T(8,128)(2,1)S(1)}, bf16[128,512]{1,0:T(8,128)(2,1)S(1)}, u32[]{:S(2)}, u32[]{:S(2)}) collective-permute-start(bf16[128,512]{1,0:T(8,128)(2,1)S(1)} %get-tuple-element.44), channel_id=1, source_target_pairs={{8,0},{3,1},{10,2},{1,3},{12,4},{7,5},{14,6},{5,7},{0,8},{11,9},{2... | collective-permute-start | bytes 393224 | tf_op jit(solution)/shard_map/ppermute | solution.py:433
  45.6 4.1 %collective-permute-start.15 = (bf16[128,512]{1,0:T(8,128)(2,1)S(1)}, bf16[128,512]{1,0:T(8,128)(2,1)S(1)}, u32[]{:S(2)}, u32[]{:S(2)}) collective-permute-start(bf16[128,512]{1,0:T(8,128)(2,1)S(1)} %get-tuple-element.45), channel_id=1, source_target_pairs={{1,0},{0,1},{3,2},{2,3},{5,4},{4,5},{7,6},{6,7},{9,8},{8,9},{11,10... | collective-permute-start | bytes 393224 | tf_op jit(solution)/shard_map/ppermute | solution.py:433

commit v7 on v6

--- a/solution.py
+++ b/solution.py
@@ -13,6 +13,7 @@
 WIDE = 256
 F32_TILE = 8
 BF16_TILE = 16
+SMALLEST = 1e-30
 VMEM_BYTES = 48 << 20
 EARLY = 5
 
@@ -177,20 +178,22 @@
     return result
 
 
-def to_message(quarter, order):
+def to_message(quarter, order, vector=None):
     fold_count, block_count = quarter_blocks(order)
     length = block_count * BLOCK
     body, tail = quarter[:length], quarter[length : length + fold_count]
-    rounded = body.astype(jnp.bfloat16)
+    rounded_body = body.astype(jnp.bfloat16)
     rows = [
         diagonal(
-            body[k * BLOCK : (k + 1) * BLOCK] - rounded[k * BLOCK : (k + 1) * BLOCK].astype(jnp.float32)
+            body[k * BLOCK : (k + 1) * BLOCK] - rounded_body[k * BLOCK : (k + 1) * BLOCK].astype(jnp.float32)
         )
         for k in range(fold_count)
     ]
     high = tail.astype(jnp.bfloat16).astype(jnp.float32)
-    extra = padded(rows + [high, tail - high], BF16_TILE)
-    return jnp.concatenate([rounded, extra.astype(jnp.bfloat16)], axis=0)
+    rows += [high, tail - high]
+    if vector is not None:
+        rows += [vector[:, k : k + BLOCK] for k in range(0, order, BLOCK)]
+    return jnp.concatenate([rounded_body, padded(rows, BF16_TILE).astype(jnp.bfloat16)], axis=0)
 
 
 def from_message(message, order):
@@ -207,6 +210,43 @@
     return jnp.concatenate(tiles + [body[fold_count * BLOCK :], padded([tail], F32_TILE)], axis=0)
 
 
+def vector_of(message, order):
+    fold_count, block_count = quarter_blocks(order)
+    start = block_count * BLOCK + 3 * fold_count
+    values = message.astype(jnp.float32)
+    return jnp.concatenate([values[start + k : start + k + 1] for k in range(order // BLOCK)], axis=1)
+
+
+def stacked(vectors):
+    rows = jnp.concatenate(vectors, axis=0)
+    filler = jnp.zeros((BF16_TILE - rows.shape[0], rows.shape[1]), jnp.float32)
+    return jnp.concatenate([rows, filler], axis=0).astype(jnp.bfloat16)
+
+
+def outer_products(vectors):
+    order = vectors.shape[1]
+    result = {}
+    for start in range(0, order, BLOCK):
+        band = lax.dot_general(
+            vectors[:, start : start + BLOCK],
+            vectors[:, start:],
+            (((0,), (0,)), ((), ())),
+            preferred_element_type=jnp.float32,
+        )
+        for offset in range(0, order - start, BLOCK):
+            place = start // BLOCK, (start + offset) // BLOCK
+            result[place] = band[:, offset : offset + BLOCK]
+    return result
+
+
+def main_direction(first_row):
+    signs = jnp.where(first_row[0][:, :1] < 0.0, -1.0, 1.0)
+    rows = [jnp.sum(signs * block, axis=0, keepdims=True) for block in first_row]
+    size = jnp.sum(jnp.where(first_row[0][:1, :] < 0.0, -rows[0], rows[0]))
+    growth = jnp.where(size > 0.0, lax.rsqrt(jnp.maximum(size, SMALLEST)), 0.0)
+    return (jnp.concatenate(rows, axis=1) * growth).astype(jnp.bfloat16).astype(jnp.float32)
+
+
 def deal_kernel(rest_count, momentum_ref, *refs):
     place = Place(rest_count)
     for number, block_ref in enumerate(refs):
@@ -231,32 +271,45 @@
         tile = tiles[row // WIDE * WIDE, column // WIDE * WIDE]
         return tile[row % WIDE :, column % WIDE :][:BLOCK, :BLOCK]
 
-    return pack(block, order)
+    return pack(block, order), [block(0, k) for k in range(order // BLOCK)]
 
 
 def early_gram_kernel(*refs):
-    for quarter, value in enumerate(packed_gram(refs[:-1])):
-        refs[-1][quarter] = value
-
-
-def gram_kernel(early_ref, *refs):
-    for quarter, value in enumerate(packed_gram(refs[:-1])):
-        refs[-1][quarter] = early_ref[quarter] + value
-
-
-def reduce_kernel(rest_count, order, sum_ref, *message_refs):
+    block_refs, packed_ref, first_row_ref = refs[:-2], refs[-2], refs[-1]
+    packed, first_row = packed_gram(block_refs)
+    for quarter, value in enumerate(packed):
+        packed_ref[quarter] = value
+    for number, value in enumerate(first_row):
+        first_row_ref[number] = value
+
+
+def gram_kernel(early_ref, early_row_ref, *refs):
+    block_refs, left_ref, direction_ref = refs[:-2], refs[-2], refs[-1]
+    order = block_refs[0].shape[1]
+    packed, first_row = packed_gram(block_refs)
+    direction = main_direction([early_row_ref[number] + value for number, value in enumerate(first_row)])
+    direction_ref[...] = stacked([direction])
+    outer = outer_products(stacked([direction]))
+    for quarter, (value, known) in enumerate(zip(packed, pack(lambda i, j: outer[i, j], order))):
+        left_ref[quarter] = early_ref[quarter] + (value - known)
+
+
+def reduce_kernel(rest_count, order, left_ref, direction_ref, *message_refs):
     place = Place(rest_count)
+    direction = direction_ref[...].astype(jnp.float32)[:1]
     for step, message_ref in enumerate(message_refs):
-        message_ref[...] = to_message(sum_ref[place.quarter_at(step)], order)
-
-
-def gather_kernel(rest_count, order, sum_ref, *refs):
-    arrived_refs, total_ref, message_refs = refs[:3], refs[3], refs[4:]
+        message_ref[...] = to_message(left_ref[place.quarter_at(step)], order, direction)
+
+
+def gather_kernel(rest_count, order, left_ref, direction_ref, *refs):
+    arrived_refs, total_ref, directions_ref, message_refs = refs[:3], refs[3], refs[4], refs[5:]
     arrived = [from_message(arrived_ref[...], order) for arrived_ref in arrived_refs]
-    total = sum_ref[Place(rest_count).quarter] + (arrived[0] + (arrived[1] + arrived[2]))
+    total = left_ref[Place(rest_count).quarter] + (arrived[0] + (arrived[1] + arrived[2]))
     total_ref[...] = total
     for value, message_ref in zip(arrived, message_refs):
         message_ref[...] = to_message(total - value, order)
+    own = direction_ref[...].astype(jnp.float32)[:1]
+    directions_ref[...] = stacked([own] + [vector_of(arrived_ref[...], order) for arrived_ref in arrived_refs])
 
 
 def assemble(upper, count):
@@ -325,14 +378,18 @@
     return accum_identity, accum
 
 
-def factor_kernel(rest_count, order, scale, sum_ref, total_ref, *refs):
+def factor_kernel(rest_count, order, scale, left_ref, total_ref, directions_ref, *refs):
     rest_refs, factor_ref, quarters_ref = refs[:3], refs[3], refs[4]
     place = Place(rest_count)
     quarters_ref[place.quarter] = total_ref[...]
     for step, rest_ref in enumerate(rest_refs):
         quarter = place.quarter_at(step)
-        quarters_ref[quarter] = sum_ref[quarter] + from_message(rest_ref[...], order)
-    blocks = unpack([quarters_ref[quarter] for quarter in range(4)], order)
+        quarters_ref[quarter] = left_ref[quarter] + from_message(rest_ref[...], order)
+    outer = outer_products(directions_ref[...])
+    blocks = {
+        key: value + outer[key]
+        for key, value in unpack([quarters_ref[quarter] for quarter in range(4)], order).items()
+    }
     trace_sum = jnp.sum(sum(diagonal(blocks[i, i]) for i in range(order // BLOCK)))
     shrink = 1.0 / (trace_sum + epsilon)
     count, ratio = order // WIDE, WIDE // BLOCK
@@ -445,20 +502,24 @@
         spread.reshape(by_block),
     )
     rows = [own] + swap(dealt, ROWS)
-    early_gram = call(early_gram_kernel, packed, *rows[:EARLY])
-    place_sum = call(gram_kernel, packed, early_gram, *rows[EARLY:])
-    parts = call(functools.partial(reduce_kernel, rest_count, order), (message,) * 3, place_sum)
-    total, *rests = call(
+    first_row = jax.ShapeDtypeStruct((order // BLOCK, BLOCK, BLOCK), jnp.float32)
+    direction = jax.ShapeDtypeStruct((BF16_TILE, order), jnp.bfloat16)
+    early = call(early_gram_kernel, (packed, first_row), *rows[:EARLY])
+    left, own_direction = call(gram_kernel, (packed, direction), *early, *rows[EARLY:])
+    parts = call(functools.partial(reduce_kernel, rest_count, order), (message,) * 3, left, own_direction)
+    total, directions, *rests = call(
         functools.partial(gather_kernel, rest_count, order),
-        (quarter,) + (message,) * 3,
-        place_sum,
+        (quarter, direction) + (message,) * 3,
+        left,
+        own_direction,
         *swap(parts, OWNERS),
     )
     factor = call(
         functools.partial(factor_kernel, rest_count, order, scale),
         jax.ShapeDtypeStruct((order, order), jnp.bfloat16),
-        place_sum,
+        left,
         total,
+        directions,
         *swap(rests, OWNERS),
         scratch=[pltpu.VMEM(packed.shape, packed.dtype)],
     )

time: 50.7 us -> 51.2 us (level)
  Pallas kernels: 7.37 us -> 7.9 us
    pallas_call x7, Pallas kernels: 5.6 us -> 6.12 us  [call(): pl.pallas_call(kernel, out_shape=out_shape, in_specs=[vmem] * len(operand...]
where the time goes in v7:
time: 51.2 us; the launch traced here: 51.1 us
  starting transfers between devices  26.7 us (52%)
  waiting for transfers between devices  15.2 us (30%)
  Pallas kernels  7.9 us (15%)
  local copies, waits for them, and re-layouts  1.23 us (2%)
    ppermute x20, starting transfers between devices, swap(): lax.ppermute(array, AXES, permute)  26.7 us
    ppermute x20, waiting for transfers between devices, swap(): lax.ppermute(array, AXES, permute)  15.2 us
    pallas_call x7, Pallas kernels, call(): pl.pallas_call(kernel, out_shape=out_shape, in_specs=[vmem] * len(operand...  6.12 us
    pallas_call x2, Pallas kernels, new_weights(): pl.pallas_call(functools.partial(weights_kernel, rest_count, numbers), ou...  1.77 us
    unnamed x4, local copies, waits for them, and re-layouts  1.23 us
  transfers between devices with their start and end apart: 20, of which 10 were waited for; matrix products, arithmetic and copies ran while one was open for 0% of the time, Pallas kernels for 3%

profile of v7, /device:TPU:0, one launch (start us, length us, event | category | flops | bytes accessed | tf_op | source)
XLA Modules:
  0.0 51.1 jit_solution(18437886784440661417)
XLA Ops:
  0.0 1.2 %copy-done.1 = bf16[1,8,128,512]{3,2,1,0:T(8,128)(2,1)S(1)} copy-done((bf16[1,8,128,512]{3,2,1,0:T(8,128)(2,1)S(1)}, bf16[1,8,128,512]{3,2,1,0:T(8,128)(2,1)}, u32[]{:S(2)}) %copy-start.1) | copy-done | bytes 1048600
  1.3 2.4 %collective-permute-start = (bf16[128,512]{1,0:T(8,128)(2,1)S(1)}, bf16[128,512]{1,0:T(8,128)(2,1)S(1)}, u32[]{:S(2)}, u32[]{:S(2)}) collective-permute-start(bf16[128,512]{1,0:T(8,128)(2,1)S(1)} %get-tuple-element.34), channel_id=1, source_target_pairs={{0,3},{1,4},{2,1},{3,6},{4,7},{5,0},{6,5},{7,2},{8,11},{9,12},{10,... | collective-permute-start | bytes 393224 | tf_op jit(solution)/shard_map/ppermute | solution.py:490
  3.8 1.8 %collective-permute-start.2 = (bf16[128,512]{1,0:T(8,128)(2,1)S(1)}, bf16[128,512]{1,0:T(8,128)(2,1)S(1)}, u32[]{:S(2)}, u32[]{:S(2)}) collective-permute-start(bf16[128,512]{1,0:T(8,128)(2,1)S(1)} %get-tuple-element.36), channel_id=1, source_target_pairs={{0,9},{1,2},{2,11},{3,0},{4,13},{5,6},{6,15},{7,4},{8,1},{9,10},{1... | collective-permute-start | bytes 393224 | tf_op jit(solution)/shard_map/ppermute | solution.py:490
  5.6 1.5 %collective-permute-start.3 = (bf16[128,512]{1,0:T(8,128)(2,1)S(1)}, bf16[128,512]{1,0:T(8,128)(2,1)S(1)}, u32[]{:S(2)}, u32[]{:S(2)}) collective-permute-start(bf16[128,512]{1,0:T(8,128)(2,1)S(1)} %get-tuple-element.37), channel_id=1, source_target_pairs={{0,2},{1,5},{2,0},{3,7},{4,6},{5,1},{6,4},{7,3},{8,10},{9,13},{10,... | collective-permute-start | bytes 393224 | tf_op jit(solution)/shard_map/ppermute | solution.py:490
  7.1 0.5 %collective-permute-start.4 = (bf16[128,512]{1,0:T(8,128)(2,1)S(1)}, bf16[128,512]{1,0:T(8,128)(2,1)S(1)}, u32[]{:S(2)}, u32[]{:S(2)}) collective-permute-start(bf16[128,512]{1,0:T(8,128)(2,1)S(1)} %get-tuple-element.40), channel_id=1, source_target_pairs={{0,4},{1,9},{2,6},{3,11},{4,0},{5,13},{6,2},{7,15},{8,12},{9,1},{1... | collective-permute-start | bytes 393224 | tf_op jit(solution)/shard_map/ppermute | solution.py:490
  7.6 1.6 %collective-permute-start.5 = (bf16[128,512]{1,0:T(8,128)(2,1)S(1)}, bf16[128,512]{1,0:T(8,128)(2,1)S(1)}, u32[]{:S(2)}, u32[]{:S(2)}) collective-permute-start(bf16[128,512]{1,0:T(8,128)(2,1)S(1)} %get-tuple-element.41), channel_id=1, source_target_pairs={{0,8},{1,3},{2,10},{3,1},{4,12},{5,7},{6,14},{7,5},{8,0},{9,11},{1... | collective-permute-start | bytes 393224 | tf_op jit(solution)/shard_map/ppermute | solution.py:490
  9.4 1.2 %collective-permute-done.3.refs_4_ = bf16[128,512]{1,0:T(8,128)(2,1)S(1)} collective-permute-done((bf16[128,512]{1,0:T(8,128)(2,1)S(1)}, bf16[128,512]{1,0:T(8,128)(2,1)S(1)}, u32[]{:S(2)}, u32[]{:S(2)}) %collective-permute-start.3) | collective-permute-done | bytes 131104 | tf_op jit(solution)/shard_map/ppermute | solution.py:490
  10.6 0.5 %shard_map.29 = (f32[4,264,128]{2,1,0:T(8,128)S(1)}, f32[4,128,128]{2,1,0:T(8,128)S(1)}) custom-call(bf16[128,512]{1,0:T(8,128)(2,1)S(1)} %get-tuple-element.33.refs_0_, bf16[128,512]{1,0:T(8,128)(2,1)S(1)} %collective-permute-done.refs_1_, bf16[128,512]{1,0:T(8,128)(2,1)S(1)} %collective-permute-done.1.refs_2_, ...), custom_call_target="tpu_custom_call" | custom-call | tf_op jit(solution)/shard_map/pallas_call | solution.py:92
  11.1 1.0 %collective-permute-done.4.refs_0_.refs_5_ = bf16[128,512]{1,0:T(8,128)(2,1)S(1)} collective-permute-done((bf16[128,512]{1,0:T(8,128)(2,1)S(1)}, bf16[128,512]{1,0:T(8,128)(2,1)S(1)}, u32[]{:S(2)}, u32[]{:S(2)}) %collective-permute-start.4) | collective-permute-done | bytes 131104 | tf_op jit(solution)/shard_map/ppermute | solution.py:490
  12.1 0.7 %collective-permute-done.5.refs_1_.refs_6_ = bf16[128,512]{1,0:T(8,128)(2,1)S(1)} collective-permute-done((bf16[128,512]{1,0:T(8,128)(2,1)S(1)}, bf16[128,512]{1,0:T(8,128)(2,1)S(1)}, u32[]{:S(2)}, u32[]{:S(2)}) %collective-permute-start.5) | collective-permute-done | bytes 131104 | tf_op jit(solution)/shard_map/ppermute | solution.py:490
  12.8 0.9 %shard_map.30 = (f32[4,264,128]{2,1,0:T(8,128)S(1)}, bf16[16,512]{1,0:T(8,128)(2,1)S(1)}) custom-call(f32[4,264,128]{2,1,0:T(8,128)S(1)} %get-tuple-element.38.early_ref, f32[4,128,128]{2,1,0:T(8,128)S(1)} %get-tuple-element.39.early_row_ref, bf16[128,512]{1,0:T(8,128)(2,1)S(1)} %collective-permute-done.4.refs_0_.refs_5_, ...), custom_call_target="tpu_custom_call" | custom-call | tf_op jit(solution)/shard_map/pallas_call | solution.py:92
  13.8 3.7 %collective-permute-start.7 = (bf16[272,128]{1,0:T(8,128)(2,1)S(1)}, bf16[272,128]{1,0:T(8,128)(2,1)S(1)}, u32[]{:S(2)}, u32[]{:S(2)}) collective-permute-start(bf16[272,128]{1,0:T(8,128)(2,1)S(1)} %get-tuple-element.45), channel_id=1, source_target_pairs={{0,24},{1,25},{2,26},{3,27},{4,28},{5,29},{6,30},{7,31},{8,16},{9,... | collective-permute-start | bytes 208904 | tf_op jit(solution)/shard_map/ppermute | solution.py:490
  17.4 1.3 %collective-permute-start.8 = (bf16[272,128]{1,0:T(8,128)(2,1)S(1)}, bf16[272,128]{1,0:T(8,128)(2,1)S(1)}, u32[]{:S(2)}, u32[]{:S(2)}) collective-permute-start(bf16[272,128]{1,0:T(8,128)(2,1)S(1)} %get-tuple-element.46), channel_id=1, source_target_pairs={{0,22},{1,23},{2,20},{3,21},{4,18},{5,19},{6,16},{7,17},{8,30},{9,... | collective-permute-start | bytes 208904 | tf_op jit(solution)/shard_map/ppermute | solution.py:490
  18.7 1.3 %collective-permute-start.9 = (bf16[272,128]{1,0:T(8,128)(2,1)S(1)}, bf16[272,128]{1,0:T(8,128)(2,1)S(1)}, u32[]{:S(2)}, u32[]{:S(2)}) collective-permute-start(bf16[272,128]{1,0:T(8,128)(2,1)S(1)} %get-tuple-element.47), channel_id=1, source_target_pairs={{0,14},{1,15},{2,12},{3,13},{4,10},{5,11},{6,8},{7,9},{8,6},{9,7},... | collective-permute-start | bytes 208904 | tf_op jit(solution)/shard_map/ppermute | solution.py:490
  20.0 4.8 %collective-permute-done.8.refs_1_ = bf16[272,128]{1,0:T(8,128)(2,1)S(1)} collective-permute-done((bf16[272,128]{1,0:T(8,128)(2,1)S(1)}, bf16[272,128]{1,0:T(8,128)(2,1)S(1)}, u32[]{:S(2)}, u32[]{:S(2)}) %collective-permute-start.8) | collective-permute-done | bytes 69664 | tf_op jit(solution)/shard_map/ppermute | solution.py:490
  24.9 0.7 %collective-permute-done.9.refs_2_ = bf16[272,128]{1,0:T(8,128)(2,1)S(1)} collective-permute-done((bf16[272,128]{1,0:T(8,128)(2,1)S(1)}, bf16[272,128]{1,0:T(8,128)(2,1)S(1)}, u32[]{:S(2)}, u32[]{:S(2)}) %collective-permute-start.9) | collective-permute-done | bytes 69664 | tf_op jit(solution)/shard_map/ppermute | solution.py:490
  25.7 2.7 %collective-permute-start.10 = (bf16[272,128]{1,0:T(8,128)(2,1)S(1)}, bf16[272,128]{1,0:T(8,128)(2,1)S(1)}, u32[]{:S(2)}, u32[]{:S(2)}) collective-permute-start(bf16[272,128]{1,0:T(8,128)(2,1)S(1)} %get-tuple-element.50), channel_id=1, source_target_pairs={{0,24},{1,25},{2,26},{3,27},{4,28},{5,29},{6,30},{7,31},{8,16},{9,... | collective-permute-start | bytes 208904 | tf_op jit(solution)/shard_map/ppermute | solution.py:490
  28.5 3.4 %collective-permute-start.12 = (bf16[272,128]{1,0:T(8,128)(2,1)S(1)}, bf16[272,128]{1,0:T(8,128)(2,1)S(1)}, u32[]{:S(2)}, u32[]{:S(2)}) collective-permute-start(bf16[272,128]{1,0:T(8,128)(2,1)S(1)} %get-tuple-element.52), channel_id=1, source_target_pairs={{0,14},{1,15},{2,12},{3,13},{4,10},{5,11},{6,8},{7,9},{8,6},{9,7},... | collective-permute-start | bytes 208904 | tf_op jit(solution)/shard_map/ppermute | solution.py:490
  31.9 4.2 %collective-permute-done.11.refs_1_ = bf16[272,128]{1,0:T(8,128)(2,1)S(1)} collective-permute-done((bf16[272,128]{1,0:T(8,128)(2,1)S(1)}, bf16[272,128]{1,0:T(8,128)(2,1)S(1)}, u32[]{:S(2)}, u32[]{:S(2)}) %collective-permute-start.11) | collective-permute-done | bytes 69664 | tf_op jit(solution)/shard_map/ppermute | solution.py:490
  36.1 3.8 %shard_map.33.factor_ref = bf16[512,512]{1,0:T(8,128)(2,1)S(1)} custom-call(f32[4,264,128]{2,1,0:T(8,128)S(1)} %get-tuple-element.43.left_ref, f32[264,128]{1,0:T(8,128)S(1)} %get-tuple-element.48.total_ref, bf16[16,512]{1,0:T(8,128)(2,1)S(1)} %get-tuple-element.49.directions_ref, bf16[272,128]{1,0:T(8,128)(2,1)S(1)} %collective-permute-done.10.refs_0_, ...), custom_call_target="tpu_custom_call" | custom-call | tf_op jit(solution)/shard_map/pallas_call | solution.py:92
  39.9 0.7 %shard_map.34 = (bf16[128,512]{1,0:T(8,128)(2,1)S(1)}, bf16[128,512]{1,0:T(8,128)(2,1)S(1)}, bf16[128,512]{1,0:T(8,128)(2,1)S(1)}, bf16[128,512]{1,0:T(8,128)(2,...) custom-call(bf16[512,512]{1,0:T(8,128)(2,1)S(1)} %shard_map.33.facto, ...), custom_call_target="tpu_custom_call" | custom-call | tf_op jit(solution)/shard_map/pallas_call | solution.py:92
  40.6 1.4 %collective-permute-start.17 = (bf16[128,512]{1,0:T(8,128)(2,1)S(1)}, bf16[128,512]{1,0:T(8,128)(2,1)S(1)}, u32[]{:S(2)}, u32[]{:S(2)}) collective-permute-start(bf16[128,512]{1,0:T(8,128)(2,1)S(1)} %get-tuple-element.58), channel_id=1, source_target_pairs={{5,0},{8,1},{7,2},{10,3},{1,4},{12,5},{3,6},{14,7},{13,8},{0,9},{1... | collective-permute-start | bytes 393224 | tf_op jit(solution)/shard_map/ppermute | solution.py:490
  42.1 0.3 collective-permute-start.18
  42.4 1.1 %collective-permute-start.19 = (bf16[128,512]{1,0:T(8,128)(2,1)S(1)}, bf16[128,512]{1,0:T(8,128)(2,1)S(1)}, u32[]{:S(2)}, u32[]{:S(2)}) collective-permute-start(bf16[128,512]{1,0:T(8,128)(2,1)S(1)} %get-tuple-element.60), channel_id=1, source_target_pairs={{2,0},{5,1},{0,2},{7,3},{6,4},{1,5},{4,6},{3,7},{10,8},{13,9},{8,1... | collective-permute-start | bytes 393224 | tf_op jit(solution)/shard_map/ppermute | solution.py:490
  43.5 1.1 %collective-permute-start.13 = (bf16[128,512]{1,0:T(8,128)(2,1)S(1)}, bf16[128,512]{1,0:T(8,128)(2,1)S(1)}, u32[]{:S(2)}, u32[]{:S(2)}) collective-permute-start(bf16[128,512]{1,0:T(8,128)(2,1)S(1)} %get-tuple-element.53), channel_id=1, source_target_pairs={{4,0},{9,1},{6,2},{11,3},{0,4},{13,5},{2,6},{15,7},{12,8},{1,9},{1... | collective-permute-start | bytes 393224 | tf_op jit(solution)/shard_map/ppermute | solution.py:490
  44.6 0.4 collective-permute-done.16.refs_1_
  45.0 1.1 %collective-permute-start.14 = (bf16[128,512]{1,0:T(8,128)(2,1)S(1)}, bf16[128,512]{1,0:T(8,128)(2,1)S(1)}, u32[]{:S(2)}, u32[]{:S(2)}) collective-permute-start(bf16[128,512]{1,0:T(8,128)(2,1)S(1)} %get-tuple-element.54), channel_id=1, source_target_pairs={{8,0},{3,1},{10,2},{1,3},{12,4},{7,5},{14,6},{5,7},{0,8},{11,9},{2... | collective-permute-start | bytes 393224 | tf_op jit(solution)/shard_map/ppermute | solution.py:490
  46.2 1.0 %collective-permute-start.15 = (bf16[128,512]{1,0:T(8,128)(2,1)S(1)}, bf16[128,512]{1,0:T(8,128)(2,1)S(1)}, u32[]{:S(2)}, u32[]{:S(2)}) collective-permute-start(bf16[128,512]{1,0:T(8,128)(2,1)S(1)} %get-tuple-element.55), channel_id=1, source_target_pairs={{1,0},{0,1},{3,2},{2,3},{5,4},{4,5},{7,6},{6,7},{9,8},{8,9},{11,10... | collective-permute-start | bytes 393224 | tf_op jit(solution)/shard_map/ppermute | solution.py:490
  47.4 0.5 collective-permute-done.19.refs_4_
  47.9 0.9 %shard_map.35.refs_3_ = bf16[4,2,128,512]{3,2,1,0:T(8,128)(2,1)} custom-call(bf16[4,2,128,512]{3,2,1,0:T(8,128)(2,1)S(1)} %bitcast.3, bf16[128,512]{1,0:T(8,128)(2,1)S(1)} %get-tuple-element.56.refs_0_, bf16[128,512]{1,0:T(8,128)(2,1)S(1)} %collective-permute-done.16.refs_1_, bf16[128,512]{1,0:T(8,128)(2,1)S(1)} %collective-permute-done.17.refs_2_, ...), custom_call_target="tpu_custom_call" | custom-call | tf_op jit(solution)/shard_map/pallas_call | solution.py:453
  48.9 1.4 %collective-permute-done.14.refs_1_ = bf16[128,512]{1,0:T(8,128)(2,1)S(1)} collective-permute-done((bf16[128,512]{1,0:T(8,128)(2,1)S(1)}, bf16[128,512]{1,0:T(8,128)(2,1)S(1)}, u32[]{:S(2)}, u32[]{:S(2)}) %collective-permute-start.14) | collective-permute-done | bytes 131104 | tf_op jit(solution)/shard_map/ppermute | solution.py:490
  50.3 0.8 %shard_map.36 = bf16[4,2,128,512]{3,2,1,0:T(8,128)(2,1)} custom-call(bf16[4,2,128,512]{3,2,1,0:T(8,128)(2,1)S(1)} %bitcast.4, bf16[128,512]{1,0:T(8,128)(2,1)S(1)} %collective-permute-done.13.refs_0_, bf16[128,512]{1,0:T(8,128)(2,1)S(1)} %collective-permute-done.14.refs_1_, ...), custom_call_target="tpu_custom_call", output_to_operand_aliasing={{}: (4, {})} | custom-call | tf_op jit(solution)/shard_map/pallas_call | solution.py:453
  (21 shorter events, 1.1 us)
Async XLA Ops:
  0.0 1.2 %copy-start.1 = (bf16[1,8,128,512]{3,2,1,0:T(8,128)(2,1)S(1)}, bf16[1,8,128,512]{3,2,1,0:T(8,128)(2,1)}, u32[]{:S(2)}) copy-start(bf16[1,8,128,512]{3,2,1,0:T(8,128)(2,1)} %param.2) | copy-start | bytes 3145732
  1.3 6.3 %collective-permute-start = (bf16[128,512]{1,0:T(8,128)(2,1)S(1)}, bf16[128,512]{1,0:T(8,128)(2,1)S(1)}, u32[]{:S(2)}, u32[]{:S(2)}) collective-permute-start(bf16[128,512]{1,0:T(8,128)(2,1)S(1)} %get-tuple-element.34), channel_id=1, source_target_pairs={{0,3},{1,4},{2,1},{3,6},{4,7},{5,0},{6,5},{7,2},{8,11},{9,12},{10,... | collective-permute-start | bytes 393224 | tf_op jit(solution)/shard_map/ppermute | solution.py:490
  3.7 5.5 %collective-permute-start.1 = (bf16[128,512]{1,0:T(8,128)(2,1)S(1)}, bf16[128,512]{1,0:T(8,128)(2,1)S(1)}, u32[]{:S(2)}, u32[]{:S(2)}) collective-permute-start(bf16[128,512]{1,0:T(8,128)(2,1)S(1)} %get-tuple-element.35), channel_id=1, source_target_pairs={{0,5},{1,8},{2,7},{3,10},{4,1},{5,12},{6,3},{7,14},{8,13},{9,0},{1... | collective-permute-start | bytes 393224 | tf_op jit(solution)/shard_map/ppermute | solution.py:490
  3.8 5.5 %collective-permute-start.2 = (bf16[128,512]{1,0:T(8,128)(2,1)S(1)}, bf16[128,512]{1,0:T(8,128)(2,1)S(1)}, u32[]{:S(2)}, u32[]{:S(2)}) collective-permute-start(bf16[128,512]{1,0:T(8,128)(2,1)S(1)} %get-tuple-element.36), channel_id=1, source_target_pairs={{0,9},{1,2},{2,11},{3,0},{4,13},{5,6},{6,15},{7,4},{8,1},{9,10},{1... | collective-permute-start | bytes 393224 | tf_op jit(solution)/shard_map/ppermute | solution.py:490
  5.6 5.0 %collective-permute-start.3 = (bf16[128,512]{1,0:T(8,128)(2,1)S(1)}, bf16[128,512]{1,0:T(8,128)(2,1)S(1)}, u32[]{:S(2)}, u32[]{:S(2)}) collective-permute-start(bf16[128,512]{1,0:T(8,128)(2,1)S(1)} %get-tuple-element.37), channel_id=1, source_target_pairs={{0,2},{1,5},{2,0},{3,7},{4,6},{5,1},{6,4},{7,3},{8,10},{9,13},{10,... | collective-permute-start | bytes 393224 | tf_op jit(solution)/shard_map/ppermute | solution.py:490
  7.1 5.0 %collective-permute-start.4 = (bf16[128,512]{1,0:T(8,128)(2,1)S(1)}, bf16[128,512]{1,0:T(8,128)(2,1)S(1)}, u32[]{:S(2)}, u32[]{:S(2)}) collective-permute-start(bf16[128,512]{1,0:T(8,128)(2,1)S(1)} %get-tuple-element.40), channel_id=1, source_target_pairs={{0,4},{1,9},{2,6},{3,11},{4,0},{5,13},{6,2},{7,15},{8,12},{9,1},{1... | collective-permute-start | bytes 393224 | tf_op jit(solution)/shard_map/ppermute | solution.py:490
  7.6 5.2 %collective-permute-start.5 = (bf16[128,512]{1,0:T(8,128)(2,1)S(1)}, bf16[128,512]{1,0:T(8,128)(2,1)S(1)}, u32[]{:S(2)}, u32[]{:S(2)}) collective-permute-start(bf16[128,512]{1,0:T(8,128)(2,1)S(1)} %get-tuple-element.41), channel_id=1, source_target_pairs={{0,8},{1,3},{2,10},{3,1},{4,12},{5,7},{6,14},{7,5},{8,0},{9,11},{1... | collective-permute-start | bytes 393224 | tf_op jit(solution)/shard_map/ppermute | solution.py:490
  9.2 3.6 %collective-permute-start.6 = (bf16[128,512]{1,0:T(8,128)(2,1)S(1)}, bf16[128,512]{1,0:T(8,128)(2,1)S(1)}, u32[]{:S(2)}, u32[]{:S(2)}) collective-permute-start(bf16[128,512]{1,0:T(8,128)(2,1)S(1)} %get-tuple-element.42), channel_id=1, source_target_pairs={{0,1},{1,0},{2,3},{3,2},{4,5},{5,4},{6,7},{7,6},{8,9},{9,8},{10,11... | collective-permute-start | bytes 393224 | tf_op jit(solution)/shard_map/ppermute | solution.py:490
  13.8 6.3 %collective-permute-start.7 = (bf16[272,128]{1,0:T(8,128)(2,1)S(1)}, bf16[272,128]{1,0:T(8,128)(2,1)S(1)}, u32[]{:S(2)}, u32[]{:S(2)}) collective-permute-start(bf16[272,128]{1,0:T(8,128)(2,1)S(1)} %get-tuple-element.45), channel_id=1, source_target_pairs={{0,24},{1,25},{2,26},{3,27},{4,28},{5,29},{6,30},{7,31},{8,16},{9,... | collective-permute-start | bytes 208904 | tf_op jit(solution)/shard_map/ppermute | solution.py:490
  17.4 7.4 %collective-permute-start.8 = (bf16[272,128]{1,0:T(8,128)(2,1)S(1)}, bf16[272,128]{1,0:T(8,128)(2,1)S(1)}, u32[]{:S(2)}, u32[]{:S(2)}) collective-permute-start(bf16[272,128]{1,0:T(8,128)(2,1)S(1)} %get-tuple-element.46), channel_id=1, source_target_pairs={{0,22},{1,23},{2,20},{3,21},{4,18},{5,19},{6,16},{7,17},{8,30},{9,... | collective-permute-start | bytes 208904 | tf_op jit(solution)/shard_map/ppermute | solution.py:490
  18.7 6.8 %collective-permute-start.9 = (bf16[272,128]{1,0:T(8,128)(2,1)S(1)}, bf16[272,128]{1,0:T(8,128)(2,1)S(1)}, u32[]{:S(2)}, u32[]{:S(2)}) collective-permute-start(bf16[272,128]{1,0:T(8,128)(2,1)S(1)} %get-tuple-element.47), channel_id=1, source_target_pairs={{0,14},{1,15},{2,12},{3,13},{4,10},{5,11},{6,8},{7,9},{8,6},{9,7},... | collective-permute-start | bytes 208904 | tf_op jit(solution)/shard_map/ppermute | solution.py:490
  25.7 6.3 %collective-permute-start.10 = (bf16[272,128]{1,0:T(8,128)(2,1)S(1)}, bf16[272,128]{1,0:T(8,128)(2,1)S(1)}, u32[]{:S(2)}, u32[]{:S(2)}) collective-permute-start(bf16[272,128]{1,0:T(8,128)(2,1)S(1)} %get-tuple-element.50), channel_id=1, source_target_pairs={{0,24},{1,25},{2,26},{3,27},{4,28},{5,29},{6,30},{7,31},{8,16},{9,... | collective-permute-start | bytes 208904 | tf_op jit(solution)/shard_map/ppermute | solution.py:490
  28.3 7.8 %collective-permute-start.11 = (bf16[272,128]{1,0:T(8,128)(2,1)S(1)}, bf16[272,128]{1,0:T(8,128)(2,1)S(1)}, u32[]{:S(2)}, u32[]{:S(2)}) collective-permute-start(bf16[272,128]{1,0:T(8,128)(2,1)S(1)} %get-tuple-element.51), channel_id=1, source_target_pairs={{0,22},{1,23},{2,20},{3,21},{4,18},{5,19},{6,16},{7,17},{8,30},{9,... | collective-permute-start | bytes 208904 | tf_op jit(solution)/shard_map/ppermute | solution.py:490
  28.5 7.6 %collective-permute-start.12 = (bf16[272,128]{1,0:T(8,128)(2,1)S(1)}, bf16[272,128]{1,0:T(8,128)(2,1)S(1)}, u32[]{:S(2)}, u32[]{:S(2)}) collective-permute-start(bf16[272,128]{1,0:T(8,128)(2,1)S(1)} %get-tuple-element.52), channel_id=1, source_target_pairs={{0,14},{1,15},{2,12},{3,13},{4,10},{5,11},{6,8},{7,9},{8,6},{9,7},... | collective-permute-start | bytes 208904 | tf_op jit(solution)/shard_map/ppermute | solution.py:490
  39.9 8.0 %copy-start = (bf16[1,8,128,512]{3,2,1,0:T(8,128)(2,1)S(1)}, bf16[1,8,128,512]{3,2,1,0:T(8,128)(2,1)}, u32[]{:S(2)}) copy-start(bf16[1,8,128,512]{3,2,1,0:T(8,128)(2,1)} %param.3) | copy-start | bytes 3145732
  40.6 4.4 %collective-permute-start.16 = (bf16[128,512]{1,0:T(8,128)(2,1)S(1)}, bf16[128,512]{1,0:T(8,128)(2,1)S(1)}, u32[]{:S(2)}, u32[]{:S(2)}) collective-permute-start(bf16[128,512]{1,0:T(8,128)(2,1)S(1)} %get-tuple-element.57), channel_id=1, source_target_pairs={{3,0},{4,1},{1,2},{6,3},{7,4},{0,5},{5,6},{2,7},{11,8},{12,9},{9,1... | collective-permute-start | bytes 393224 | tf_op jit(solution)/shard_map/ppermute | solution.py:490
  40.6 5.5 %collective-permute-start.17 = (bf16[128,512]{1,0:T(8,128)(2,1)S(1)}, bf16[128,512]{1,0:T(8,128)(2,1)S(1)}, u32[]{:S(2)}, u32[]{:S(2)}) collective-permute-start(bf16[128,512]{1,0:T(8,128)(2,1)S(1)} %get-tuple-element.58), channel_id=1, source_target_pairs={{5,0},{8,1},{7,2},{10,3},{1,4},{12,5},{3,6},{14,7},{13,8},{0,9},{1... | collective-permute-start | bytes 393224 | tf_op jit(solution)/shard_map/ppermute | solution.py:490
  42.1 5.4 %collective-permute-start.18 = (bf16[128,512]{1,0:T(8,128)(2,1)S(1)}, bf16[128,512]{1,0:T(8,128)(2,1)S(1)}, u32[]{:S(2)}, u32[]{:S(2)}) collective-permute-start(bf16[128,512]{1,0:T(8,128)(2,1)S(1)} %get-tuple-element.59), channel_id=1, source_target_pairs={{9,0},{2,1},{11,2},{0,3},{13,4},{6,5},{15,6},{4,7},{1,8},{10,9},{3... | collective-permute-start | bytes 393224 | tf_op jit(solution)/shard_map/ppermute | solution.py:490
  42.4 5.5 %collective-permute-start.19 = (bf16[128,512]{1,0:T(8,128)(2,1)S(1)}, bf16[128,512]{1,0:T(8,128)(2,1)S(1)}, u32[]{:S(2)}, u32[]{:S(2)}) collective-permute-start(bf16[128,512]{1,0:T(8,128)(2,1)S(1)} %get-tuple-element.60), channel_id=1, source_target_pairs={{2,0},{5,1},{0,2},{7,3},{6,4},{1,5},{4,6},{3,7},{10,8},{13,9},{8,1... | collective-permute-start | bytes 393224 | tf_op jit(solution)/shard_map/ppermute | solution.py:490
  43.5 5.3 %collective-permute-start.13 = (bf16[128,512]{1,0:T(8,128)(2,1)S(1)}, bf16[128,512]{1,0:T(8,128)(2,1)S(1)}, u32[]{:S(2)}, u32[]{:S(2)}) collective-permute-start(bf16[128,512]{1,0:T(8,128)(2,1)S(1)} %get-tuple-element.53), channel_id=1, source_target_pairs={{4,0},{9,1},{6,2},{11,3},{0,4},{13,5},{2,6},{15,7},{12,8},{1,9},{1... | collective-permute-start | bytes 393224 | tf_op jit(solution)/shard_map/ppermute | solution.py:490
  45.0 5.2 %collective-permute-start.14 = (bf16[128,512]{1,0:T(8,128)(2,1)S(1)}, bf16[128,512]{1,0:T(8,128)(2,1)S(1)}, u32[]{:S(2)}, u32[]{:S(2)}) collective-permute-start(bf16[128,512]{1,0:T(8,128)(2,1)S(1)} %get-tuple-element.54), channel_id=1, source_target_pairs={{8,0},{3,1},{10,2},{1,3},{12,4},{7,5},{14,6},{5,7},{0,8},{11,9},{2... | collective-permute-start | bytes 393224 | tf_op jit(solution)/shard_map/ppermute | solution.py:490
  46.2 4.1 %collective-permute-start.15 = (bf16[128,512]{1,0:T(8,128)(2,1)S(1)}, bf16[128,512]{1,0:T(8,128)(2,1)S(1)}, u32[]{:S(2)}, u32[]{:S(2)}) collective-permute-start(bf16[128,512]{1,0:T(8,128)(2,1)S(1)} %get-tuple-element.55), channel_id=1, source_target_pairs={{1,0},{0,1},{3,2},{2,3},{5,4},{4,5},{7,6},{6,7},{9,8},{8,9},{11,10... | collective-permute-start | bytes 393224 | tf_op jit(solution)/shard_map/ppermute | solution.py:490

commit v8 on v7

--- a/solution.py
+++ b/solution.py
@@ -283,8 +283,8 @@
         first_row_ref[number] = value
 
 
-def gram_kernel(early_ref, early_row_ref, *refs):
-    block_refs, left_ref, direction_ref = refs[:-2], refs[-2], refs[-1]
+def gram_kernel(rest_count, early_ref, early_row_ref, *refs):
+    block_refs, left_ref, direction_ref, message_refs = refs[:-5], refs[-5], refs[-4], refs[-3:]
     order = block_refs[0].shape[1]
     packed, first_row = packed_gram(block_refs)
     direction = main_direction([early_row_ref[number] + value for number, value in enumerate(first_row)])
@@ -292,11 +292,7 @@
     outer = outer_products(stacked([direction]))
     for quarter, (value, known) in enumerate(zip(packed, pack(lambda i, j: outer[i, j], order))):
         left_ref[quarter] = early_ref[quarter] + (value - known)
-
-
-def reduce_kernel(rest_count, order, left_ref, direction_ref, *message_refs):
     place = Place(rest_count)
-    direction = direction_ref[...].astype(jnp.float32)[:1]
     for step, message_ref in enumerate(message_refs):
         message_ref[...] = to_message(left_ref[place.quarter_at(step)], order, direction)
 
@@ -335,17 +331,6 @@
     }
 
 
-def exact_square(upper, count):
-    high = rounded(upper, count)
-    low = rounded(
-        {key: value - value.astype(jnp.bfloat16).astype(jnp.float32) for key, value in upper.items()}, count
-    )
-    return combine(
-        (1.0, symmetric_product(high, high, count)),
-        (1.0, combine((1.0, symmetric_product(high, low, count)), (1.0, symmetric_product(low, high, count)))),
-    )
-
-
 def combine(*terms):
     return {
         key: functools.reduce(jnp.add, [value[key] if factor == 1.0 else factor * value[key] for factor, value in terms])
@@ -353,14 +338,40 @@
     }
 
 
+def square_beside_diagonal(upper, count):
+    shape = upper[0, 0].shape
+    identity = lax.broadcasted_iota(jnp.int32, shape, 0) == lax.broadcasted_iota(jnp.int32, shape, 1)
+    diagonals = [jnp.where(identity, upper[i, i], 0.0) for i in range(count)]
+    columns = [jnp.sum(value, axis=1, keepdims=True) for value in diagonals]
+    rows = [jnp.sum(value, axis=0, keepdims=True) for value in diagonals]
+    beside = {
+        (i, j): jnp.where(identity, 0.0, value) if i == j else value for (i, j), value in upper.items()
+    }
+    beside_high = rounded(beside, count)
+    entries = {(i, j): (columns[i] + rows[j]) * value for (i, j), value in beside.items()}
+    for i in range(count):
+        entries[i, i] = entries[i, i] + diagonals[i] * diagonals[i]
+    return combine((1.0, entries), (1.0, symmetric_product(beside_high, beside_high, count)))
+
+
 def newton(current, count):
     accum_identity, accum = 1.0, None
     for iteration in range(ITERS):
         last = iteration + 1 == ITERS
         current_high = None if last else rounded(current, count)
-        squared = exact_square(current, count) if last else symmetric_product(current_high, current_high, count)
+        if last:
+            squared = square_beside_diagonal(current, count)
+        else:
+            squared = symmetric_product(current_high, current_high, count)
         rest = combine((second_coef, current), (third_coef, squared))
         rest_high = rounded(rest, count)
+        if not last:
+            inner = symmetric_product(current_high, rest_high, count)
+            current = combine(
+                (first_coef * first_coef, current),
+                (2.0 * first_coef, inner),
+                (1.0, symmetric_product(rounded(inner, count), rest_high, count)),
+            )
         if accum is None:
             accum = rest
         else:
@@ -370,16 +381,12 @@
                 (1.0, symmetric_product(rounded(accum, count), rest_high, count)),
             )
         accum_identity *= first_coef
-        if not last:
-            inner = combine((first_coef, current), (1.0, symmetric_product(current_high, rest_high, count)))
-            current = combine(
-                (first_coef, inner), (1.0, symmetric_product(rounded(inner, count), rest_high, count))
-            )
     return accum_identity, accum
 
 
-def factor_kernel(rest_count, order, scale, left_ref, total_ref, directions_ref, *refs):
-    rest_refs, factor_ref, quarters_ref = refs[:3], refs[3], refs[4]
+def update_kernel(rest_count, order, scale, left_ref, total_ref, directions_ref, *refs):
+    rest_refs, quarters_ref = refs[:3], refs[-1]
+    block_refs, update_refs = refs[3 : 3 + len(refs[4:]) // 2], refs[3 + len(refs[4:]) // 2 : -1]
     place = Place(rest_count)
     quarters_ref[place.quarter] = total_ref[...]
     for step, rest_ref in enumerate(rest_refs):
@@ -414,21 +421,17 @@
     growth = jnp.sqrt(scale / (trace_sum + epsilon))
     shape = (WIDE, WIDE)
     identity = lax.broadcasted_iota(jnp.int32, shape, 0) == lax.broadcasted_iota(jnp.int32, shape, 1)
-    factor_ref[...] = rounded(
+    factor = rounded(
         {
             (i, j): (value + jnp.where(identity, accum_identity, 0.0) if i == j else value) * growth
             for (i, j), value in accum.items()
         },
         count,
     )
-
-
-def update_kernel(factor_ref, *refs):
-    block_refs, update_refs = refs[: len(refs) // 2], refs[len(refs) // 2 :]
-    update = product(jnp.concatenate([block_ref[...] for block_ref in block_refs], axis=0), factor_ref[...])
-    count = block_refs[0].shape[0]
+    update = product(jnp.concatenate([block_ref[...] for block_ref in block_refs], axis=0), factor)
+    row_count = block_refs[0].shape[0]
     for number, update_ref in enumerate(update_refs):
-        update_ref[...] = update[number * count : (number + 1) * count].astype(update_ref.dtype)
+        update_ref[...] = update[number * row_count : (number + 1) * row_count].astype(update_ref.dtype)
 
 
 def weights_kernel(rest_count, numbers, weights_ref, *refs):
@@ -505,8 +508,12 @@
     first_row = jax.ShapeDtypeStruct((order // BLOCK, BLOCK, BLOCK), jnp.float32)
     direction = jax.ShapeDtypeStruct((BF16_TILE, order), jnp.bfloat16)
     early = call(early_gram_kernel, (packed, first_row), *rows[:EARLY])
-    left, own_direction = call(gram_kernel, (packed, direction), *early, *rows[EARLY:])
-    parts = call(functools.partial(reduce_kernel, rest_count, order), (message,) * 3, left, own_direction)
+    left, own_direction, *parts = call(
+        functools.partial(gram_kernel, rest_count),
+        (packed, direction) + (message,) * 3,
+        *early,
+        *rows[EARLY:],
+    )
     total, directions, *rests = call(
         functools.partial(gather_kernel, rest_count, order),
         (quarter, direction) + (message,) * 3,
@@ -514,16 +521,16 @@
         own_direction,
         *swap(parts, OWNERS),
     )
-    factor = call(
-        functools.partial(factor_kernel, rest_count, order, scale),
-        jax.ShapeDtypeStruct((order, order), jnp.bfloat16),
+    own_update, *updates = call(
+        functools.partial(update_kernel, rest_count, order, scale),
+        blocks,
         left,
         total,
         directions,
         *swap(rests, OWNERS),
+        *rows,
         scratch=[pltpu.VMEM(packed.shape, packed.dtype)],
     )
-    own_update, *updates = call(update_kernel, blocks, factor, *rows)
     held = regroup(weights[0], 0, 1).reshape(by_block)
     returned = [own_update] + swap(updates, ROWS, back=True)
     numbers = range(len(blocks))

time: 51.2 us -> 50.5 us (0.986)
  Pallas kernels: 7.9 us -> 7.16 us
    pallas_call x7 -> x5, Pallas kernels: 6.12 us -> 5.39 us  [call(): pl.pallas_call(kernel, out_shape=out_shape, in_specs=[vmem] * len(operand...]
where the time goes in v8:
time: 50.5 us; the launch traced here: 50.4 us
  starting transfers between devices  26.7 us (53%)
  waiting for transfers between devices  15.2 us (30%)
  Pallas kernels  7.16 us (14%)
  local copies, waits for them, and re-layouts  1.23 us (2%)
    ppermute x20, starting transfers between devices, swap(): lax.ppermute(array, AXES, permute)  26.7 us
    ppermute x20, waiting for transfers between devices, swap(): lax.ppermute(array, AXES, permute)  15.2 us
    pallas_call x5, Pallas kernels, call(): pl.pallas_call(kernel, out_shape=out_shape, in_specs=[vmem] * len(operand...  5.39 us
    pallas_call x2, Pallas kernels, new_weights(): pl.pallas_call(functools.partial(weights_kernel, rest_count, numbers), ou...  1.77 us
    unnamed x4, local copies, waits for them, and re-layouts  1.23 us
  transfers between devices with their start and end apart: 20, of which 10 were waited for; matrix products, arithmetic and copies ran while one was open for 0% of the time, Pallas kernels for 3%

profile of v8, /device:TPU:0, one launch (start us, length us, event | category | flops | bytes accessed | tf_op | source)
XLA Modules:
  0.0 50.4 jit_solution(12437411333698026159)
XLA Ops:
  0.0 1.2 %copy-done.1 = bf16[1,8,128,512]{3,2,1,0:T(8,128)(2,1)S(1)} copy-done((bf16[1,8,128,512]{3,2,1,0:T(8,128)(2,1)S(1)}, bf16[1,8,128,512]{3,2,1,0:T(8,128)(2,1)}, u32[]{:S(2)}) %copy-start.1) | copy-done | bytes 1048600
  1.3 2.4 %collective-permute-start = (bf16[128,512]{1,0:T(8,128)(2,1)S(1)}, bf16[128,512]{1,0:T(8,128)(2,1)S(1)}, u32[]{:S(2)}, u32[]{:S(2)}) collective-permute-start(bf16[128,512]{1,0:T(8,128)(2,1)S(1)} %get-tuple-element.34), channel_id=1, source_target_pairs={{0,3},{1,4},{2,1},{3,6},{4,7},{5,0},{6,5},{7,2},{8,11},{9,12},{10,... | collective-permute-start | bytes 393224 | tf_op jit(solution)/shard_map/ppermute | solution.py:493
  3.8 1.8 %collective-permute-start.2 = (bf16[128,512]{1,0:T(8,128)(2,1)S(1)}, bf16[128,512]{1,0:T(8,128)(2,1)S(1)}, u32[]{:S(2)}, u32[]{:S(2)}) collective-permute-start(bf16[128,512]{1,0:T(8,128)(2,1)S(1)} %get-tuple-element.36), channel_id=1, source_target_pairs={{0,9},{1,2},{2,11},{3,0},{4,13},{5,6},{6,15},{7,4},{8,1},{9,10},{1... | collective-permute-start | bytes 393224 | tf_op jit(solution)/shard_map/ppermute | solution.py:493
  5.6 1.5 %collective-permute-start.3 = (bf16[128,512]{1,0:T(8,128)(2,1)S(1)}, bf16[128,512]{1,0:T(8,128)(2,1)S(1)}, u32[]{:S(2)}, u32[]{:S(2)}) collective-permute-start(bf16[128,512]{1,0:T(8,128)(2,1)S(1)} %get-tuple-element.37), channel_id=1, source_target_pairs={{0,2},{1,5},{2,0},{3,7},{4,6},{5,1},{6,4},{7,3},{8,10},{9,13},{10,... | collective-permute-start | bytes 393224 | tf_op jit(solution)/shard_map/ppermute | solution.py:493
  7.1 0.5 %collective-permute-start.4 = (bf16[128,512]{1,0:T(8,128)(2,1)S(1)}, bf16[128,512]{1,0:T(8,128)(2,1)S(1)}, u32[]{:S(2)}, u32[]{:S(2)}) collective-permute-start(bf16[128,512]{1,0:T(8,128)(2,1)S(1)} %get-tuple-element.40), channel_id=1, source_target_pairs={{0,4},{1,9},{2,6},{3,11},{4,0},{5,13},{6,2},{7,15},{8,12},{9,1},{1... | collective-permute-start | bytes 393224 | tf_op jit(solution)/shard_map/ppermute | solution.py:493
  7.6 1.6 %collective-permute-start.5 = (bf16[128,512]{1,0:T(8,128)(2,1)S(1)}, bf16[128,512]{1,0:T(8,128)(2,1)S(1)}, u32[]{:S(2)}, u32[]{:S(2)}) collective-permute-start(bf16[128,512]{1,0:T(8,128)(2,1)S(1)} %get-tuple-element.41), channel_id=1, source_target_pairs={{0,8},{1,3},{2,10},{3,1},{4,12},{5,7},{6,14},{7,5},{8,0},{9,11},{1... | collective-permute-start | bytes 393224 | tf_op jit(solution)/shard_map/ppermute | solution.py:493
  9.4 1.2 %collective-permute-done.3.refs_4_.refs_7_ = bf16[128,512]{1,0:T(8,128)(2,1)S(1)} collective-permute-done((bf16[128,512]{1,0:T(8,128)(2,1)S(1)}, bf16[128,512]{1,0:T(8,128)(2,1)S(1)}, u32[]{:S(2)}, u32[]{:S(2)}) %collective-permute-start.3) | collective-permute-done | bytes 131104 | tf_op jit(solution)/shard_map/ppermute | solution.py:493
  10.6 0.5 %shard_map.29 = (f32[4,264,128]{2,1,0:T(8,128)S(1)}, f32[4,128,128]{2,1,0:T(8,128)S(1)}) custom-call(bf16[128,512]{1,0:T(8,128)(2,1)S(1)} %get-tuple-element.33.refs_0_.refs_3_, bf16[128,512]{1,0:T(8,128)(2,1)S(1)} %collective-permute-done.refs_1_.refs_4_, bf16[128,512]{1,0:T(8,128)(2,1)S(1)} %collective-permute-done.1.refs_2_.refs_5_, ...), custom_call_target="tpu_custom_call" | custom-call | tf_op jit(solution)/shard_map/pallas_call | solution.py:92
  11.1 1.0 %collective-permute-done.4.refs_0_.refs_8_ = bf16[128,512]{1,0:T(8,128)(2,1)S(1)} collective-permute-done((bf16[128,512]{1,0:T(8,128)(2,1)S(1)}, bf16[128,512]{1,0:T(8,128)(2,1)S(1)}, u32[]{:S(2)}, u32[]{:S(2)}) %collective-permute-start.4) | collective-permute-done | bytes 131104 | tf_op jit(solution)/shard_map/ppermute | solution.py:493
  12.1 0.7 %collective-permute-done.5.refs_1_.refs_9_ = bf16[128,512]{1,0:T(8,128)(2,1)S(1)} collective-permute-done((bf16[128,512]{1,0:T(8,128)(2,1)S(1)}, bf16[128,512]{1,0:T(8,128)(2,1)S(1)}, u32[]{:S(2)}, u32[]{:S(2)}) %collective-permute-start.5) | collective-permute-done | bytes 131104 | tf_op jit(solution)/shard_map/ppermute | solution.py:493
  12.8 0.9 %shard_map.30 = (f32[4,264,128]{2,1,0:T(8,128)S(1)}, bf16[16,512]{1,0:T(8,128)(2,1)S(1)}, bf16[272,128]{1,0:T(8,128)(2,1)S(1)}, bf16[272,128]{1,0:T(8,128)(2,1)S(1)}, bf16[272,128]{1,0:T(8,128)(2,1)S(1)}) custom-call(f32[4,264,128]{2,1,0:T(8,128)S(1)} %get-tuple-element.38.early_ref, f32[4,128,128]{2,1,0:T(8,128)S(1)} %get-tuple-element.39.early_row_ref, ...), custom_call_target="tpu_custom_call" | custom-call | tf_op jit(solution)/shard_map/pallas_call | solution.py:92
  13.7 3.7 %collective-permute-start.7 = (bf16[272,128]{1,0:T(8,128)(2,1)S(1)}, bf16[272,128]{1,0:T(8,128)(2,1)S(1)}, u32[]{:S(2)}, u32[]{:S(2)}) collective-permute-start(bf16[272,128]{1,0:T(8,128)(2,1)S(1)} %get-tuple-element.45), channel_id=1, source_target_pairs={{0,24},{1,25},{2,26},{3,27},{4,28},{5,29},{6,30},{7,31},{8,16},{9,... | collective-permute-start | bytes 208904 | tf_op jit(solution)/shard_map/ppermute | solution.py:493
  17.4 1.3 %collective-permute-start.8 = (bf16[272,128]{1,0:T(8,128)(2,1)S(1)}, bf16[272,128]{1,0:T(8,128)(2,1)S(1)}, u32[]{:S(2)}, u32[]{:S(2)}) collective-permute-start(bf16[272,128]{1,0:T(8,128)(2,1)S(1)} %get-tuple-element.46), channel_id=1, source_target_pairs={{0,22},{1,23},{2,20},{3,21},{4,18},{5,19},{6,16},{7,17},{8,30},{9,... | collective-permute-start | bytes 208904 | tf_op jit(solution)/shard_map/ppermute | solution.py:493
  18.7 1.3 %collective-permute-start.9 = (bf16[272,128]{1,0:T(8,128)(2,1)S(1)}, bf16[272,128]{1,0:T(8,128)(2,1)S(1)}, u32[]{:S(2)}, u32[]{:S(2)}) collective-permute-start(bf16[272,128]{1,0:T(8,128)(2,1)S(1)} %get-tuple-element.47), channel_id=1, source_target_pairs={{0,14},{1,15},{2,12},{3,13},{4,10},{5,11},{6,8},{7,9},{8,6},{9,7},... | collective-permute-start | bytes 208904 | tf_op jit(solution)/shard_map/ppermute | solution.py:493
  20.0 4.8 %collective-permute-done.8.refs_1_ = bf16[272,128]{1,0:T(8,128)(2,1)S(1)} collective-permute-done((bf16[272,128]{1,0:T(8,128)(2,1)S(1)}, bf16[272,128]{1,0:T(8,128)(2,1)S(1)}, u32[]{:S(2)}, u32[]{:S(2)}) %collective-permute-start.8) | collective-permute-done | bytes 69664 | tf_op jit(solution)/shard_map/ppermute | solution.py:493
  24.8 0.7 %collective-permute-done.9.refs_2_ = bf16[272,128]{1,0:T(8,128)(2,1)S(1)} collective-permute-done((bf16[272,128]{1,0:T(8,128)(2,1)S(1)}, bf16[272,128]{1,0:T(8,128)(2,1)S(1)}, u32[]{:S(2)}, u32[]{:S(2)}) %collective-permute-start.9) | collective-permute-done | bytes 69664 | tf_op jit(solution)/shard_map/ppermute | solution.py:493
  25.7 2.7 %collective-permute-start.10 = (bf16[272,128]{1,0:T(8,128)(2,1)S(1)}, bf16[272,128]{1,0:T(8,128)(2,1)S(1)}, u32[]{:S(2)}, u32[]{:S(2)}) collective-permute-start(bf16[272,128]{1,0:T(8,128)(2,1)S(1)} %get-tuple-element.50), channel_id=1, source_target_pairs={{0,24},{1,25},{2,26},{3,27},{4,28},{5,29},{6,30},{7,31},{8,16},{9,... | collective-permute-start | bytes 208904 | tf_op jit(solution)/shard_map/ppermute | solution.py:493
  28.5 3.4 %collective-permute-start.12 = (bf16[272,128]{1,0:T(8,128)(2,1)S(1)}, bf16[272,128]{1,0:T(8,128)(2,1)S(1)}, u32[]{:S(2)}, u32[]{:S(2)}) collective-permute-start(bf16[272,128]{1,0:T(8,128)(2,1)S(1)} %get-tuple-element.52), channel_id=1, source_target_pairs={{0,14},{1,15},{2,12},{3,13},{4,10},{5,11},{6,8},{7,9},{8,6},{9,7},... | collective-permute-start | bytes 208904 | tf_op jit(solution)/shard_map/ppermute | solution.py:493
  31.9 4.2 %collective-permute-done.11.refs_1_ = bf16[272,128]{1,0:T(8,128)(2,1)S(1)} collective-permute-done((bf16[272,128]{1,0:T(8,128)(2,1)S(1)}, bf16[272,128]{1,0:T(8,128)(2,1)S(1)}, u32[]{:S(2)}, u32[]{:S(2)}) %collective-permute-start.11) | collective-permute-done | bytes 69664 | tf_op jit(solution)/shard_map/ppermute | solution.py:493
  36.1 3.7 %shard_map.32 = (bf16[128,512]{1,0:T(8,128)(2,1)S(1)}, bf16[128,512]{1,0:T(8,128)(2,1)S(1)}, bf16[128,512]{1,0:T(8,128)(2,1)S(1)}, bf16[128,512]{1,0:T(8,128)(2,...) custom-call(f32[4,264,128]{2,1,0:T(8,128)S(1)} %get-tuple-element.43, ...), custom_call_target="tpu_custom_call" | custom-call | tf_op jit(solution)/shard_map/pallas_call | solution.py:92
  39.9 1.4 %collective-permute-start.17 = (bf16[128,512]{1,0:T(8,128)(2,1)S(1)}, bf16[128,512]{1,0:T(8,128)(2,1)S(1)}, u32[]{:S(2)}, u32[]{:S(2)}) collective-permute-start(bf16[128,512]{1,0:T(8,128)(2,1)S(1)} %get-tuple-element.58), channel_id=1, source_target_pairs={{5,0},{8,1},{7,2},{10,3},{1,4},{12,5},{3,6},{14,7},{13,8},{0,9},{1... | collective-permute-start | bytes 393224 | tf_op jit(solution)/shard_map/ppermute | solution.py:493
  41.4 0.3 collective-permute-start.18
  41.6 1.1 %collective-permute-start.19 = (bf16[128,512]{1,0:T(8,128)(2,1)S(1)}, bf16[128,512]{1,0:T(8,128)(2,1)S(1)}, u32[]{:S(2)}, u32[]{:S(2)}) collective-permute-start(bf16[128,512]{1,0:T(8,128)(2,1)S(1)} %get-tuple-element.60), channel_id=1, source_target_pairs={{2,0},{5,1},{0,2},{7,3},{6,4},{1,5},{4,6},{3,7},{10,8},{13,9},{8,1... | collective-permute-start | bytes 393224 | tf_op jit(solution)/shard_map/ppermute | solution.py:493
  42.8 1.1 %collective-permute-start.13 = (bf16[128,512]{1,0:T(8,128)(2,1)S(1)}, bf16[128,512]{1,0:T(8,128)(2,1)S(1)}, u32[]{:S(2)}, u32[]{:S(2)}) collective-permute-start(bf16[128,512]{1,0:T(8,128)(2,1)S(1)} %get-tuple-element.53), channel_id=1, source_target_pairs={{4,0},{9,1},{6,2},{11,3},{0,4},{13,5},{2,6},{15,7},{12,8},{1,9},{1... | collective-permute-start | bytes 393224 | tf_op jit(solution)/shard_map/ppermute | solution.py:493
  43.8 0.5 collective-permute-done.16.refs_1_
  44.3 1.1 %collective-permute-start.14 = (bf16[128,512]{1,0:T(8,128)(2,1)S(1)}, bf16[128,512]{1,0:T(8,128)(2,1)S(1)}, u32[]{:S(2)}, u32[]{:S(2)}) collective-permute-start(bf16[128,512]{1,0:T(8,128)(2,1)S(1)} %get-tuple-element.54), channel_id=1, source_target_pairs={{8,0},{3,1},{10,2},{1,3},{12,4},{7,5},{14,6},{5,7},{0,8},{11,9},{2... | collective-permute-start | bytes 393224 | tf_op jit(solution)/shard_map/ppermute | solution.py:493
  45.4 1.0 %collective-permute-start.15 = (bf16[128,512]{1,0:T(8,128)(2,1)S(1)}, bf16[128,512]{1,0:T(8,128)(2,1)S(1)}, u32[]{:S(2)}, u32[]{:S(2)}) collective-permute-start(bf16[128,512]{1,0:T(8,128)(2,1)S(1)} %get-tuple-element.55), channel_id=1, source_target_pairs={{1,0},{0,1},{3,2},{2,3},{5,4},{4,5},{7,6},{6,7},{9,8},{8,9},{11,10... | collective-permute-start | bytes 393224 | tf_op jit(solution)/shard_map/ppermute | solution.py:493
  46.5 0.3 collective-permute-done.18.refs_3_
  46.7 0.4 collective-permute-done.19.refs_4_
  47.1 0.9 %shard_map.33.refs_3_ = bf16[4,2,128,512]{3,2,1,0:T(8,128)(2,1)} custom-call(bf16[4,2,128,512]{3,2,1,0:T(8,128)(2,1)S(1)} %bitcast.3, bf16[128,512]{1,0:T(8,128)(2,1)S(1)} %get-tuple-element.56.refs_0_, bf16[128,512]{1,0:T(8,128)(2,1)S(1)} %collective-permute-done.16.refs_1_, bf16[128,512]{1,0:T(8,128)(2,1)S(1)} %collective-permute-done.17.refs_2_, ...), custom_call_target="tpu_custom_call" | custom-call | tf_op jit(solution)/shard_map/pallas_call | solution.py:456
  48.1 1.4 %collective-permute-done.14.refs_1_ = bf16[128,512]{1,0:T(8,128)(2,1)S(1)} collective-permute-done((bf16[128,512]{1,0:T(8,128)(2,1)S(1)}, bf16[128,512]{1,0:T(8,128)(2,1)S(1)}, u32[]{:S(2)}, u32[]{:S(2)}) %collective-permute-start.14) | collective-permute-done | bytes 131104 | tf_op jit(solution)/shard_map/ppermute | solution.py:493
  49.5 0.8 %shard_map.34 = bf16[4,2,128,512]{3,2,1,0:T(8,128)(2,1)} custom-call(bf16[4,2,128,512]{3,2,1,0:T(8,128)(2,1)S(1)} %bitcast.4, bf16[128,512]{1,0:T(8,128)(2,1)S(1)} %collective-permute-done.13.refs_0_, bf16[128,512]{1,0:T(8,128)(2,1)S(1)} %collective-permute-done.14.refs_1_, ...), custom_call_target="tpu_custom_call", output_to_operand_aliasing={{}: (4, {})} | custom-call | tf_op jit(solution)/shard_map/pallas_call | solution.py:456
  (19 shorter events, 0.7 us)
Async XLA Ops:
  0.0 1.2 %copy-start.1 = (bf16[1,8,128,512]{3,2,1,0:T(8,128)(2,1)S(1)}, bf16[1,8,128,512]{3,2,1,0:T(8,128)(2,1)}, u32[]{:S(2)}) copy-start(bf16[1,8,128,512]{3,2,1,0:T(8,128)(2,1)} %param.2) | copy-start | bytes 3145732
  1.3 6.3 %collective-permute-start = (bf16[128,512]{1,0:T(8,128)(2,1)S(1)}, bf16[128,512]{1,0:T(8,128)(2,1)S(1)}, u32[]{:S(2)}, u32[]{:S(2)}) collective-permute-start(bf16[128,512]{1,0:T(8,128)(2,1)S(1)} %get-tuple-element.34), channel_id=1, source_target_pairs={{0,3},{1,4},{2,1},{3,6},{4,7},{5,0},{6,5},{7,2},{8,11},{9,12},{10,... | collective-permute-start | bytes 393224 | tf_op jit(solution)/shard_map/ppermute | solution.py:493
  3.7 5.5 %collective-permute-start.1 = (bf16[128,512]{1,0:T(8,128)(2,1)S(1)}, bf16[128,512]{1,0:T(8,128)(2,1)S(1)}, u32[]{:S(2)}, u32[]{:S(2)}) collective-permute-start(bf16[128,512]{1,0:T(8,128)(2,1)S(1)} %get-tuple-element.35), channel_id=1, source_target_pairs={{0,5},{1,8},{2,7},{3,10},{4,1},{5,12},{6,3},{7,14},{8,13},{9,0},{1... | collective-permute-start | bytes 393224 | tf_op jit(solution)/shard_map/ppermute | solution.py:493
  3.8 5.5 %collective-permute-start.2 = (bf16[128,512]{1,0:T(8,128)(2,1)S(1)}, bf16[128,512]{1,0:T(8,128)(2,1)S(1)}, u32[]{:S(2)}, u32[]{:S(2)}) collective-permute-start(bf16[128,512]{1,0:T(8,128)(2,1)S(1)} %get-tuple-element.36), channel_id=1, source_target_pairs={{0,9},{1,2},{2,11},{3,0},{4,13},{5,6},{6,15},{7,4},{8,1},{9,10},{1... | collective-permute-start | bytes 393224 | tf_op jit(solution)/shard_map/ppermute | solution.py:493
  5.6 5.0 %collective-permute-start.3 = (bf16[128,512]{1,0:T(8,128)(2,1)S(1)}, bf16[128,512]{1,0:T(8,128)(2,1)S(1)}, u32[]{:S(2)}, u32[]{:S(2)}) collective-permute-start(bf16[128,512]{1,0:T(8,128)(2,1)S(1)} %get-tuple-element.37), channel_id=1, source_target_pairs={{0,2},{1,5},{2,0},{3,7},{4,6},{5,1},{6,4},{7,3},{8,10},{9,13},{10,... | collective-permute-start | bytes 393224 | tf_op jit(solution)/shard_map/ppermute | solution.py:493
  7.1 5.0 %collective-permute-start.4 = (bf16[128,512]{1,0:T(8,128)(2,1)S(1)}, bf16[128,512]{1,0:T(8,128)(2,1)S(1)}, u32[]{:S(2)}, u32[]{:S(2)}) collective-permute-start(bf16[128,512]{1,0:T(8,128)(2,1)S(1)} %get-tuple-element.40), channel_id=1, source_target_pairs={{0,4},{1,9},{2,6},{3,11},{4,0},{5,13},{6,2},{7,15},{8,12},{9,1},{1... | collective-permute-start | bytes 393224 | tf_op jit(solution)/shard_map/ppermute | solution.py:493
  7.6 5.2 %collective-permute-start.5 = (bf16[128,512]{1,0:T(8,128)(2,1)S(1)}, bf16[128,512]{1,0:T(8,128)(2,1)S(1)}, u32[]{:S(2)}, u32[]{:S(2)}) collective-permute-start(bf16[128,512]{1,0:T(8,128)(2,1)S(1)} %get-tuple-element.41), channel_id=1, source_target_pairs={{0,8},{1,3},{2,10},{3,1},{4,12},{5,7},{6,14},{7,5},{8,0},{9,11},{1... | collective-permute-start | bytes 393224 | tf_op jit(solution)/shard_map/ppermute | solution.py:493
  9.2 3.6 %collective-permute-start.6 = (bf16[128,512]{1,0:T(8,128)(2,1)S(1)}, bf16[128,512]{1,0:T(8,128)(2,1)S(1)}, u32[]{:S(2)}, u32[]{:S(2)}) collective-permute-start(bf16[128,512]{1,0:T(8,128)(2,1)S(1)} %get-tuple-element.42), channel_id=1, source_target_pairs={{0,1},{1,0},{2,3},{3,2},{4,5},{5,4},{6,7},{7,6},{8,9},{9,8},{10,11... | collective-permute-start | bytes 393224 | tf_op jit(solution)/shard_map/ppermute | solution.py:493
  13.7 6.3 %collective-permute-start.7 = (bf16[272,128]{1,0:T(8,128)(2,1)S(1)}, bf16[272,128]{1,0:T(8,128)(2,1)S(1)}, u32[]{:S(2)}, u32[]{:S(2)}) collective-permute-start(bf16[272,128]{1,0:T(8,128)(2,1)S(1)} %get-tuple-element.45), channel_id=1, source_target_pairs={{0,24},{1,25},{2,26},{3,27},{4,28},{5,29},{6,30},{7,31},{8,16},{9,... | collective-permute-start | bytes 208904 | tf_op jit(solution)/shard_map/ppermute | solution.py:493
  17.4 7.4 %collective-permute-start.8 = (bf16[272,128]{1,0:T(8,128)(2,1)S(1)}, bf16[272,128]{1,0:T(8,128)(2,1)S(1)}, u32[]{:S(2)}, u32[]{:S(2)}) collective-permute-start(bf16[272,128]{1,0:T(8,128)(2,1)S(1)} %get-tuple-element.46), channel_id=1, source_target_pairs={{0,22},{1,23},{2,20},{3,21},{4,18},{5,19},{6,16},{7,17},{8,30},{9,... | collective-permute-start | bytes 208904 | tf_op jit(solution)/shard_map/ppermute | solution.py:493
  18.7 6.8 %collective-permute-start.9 = (bf16[272,128]{1,0:T(8,128)(2,1)S(1)}, bf16[272,128]{1,0:T(8,128)(2,1)S(1)}, u32[]{:S(2)}, u32[]{:S(2)}) collective-permute-start(bf16[272,128]{1,0:T(8,128)(2,1)S(1)} %get-tuple-element.47), channel_id=1, source_target_pairs={{0,14},{1,15},{2,12},{3,13},{4,10},{5,11},{6,8},{7,9},{8,6},{9,7},... | collective-permute-start | bytes 208904 | tf_op jit(solution)/shard_map/ppermute | solution.py:493
  25.6 21.5 %copy-start = (bf16[1,8,128,512]{3,2,1,0:T(8,128)(2,1)S(1)}, bf16[1,8,128,512]{3,2,1,0:T(8,128)(2,1)}, u32[]{:S(2)}) copy-start(bf16[1,8,128,512]{3,2,1,0:T(8,128)(2,1)} %param.3) | copy-start | bytes 3145732
  25.7 6.3 %collective-permute-start.10 = (bf16[272,128]{1,0:T(8,128)(2,1)S(1)}, bf16[272,128]{1,0:T(8,128)(2,1)S(1)}, u32[]{:S(2)}, u32[]{:S(2)}) collective-permute-start(bf16[272,128]{1,0:T(8,128)(2,1)S(1)} %get-tuple-element.50), channel_id=1, source_target_pairs={{0,24},{1,25},{2,26},{3,27},{4,28},{5,29},{6,30},{7,31},{8,16},{9,... | collective-permute-start | bytes 208904 | tf_op jit(solution)/shard_map/ppermute | solution.py:493
  28.3 7.8 %collective-permute-start.11 = (bf16[272,128]{1,0:T(8,128)(2,1)S(1)}, bf16[272,128]{1,0:T(8,128)(2,1)S(1)}, u32[]{:S(2)}, u32[]{:S(2)}) collective-permute-start(bf16[272,128]{1,0:T(8,128)(2,1)S(1)} %get-tuple-element.51), channel_id=1, source_target_pairs={{0,22},{1,23},{2,20},{3,21},{4,18},{5,19},{6,16},{7,17},{8,30},{9,... | collective-permute-start | bytes 208904 | tf_op jit(solution)/shard_map/ppermute | solution.py:493
  28.5 7.6 %collective-permute-start.12 = (bf16[272,128]{1,0:T(8,128)(2,1)S(1)}, bf16[272,128]{1,0:T(8,128)(2,1)S(1)}, u32[]{:S(2)}, u32[]{:S(2)}) collective-permute-start(bf16[272,128]{1,0:T(8,128)(2,1)S(1)} %get-tuple-element.52), channel_id=1, source_target_pairs={{0,14},{1,15},{2,12},{3,13},{4,10},{5,11},{6,8},{7,9},{8,6},{9,7},... | collective-permute-start | bytes 208904 | tf_op jit(solution)/shard_map/ppermute | solution.py:493
  39.8 4.4 %collective-permute-start.16 = (bf16[128,512]{1,0:T(8,128)(2,1)S(1)}, bf16[128,512]{1,0:T(8,128)(2,1)S(1)}, u32[]{:S(2)}, u32[]{:S(2)}) collective-permute-start(bf16[128,512]{1,0:T(8,128)(2,1)S(1)} %get-tuple-element.57), channel_id=1, source_target_pairs={{3,0},{4,1},{1,2},{6,3},{7,4},{0,5},{5,6},{2,7},{11,8},{12,9},{9,1... | collective-permute-start | bytes 393224 | tf_op jit(solution)/shard_map/ppermute | solution.py:493
  39.9 5.5 %collective-permute-start.17 = (bf16[128,512]{1,0:T(8,128)(2,1)S(1)}, bf16[128,512]{1,0:T(8,128)(2,1)S(1)}, u32[]{:S(2)}, u32[]{:S(2)}) collective-permute-start(bf16[128,512]{1,0:T(8,128)(2,1)S(1)} %get-tuple-element.58), channel_id=1, source_target_pairs={{5,0},{8,1},{7,2},{10,3},{1,4},{12,5},{3,6},{14,7},{13,8},{0,9},{1... | collective-permute-start | bytes 393224 | tf_op jit(solution)/shard_map/ppermute | solution.py:493
  41.4 5.3 %collective-permute-start.18 = (bf16[128,512]{1,0:T(8,128)(2,1)S(1)}, bf16[128,512]{1,0:T(8,128)(2,1)S(1)}, u32[]{:S(2)}, u32[]{:S(2)}) collective-permute-start(bf16[128,512]{1,0:T(8,128)(2,1)S(1)} %get-tuple-element.59), channel_id=1, source_target_pairs={{9,0},{2,1},{11,2},{0,3},{13,4},{6,5},{15,6},{4,7},{1,8},{10,9},{3... | collective-permute-start | bytes 393224 | tf_op jit(solution)/shard_map/ppermute | solution.py:493
  41.6 5.5 %collective-permute-start.19 = (bf16[128,512]{1,0:T(8,128)(2,1)S(1)}, bf16[128,512]{1,0:T(8,128)(2,1)S(1)}, u32[]{:S(2)}, u32[]{:S(2)}) collective-permute-start(bf16[128,512]{1,0:T(8,128)(2,1)S(1)} %get-tuple-element.60), channel_id=1, source_target_pairs={{2,0},{5,1},{0,2},{7,3},{6,4},{1,5},{4,6},{3,7},{10,8},{13,9},{8,1... | collective-permute-start | bytes 393224 | tf_op jit(solution)/shard_map/ppermute | solution.py:493
  42.8 5.3 %collective-permute-start.13 = (bf16[128,512]{1,0:T(8,128)(2,1)S(1)}, bf16[128,512]{1,0:T(8,128)(2,1)S(1)}, u32[]{:S(2)}, u32[]{:S(2)}) collective-permute-start(bf16[128,512]{1,0:T(8,128)(2,1)S(1)} %get-tuple-element.53), channel_id=1, source_target_pairs={{4,0},{9,1},{6,2},{11,3},{0,4},{13,5},{2,6},{15,7},{12,8},{1,9},{1... | collective-permute-start | bytes 393224 | tf_op jit(solution)/shard_map/ppermute | solution.py:493
  44.3 5.2 %collective-permute-start.14 = (bf16[128,512]{1,0:T(8,128)(2,1)S(1)}, bf16[128,512]{1,0:T(8,128)(2,1)S(1)}, u32[]{:S(2)}, u32[]{:S(2)}) collective-permute-start(bf16[128,512]{1,0:T(8,128)(2,1)S(1)} %get-tuple-element.54), channel_id=1, source_target_pairs={{8,0},{3,1},{10,2},{1,3},{12,4},{7,5},{14,6},{5,7},{0,8},{11,9},{2... | collective-permute-start | bytes 393224 | tf_op jit(solution)/shard_map/ppermute | solution.py:493
  45.4 4.1 %collective-permute-start.15 = (bf16[128,512]{1,0:T(8,128)(2,1)S(1)}, bf16[128,512]{1,0:T(8,128)(2,1)S(1)}, u32[]{:S(2)}, u32[]{:S(2)}) collective-permute-start(bf16[128,512]{1,0:T(8,128)(2,1)S(1)} %get-tuple-element.55), channel_id=1, source_target_pairs={{1,0},{0,1},{3,2},{2,3},{5,4},{4,5},{7,6},{6,7},{9,8},{8,9},{11,10... | collective-permute-start | bytes 393224 | tf_op jit(solution)/shard_map/ppermute | solution.py:493

commit v9 on v8

--- a/solution.py
+++ b/solution.py
@@ -32,13 +32,14 @@
 
 
 def neighbour_steps():
-    ways = [(0, 0, 1), (0, 1, 0), (1, 0, 0)]
-    order = [(ways[step], ways[(step + 1) % 3]) for step in range(3)]
+    x, y, z = (0, 0, 1), (0, 1, 0), (1, 0, 0)
+    order = [(x, y), (z, x), (y, z)]
     return [tuple(flips_of(*way, pair=cross) for way in step) for cross in (1, 0) for step in order]
 
 
 ROWS = neighbour_steps() + [(flips_of(0, 0, 0, pair=1),) * 2]
-OWNERS = [(flips,) * 2 for flips in (flips_of(1, 0, 0, half=1), flips_of(0, 1, 1, half=1), flips_of(1, 1, 1))]
+BOTH, ANTIPODE, MIRROR = flips_of(0, 1, 1, half=1), flips_of(1, 1, 1), flips_of(1, 0, 0, half=1)
+OWNERS = [(flips,) * 2 for flips in (BOTH, ANTIPODE, MIRROR)]
 
 
 def colour_step(flips):

time: 50.5 us -> 50.2 us (level)
  starting transfers between devices: 26.7 us -> 25.9 us
    ppermute x20, starting transfers between devices: 26.7 us -> 25.9 us  [swap(): lax.ppermute(array, AXES, permute)]
  transfers between devices with their start and end apart: 20 -> 20, of which waited for: 10 -> 15; matrix products, arithmetic and copies ran while one was open for 0% -> 0% of each run, Pallas kernels for 3% -> 3%
where the time goes in v9:
time: 50.2 us; the launch traced here: 50 us
  starting transfers between devices  25.9 us (52%)
  waiting for transfers between devices  15.7 us (31%)
  Pallas kernels  7.16 us (14%)
  local copies, waits for them, and re-layouts  1.23 us (2%)
    ppermute x20, starting transfers between devices, swap(): lax.ppermute(array, AXES, permute)  25.9 us
    ppermute x20, waiting for transfers between devices, swap(): lax.ppermute(array, AXES, permute)  15.7 us
    pallas_call x5, Pallas kernels, call(): pl.pallas_call(kernel, out_shape=out_shape, in_specs=[vmem] * len(operand...  5.38 us
    pallas_call x2, Pallas kernels, new_weights(): pl.pallas_call(functools.partial(weights_kernel, rest_count, numbers), ou...  1.77 us
    unnamed x4, local copies, waits for them, and re-layouts  1.23 us
  transfers between devices with their start and end apart: 20, of which 15 were waited for; matrix products, arithmetic and copies ran while one was open for 0% of the time, Pallas kernels for 3%

profile of v9, /device:TPU:0, one launch (start us, length us, event | category | flops | bytes accessed | tf_op | source)
XLA Modules:
  0.0 50.0 jit_solution(1085550885126527291)
XLA Ops:
  0.0 1.2 %copy-done.1 = bf16[1,8,128,512]{3,2,1,0:T(8,128)(2,1)S(1)} copy-done((bf16[1,8,128,512]{3,2,1,0:T(8,128)(2,1)S(1)}, bf16[1,8,128,512]{3,2,1,0:T(8,128)(2,1)}, u32[]{:S(2)}) %copy-start.1) | copy-done | bytes 1048600
  1.3 2.4 %collective-permute-start = (bf16[128,512]{1,0:T(8,128)(2,1)S(1)}, bf16[128,512]{1,0:T(8,128)(2,1)S(1)}, u32[]{:S(2)}, u32[]{:S(2)}) collective-permute-start(bf16[128,512]{1,0:T(8,128)(2,1)S(1)} %get-tuple-element.34), channel_id=1, source_target_pairs={{0,3},{1,4},{2,1},{3,6},{4,7},{5,0},{6,5},{7,2},{8,11},{9,12},{10,... | collective-permute-start | bytes 393224 | tf_op jit(solution)/shard_map/ppermute | solution.py:494
  3.7 1.9 %collective-permute-start.1 = (bf16[128,512]{1,0:T(8,128)(2,1)S(1)}, bf16[128,512]{1,0:T(8,128)(2,1)S(1)}, u32[]{:S(2)}, u32[]{:S(2)}) collective-permute-start(bf16[128,512]{1,0:T(8,128)(2,1)S(1)} %get-tuple-element.35), channel_id=1, source_target_pairs={{0,9},{1,2},{2,11},{3,0},{4,13},{5,6},{6,15},{7,4},{8,1},{9,10},{1... | collective-permute-start | bytes 393224 | tf_op jit(solution)/shard_map/ppermute | solution.py:494
  5.6 1.5 %collective-permute-start.3 = (bf16[128,512]{1,0:T(8,128)(2,1)S(1)}, bf16[128,512]{1,0:T(8,128)(2,1)S(1)}, u32[]{:S(2)}, u32[]{:S(2)}) collective-permute-start(bf16[128,512]{1,0:T(8,128)(2,1)S(1)} %get-tuple-element.37), channel_id=1, source_target_pairs={{0,2},{1,5},{2,0},{3,7},{4,6},{5,1},{6,4},{7,3},{8,10},{9,13},{10,... | collective-permute-start | bytes 393224 | tf_op jit(solution)/shard_map/ppermute | solution.py:494
  7.1 1.5 %collective-permute-start.4 = (bf16[128,512]{1,0:T(8,128)(2,1)S(1)}, bf16[128,512]{1,0:T(8,128)(2,1)S(1)}, u32[]{:S(2)}, u32[]{:S(2)}) collective-permute-start(bf16[128,512]{1,0:T(8,128)(2,1)S(1)} %get-tuple-element.40), channel_id=1, source_target_pairs={{0,8},{1,3},{2,10},{3,1},{4,12},{5,7},{6,14},{7,5},{8,0},{9,11},{1... | collective-permute-start | bytes 393224 | tf_op jit(solution)/shard_map/ppermute | solution.py:494
  8.6 0.6 %collective-permute-start.5 = (bf16[128,512]{1,0:T(8,128)(2,1)S(1)}, bf16[128,512]{1,0:T(8,128)(2,1)S(1)}, u32[]{:S(2)}, u32[]{:S(2)}) collective-permute-start(bf16[128,512]{1,0:T(8,128)(2,1)S(1)} %get-tuple-element.41), channel_id=1, source_target_pairs={{0,4},{1,9},{2,6},{3,11},{4,0},{5,13},{6,2},{7,15},{8,12},{9,1},{1... | collective-permute-start | bytes 393224 | tf_op jit(solution)/shard_map/ppermute | solution.py:494
  9.5 0.9 %collective-permute-done.2.refs_3_.refs_6_ = bf16[128,512]{1,0:T(8,128)(2,1)S(1)} collective-permute-done((bf16[128,512]{1,0:T(8,128)(2,1)S(1)}, bf16[128,512]{1,0:T(8,128)(2,1)S(1)}, u32[]{:S(2)}, u32[]{:S(2)}) %collective-permute-start.2) | collective-permute-done | bytes 131104 | tf_op jit(solution)/shard_map/ppermute | solution.py:494
  10.4 1.5 %collective-permute-done.3.refs_4_.refs_7_ = bf16[128,512]{1,0:T(8,128)(2,1)S(1)} collective-permute-done((bf16[128,512]{1,0:T(8,128)(2,1)S(1)}, bf16[128,512]{1,0:T(8,128)(2,1)S(1)}, u32[]{:S(2)}, u32[]{:S(2)}) %collective-permute-start.3) | collective-permute-done | bytes 131104 | tf_op jit(solution)/shard_map/ppermute | solution.py:494
  12.4 0.8 %collective-permute-done.4.refs_0_.refs_8_ = bf16[128,512]{1,0:T(8,128)(2,1)S(1)} collective-permute-done((bf16[128,512]{1,0:T(8,128)(2,1)S(1)}, bf16[128,512]{1,0:T(8,128)(2,1)S(1)}, u32[]{:S(2)}, u32[]{:S(2)}) %collective-permute-start.4) | collective-permute-done | bytes 131104 | tf_op jit(solution)/shard_map/ppermute | solution.py:494
  13.5 0.9 %shard_map.30 = (f32[4,264,128]{2,1,0:T(8,128)S(1)}, bf16[16,512]{1,0:T(8,128)(2,1)S(1)}, bf16[272,128]{1,0:T(8,128)(2,1)S(1)}, bf16[272,128]{1,0:T(8,128)(2,1)S(1)}, bf16[272,128]{1,0:T(8,128)(2,1)S(1)}) custom-call(f32[4,264,128]{2,1,0:T(8,128)S(1)} %get-tuple-element.38.early_ref, f32[4,128,128]{2,1,0:T(8,128)S(1)} %get-tuple-element.39.early_row_ref, ...), custom_call_target="tpu_custom_call" | custom-call | tf_op jit(solution)/shard_map/pallas_call | solution.py:93
  14.5 3.2 %collective-permute-start.7 = (bf16[272,128]{1,0:T(8,128)(2,1)S(1)}, bf16[272,128]{1,0:T(8,128)(2,1)S(1)}, u32[]{:S(2)}, u32[]{:S(2)}) collective-permute-start(bf16[272,128]{1,0:T(8,128)(2,1)S(1)} %get-tuple-element.45), channel_id=1, source_target_pairs={{0,22},{1,23},{2,20},{3,21},{4,18},{5,19},{6,16},{7,17},{8,30},{9,... | collective-permute-start | bytes 208904 | tf_op jit(solution)/shard_map/ppermute | solution.py:494
  17.6 2.6 %collective-permute-start.8 = (bf16[272,128]{1,0:T(8,128)(2,1)S(1)}, bf16[272,128]{1,0:T(8,128)(2,1)S(1)}, u32[]{:S(2)}, u32[]{:S(2)}) collective-permute-start(bf16[272,128]{1,0:T(8,128)(2,1)S(1)} %get-tuple-element.46), channel_id=1, source_target_pairs={{0,14},{1,15},{2,12},{3,13},{4,10},{5,11},{6,8},{7,9},{8,6},{9,7},... | collective-permute-start | bytes 208904 | tf_op jit(solution)/shard_map/ppermute | solution.py:494
  20.2 0.5 %collective-permute-start.9 = (bf16[272,128]{1,0:T(8,128)(2,1)S(1)}, bf16[272,128]{1,0:T(8,128)(2,1)S(1)}, u32[]{:S(2)}, u32[]{:S(2)}) collective-permute-start(bf16[272,128]{1,0:T(8,128)(2,1)S(1)} %get-tuple-element.47), channel_id=1, source_target_pairs={{0,24},{1,25},{2,26},{3,27},{4,28},{5,29},{6,30},{7,31},{8,16},{9,... | collective-permute-start | bytes 208904 | tf_op jit(solution)/shard_map/ppermute | solution.py:494
  20.7 2.1 %collective-permute-done.7.refs_0_ = bf16[272,128]{1,0:T(8,128)(2,1)S(1)} collective-permute-done((bf16[272,128]{1,0:T(8,128)(2,1)S(1)}, bf16[272,128]{1,0:T(8,128)(2,1)S(1)}, u32[]{:S(2)}, u32[]{:S(2)}) %collective-permute-start.7) | collective-permute-done | bytes 69664 | tf_op jit(solution)/shard_map/ppermute | solution.py:494
  22.9 1.1 %collective-permute-done.8.refs_1_ = bf16[272,128]{1,0:T(8,128)(2,1)S(1)} collective-permute-done((bf16[272,128]{1,0:T(8,128)(2,1)S(1)}, bf16[272,128]{1,0:T(8,128)(2,1)S(1)}, u32[]{:S(2)}, u32[]{:S(2)}) %collective-permute-start.8) | collective-permute-done | bytes 69664 | tf_op jit(solution)/shard_map/ppermute | solution.py:494
  23.9 2.4 %collective-permute-done.9.refs_2_ = bf16[272,128]{1,0:T(8,128)(2,1)S(1)} collective-permute-done((bf16[272,128]{1,0:T(8,128)(2,1)S(1)}, bf16[272,128]{1,0:T(8,128)(2,1)S(1)}, u32[]{:S(2)}, u32[]{:S(2)}) %collective-permute-start.9) | collective-permute-done | bytes 69664 | tf_op jit(solution)/shard_map/ppermute | solution.py:494
  26.5 1.7 %collective-permute-start.10 = (bf16[272,128]{1,0:T(8,128)(2,1)S(1)}, bf16[272,128]{1,0:T(8,128)(2,1)S(1)}, u32[]{:S(2)}, u32[]{:S(2)}) collective-permute-start(bf16[272,128]{1,0:T(8,128)(2,1)S(1)} %get-tuple-element.50), channel_id=1, source_target_pairs={{0,22},{1,23},{2,20},{3,21},{4,18},{5,19},{6,16},{7,17},{8,30},{9,... | collective-permute-start | bytes 208904 | tf_op jit(solution)/shard_map/ppermute | solution.py:494
  28.2 1.8 %collective-permute-start.11 = (bf16[272,128]{1,0:T(8,128)(2,1)S(1)}, bf16[272,128]{1,0:T(8,128)(2,1)S(1)}, u32[]{:S(2)}, u32[]{:S(2)}) collective-permute-start(bf16[272,128]{1,0:T(8,128)(2,1)S(1)} %get-tuple-element.51), channel_id=1, source_target_pairs={{0,14},{1,15},{2,12},{3,13},{4,10},{5,11},{6,8},{7,9},{8,6},{9,7},... | collective-permute-start | bytes 208904 | tf_op jit(solution)/shard_map/ppermute | solution.py:494
  29.9 2.8 %collective-permute-start.12 = (bf16[272,128]{1,0:T(8,128)(2,1)S(1)}, bf16[272,128]{1,0:T(8,128)(2,1)S(1)}, u32[]{:S(2)}, u32[]{:S(2)}) collective-permute-start(bf16[272,128]{1,0:T(8,128)(2,1)S(1)} %get-tuple-element.52), channel_id=1, source_target_pairs={{0,24},{1,25},{2,26},{3,27},{4,28},{5,29},{6,30},{7,31},{8,16},{9,... | collective-permute-start | bytes 208904 | tf_op jit(solution)/shard_map/ppermute | solution.py:494
  32.7 1.6 %collective-permute-done.10.refs_0_ = bf16[272,128]{1,0:T(8,128)(2,1)S(1)} collective-permute-done((bf16[272,128]{1,0:T(8,128)(2,1)S(1)}, bf16[272,128]{1,0:T(8,128)(2,1)S(1)}, u32[]{:S(2)}, u32[]{:S(2)}) %collective-permute-start.10) | collective-permute-done | bytes 69664 | tf_op jit(solution)/shard_map/ppermute | solution.py:494
  34.3 1.2 %collective-permute-done.11.refs_1_ = bf16[272,128]{1,0:T(8,128)(2,1)S(1)} collective-permute-done((bf16[272,128]{1,0:T(8,128)(2,1)S(1)}, bf16[272,128]{1,0:T(8,128)(2,1)S(1)}, u32[]{:S(2)}, u32[]{:S(2)}) %collective-permute-start.11) | collective-permute-done | bytes 69664 | tf_op jit(solution)/shard_map/ppermute | solution.py:494
  35.4 0.6 %collective-permute-done.12.refs_2_ = bf16[272,128]{1,0:T(8,128)(2,1)S(1)} collective-permute-done((bf16[272,128]{1,0:T(8,128)(2,1)S(1)}, bf16[272,128]{1,0:T(8,128)(2,1)S(1)}, u32[]{:S(2)}, u32[]{:S(2)}) %collective-permute-start.12) | collective-permute-done | bytes 69664 | tf_op jit(solution)/shard_map/ppermute | solution.py:494
  36.1 3.7 %shard_map.32 = (bf16[128,512]{1,0:T(8,128)(2,1)S(1)}, bf16[128,512]{1,0:T(8,128)(2,1)S(1)}, bf16[128,512]{1,0:T(8,128)(2,1)S(1)}, bf16[128,512]{1,0:T(8,128)(2,...) custom-call(f32[4,264,128]{2,1,0:T(8,128)S(1)} %get-tuple-element.43, ...), custom_call_target="tpu_custom_call" | custom-call | tf_op jit(solution)/shard_map/pallas_call | solution.py:93
  39.9 1.7 %collective-permute-start.17 = (bf16[128,512]{1,0:T(8,128)(2,1)S(1)}, bf16[128,512]{1,0:T(8,128)(2,1)S(1)}, u32[]{:S(2)}, u32[]{:S(2)}) collective-permute-start(bf16[128,512]{1,0:T(8,128)(2,1)S(1)} %get-tuple-element.58), channel_id=1, source_target_pairs={{9,0},{2,1},{11,2},{0,3},{13,4},{6,5},{15,6},{4,7},{1,8},{10,9},{3... | collective-permute-start | bytes 393224 | tf_op jit(solution)/shard_map/ppermute | solution.py:494
  41.7 1.2 %collective-permute-start.19 = (bf16[128,512]{1,0:T(8,128)(2,1)S(1)}, bf16[128,512]{1,0:T(8,128)(2,1)S(1)}, u32[]{:S(2)}, u32[]{:S(2)}) collective-permute-start(bf16[128,512]{1,0:T(8,128)(2,1)S(1)} %get-tuple-element.60), channel_id=1, source_target_pairs={{2,0},{5,1},{0,2},{7,3},{6,4},{1,5},{4,6},{3,7},{10,8},{13,9},{8,1... | collective-permute-start | bytes 393224 | tf_op jit(solution)/shard_map/ppermute | solution.py:494
  42.9 0.7 %collective-permute-start.13 = (bf16[128,512]{1,0:T(8,128)(2,1)S(1)}, bf16[128,512]{1,0:T(8,128)(2,1)S(1)}, u32[]{:S(2)}, u32[]{:S(2)}) collective-permute-start(bf16[128,512]{1,0:T(8,128)(2,1)S(1)} %get-tuple-element.53), channel_id=1, source_target_pairs={{8,0},{3,1},{10,2},{1,3},{12,4},{7,5},{14,6},{5,7},{0,8},{11,9},{2... | collective-permute-start | bytes 393224 | tf_op jit(solution)/shard_map/ppermute | solution.py:494
  43.6 0.6 %collective-permute-done.16.refs_1_ = bf16[128,512]{1,0:T(8,128)(2,1)S(1)} collective-permute-done((bf16[128,512]{1,0:T(8,128)(2,1)S(1)}, bf16[128,512]{1,0:T(8,128)(2,1)S(1)}, u32[]{:S(2)}, u32[]{:S(2)}) %collective-permute-start.16) | collective-permute-done | bytes 131104 | tf_op jit(solution)/shard_map/ppermute | solution.py:494
  44.2 1.0 %collective-permute-start.14 = (bf16[128,512]{1,0:T(8,128)(2,1)S(1)}, bf16[128,512]{1,0:T(8,128)(2,1)S(1)}, u32[]{:S(2)}, u32[]{:S(2)}) collective-permute-start(bf16[128,512]{1,0:T(8,128)(2,1)S(1)} %get-tuple-element.54), channel_id=1, source_target_pairs={{4,0},{9,1},{6,2},{11,3},{0,4},{13,5},{2,6},{15,7},{12,8},{1,9},{1... | collective-permute-start | bytes 393224 | tf_op jit(solution)/shard_map/ppermute | solution.py:494
  45.2 0.7 %collective-permute-start.15 = (bf16[128,512]{1,0:T(8,128)(2,1)S(1)}, bf16[128,512]{1,0:T(8,128)(2,1)S(1)}, u32[]{:S(2)}, u32[]{:S(2)}) collective-permute-start(bf16[128,512]{1,0:T(8,128)(2,1)S(1)} %get-tuple-element.55), channel_id=1, source_target_pairs={{1,0},{0,1},{3,2},{2,3},{5,4},{4,5},{7,6},{6,7},{9,8},{8,9},{11,10... | collective-permute-start | bytes 393224 | tf_op jit(solution)/shard_map/ppermute | solution.py:494
  46.0 2.2 %collective-permute-done.19.refs_4_ = bf16[128,512]{1,0:T(8,128)(2,1)S(1)} collective-permute-done((bf16[128,512]{1,0:T(8,128)(2,1)S(1)}, bf16[128,512]{1,0:T(8,128)(2,1)S(1)}, u32[]{:S(2)}, u32[]{:S(2)}) %collective-permute-start.19) | collective-permute-done | bytes 131104 | tf_op jit(solution)/shard_map/ppermute | solution.py:494
  48.2 0.9 %shard_map.33.refs_3_ = bf16[4,2,128,512]{3,2,1,0:T(8,128)(2,1)} custom-call(bf16[4,2,128,512]{3,2,1,0:T(8,128)(2,1)S(1)} %bitcast.3, bf16[128,512]{1,0:T(8,128)(2,1)S(1)} %get-tuple-element.56.refs_0_, bf16[128,512]{1,0:T(8,128)(2,1)S(1)} %collective-permute-done.16.refs_1_, bf16[128,512]{1,0:T(8,128)(2,1)S(1)} %collective-permute-done.17.refs_2_, ...), custom_call_target="tpu_custom_call" | custom-call | tf_op jit(solution)/shard_map/pallas_call | solution.py:457
  49.2 0.8 %shard_map.34 = bf16[4,2,128,512]{3,2,1,0:T(8,128)(2,1)} custom-call(bf16[4,2,128,512]{3,2,1,0:T(8,128)(2,1)S(1)} %bitcast.4, bf16[128,512]{1,0:T(8,128)(2,1)S(1)} %collective-permute-done.13.refs_0_, bf16[128,512]{1,0:T(8,128)(2,1)S(1)} %collective-permute-done.14.refs_1_, ...), custom_call_target="tpu_custom_call", output_to_operand_aliasing={{}: (4, {})} | custom-call | tf_op jit(solution)/shard_map/pallas_call | solution.py:457
  (19 shorter events, 1.7 us)
Async XLA Ops:
  0.0 1.2 %copy-start.1 = (bf16[1,8,128,512]{3,2,1,0:T(8,128)(2,1)S(1)}, bf16[1,8,128,512]{3,2,1,0:T(8,128)(2,1)}, u32[]{:S(2)}) copy-start(bf16[1,8,128,512]{3,2,1,0:T(8,128)(2,1)} %param.2) | copy-start | bytes 3145732
  1.3 7.3 %collective-permute-start = (bf16[128,512]{1,0:T(8,128)(2,1)S(1)}, bf16[128,512]{1,0:T(8,128)(2,1)S(1)}, u32[]{:S(2)}, u32[]{:S(2)}) collective-permute-start(bf16[128,512]{1,0:T(8,128)(2,1)S(1)} %get-tuple-element.34), channel_id=1, source_target_pairs={{0,3},{1,4},{2,1},{3,6},{4,7},{5,0},{6,5},{7,2},{8,11},{9,12},{10,... | collective-permute-start | bytes 393224 | tf_op jit(solution)/shard_map/ppermute | solution.py:494
  3.7 5.7 %collective-permute-start.1 = (bf16[128,512]{1,0:T(8,128)(2,1)S(1)}, bf16[128,512]{1,0:T(8,128)(2,1)S(1)}, u32[]{:S(2)}, u32[]{:S(2)}) collective-permute-start(bf16[128,512]{1,0:T(8,128)(2,1)S(1)} %get-tuple-element.35), channel_id=1, source_target_pairs={{0,9},{1,2},{2,11},{3,0},{4,13},{5,6},{6,15},{7,4},{8,1},{9,10},{1... | collective-permute-start | bytes 393224 | tf_op jit(solution)/shard_map/ppermute | solution.py:494
  5.6 4.8 %collective-permute-start.2 = (bf16[128,512]{1,0:T(8,128)(2,1)S(1)}, bf16[128,512]{1,0:T(8,128)(2,1)S(1)}, u32[]{:S(2)}, u32[]{:S(2)}) collective-permute-start(bf16[128,512]{1,0:T(8,128)(2,1)S(1)} %get-tuple-element.36), channel_id=1, source_target_pairs={{0,5},{1,8},{2,7},{3,10},{4,1},{5,12},{6,3},{7,14},{8,13},{9,0},{1... | collective-permute-start | bytes 393224 | tf_op jit(solution)/shard_map/ppermute | solution.py:494
  5.6 6.3 %collective-permute-start.3 = (bf16[128,512]{1,0:T(8,128)(2,1)S(1)}, bf16[128,512]{1,0:T(8,128)(2,1)S(1)}, u32[]{:S(2)}, u32[]{:S(2)}) collective-permute-start(bf16[128,512]{1,0:T(8,128)(2,1)S(1)} %get-tuple-element.37), channel_id=1, source_target_pairs={{0,2},{1,5},{2,0},{3,7},{4,6},{5,1},{6,4},{7,3},{8,10},{9,13},{10,... | collective-permute-start | bytes 393224 | tf_op jit(solution)/shard_map/ppermute | solution.py:494
  7.1 6.1 %collective-permute-start.4 = (bf16[128,512]{1,0:T(8,128)(2,1)S(1)}, bf16[128,512]{1,0:T(8,128)(2,1)S(1)}, u32[]{:S(2)}, u32[]{:S(2)}) collective-permute-start(bf16[128,512]{1,0:T(8,128)(2,1)S(1)} %get-tuple-element.40), channel_id=1, source_target_pairs={{0,8},{1,3},{2,10},{3,1},{4,12},{5,7},{6,14},{7,5},{8,0},{9,11},{1... | collective-permute-start | bytes 393224 | tf_op jit(solution)/shard_map/ppermute | solution.py:494
  8.6 5.0 %collective-permute-start.5 = (bf16[128,512]{1,0:T(8,128)(2,1)S(1)}, bf16[128,512]{1,0:T(8,128)(2,1)S(1)}, u32[]{:S(2)}, u32[]{:S(2)}) collective-permute-start(bf16[128,512]{1,0:T(8,128)(2,1)S(1)} %get-tuple-element.41), channel_id=1, source_target_pairs={{0,4},{1,9},{2,6},{3,11},{4,0},{5,13},{6,2},{7,15},{8,12},{9,1},{1... | collective-permute-start | bytes 393224 | tf_op jit(solution)/shard_map/ppermute | solution.py:494
  9.4 4.2 %collective-permute-start.6 = (bf16[128,512]{1,0:T(8,128)(2,1)S(1)}, bf16[128,512]{1,0:T(8,128)(2,1)S(1)}, u32[]{:S(2)}, u32[]{:S(2)}) collective-permute-start(bf16[128,512]{1,0:T(8,128)(2,1)S(1)} %get-tuple-element.42), channel_id=1, source_target_pairs={{0,1},{1,0},{2,3},{3,2},{4,5},{5,4},{6,7},{7,6},{8,9},{9,8},{10,11... | collective-permute-start | bytes 393224 | tf_op jit(solution)/shard_map/ppermute | solution.py:494
  14.5 8.4 %collective-permute-start.7 = (bf16[272,128]{1,0:T(8,128)(2,1)S(1)}, bf16[272,128]{1,0:T(8,128)(2,1)S(1)}, u32[]{:S(2)}, u32[]{:S(2)}) collective-permute-start(bf16[272,128]{1,0:T(8,128)(2,1)S(1)} %get-tuple-element.45), channel_id=1, source_target_pairs={{0,22},{1,23},{2,20},{3,21},{4,18},{5,19},{6,16},{7,17},{8,30},{9,... | collective-permute-start | bytes 208904 | tf_op jit(solution)/shard_map/ppermute | solution.py:494
  17.6 6.3 %collective-permute-start.8 = (bf16[272,128]{1,0:T(8,128)(2,1)S(1)}, bf16[272,128]{1,0:T(8,128)(2,1)S(1)}, u32[]{:S(2)}, u32[]{:S(2)}) collective-permute-start(bf16[272,128]{1,0:T(8,128)(2,1)S(1)} %get-tuple-element.46), channel_id=1, source_target_pairs={{0,14},{1,15},{2,12},{3,13},{4,10},{5,11},{6,8},{7,9},{8,6},{9,7},... | collective-permute-start | bytes 208904 | tf_op jit(solution)/shard_map/ppermute | solution.py:494
  20.2 6.1 %collective-permute-start.9 = (bf16[272,128]{1,0:T(8,128)(2,1)S(1)}, bf16[272,128]{1,0:T(8,128)(2,1)S(1)}, u32[]{:S(2)}, u32[]{:S(2)}) collective-permute-start(bf16[272,128]{1,0:T(8,128)(2,1)S(1)} %get-tuple-element.47), channel_id=1, source_target_pairs={{0,24},{1,25},{2,26},{3,27},{4,28},{5,29},{6,30},{7,31},{8,16},{9,... | collective-permute-start | bytes 208904 | tf_op jit(solution)/shard_map/ppermute | solution.py:494
  26.4 21.8 %copy-start = (bf16[1,8,128,512]{3,2,1,0:T(8,128)(2,1)S(1)}, bf16[1,8,128,512]{3,2,1,0:T(8,128)(2,1)}, u32[]{:S(2)}) copy-start(bf16[1,8,128,512]{3,2,1,0:T(8,128)(2,1)} %param.3) | copy-start | bytes 3145732
  26.5 7.8 %collective-permute-start.10 = (bf16[272,128]{1,0:T(8,128)(2,1)S(1)}, bf16[272,128]{1,0:T(8,128)(2,1)S(1)}, u32[]{:S(2)}, u32[]{:S(2)}) collective-permute-start(bf16[272,128]{1,0:T(8,128)(2,1)S(1)} %get-tuple-element.50), channel_id=1, source_target_pairs={{0,22},{1,23},{2,20},{3,21},{4,18},{5,19},{6,16},{7,17},{8,30},{9,... | collective-permute-start | bytes 208904 | tf_op jit(solution)/shard_map/ppermute | solution.py:494
  28.2 7.3 %collective-permute-start.11 = (bf16[272,128]{1,0:T(8,128)(2,1)S(1)}, bf16[272,128]{1,0:T(8,128)(2,1)S(1)}, u32[]{:S(2)}, u32[]{:S(2)}) collective-permute-start(bf16[272,128]{1,0:T(8,128)(2,1)S(1)} %get-tuple-element.51), channel_id=1, source_target_pairs={{0,14},{1,15},{2,12},{3,13},{4,10},{5,11},{6,8},{7,9},{8,6},{9,7},... | collective-permute-start | bytes 208904 | tf_op jit(solution)/shard_map/ppermute | solution.py:494
  29.9 6.1 %collective-permute-start.12 = (bf16[272,128]{1,0:T(8,128)(2,1)S(1)}, bf16[272,128]{1,0:T(8,128)(2,1)S(1)}, u32[]{:S(2)}, u32[]{:S(2)}) collective-permute-start(bf16[272,128]{1,0:T(8,128)(2,1)S(1)} %get-tuple-element.52), channel_id=1, source_target_pairs={{0,24},{1,25},{2,26},{3,27},{4,28},{5,29},{6,30},{7,31},{8,16},{9,... | collective-permute-start | bytes 208904 | tf_op jit(solution)/shard_map/ppermute | solution.py:494
  39.8 4.4 %collective-permute-start.16 = (bf16[128,512]{1,0:T(8,128)(2,1)S(1)}, bf16[128,512]{1,0:T(8,128)(2,1)S(1)}, u32[]{:S(2)}, u32[]{:S(2)}) collective-permute-start(bf16[128,512]{1,0:T(8,128)(2,1)S(1)} %get-tuple-element.57), channel_id=1, source_target_pairs={{3,0},{4,1},{1,2},{6,3},{7,4},{0,5},{5,6},{2,7},{11,8},{12,9},{9,1... | collective-permute-start | bytes 393224 | tf_op jit(solution)/shard_map/ppermute | solution.py:494
  39.9 5.3 %collective-permute-start.17 = (bf16[128,512]{1,0:T(8,128)(2,1)S(1)}, bf16[128,512]{1,0:T(8,128)(2,1)S(1)}, u32[]{:S(2)}, u32[]{:S(2)}) collective-permute-start(bf16[128,512]{1,0:T(8,128)(2,1)S(1)} %get-tuple-element.58), channel_id=1, source_target_pairs={{9,0},{2,1},{11,2},{0,3},{13,4},{6,5},{15,6},{4,7},{1,8},{10,9},{3... | collective-permute-start | bytes 393224 | tf_op jit(solution)/shard_map/ppermute | solution.py:494
  41.6 4.4 %collective-permute-start.18 = (bf16[128,512]{1,0:T(8,128)(2,1)S(1)}, bf16[128,512]{1,0:T(8,128)(2,1)S(1)}, u32[]{:S(2)}, u32[]{:S(2)}) collective-permute-start(bf16[128,512]{1,0:T(8,128)(2,1)S(1)} %get-tuple-element.59), channel_id=1, source_target_pairs={{5,0},{8,1},{7,2},{10,3},{1,4},{12,5},{3,6},{14,7},{13,8},{0,9},{1... | collective-permute-start | bytes 393224 | tf_op jit(solution)/shard_map/ppermute | solution.py:494
  41.7 6.5 %collective-permute-start.19 = (bf16[128,512]{1,0:T(8,128)(2,1)S(1)}, bf16[128,512]{1,0:T(8,128)(2,1)S(1)}, u32[]{:S(2)}, u32[]{:S(2)}) collective-permute-start(bf16[128,512]{1,0:T(8,128)(2,1)S(1)} %get-tuple-element.60), channel_id=1, source_target_pairs={{2,0},{5,1},{0,2},{7,3},{6,4},{1,5},{4,6},{3,7},{10,8},{13,9},{8,1... | collective-permute-start | bytes 393224 | tf_op jit(solution)/shard_map/ppermute | solution.py:494
  42.9 6.3 %collective-permute-start.13 = (bf16[128,512]{1,0:T(8,128)(2,1)S(1)}, bf16[128,512]{1,0:T(8,128)(2,1)S(1)}, u32[]{:S(2)}, u32[]{:S(2)}) collective-permute-start(bf16[128,512]{1,0:T(8,128)(2,1)S(1)} %get-tuple-element.53), channel_id=1, source_target_pairs={{8,0},{3,1},{10,2},{1,3},{12,4},{7,5},{14,6},{5,7},{0,8},{11,9},{2... | collective-permute-start | bytes 393224 | tf_op jit(solution)/shard_map/ppermute | solution.py:494
  44.2 5.0 %collective-permute-start.14 = (bf16[128,512]{1,0:T(8,128)(2,1)S(1)}, bf16[128,512]{1,0:T(8,128)(2,1)S(1)}, u32[]{:S(2)}, u32[]{:S(2)}) collective-permute-start(bf16[128,512]{1,0:T(8,128)(2,1)S(1)} %get-tuple-element.54), channel_id=1, source_target_pairs={{4,0},{9,1},{6,2},{11,3},{0,4},{13,5},{2,6},{15,7},{12,8},{1,9},{1... | collective-permute-start | bytes 393224 | tf_op jit(solution)/shard_map/ppermute | solution.py:494
  45.2 4.0 %collective-permute-start.15 = (bf16[128,512]{1,0:T(8,128)(2,1)S(1)}, bf16[128,512]{1,0:T(8,128)(2,1)S(1)}, u32[]{:S(2)}, u32[]{:S(2)}) collective-permute-start(bf16[128,512]{1,0:T(8,128)(2,1)S(1)} %get-tuple-element.55), channel_id=1, source_target_pairs={{1,0},{0,1},{3,2},{2,3},{5,4},{4,5},{7,6},{6,7},{9,8},{8,9},{11,10... | collective-permute-start | bytes 393224 | tf_op jit(solution)/shard_map/ppermute | solution.py:494

commit v10 on v9

--- a/solution.py
+++ b/solution.py
@@ -240,11 +240,11 @@
     return result
 
 
-def main_direction(first_row):
+def main_direction(first_row, share):
     signs = jnp.where(first_row[0][:, :1] < 0.0, -1.0, 1.0)
     rows = [jnp.sum(signs * block, axis=0, keepdims=True) for block in first_row]
     size = jnp.sum(jnp.where(first_row[0][:1, :] < 0.0, -rows[0], rows[0]))
-    growth = jnp.where(size > 0.0, lax.rsqrt(jnp.maximum(size, SMALLEST)), 0.0)
+    growth = jnp.where(size > 0.0, lax.rsqrt(jnp.maximum(share * size, SMALLEST)), 0.0)
     return (jnp.concatenate(rows, axis=1) * growth).astype(jnp.bfloat16).astype(jnp.float32)
 
 
@@ -275,25 +275,24 @@
     return pack(block, order), [block(0, k) for k in range(order // BLOCK)]
 
 
-def early_gram_kernel(*refs):
-    block_refs, packed_ref, first_row_ref = refs[:-2], refs[-2], refs[-1]
-    packed, first_row = packed_gram(block_refs)
-    for quarter, value in enumerate(packed):
-        packed_ref[quarter] = value
-    for number, value in enumerate(first_row):
-        first_row_ref[number] = value
-
-
-def gram_kernel(rest_count, early_ref, early_row_ref, *refs):
-    block_refs, left_ref, direction_ref, message_refs = refs[:-5], refs[-5], refs[-4], refs[-3:]
+def early_gram_kernel(share, *refs):
+    block_refs, left_ref, direction_ref = refs[:-2], refs[-2], refs[-1]
     order = block_refs[0].shape[1]
     packed, first_row = packed_gram(block_refs)
-    direction = main_direction([early_row_ref[number] + value for number, value in enumerate(first_row)])
+    direction = main_direction(first_row, share)
     direction_ref[...] = stacked([direction])
     outer = outer_products(stacked([direction]))
     for quarter, (value, known) in enumerate(zip(packed, pack(lambda i, j: outer[i, j], order))):
-        left_ref[quarter] = early_ref[quarter] + (value - known)
+        left_ref[quarter] = value - known
+
+
+def gram_kernel(rest_count, early_ref, direction_ref, *refs):
+    block_refs, left_ref, message_refs = refs[:-4], refs[-4], refs[-3:]
+    order = block_refs[0].shape[1]
+    for quarter, value in enumerate(packed_gram(block_refs)[0]):
+        left_ref[quarter] = early_ref[quarter] + value
     place = Place(rest_count)
+    direction = direction_ref[...].astype(jnp.float32)[:1]
     for step, message_ref in enumerate(message_refs):
         message_ref[...] = to_message(left_ref[place.quarter_at(step)], order, direction)
 
@@ -506,13 +505,15 @@
         spread.reshape(by_block),
     )
     rows = [own] + swap(dealt, ROWS)
-    first_row = jax.ShapeDtypeStruct((order // BLOCK, BLOCK, BLOCK), jnp.float32)
     direction = jax.ShapeDtypeStruct((BF16_TILE, order), jnp.bfloat16)
-    early = call(early_gram_kernel, (packed, first_row), *rows[:EARLY])
-    left, own_direction, *parts = call(
+    early_left, own_direction = call(
+        functools.partial(early_gram_kernel, EARLY / len(rows)), (packed, direction), *rows[:EARLY]
+    )
+    left, *parts = call(
         functools.partial(gram_kernel, rest_count),
-        (packed, direction) + (message,) * 3,
-        *early,
+        (packed,) + (message,) * 3,
+        early_left,
+        own_direction,
         *rows[EARLY:],
     )
     total, directions, *rests = call(

time: 50.2 us -> 49.7 us (0.990)
  transfers between devices with their start and end apart: 20 -> 20, of which waited for: 15 -> 15; matrix products, arithmetic and copies ran while one was open for 0% -> 0% of each run, Pallas kernels for 3% -> 4%
where the time goes in v10:
time: 49.7 us; the launch traced here: 49.6 us
  starting transfers between devices  25.9 us (52%)
  waiting for transfers between devices  15.3 us (31%)
  Pallas kernels  7.11 us (14%)
  local copies, waits for them, and re-layouts  1.23 us (2%)
    ppermute x20, starting transfers between devices, swap(): lax.ppermute(array, AXES, permute)  25.9 us
    ppermute x20, waiting for transfers between devices, swap(): lax.ppermute(array, AXES, permute)  15.3 us
    pallas_call x5, Pallas kernels, call(): pl.pallas_call(kernel, out_shape=out_shape, in_specs=[vmem] * len(operand...  5.33 us
    pallas_call x2, Pallas kernels, new_weights(): pl.pallas_call(functools.partial(weights_kernel, rest_count, numbers), ou...  1.77 us
    unnamed x4, local copies, waits for them, and re-layouts  1.23 us
  transfers between devices with their start and end apart: 20, of which 15 were waited for; matrix products, arithmetic and copies ran while one was open for 0% of the time, Pallas kernels for 4%

profile of v10, /device:TPU:0, one launch (start us, length us, event | category | flops | bytes accessed | tf_op | source)
XLA Modules:
  0.0 49.6 jit_solution(17882590240250389935)
XLA Ops:
  0.0 1.2 %copy-done.1 = bf16[1,8,128,512]{3,2,1,0:T(8,128)(2,1)S(1)} copy-done((bf16[1,8,128,512]{3,2,1,0:T(8,128)(2,1)S(1)}, bf16[1,8,128,512]{3,2,1,0:T(8,128)(2,1)}, u32[]{:S(2)}) %copy-start.1) | copy-done | bytes 1048600
  1.3 2.4 %collective-permute-start = (bf16[128,512]{1,0:T(8,128)(2,1)S(1)}, bf16[128,512]{1,0:T(8,128)(2,1)S(1)}, u32[]{:S(2)}, u32[]{:S(2)}) collective-permute-start(bf16[128,512]{1,0:T(8,128)(2,1)S(1)} %get-tuple-element.33), channel_id=1, source_target_pairs={{0,3},{1,4},{2,1},{3,6},{4,7},{5,0},{6,5},{7,2},{8,11},{9,12},{10,... | collective-permute-start | bytes 393224 | tf_op jit(solution)/shard_map/ppermute | solution.py:493
  3.7 1.9 %collective-permute-start.1 = (bf16[128,512]{1,0:T(8,128)(2,1)S(1)}, bf16[128,512]{1,0:T(8,128)(2,1)S(1)}, u32[]{:S(2)}, u32[]{:S(2)}) collective-permute-start(bf16[128,512]{1,0:T(8,128)(2,1)S(1)} %get-tuple-element.34), channel_id=1, source_target_pairs={{0,9},{1,2},{2,11},{3,0},{4,13},{5,6},{6,15},{7,4},{8,1},{9,10},{1... | collective-permute-start | bytes 393224 | tf_op jit(solution)/shard_map/ppermute | solution.py:493
  5.6 1.5 %collective-permute-start.3 = (bf16[128,512]{1,0:T(8,128)(2,1)S(1)}, bf16[128,512]{1,0:T(8,128)(2,1)S(1)}, u32[]{:S(2)}, u32[]{:S(2)}) collective-permute-start(bf16[128,512]{1,0:T(8,128)(2,1)S(1)} %get-tuple-element.36), channel_id=1, source_target_pairs={{0,2},{1,5},{2,0},{3,7},{4,6},{5,1},{6,4},{7,3},{8,10},{9,13},{10,... | collective-permute-start | bytes 393224 | tf_op jit(solution)/shard_map/ppermute | solution.py:493
  7.1 1.5 %collective-permute-start.4 = (bf16[128,512]{1,0:T(8,128)(2,1)S(1)}, bf16[128,512]{1,0:T(8,128)(2,1)S(1)}, u32[]{:S(2)}, u32[]{:S(2)}) collective-permute-start(bf16[128,512]{1,0:T(8,128)(2,1)S(1)} %get-tuple-element.39), channel_id=1, source_target_pairs={{0,8},{1,3},{2,10},{3,1},{4,12},{5,7},{6,14},{7,5},{8,0},{9,11},{1... | collective-permute-start | bytes 393224 | tf_op jit(solution)/shard_map/ppermute | solution.py:493
  8.6 0.6 %collective-permute-start.5 = (bf16[128,512]{1,0:T(8,128)(2,1)S(1)}, bf16[128,512]{1,0:T(8,128)(2,1)S(1)}, u32[]{:S(2)}, u32[]{:S(2)}) collective-permute-start(bf16[128,512]{1,0:T(8,128)(2,1)S(1)} %get-tuple-element.40), channel_id=1, source_target_pairs={{0,4},{1,9},{2,6},{3,11},{4,0},{5,13},{6,2},{7,15},{8,12},{9,1},{1... | collective-permute-start | bytes 393224 | tf_op jit(solution)/shard_map/ppermute | solution.py:493
  9.5 0.9 %collective-permute-done.2.refs_3_.refs_6_ = bf16[128,512]{1,0:T(8,128)(2,1)S(1)} collective-permute-done((bf16[128,512]{1,0:T(8,128)(2,1)S(1)}, bf16[128,512]{1,0:T(8,128)(2,1)S(1)}, u32[]{:S(2)}, u32[]{:S(2)}) %collective-permute-start.2) | collective-permute-done | bytes 131104 | tf_op jit(solution)/shard_map/ppermute | solution.py:493
  10.4 1.5 %collective-permute-done.3.refs_4_.refs_7_ = bf16[128,512]{1,0:T(8,128)(2,1)S(1)} collective-permute-done((bf16[128,512]{1,0:T(8,128)(2,1)S(1)}, bf16[128,512]{1,0:T(8,128)(2,1)S(1)}, u32[]{:S(2)}, u32[]{:S(2)}) %collective-permute-start.3) | collective-permute-done | bytes 131104 | tf_op jit(solution)/shard_map/ppermute | solution.py:493
  11.9 0.9 %shard_map.29 = (f32[4,264,128]{2,1,0:T(8,128)S(1)}, bf16[16,512]{1,0:T(8,128)(2,1)S(1)}) custom-call(bf16[128,512]{1,0:T(8,128)(2,1)S(1)} %get-tuple-element.32.refs_0_.refs_3_, bf16[128,512]{1,0:T(8,128)(2,1)S(1)} %collective-permute-done.refs_1_.refs_4_, bf16[128,512]{1,0:T(8,128)(2,1)S(1)} %collective-permute-done.1.refs_2_.refs_5_, ...), custom_call_target="tpu_custom_call" | custom-call | tf_op jit(solution)/shard_map/pallas_call | solution.py:93
  13.5 0.5 shard_map.30
  14.0 3.2 %collective-permute-start.7 = (bf16[272,128]{1,0:T(8,128)(2,1)S(1)}, bf16[272,128]{1,0:T(8,128)(2,1)S(1)}, u32[]{:S(2)}, u32[]{:S(2)}) collective-permute-start(bf16[272,128]{1,0:T(8,128)(2,1)S(1)} %get-tuple-element.43), channel_id=1, source_target_pairs={{0,22},{1,23},{2,20},{3,21},{4,18},{5,19},{6,16},{7,17},{8,30},{9,... | collective-permute-start | bytes 208904 | tf_op jit(solution)/shard_map/ppermute | solution.py:493
  17.2 2.6 %collective-permute-start.8 = (bf16[272,128]{1,0:T(8,128)(2,1)S(1)}, bf16[272,128]{1,0:T(8,128)(2,1)S(1)}, u32[]{:S(2)}, u32[]{:S(2)}) collective-permute-start(bf16[272,128]{1,0:T(8,128)(2,1)S(1)} %get-tuple-element.44), channel_id=1, source_target_pairs={{0,14},{1,15},{2,12},{3,13},{4,10},{5,11},{6,8},{7,9},{8,6},{9,7},... | collective-permute-start | bytes 208904 | tf_op jit(solution)/shard_map/ppermute | solution.py:493
  19.7 0.5 %collective-permute-start.9 = (bf16[272,128]{1,0:T(8,128)(2,1)S(1)}, bf16[272,128]{1,0:T(8,128)(2,1)S(1)}, u32[]{:S(2)}, u32[]{:S(2)}) collective-permute-start(bf16[272,128]{1,0:T(8,128)(2,1)S(1)} %get-tuple-element.45), channel_id=1, source_target_pairs={{0,24},{1,25},{2,26},{3,27},{4,28},{5,29},{6,30},{7,31},{8,16},{9,... | collective-permute-start | bytes 208904 | tf_op jit(solution)/shard_map/ppermute | solution.py:493
  20.3 2.1 %collective-permute-done.7.refs_0_ = bf16[272,128]{1,0:T(8,128)(2,1)S(1)} collective-permute-done((bf16[272,128]{1,0:T(8,128)(2,1)S(1)}, bf16[272,128]{1,0:T(8,128)(2,1)S(1)}, u32[]{:S(2)}, u32[]{:S(2)}) %collective-permute-start.7) | collective-permute-done | bytes 69664 | tf_op jit(solution)/shard_map/ppermute | solution.py:493
  22.4 1.1 %collective-permute-done.8.refs_1_ = bf16[272,128]{1,0:T(8,128)(2,1)S(1)} collective-permute-done((bf16[272,128]{1,0:T(8,128)(2,1)S(1)}, bf16[272,128]{1,0:T(8,128)(2,1)S(1)}, u32[]{:S(2)}, u32[]{:S(2)}) %collective-permute-start.8) | collective-permute-done | bytes 69664 | tf_op jit(solution)/shard_map/ppermute | solution.py:493
  23.5 2.4 %collective-permute-done.9.refs_2_ = bf16[272,128]{1,0:T(8,128)(2,1)S(1)} collective-permute-done((bf16[272,128]{1,0:T(8,128)(2,1)S(1)}, bf16[272,128]{1,0:T(8,128)(2,1)S(1)}, u32[]{:S(2)}, u32[]{:S(2)}) %collective-permute-start.9) | collective-permute-done | bytes 69664 | tf_op jit(solution)/shard_map/ppermute | solution.py:493
  26.0 1.7 %collective-permute-start.10 = (bf16[272,128]{1,0:T(8,128)(2,1)S(1)}, bf16[272,128]{1,0:T(8,128)(2,1)S(1)}, u32[]{:S(2)}, u32[]{:S(2)}) collective-permute-start(bf16[272,128]{1,0:T(8,128)(2,1)S(1)} %get-tuple-element.48), channel_id=1, source_target_pairs={{0,22},{1,23},{2,20},{3,21},{4,18},{5,19},{6,16},{7,17},{8,30},{9,... | collective-permute-start | bytes 208904 | tf_op jit(solution)/shard_map/ppermute | solution.py:493
  27.7 1.8 %collective-permute-start.11 = (bf16[272,128]{1,0:T(8,128)(2,1)S(1)}, bf16[272,128]{1,0:T(8,128)(2,1)S(1)}, u32[]{:S(2)}, u32[]{:S(2)}) collective-permute-start(bf16[272,128]{1,0:T(8,128)(2,1)S(1)} %get-tuple-element.49), channel_id=1, source_target_pairs={{0,14},{1,15},{2,12},{3,13},{4,10},{5,11},{6,8},{7,9},{8,6},{9,7},... | collective-permute-start | bytes 208904 | tf_op jit(solution)/shard_map/ppermute | solution.py:493
  29.5 2.8 %collective-permute-start.12 = (bf16[272,128]{1,0:T(8,128)(2,1)S(1)}, bf16[272,128]{1,0:T(8,128)(2,1)S(1)}, u32[]{:S(2)}, u32[]{:S(2)}) collective-permute-start(bf16[272,128]{1,0:T(8,128)(2,1)S(1)} %get-tuple-element.50), channel_id=1, source_target_pairs={{0,24},{1,25},{2,26},{3,27},{4,28},{5,29},{6,30},{7,31},{8,16},{9,... | collective-permute-start | bytes 208904 | tf_op jit(solution)/shard_map/ppermute | solution.py:493
  32.2 1.6 %collective-permute-done.10.refs_0_ = bf16[272,128]{1,0:T(8,128)(2,1)S(1)} collective-permute-done((bf16[272,128]{1,0:T(8,128)(2,1)S(1)}, bf16[272,128]{1,0:T(8,128)(2,1)S(1)}, u32[]{:S(2)}, u32[]{:S(2)}) %collective-permute-start.10) | collective-permute-done | bytes 69664 | tf_op jit(solution)/shard_map/ppermute | solution.py:493
  33.8 1.2 %collective-permute-done.11.refs_1_ = bf16[272,128]{1,0:T(8,128)(2,1)S(1)} collective-permute-done((bf16[272,128]{1,0:T(8,128)(2,1)S(1)}, bf16[272,128]{1,0:T(8,128)(2,1)S(1)}, u32[]{:S(2)}, u32[]{:S(2)}) %collective-permute-start.11) | collective-permute-done | bytes 69664 | tf_op jit(solution)/shard_map/ppermute | solution.py:493
  34.9 0.6 %collective-permute-done.12.refs_2_ = bf16[272,128]{1,0:T(8,128)(2,1)S(1)} collective-permute-done((bf16[272,128]{1,0:T(8,128)(2,1)S(1)}, bf16[272,128]{1,0:T(8,128)(2,1)S(1)}, u32[]{:S(2)}, u32[]{:S(2)}) %collective-permute-start.12) | collective-permute-done | bytes 69664 | tf_op jit(solution)/shard_map/ppermute | solution.py:493
  35.6 3.7 %shard_map.32 = (bf16[128,512]{1,0:T(8,128)(2,1)S(1)}, bf16[128,512]{1,0:T(8,128)(2,1)S(1)}, bf16[128,512]{1,0:T(8,128)(2,1)S(1)}, bf16[128,512]{1,0:T(8,128)(2,...) custom-call(f32[4,264,128]{2,1,0:T(8,128)S(1)} %get-tuple-element.42, ...), custom_call_target="tpu_custom_call" | custom-call | tf_op jit(solution)/shard_map/pallas_call | solution.py:93
  39.4 1.7 %collective-permute-start.17 = (bf16[128,512]{1,0:T(8,128)(2,1)S(1)}, bf16[128,512]{1,0:T(8,128)(2,1)S(1)}, u32[]{:S(2)}, u32[]{:S(2)}) collective-permute-start(bf16[128,512]{1,0:T(8,128)(2,1)S(1)} %get-tuple-element.56), channel_id=1, source_target_pairs={{9,0},{2,1},{11,2},{0,3},{13,4},{6,5},{15,6},{4,7},{1,8},{10,9},{3... | collective-permute-start | bytes 393224 | tf_op jit(solution)/shard_map/ppermute | solution.py:493
  41.2 1.2 %collective-permute-start.19 = (bf16[128,512]{1,0:T(8,128)(2,1)S(1)}, bf16[128,512]{1,0:T(8,128)(2,1)S(1)}, u32[]{:S(2)}, u32[]{:S(2)}) collective-permute-start(bf16[128,512]{1,0:T(8,128)(2,1)S(1)} %get-tuple-element.58), channel_id=1, source_target_pairs={{2,0},{5,1},{0,2},{7,3},{6,4},{1,5},{4,6},{3,7},{10,8},{13,9},{8,1... | collective-permute-start | bytes 393224 | tf_op jit(solution)/shard_map/ppermute | solution.py:493
  42.4 0.8 %collective-permute-start.13 = (bf16[128,512]{1,0:T(8,128)(2,1)S(1)}, bf16[128,512]{1,0:T(8,128)(2,1)S(1)}, u32[]{:S(2)}, u32[]{:S(2)}) collective-permute-start(bf16[128,512]{1,0:T(8,128)(2,1)S(1)} %get-tuple-element.51), channel_id=1, source_target_pairs={{8,0},{3,1},{10,2},{1,3},{12,4},{7,5},{14,6},{5,7},{0,8},{11,9},{2... | collective-permute-start | bytes 393224 | tf_op jit(solution)/shard_map/ppermute | solution.py:493
  43.1 0.6 %collective-permute-done.16.refs_1_ = bf16[128,512]{1,0:T(8,128)(2,1)S(1)} collective-permute-done((bf16[128,512]{1,0:T(8,128)(2,1)S(1)}, bf16[128,512]{1,0:T(8,128)(2,1)S(1)}, u32[]{:S(2)}, u32[]{:S(2)}) %collective-permute-start.16) | collective-permute-done | bytes 131104 | tf_op jit(solution)/shard_map/ppermute | solution.py:493
  43.8 1.0 %collective-permute-start.14 = (bf16[128,512]{1,0:T(8,128)(2,1)S(1)}, bf16[128,512]{1,0:T(8,128)(2,1)S(1)}, u32[]{:S(2)}, u32[]{:S(2)}) collective-permute-start(bf16[128,512]{1,0:T(8,128)(2,1)S(1)} %get-tuple-element.52), channel_id=1, source_target_pairs={{4,0},{9,1},{6,2},{11,3},{0,4},{13,5},{2,6},{15,7},{12,8},{1,9},{1... | collective-permute-start | bytes 393224 | tf_op jit(solution)/shard_map/ppermute | solution.py:493
  44.7 0.6 %collective-permute-start.15 = (bf16[128,512]{1,0:T(8,128)(2,1)S(1)}, bf16[128,512]{1,0:T(8,128)(2,1)S(1)}, u32[]{:S(2)}, u32[]{:S(2)}) collective-permute-start(bf16[128,512]{1,0:T(8,128)(2,1)S(1)} %get-tuple-element.53), channel_id=1, source_target_pairs={{1,0},{0,1},{3,2},{2,3},{5,4},{4,5},{7,6},{6,7},{9,8},{8,9},{11,10... | collective-permute-start | bytes 393224 | tf_op jit(solution)/shard_map/ppermute | solution.py:493
  45.5 2.1 %collective-permute-done.19.refs_4_ = bf16[128,512]{1,0:T(8,128)(2,1)S(1)} collective-permute-done((bf16[128,512]{1,0:T(8,128)(2,1)S(1)}, bf16[128,512]{1,0:T(8,128)(2,1)S(1)}, u32[]{:S(2)}, u32[]{:S(2)}) %collective-permute-start.19) | collective-permute-done | bytes 131104 | tf_op jit(solution)/shard_map/ppermute | solution.py:493
  47.6 0.9 %shard_map.33.refs_3_ = bf16[4,2,128,512]{3,2,1,0:T(8,128)(2,1)} custom-call(bf16[4,2,128,512]{3,2,1,0:T(8,128)(2,1)S(1)} %bitcast.3, bf16[128,512]{1,0:T(8,128)(2,1)S(1)} %get-tuple-element.54.refs_0_, bf16[128,512]{1,0:T(8,128)(2,1)S(1)} %collective-permute-done.16.refs_1_, bf16[128,512]{1,0:T(8,128)(2,1)S(1)} %collective-permute-done.17.refs_2_, ...), custom_call_target="tpu_custom_call" | custom-call | tf_op jit(solution)/shard_map/pallas_call | solution.py:456
  48.7 0.8 %shard_map.34 = bf16[4,2,128,512]{3,2,1,0:T(8,128)(2,1)} custom-call(bf16[4,2,128,512]{3,2,1,0:T(8,128)(2,1)S(1)} %bitcast.4, bf16[128,512]{1,0:T(8,128)(2,1)S(1)} %collective-permute-done.13.refs_0_, bf16[128,512]{1,0:T(8,128)(2,1)S(1)} %collective-permute-done.14.refs_1_, ...), custom_call_target="tpu_custom_call", output_to_operand_aliasing={{}: (4, {})} | custom-call | tf_op jit(solution)/shard_map/pallas_call | solution.py:456
  (19 shorter events, 1.8 us)
Async XLA Ops:
  0.0 1.2 %copy-start.1 = (bf16[1,8,128,512]{3,2,1,0:T(8,128)(2,1)S(1)}, bf16[1,8,128,512]{3,2,1,0:T(8,128)(2,1)}, u32[]{:S(2)}) copy-start(bf16[1,8,128,512]{3,2,1,0:T(8,128)(2,1)} %param.2) | copy-start | bytes 3145732
  1.3 7.3 %collective-permute-start = (bf16[128,512]{1,0:T(8,128)(2,1)S(1)}, bf16[128,512]{1,0:T(8,128)(2,1)S(1)}, u32[]{:S(2)}, u32[]{:S(2)}) collective-permute-start(bf16[128,512]{1,0:T(8,128)(2,1)S(1)} %get-tuple-element.33), channel_id=1, source_target_pairs={{0,3},{1,4},{2,1},{3,6},{4,7},{5,0},{6,5},{7,2},{8,11},{9,12},{10,... | collective-permute-start | bytes 393224 | tf_op jit(solution)/shard_map/ppermute | solution.py:493
  3.7 5.7 %collective-permute-start.1 = (bf16[128,512]{1,0:T(8,128)(2,1)S(1)}, bf16[128,512]{1,0:T(8,128)(2,1)S(1)}, u32[]{:S(2)}, u32[]{:S(2)}) collective-permute-start(bf16[128,512]{1,0:T(8,128)(2,1)S(1)} %get-tuple-element.34), channel_id=1, source_target_pairs={{0,9},{1,2},{2,11},{3,0},{4,13},{5,6},{6,15},{7,4},{8,1},{9,10},{1... | collective-permute-start | bytes 393224 | tf_op jit(solution)/shard_map/ppermute | solution.py:493
  5.6 4.8 %collective-permute-start.2 = (bf16[128,512]{1,0:T(8,128)(2,1)S(1)}, bf16[128,512]{1,0:T(8,128)(2,1)S(1)}, u32[]{:S(2)}, u32[]{:S(2)}) collective-permute-start(bf16[128,512]{1,0:T(8,128)(2,1)S(1)} %get-tuple-element.35), channel_id=1, source_target_pairs={{0,5},{1,8},{2,7},{3,10},{4,1},{5,12},{6,3},{7,14},{8,13},{9,0},{1... | collective-permute-start | bytes 393224 | tf_op jit(solution)/shard_map/ppermute | solution.py:493
  5.6 6.3 %collective-permute-start.3 = (bf16[128,512]{1,0:T(8,128)(2,1)S(1)}, bf16[128,512]{1,0:T(8,128)(2,1)S(1)}, u32[]{:S(2)}, u32[]{:S(2)}) collective-permute-start(bf16[128,512]{1,0:T(8,128)(2,1)S(1)} %get-tuple-element.36), channel_id=1, source_target_pairs={{0,2},{1,5},{2,0},{3,7},{4,6},{5,1},{6,4},{7,3},{8,10},{9,13},{10,... | collective-permute-start | bytes 393224 | tf_op jit(solution)/shard_map/ppermute | solution.py:493
  7.1 6.1 %collective-permute-start.4 = (bf16[128,512]{1,0:T(8,128)(2,1)S(1)}, bf16[128,512]{1,0:T(8,128)(2,1)S(1)}, u32[]{:S(2)}, u32[]{:S(2)}) collective-permute-start(bf16[128,512]{1,0:T(8,128)(2,1)S(1)} %get-tuple-element.39), channel_id=1, source_target_pairs={{0,8},{1,3},{2,10},{3,1},{4,12},{5,7},{6,14},{7,5},{8,0},{9,11},{1... | collective-permute-start | bytes 393224 | tf_op jit(solution)/shard_map/ppermute | solution.py:493
  8.6 5.0 %collective-permute-start.5 = (bf16[128,512]{1,0:T(8,128)(2,1)S(1)}, bf16[128,512]{1,0:T(8,128)(2,1)S(1)}, u32[]{:S(2)}, u32[]{:S(2)}) collective-permute-start(bf16[128,512]{1,0:T(8,128)(2,1)S(1)} %get-tuple-element.40), channel_id=1, source_target_pairs={{0,4},{1,9},{2,6},{3,11},{4,0},{5,13},{6,2},{7,15},{8,12},{9,1},{1... | collective-permute-start | bytes 393224 | tf_op jit(solution)/shard_map/ppermute | solution.py:493
  9.4 4.2 %collective-permute-start.6 = (bf16[128,512]{1,0:T(8,128)(2,1)S(1)}, bf16[128,512]{1,0:T(8,128)(2,1)S(1)}, u32[]{:S(2)}, u32[]{:S(2)}) collective-permute-start(bf16[128,512]{1,0:T(8,128)(2,1)S(1)} %get-tuple-element.41), channel_id=1, source_target_pairs={{0,1},{1,0},{2,3},{3,2},{4,5},{5,4},{6,7},{7,6},{8,9},{9,8},{10,11... | collective-permute-start | bytes 393224 | tf_op jit(solution)/shard_map/ppermute | solution.py:493
  14.0 8.4 %collective-permute-start.7 = (bf16[272,128]{1,0:T(8,128)(2,1)S(1)}, bf16[272,128]{1,0:T(8,128)(2,1)S(1)}, u32[]{:S(2)}, u32[]{:S(2)}) collective-permute-start(bf16[272,128]{1,0:T(8,128)(2,1)S(1)} %get-tuple-element.43), channel_id=1, source_target_pairs={{0,22},{1,23},{2,20},{3,21},{4,18},{5,19},{6,16},{7,17},{8,30},{9,... | collective-permute-start | bytes 208904 | tf_op jit(solution)/shard_map/ppermute | solution.py:493
  17.2 6.3 %collective-permute-start.8 = (bf16[272,128]{1,0:T(8,128)(2,1)S(1)}, bf16[272,128]{1,0:T(8,128)(2,1)S(1)}, u32[]{:S(2)}, u32[]{:S(2)}) collective-permute-start(bf16[272,128]{1,0:T(8,128)(2,1)S(1)} %get-tuple-element.44), channel_id=1, source_target_pairs={{0,14},{1,15},{2,12},{3,13},{4,10},{5,11},{6,8},{7,9},{8,6},{9,7},... | collective-permute-start | bytes 208904 | tf_op jit(solution)/shard_map/ppermute | solution.py:493
  19.7 6.1 %collective-permute-start.9 = (bf16[272,128]{1,0:T(8,128)(2,1)S(1)}, bf16[272,128]{1,0:T(8,128)(2,1)S(1)}, u32[]{:S(2)}, u32[]{:S(2)}) collective-permute-start(bf16[272,128]{1,0:T(8,128)(2,1)S(1)} %get-tuple-element.45), channel_id=1, source_target_pairs={{0,24},{1,25},{2,26},{3,27},{4,28},{5,29},{6,30},{7,31},{8,16},{9,... | collective-permute-start | bytes 208904 | tf_op jit(solution)/shard_map/ppermute | solution.py:493
  26.0 21.6 %copy-start = (bf16[1,8,128,512]{3,2,1,0:T(8,128)(2,1)S(1)}, bf16[1,8,128,512]{3,2,1,0:T(8,128)(2,1)}, u32[]{:S(2)}) copy-start(bf16[1,8,128,512]{3,2,1,0:T(8,128)(2,1)} %param.3) | copy-start | bytes 3145732
  26.0 7.8 %collective-permute-start.10 = (bf16[272,128]{1,0:T(8,128)(2,1)S(1)}, bf16[272,128]{1,0:T(8,128)(2,1)S(1)}, u32[]{:S(2)}, u32[]{:S(2)}) collective-permute-start(bf16[272,128]{1,0:T(8,128)(2,1)S(1)} %get-tuple-element.48), channel_id=1, source_target_pairs={{0,22},{1,23},{2,20},{3,21},{4,18},{5,19},{6,16},{7,17},{8,30},{9,... | collective-permute-start | bytes 208904 | tf_op jit(solution)/shard_map/ppermute | solution.py:493
  27.7 7.3 %collective-permute-start.11 = (bf16[272,128]{1,0:T(8,128)(2,1)S(1)}, bf16[272,128]{1,0:T(8,128)(2,1)S(1)}, u32[]{:S(2)}, u32[]{:S(2)}) collective-permute-start(bf16[272,128]{1,0:T(8,128)(2,1)S(1)} %get-tuple-element.49), channel_id=1, source_target_pairs={{0,14},{1,15},{2,12},{3,13},{4,10},{5,11},{6,8},{7,9},{8,6},{9,7},... | collective-permute-start | bytes 208904 | tf_op jit(solution)/shard_map/ppermute | solution.py:493
  29.5 6.1 %collective-permute-start.12 = (bf16[272,128]{1,0:T(8,128)(2,1)S(1)}, bf16[272,128]{1,0:T(8,128)(2,1)S(1)}, u32[]{:S(2)}, u32[]{:S(2)}) collective-permute-start(bf16[272,128]{1,0:T(8,128)(2,1)S(1)} %get-tuple-element.50), channel_id=1, source_target_pairs={{0,24},{1,25},{2,26},{3,27},{4,28},{5,29},{6,30},{7,31},{8,16},{9,... | collective-permute-start | bytes 208904 | tf_op jit(solution)/shard_map/ppermute | solution.py:493
  39.3 4.4 %collective-permute-start.16 = (bf16[128,512]{1,0:T(8,128)(2,1)S(1)}, bf16[128,512]{1,0:T(8,128)(2,1)S(1)}, u32[]{:S(2)}, u32[]{:S(2)}) collective-permute-start(bf16[128,512]{1,0:T(8,128)(2,1)S(1)} %get-tuple-element.55), channel_id=1, source_target_pairs={{3,0},{4,1},{1,2},{6,3},{7,4},{0,5},{5,6},{2,7},{11,8},{12,9},{9,1... | collective-permute-start | bytes 393224 | tf_op jit(solution)/shard_map/ppermute | solution.py:493
  39.4 5.3 %collective-permute-start.17 = (bf16[128,512]{1,0:T(8,128)(2,1)S(1)}, bf16[128,512]{1,0:T(8,128)(2,1)S(1)}, u32[]{:S(2)}, u32[]{:S(2)}) collective-permute-start(bf16[128,512]{1,0:T(8,128)(2,1)S(1)} %get-tuple-element.56), channel_id=1, source_target_pairs={{9,0},{2,1},{11,2},{0,3},{13,4},{6,5},{15,6},{4,7},{1,8},{10,9},{3... | collective-permute-start | bytes 393224 | tf_op jit(solution)/shard_map/ppermute | solution.py:493
  41.1 4.4 %collective-permute-start.18 = (bf16[128,512]{1,0:T(8,128)(2,1)S(1)}, bf16[128,512]{1,0:T(8,128)(2,1)S(1)}, u32[]{:S(2)}, u32[]{:S(2)}) collective-permute-start(bf16[128,512]{1,0:T(8,128)(2,1)S(1)} %get-tuple-element.57), channel_id=1, source_target_pairs={{5,0},{8,1},{7,2},{10,3},{1,4},{12,5},{3,6},{14,7},{13,8},{0,9},{1... | collective-permute-start | bytes 393224 | tf_op jit(solution)/shard_map/ppermute | solution.py:493
  41.2 6.4 %collective-permute-start.19 = (bf16[128,512]{1,0:T(8,128)(2,1)S(1)}, bf16[128,512]{1,0:T(8,128)(2,1)S(1)}, u32[]{:S(2)}, u32[]{:S(2)}) collective-permute-start(bf16[128,512]{1,0:T(8,128)(2,1)S(1)} %get-tuple-element.58), channel_id=1, source_target_pairs={{2,0},{5,1},{0,2},{7,3},{6,4},{1,5},{4,6},{3,7},{10,8},{13,9},{8,1... | collective-permute-start | bytes 393224 | tf_op jit(solution)/shard_map/ppermute | solution.py:493
  42.4 6.2 %collective-permute-start.13 = (bf16[128,512]{1,0:T(8,128)(2,1)S(1)}, bf16[128,512]{1,0:T(8,128)(2,1)S(1)}, u32[]{:S(2)}, u32[]{:S(2)}) collective-permute-start(bf16[128,512]{1,0:T(8,128)(2,1)S(1)} %get-tuple-element.51), channel_id=1, source_target_pairs={{8,0},{3,1},{10,2},{1,3},{12,4},{7,5},{14,6},{5,7},{0,8},{11,9},{2... | collective-permute-start | bytes 393224 | tf_op jit(solution)/shard_map/ppermute | solution.py:493
  43.8 5.0 %collective-permute-start.14 = (bf16[128,512]{1,0:T(8,128)(2,1)S(1)}, bf16[128,512]{1,0:T(8,128)(2,1)S(1)}, u32[]{:S(2)}, u32[]{:S(2)}) collective-permute-start(bf16[128,512]{1,0:T(8,128)(2,1)S(1)} %get-tuple-element.52), channel_id=1, source_target_pairs={{4,0},{9,1},{6,2},{11,3},{0,4},{13,5},{2,6},{15,7},{12,8},{1,9},{1... | collective-permute-start | bytes 393224 | tf_op jit(solution)/shard_map/ppermute | solution.py:493
  44.7 4.0 %collective-permute-start.15 = (bf16[128,512]{1,0:T(8,128)(2,1)S(1)}, bf16[128,512]{1,0:T(8,128)(2,1)S(1)}, u32[]{:S(2)}, u32[]{:S(2)}) collective-permute-start(bf16[128,512]{1,0:T(8,128)(2,1)S(1)} %get-tuple-element.53), channel_id=1, source_target_pairs={{1,0},{0,1},{3,2},{2,3},{5,4},{4,5},{7,6},{6,7},{9,8},{8,9},{11,10... | collective-permute-start | bytes 393224 | tf_op jit(solution)/shard_map/ppermute | solution.py:493

commit v11 on v10

--- a/solution.py
+++ b/solution.py
@@ -306,6 +306,13 @@
         message_ref[...] = to_message(total - value, order)
     own = direction_ref[...].astype(jnp.float32)[:1]
     directions_ref[...] = stacked([own] + [vector_of(arrived_ref[...], order) for arrived_ref in arrived_refs])
+
+
+def base_kernel(rest_count, order, left_ref, total_ref, directions_ref, base_ref):
+    outer = outer_products(directions_ref[...])
+    own = Place(rest_count).quarter
+    for quarter, value in enumerate(pack(lambda i, j: outer[i, j], order)):
+        base_ref[quarter] = jnp.where(quarter == own, total_ref[...], left_ref[quarter]) + value
 
 
 def assemble(upper, count):
@@ -384,19 +391,15 @@
     return accum_identity, accum
 
 
-def update_kernel(rest_count, order, scale, left_ref, total_ref, directions_ref, *refs):
+def update_kernel(rest_count, order, scale, base_ref, *refs):
     rest_refs, quarters_ref = refs[:3], refs[-1]
     block_refs, update_refs = refs[3 : 3 + len(refs[4:]) // 2], refs[3 + len(refs[4:]) // 2 : -1]
     place = Place(rest_count)
-    quarters_ref[place.quarter] = total_ref[...]
+    quarters_ref[place.quarter] = base_ref[place.quarter]
     for step, rest_ref in enumerate(rest_refs):
         quarter = place.quarter_at(step)
-        quarters_ref[quarter] = left_ref[quarter] + from_message(rest_ref[...], order)
-    outer = outer_products(directions_ref[...])
-    blocks = {
-        key: value + outer[key]
-        for key, value in unpack([quarters_ref[quarter] for quarter in range(4)], order).items()
-    }
+        quarters_ref[quarter] = base_ref[quarter] + from_message(rest_ref[...], order)
+    blocks = unpack([quarters_ref[quarter] for quarter in range(4)], order)
     trace_sum = jnp.sum(sum(diagonal(blocks[i, i]) for i in range(order // BLOCK)))
     shrink = 1.0 / (trace_sum + epsilon)
     count, ratio = order // WIDE, WIDE // BLOCK
@@ -523,12 +526,11 @@
         own_direction,
         *swap(parts, OWNERS),
     )
+    base = call(functools.partial(base_kernel, rest_count, order), packed, left, total, directions)
     own_update, *updates = call(
         functools.partial(update_kernel, rest_count, order, scale),
         blocks,
-        left,
-        total,
-        directions,
+        base,
         *swap(rests, OWNERS),
         *rows,
         scratch=[pltpu.VMEM(packed.shape, packed.dtype)],

time: 49.7 us -> 49.5 us (level)
    pallas_call x5 -> x6, Pallas kernels: 5.33 us -> 5.45 us  [call(): pl.pallas_call(kernel, out_shape=out_shape, in_specs=[vmem] * len(operand...]
where the time goes in v11:
time: 49.5 us; the launch traced here: 49.4 us
  starting transfers between devices  25.9 us (52%)
  waiting for transfers between devices  15 us (30%)
  Pallas kernels  7.24 us (15%)
  local copies, waits for them, and re-layouts  1.23 us (2%)
    ppermute x20, starting transfers between devices, swap(): lax.ppermute(array, AXES, permute)  25.9 us
    ppermute x20, waiting for transfers between devices, swap(): lax.ppermute(array, AXES, permute)  15 us
    pallas_call x6, Pallas kernels, call(): pl.pallas_call(kernel, out_shape=out_shape, in_specs=[vmem] * len(operand...  5.45 us
    pallas_call x2, Pallas kernels, new_weights(): pl.pallas_call(functools.partial(weights_kernel, rest_count, numbers), ou...  1.79 us
    unnamed x4, local copies, waits for them, and re-layouts  1.23 us
  transfers between devices with their start and end apart: 20, of which 15 were waited for; matrix products, arithmetic and copies ran while one was open for 0% of the time, Pallas kernels for 4%

profile of v11, /device:TPU:0, one launch (start us, length us, event | category | flops | bytes accessed | tf_op | source)
XLA Modules:
  0.0 49.4 jit_solution(10138847782907717825)
XLA Ops:
  0.0 1.2 %copy-done.1 = bf16[1,8,128,512]{3,2,1,0:T(8,128)(2,1)S(1)} copy-done((bf16[1,8,128,512]{3,2,1,0:T(8,128)(2,1)S(1)}, bf16[1,8,128,512]{3,2,1,0:T(8,128)(2,1)}, u32[]{:S(2)}) %copy-start.1) | copy-done | bytes 1048600
  1.3 2.4 %collective-permute-start = (bf16[128,512]{1,0:T(8,128)(2,1)S(1)}, bf16[128,512]{1,0:T(8,128)(2,1)S(1)}, u32[]{:S(2)}, u32[]{:S(2)}) collective-permute-start(bf16[128,512]{1,0:T(8,128)(2,1)S(1)} %get-tuple-element.33), channel_id=1, source_target_pairs={{0,3},{1,4},{2,1},{3,6},{4,7},{5,0},{6,5},{7,2},{8,11},{9,12},{10,... | collective-permute-start | bytes 393224 | tf_op jit(solution)/shard_map/ppermute | solution.py:496
  3.7 1.9 %collective-permute-start.1 = (bf16[128,512]{1,0:T(8,128)(2,1)S(1)}, bf16[128,512]{1,0:T(8,128)(2,1)S(1)}, u32[]{:S(2)}, u32[]{:S(2)}) collective-permute-start(bf16[128,512]{1,0:T(8,128)(2,1)S(1)} %get-tuple-element.34), channel_id=1, source_target_pairs={{0,9},{1,2},{2,11},{3,0},{4,13},{5,6},{6,15},{7,4},{8,1},{9,10},{1... | collective-permute-start | bytes 393224 | tf_op jit(solution)/shard_map/ppermute | solution.py:496
  5.6 1.5 %collective-permute-start.3 = (bf16[128,512]{1,0:T(8,128)(2,1)S(1)}, bf16[128,512]{1,0:T(8,128)(2,1)S(1)}, u32[]{:S(2)}, u32[]{:S(2)}) collective-permute-start(bf16[128,512]{1,0:T(8,128)(2,1)S(1)} %get-tuple-element.36), channel_id=1, source_target_pairs={{0,2},{1,5},{2,0},{3,7},{4,6},{5,1},{6,4},{7,3},{8,10},{9,13},{10,... | collective-permute-start | bytes 393224 | tf_op jit(solution)/shard_map/ppermute | solution.py:496
  7.1 1.5 %collective-permute-start.4 = (bf16[128,512]{1,0:T(8,128)(2,1)S(1)}, bf16[128,512]{1,0:T(8,128)(2,1)S(1)}, u32[]{:S(2)}, u32[]{:S(2)}) collective-permute-start(bf16[128,512]{1,0:T(8,128)(2,1)S(1)} %get-tuple-element.39), channel_id=1, source_target_pairs={{0,8},{1,3},{2,10},{3,1},{4,12},{5,7},{6,14},{7,5},{8,0},{9,11},{1... | collective-permute-start | bytes 393224 | tf_op jit(solution)/shard_map/ppermute | solution.py:496
  8.6 0.6 %collective-permute-start.5 = (bf16[128,512]{1,0:T(8,128)(2,1)S(1)}, bf16[128,512]{1,0:T(8,128)(2,1)S(1)}, u32[]{:S(2)}, u32[]{:S(2)}) collective-permute-start(bf16[128,512]{1,0:T(8,128)(2,1)S(1)} %get-tuple-element.40), channel_id=1, source_target_pairs={{0,4},{1,9},{2,6},{3,11},{4,0},{5,13},{6,2},{7,15},{8,12},{9,1},{1... | collective-permute-start | bytes 393224 | tf_op jit(solution)/shard_map/ppermute | solution.py:496
  9.5 0.9 %collective-permute-done.2.refs_3_.refs_6_ = bf16[128,512]{1,0:T(8,128)(2,1)S(1)} collective-permute-done((bf16[128,512]{1,0:T(8,128)(2,1)S(1)}, bf16[128,512]{1,0:T(8,128)(2,1)S(1)}, u32[]{:S(2)}, u32[]{:S(2)}) %collective-permute-start.2) | collective-permute-done | bytes 131104 | tf_op jit(solution)/shard_map/ppermute | solution.py:496
  10.4 1.5 %collective-permute-done.3.refs_4_.refs_7_ = bf16[128,512]{1,0:T(8,128)(2,1)S(1)} collective-permute-done((bf16[128,512]{1,0:T(8,128)(2,1)S(1)}, bf16[128,512]{1,0:T(8,128)(2,1)S(1)}, u32[]{:S(2)}, u32[]{:S(2)}) %collective-permute-start.3) | collective-permute-done | bytes 131104 | tf_op jit(solution)/shard_map/ppermute | solution.py:496
  11.9 0.9 %shard_map.29 = (f32[4,264,128]{2,1,0:T(8,128)S(1)}, bf16[16,512]{1,0:T(8,128)(2,1)S(1)}) custom-call(bf16[128,512]{1,0:T(8,128)(2,1)S(1)} %get-tuple-element.32.refs_0_.refs_3_, bf16[128,512]{1,0:T(8,128)(2,1)S(1)} %collective-permute-done.refs_1_.refs_4_, bf16[128,512]{1,0:T(8,128)(2,1)S(1)} %collective-permute-done.1.refs_2_.refs_5_, ...), custom_call_target="tpu_custom_call" | custom-call | tf_op jit(solution)/shard_map/pallas_call | solution.py:93
  13.5 0.5 shard_map.30
  14.0 3.1 %collective-permute-start.7 = (bf16[272,128]{1,0:T(8,128)(2,1)S(1)}, bf16[272,128]{1,0:T(8,128)(2,1)S(1)}, u32[]{:S(2)}, u32[]{:S(2)}) collective-permute-start(bf16[272,128]{1,0:T(8,128)(2,1)S(1)} %get-tuple-element.43), channel_id=1, source_target_pairs={{0,22},{1,23},{2,20},{3,21},{4,18},{5,19},{6,16},{7,17},{8,30},{9,... | collective-permute-start | bytes 208904 | tf_op jit(solution)/shard_map/ppermute | solution.py:496
  17.2 2.6 %collective-permute-start.8 = (bf16[272,128]{1,0:T(8,128)(2,1)S(1)}, bf16[272,128]{1,0:T(8,128)(2,1)S(1)}, u32[]{:S(2)}, u32[]{:S(2)}) collective-permute-start(bf16[272,128]{1,0:T(8,128)(2,1)S(1)} %get-tuple-element.44), channel_id=1, source_target_pairs={{0,14},{1,15},{2,12},{3,13},{4,10},{5,11},{6,8},{7,9},{8,6},{9,7},... | collective-permute-start | bytes 208904 | tf_op jit(solution)/shard_map/ppermute | solution.py:496
  19.7 0.5 %collective-permute-start.9 = (bf16[272,128]{1,0:T(8,128)(2,1)S(1)}, bf16[272,128]{1,0:T(8,128)(2,1)S(1)}, u32[]{:S(2)}, u32[]{:S(2)}) collective-permute-start(bf16[272,128]{1,0:T(8,128)(2,1)S(1)} %get-tuple-element.45), channel_id=1, source_target_pairs={{0,24},{1,25},{2,26},{3,27},{4,28},{5,29},{6,30},{7,31},{8,16},{9,... | collective-permute-start | bytes 208904 | tf_op jit(solution)/shard_map/ppermute | solution.py:496
  20.3 2.1 %collective-permute-done.7.refs_0_ = bf16[272,128]{1,0:T(8,128)(2,1)S(1)} collective-permute-done((bf16[272,128]{1,0:T(8,128)(2,1)S(1)}, bf16[272,128]{1,0:T(8,128)(2,1)S(1)}, u32[]{:S(2)}, u32[]{:S(2)}) %collective-permute-start.7) | collective-permute-done | bytes 69664 | tf_op jit(solution)/shard_map/ppermute | solution.py:496
  22.4 1.1 %collective-permute-done.8.refs_1_ = bf16[272,128]{1,0:T(8,128)(2,1)S(1)} collective-permute-done((bf16[272,128]{1,0:T(8,128)(2,1)S(1)}, bf16[272,128]{1,0:T(8,128)(2,1)S(1)}, u32[]{:S(2)}, u32[]{:S(2)}) %collective-permute-start.8) | collective-permute-done | bytes 69664 | tf_op jit(solution)/shard_map/ppermute | solution.py:496
  23.5 2.4 %collective-permute-done.9.refs_2_ = bf16[272,128]{1,0:T(8,128)(2,1)S(1)} collective-permute-done((bf16[272,128]{1,0:T(8,128)(2,1)S(1)}, bf16[272,128]{1,0:T(8,128)(2,1)S(1)}, u32[]{:S(2)}, u32[]{:S(2)}) %collective-permute-start.9) | collective-permute-done | bytes 69664 | tf_op jit(solution)/shard_map/ppermute | solution.py:496
  26.0 1.7 %collective-permute-start.10 = (bf16[272,128]{1,0:T(8,128)(2,1)S(1)}, bf16[272,128]{1,0:T(8,128)(2,1)S(1)}, u32[]{:S(2)}, u32[]{:S(2)}) collective-permute-start(bf16[272,128]{1,0:T(8,128)(2,1)S(1)} %get-tuple-element.48), channel_id=1, source_target_pairs={{0,22},{1,23},{2,20},{3,21},{4,18},{5,19},{6,16},{7,17},{8,30},{9,... | collective-permute-start | bytes 208904 | tf_op jit(solution)/shard_map/ppermute | solution.py:496
  27.7 1.8 %collective-permute-start.11 = (bf16[272,128]{1,0:T(8,128)(2,1)S(1)}, bf16[272,128]{1,0:T(8,128)(2,1)S(1)}, u32[]{:S(2)}, u32[]{:S(2)}) collective-permute-start(bf16[272,128]{1,0:T(8,128)(2,1)S(1)} %get-tuple-element.49), channel_id=1, source_target_pairs={{0,14},{1,15},{2,12},{3,13},{4,10},{5,11},{6,8},{7,9},{8,6},{9,7},... | collective-permute-start | bytes 208904 | tf_op jit(solution)/shard_map/ppermute | solution.py:496
  29.5 2.8 %collective-permute-start.12 = (bf16[272,128]{1,0:T(8,128)(2,1)S(1)}, bf16[272,128]{1,0:T(8,128)(2,1)S(1)}, u32[]{:S(2)}, u32[]{:S(2)}) collective-permute-start(bf16[272,128]{1,0:T(8,128)(2,1)S(1)} %get-tuple-element.50), channel_id=1, source_target_pairs={{0,24},{1,25},{2,26},{3,27},{4,28},{5,29},{6,30},{7,31},{8,16},{9,... | collective-permute-start | bytes 208904 | tf_op jit(solution)/shard_map/ppermute | solution.py:496
  32.5 1.3 %collective-permute-done.10.refs_0_ = bf16[272,128]{1,0:T(8,128)(2,1)S(1)} collective-permute-done((bf16[272,128]{1,0:T(8,128)(2,1)S(1)}, bf16[272,128]{1,0:T(8,128)(2,1)S(1)}, u32[]{:S(2)}, u32[]{:S(2)}) %collective-permute-start.10) | collective-permute-done | bytes 69664 | tf_op jit(solution)/shard_map/ppermute | solution.py:496
  33.8 1.2 %collective-permute-done.11.refs_1_ = bf16[272,128]{1,0:T(8,128)(2,1)S(1)} collective-permute-done((bf16[272,128]{1,0:T(8,128)(2,1)S(1)}, bf16[272,128]{1,0:T(8,128)(2,1)S(1)}, u32[]{:S(2)}, u32[]{:S(2)}) %collective-permute-start.11) | collective-permute-done | bytes 69664 | tf_op jit(solution)/shard_map/ppermute | solution.py:496
  34.9 0.6 %collective-permute-done.12.refs_2_ = bf16[272,128]{1,0:T(8,128)(2,1)S(1)} collective-permute-done((bf16[272,128]{1,0:T(8,128)(2,1)S(1)}, bf16[272,128]{1,0:T(8,128)(2,1)S(1)}, u32[]{:S(2)}, u32[]{:S(2)}) %collective-permute-start.12) | collective-permute-done | bytes 69664 | tf_op jit(solution)/shard_map/ppermute | solution.py:496
  35.6 3.6 %shard_map.33 = (bf16[128,512]{1,0:T(8,128)(2,1)S(1)}, bf16[128,512]{1,0:T(8,128)(2,1)S(1)}, bf16[128,512]{1,0:T(8,128)(2,1)S(1)}, bf16[128,512]{1,0:T(8,128)(2,...) custom-call(f32[4,264,128]{2,1,0:T(8,128)S(1)} %shard_map.32.base_re, ...), custom_call_target="tpu_custom_call" | custom-call | tf_op jit(solution)/shard_map/pallas_call | solution.py:93
  39.2 1.7 %collective-permute-start.17 = (bf16[128,512]{1,0:T(8,128)(2,1)S(1)}, bf16[128,512]{1,0:T(8,128)(2,1)S(1)}, u32[]{:S(2)}, u32[]{:S(2)}) collective-permute-start(bf16[128,512]{1,0:T(8,128)(2,1)S(1)} %get-tuple-element.56), channel_id=1, source_target_pairs={{9,0},{2,1},{11,2},{0,3},{13,4},{6,5},{15,6},{4,7},{1,8},{10,9},{3... | collective-permute-start | bytes 393224 | tf_op jit(solution)/shard_map/ppermute | solution.py:496
  41.0 1.2 %collective-permute-start.19 = (bf16[128,512]{1,0:T(8,128)(2,1)S(1)}, bf16[128,512]{1,0:T(8,128)(2,1)S(1)}, u32[]{:S(2)}, u32[]{:S(2)}) collective-permute-start(bf16[128,512]{1,0:T(8,128)(2,1)S(1)} %get-tuple-element.58), channel_id=1, source_target_pairs={{2,0},{5,1},{0,2},{7,3},{6,4},{1,5},{4,6},{3,7},{10,8},{13,9},{8,1... | collective-permute-start | bytes 393224 | tf_op jit(solution)/shard_map/ppermute | solution.py:496
  42.2 0.8 %collective-permute-start.13 = (bf16[128,512]{1,0:T(8,128)(2,1)S(1)}, bf16[128,512]{1,0:T(8,128)(2,1)S(1)}, u32[]{:S(2)}, u32[]{:S(2)}) collective-permute-start(bf16[128,512]{1,0:T(8,128)(2,1)S(1)} %get-tuple-element.51), channel_id=1, source_target_pairs={{8,0},{3,1},{10,2},{1,3},{12,4},{7,5},{14,6},{5,7},{0,8},{11,9},{2... | collective-permute-start | bytes 393224 | tf_op jit(solution)/shard_map/ppermute | solution.py:496
  43.0 0.6 %collective-permute-done.16.refs_1_ = bf16[128,512]{1,0:T(8,128)(2,1)S(1)} collective-permute-done((bf16[128,512]{1,0:T(8,128)(2,1)S(1)}, bf16[128,512]{1,0:T(8,128)(2,1)S(1)}, u32[]{:S(2)}, u32[]{:S(2)}) %collective-permute-start.16) | collective-permute-done | bytes 131104 | tf_op jit(solution)/shard_map/ppermute | solution.py:496
  43.6 1.0 %collective-permute-start.14 = (bf16[128,512]{1,0:T(8,128)(2,1)S(1)}, bf16[128,512]{1,0:T(8,128)(2,1)S(1)}, u32[]{:S(2)}, u32[]{:S(2)}) collective-permute-start(bf16[128,512]{1,0:T(8,128)(2,1)S(1)} %get-tuple-element.52), channel_id=1, source_target_pairs={{4,0},{9,1},{6,2},{11,3},{0,4},{13,5},{2,6},{15,7},{12,8},{1,9},{1... | collective-permute-start | bytes 393224 | tf_op jit(solution)/shard_map/ppermute | solution.py:496
  44.5 0.6 %collective-permute-start.15 = (bf16[128,512]{1,0:T(8,128)(2,1)S(1)}, bf16[128,512]{1,0:T(8,128)(2,1)S(1)}, u32[]{:S(2)}, u32[]{:S(2)}) collective-permute-start(bf16[128,512]{1,0:T(8,128)(2,1)S(1)} %get-tuple-element.53), channel_id=1, source_target_pairs={{1,0},{0,1},{3,2},{2,3},{5,4},{4,5},{7,6},{6,7},{9,8},{8,9},{11,10... | collective-permute-start | bytes 393224 | tf_op jit(solution)/shard_map/ppermute | solution.py:496
  45.3 2.1 %collective-permute-done.19.refs_4_ = bf16[128,512]{1,0:T(8,128)(2,1)S(1)} collective-permute-done((bf16[128,512]{1,0:T(8,128)(2,1)S(1)}, bf16[128,512]{1,0:T(8,128)(2,1)S(1)}, u32[]{:S(2)}, u32[]{:S(2)}) %collective-permute-start.19) | collective-permute-done | bytes 131104 | tf_op jit(solution)/shard_map/ppermute | solution.py:496
  47.4 1.0 %shard_map.34.refs_3_ = bf16[4,2,128,512]{3,2,1,0:T(8,128)(2,1)} custom-call(bf16[4,2,128,512]{3,2,1,0:T(8,128)(2,1)S(1)} %bitcast.3, bf16[128,512]{1,0:T(8,128)(2,1)S(1)} %get-tuple-element.54.refs_0_, bf16[128,512]{1,0:T(8,128)(2,1)S(1)} %collective-permute-done.16.refs_1_, bf16[128,512]{1,0:T(8,128)(2,1)S(1)} %collective-permute-done.17.refs_2_, ...), custom_call_target="tpu_custom_call" | custom-call | tf_op jit(solution)/shard_map/pallas_call | solution.py:459
  48.6 0.8 %shard_map.35 = bf16[4,2,128,512]{3,2,1,0:T(8,128)(2,1)} custom-call(bf16[4,2,128,512]{3,2,1,0:T(8,128)(2,1)S(1)} %bitcast.4, bf16[128,512]{1,0:T(8,128)(2,1)S(1)} %collective-permute-done.13.refs_0_, bf16[128,512]{1,0:T(8,128)(2,1)S(1)} %collective-permute-done.14.refs_1_, ...), custom_call_target="tpu_custom_call", output_to_operand_aliasing={{}: (4, {})} | custom-call | tf_op jit(solution)/shard_map/pallas_call | solution.py:459
  (20 shorter events, 2.0 us)
Async XLA Ops:
  0.0 1.2 %copy-start.1 = (bf16[1,8,128,512]{3,2,1,0:T(8,128)(2,1)S(1)}, bf16[1,8,128,512]{3,2,1,0:T(8,128)(2,1)}, u32[]{:S(2)}) copy-start(bf16[1,8,128,512]{3,2,1,0:T(8,128)(2,1)} %param.2) | copy-start | bytes 3145732
  1.3 7.3 %collective-permute-start = (bf16[128,512]{1,0:T(8,128)(2,1)S(1)}, bf16[128,512]{1,0:T(8,128)(2,1)S(1)}, u32[]{:S(2)}, u32[]{:S(2)}) collective-permute-start(bf16[128,512]{1,0:T(8,128)(2,1)S(1)} %get-tuple-element.33), channel_id=1, source_target_pairs={{0,3},{1,4},{2,1},{3,6},{4,7},{5,0},{6,5},{7,2},{8,11},{9,12},{10,... | collective-permute-start | bytes 393224 | tf_op jit(solution)/shard_map/ppermute | solution.py:496
  3.7 5.7 %collective-permute-start.1 = (bf16[128,512]{1,0:T(8,128)(2,1)S(1)}, bf16[128,512]{1,0:T(8,128)(2,1)S(1)}, u32[]{:S(2)}, u32[]{:S(2)}) collective-permute-start(bf16[128,512]{1,0:T(8,128)(2,1)S(1)} %get-tuple-element.34), channel_id=1, source_target_pairs={{0,9},{1,2},{2,11},{3,0},{4,13},{5,6},{6,15},{7,4},{8,1},{9,10},{1... | collective-permute-start | bytes 393224 | tf_op jit(solution)/shard_map/ppermute | solution.py:496
  5.6 4.8 %collective-permute-start.2 = (bf16[128,512]{1,0:T(8,128)(2,1)S(1)}, bf16[128,512]{1,0:T(8,128)(2,1)S(1)}, u32[]{:S(2)}, u32[]{:S(2)}) collective-permute-start(bf16[128,512]{1,0:T(8,128)(2,1)S(1)} %get-tuple-element.35), channel_id=1, source_target_pairs={{0,5},{1,8},{2,7},{3,10},{4,1},{5,12},{6,3},{7,14},{8,13},{9,0},{1... | collective-permute-start | bytes 393224 | tf_op jit(solution)/shard_map/ppermute | solution.py:496
  5.6 6.3 %collective-permute-start.3 = (bf16[128,512]{1,0:T(8,128)(2,1)S(1)}, bf16[128,512]{1,0:T(8,128)(2,1)S(1)}, u32[]{:S(2)}, u32[]{:S(2)}) collective-permute-start(bf16[128,512]{1,0:T(8,128)(2,1)S(1)} %get-tuple-element.36), channel_id=1, source_target_pairs={{0,2},{1,5},{2,0},{3,7},{4,6},{5,1},{6,4},{7,3},{8,10},{9,13},{10,... | collective-permute-start | bytes 393224 | tf_op jit(solution)/shard_map/ppermute | solution.py:496
  7.1 6.1 %collective-permute-start.4 = (bf16[128,512]{1,0:T(8,128)(2,1)S(1)}, bf16[128,512]{1,0:T(8,128)(2,1)S(1)}, u32[]{:S(2)}, u32[]{:S(2)}) collective-permute-start(bf16[128,512]{1,0:T(8,128)(2,1)S(1)} %get-tuple-element.39), channel_id=1, source_target_pairs={{0,8},{1,3},{2,10},{3,1},{4,12},{5,7},{6,14},{7,5},{8,0},{9,11},{1... | collective-permute-start | bytes 393224 | tf_op jit(solution)/shard_map/ppermute | solution.py:496
  8.6 5.0 %collective-permute-start.5 = (bf16[128,512]{1,0:T(8,128)(2,1)S(1)}, bf16[128,512]{1,0:T(8,128)(2,1)S(1)}, u32[]{:S(2)}, u32[]{:S(2)}) collective-permute-start(bf16[128,512]{1,0:T(8,128)(2,1)S(1)} %get-tuple-element.40), channel_id=1, source_target_pairs={{0,4},{1,9},{2,6},{3,11},{4,0},{5,13},{6,2},{7,15},{8,12},{9,1},{1... | collective-permute-start | bytes 393224 | tf_op jit(solution)/shard_map/ppermute | solution.py:496
  9.4 4.2 %collective-permute-start.6 = (bf16[128,512]{1,0:T(8,128)(2,1)S(1)}, bf16[128,512]{1,0:T(8,128)(2,1)S(1)}, u32[]{:S(2)}, u32[]{:S(2)}) collective-permute-start(bf16[128,512]{1,0:T(8,128)(2,1)S(1)} %get-tuple-element.41), channel_id=1, source_target_pairs={{0,1},{1,0},{2,3},{3,2},{4,5},{5,4},{6,7},{7,6},{8,9},{9,8},{10,11... | collective-permute-start | bytes 393224 | tf_op jit(solution)/shard_map/ppermute | solution.py:496
  14.0 8.4 %collective-permute-start.7 = (bf16[272,128]{1,0:T(8,128)(2,1)S(1)}, bf16[272,128]{1,0:T(8,128)(2,1)S(1)}, u32[]{:S(2)}, u32[]{:S(2)}) collective-permute-start(bf16[272,128]{1,0:T(8,128)(2,1)S(1)} %get-tuple-element.43), channel_id=1, source_target_pairs={{0,22},{1,23},{2,20},{3,21},{4,18},{5,19},{6,16},{7,17},{8,30},{9,... | collective-permute-start | bytes 208904 | tf_op jit(solution)/shard_map/ppermute | solution.py:496
  17.2 6.3 %collective-permute-start.8 = (bf16[272,128]{1,0:T(8,128)(2,1)S(1)}, bf16[272,128]{1,0:T(8,128)(2,1)S(1)}, u32[]{:S(2)}, u32[]{:S(2)}) collective-permute-start(bf16[272,128]{1,0:T(8,128)(2,1)S(1)} %get-tuple-element.44), channel_id=1, source_target_pairs={{0,14},{1,15},{2,12},{3,13},{4,10},{5,11},{6,8},{7,9},{8,6},{9,7},... | collective-permute-start | bytes 208904 | tf_op jit(solution)/shard_map/ppermute | solution.py:496
  19.7 6.1 %collective-permute-start.9 = (bf16[272,128]{1,0:T(8,128)(2,1)S(1)}, bf16[272,128]{1,0:T(8,128)(2,1)S(1)}, u32[]{:S(2)}, u32[]{:S(2)}) collective-permute-start(bf16[272,128]{1,0:T(8,128)(2,1)S(1)} %get-tuple-element.45), channel_id=1, source_target_pairs={{0,24},{1,25},{2,26},{3,27},{4,28},{5,29},{6,30},{7,31},{8,16},{9,... | collective-permute-start | bytes 208904 | tf_op jit(solution)/shard_map/ppermute | solution.py:496
  26.0 7.8 %collective-permute-start.10 = (bf16[272,128]{1,0:T(8,128)(2,1)S(1)}, bf16[272,128]{1,0:T(8,128)(2,1)S(1)}, u32[]{:S(2)}, u32[]{:S(2)}) collective-permute-start(bf16[272,128]{1,0:T(8,128)(2,1)S(1)} %get-tuple-element.48), channel_id=1, source_target_pairs={{0,22},{1,23},{2,20},{3,21},{4,18},{5,19},{6,16},{7,17},{8,30},{9,... | collective-permute-start | bytes 208904 | tf_op jit(solution)/shard_map/ppermute | solution.py:496
  27.7 7.3 %collective-permute-start.11 = (bf16[272,128]{1,0:T(8,128)(2,1)S(1)}, bf16[272,128]{1,0:T(8,128)(2,1)S(1)}, u32[]{:S(2)}, u32[]{:S(2)}) collective-permute-start(bf16[272,128]{1,0:T(8,128)(2,1)S(1)} %get-tuple-element.49), channel_id=1, source_target_pairs={{0,14},{1,15},{2,12},{3,13},{4,10},{5,11},{6,8},{7,9},{8,6},{9,7},... | collective-permute-start | bytes 208904 | tf_op jit(solution)/shard_map/ppermute | solution.py:496
  29.5 6.1 %collective-permute-start.12 = (bf16[272,128]{1,0:T(8,128)(2,1)S(1)}, bf16[272,128]{1,0:T(8,128)(2,1)S(1)}, u32[]{:S(2)}, u32[]{:S(2)}) collective-permute-start(bf16[272,128]{1,0:T(8,128)(2,1)S(1)} %get-tuple-element.50), channel_id=1, source_target_pairs={{0,24},{1,25},{2,26},{3,27},{4,28},{5,29},{6,30},{7,31},{8,16},{9,... | collective-permute-start | bytes 208904 | tf_op jit(solution)/shard_map/ppermute | solution.py:496
  32.5 14.9 %copy-start = (bf16[1,8,128,512]{3,2,1,0:T(8,128)(2,1)S(1)}, bf16[1,8,128,512]{3,2,1,0:T(8,128)(2,1)}, u32[]{:S(2)}) copy-start(bf16[1,8,128,512]{3,2,1,0:T(8,128)(2,1)} %param.3) | copy-start | bytes 3145732
  39.1 4.4 %collective-permute-start.16 = (bf16[128,512]{1,0:T(8,128)(2,1)S(1)}, bf16[128,512]{1,0:T(8,128)(2,1)S(1)}, u32[]{:S(2)}, u32[]{:S(2)}) collective-permute-start(bf16[128,512]{1,0:T(8,128)(2,1)S(1)} %get-tuple-element.55), channel_id=1, source_target_pairs={{3,0},{4,1},{1,2},{6,3},{7,4},{0,5},{5,6},{2,7},{11,8},{12,9},{9,1... | collective-permute-start | bytes 393224 | tf_op jit(solution)/shard_map/ppermute | solution.py:496
  39.2 5.3 %collective-permute-start.17 = (bf16[128,512]{1,0:T(8,128)(2,1)S(1)}, bf16[128,512]{1,0:T(8,128)(2,1)S(1)}, u32[]{:S(2)}, u32[]{:S(2)}) collective-permute-start(bf16[128,512]{1,0:T(8,128)(2,1)S(1)} %get-tuple-element.56), channel_id=1, source_target_pairs={{9,0},{2,1},{11,2},{0,3},{13,4},{6,5},{15,6},{4,7},{1,8},{10,9},{3... | collective-permute-start | bytes 393224 | tf_op jit(solution)/shard_map/ppermute | solution.py:496
  40.9 4.4 %collective-permute-start.18 = (bf16[128,512]{1,0:T(8,128)(2,1)S(1)}, bf16[128,512]{1,0:T(8,128)(2,1)S(1)}, u32[]{:S(2)}, u32[]{:S(2)}) collective-permute-start(bf16[128,512]{1,0:T(8,128)(2,1)S(1)} %get-tuple-element.57), channel_id=1, source_target_pairs={{5,0},{8,1},{7,2},{10,3},{1,4},{12,5},{3,6},{14,7},{13,8},{0,9},{1... | collective-permute-start | bytes 393224 | tf_op jit(solution)/shard_map/ppermute | solution.py:496
  41.0 6.4 %collective-permute-start.19 = (bf16[128,512]{1,0:T(8,128)(2,1)S(1)}, bf16[128,512]{1,0:T(8,128)(2,1)S(1)}, u32[]{:S(2)}, u32[]{:S(2)}) collective-permute-start(bf16[128,512]{1,0:T(8,128)(2,1)S(1)} %get-tuple-element.58), channel_id=1, source_target_pairs={{2,0},{5,1},{0,2},{7,3},{6,4},{1,5},{4,6},{3,7},{10,8},{13,9},{8,1... | collective-permute-start | bytes 393224 | tf_op jit(solution)/shard_map/ppermute | solution.py:496
  42.2 6.2 %collective-permute-start.13 = (bf16[128,512]{1,0:T(8,128)(2,1)S(1)}, bf16[128,512]{1,0:T(8,128)(2,1)S(1)}, u32[]{:S(2)}, u32[]{:S(2)}) collective-permute-start(bf16[128,512]{1,0:T(8,128)(2,1)S(1)} %get-tuple-element.51), channel_id=1, source_target_pairs={{8,0},{3,1},{10,2},{1,3},{12,4},{7,5},{14,6},{5,7},{0,8},{11,9},{2... | collective-permute-start | bytes 393224 | tf_op jit(solution)/shard_map/ppermute | solution.py:496
  43.6 5.0 %collective-permute-start.14 = (bf16[128,512]{1,0:T(8,128)(2,1)S(1)}, bf16[128,512]{1,0:T(8,128)(2,1)S(1)}, u32[]{:S(2)}, u32[]{:S(2)}) collective-permute-start(bf16[128,512]{1,0:T(8,128)(2,1)S(1)} %get-tuple-element.52), channel_id=1, source_target_pairs={{4,0},{9,1},{6,2},{11,3},{0,4},{13,5},{2,6},{15,7},{12,8},{1,9},{1... | collective-permute-start | bytes 393224 | tf_op jit(solution)/shard_map/ppermute | solution.py:496
  44.5 4.0 %collective-permute-start.15 = (bf16[128,512]{1,0:T(8,128)(2,1)S(1)}, bf16[128,512]{1,0:T(8,128)(2,1)S(1)}, u32[]{:S(2)}, u32[]{:S(2)}) collective-permute-start(bf16[128,512]{1,0:T(8,128)(2,1)S(1)} %get-tuple-element.53), channel_id=1, source_target_pairs={{1,0},{0,1},{3,2},{2,3},{5,4},{4,5},{7,6},{6,7},{9,8},{8,9},{11,10... | collective-permute-start | bytes 393224 | tf_op jit(solution)/shard_map/ppermute | solution.py:496

commit v12 on v11

--- a/solution.py
+++ b/solution.py
@@ -33,7 +33,7 @@
 
 def neighbour_steps():
     x, y, z = (0, 0, 1), (0, 1, 0), (1, 0, 0)
-    order = [(x, y), (z, x), (y, z)]
+    order = [(y, x), (x, z), (z, y)]
     return [tuple(flips_of(*way, pair=cross) for way in step) for cross in (1, 0) for step in order]
 
 
@@ -284,6 +284,11 @@
     outer = outer_products(stacked([direction]))
     for quarter, (value, known) in enumerate(zip(packed, pack(lambda i, j: outer[i, j], order))):
         left_ref[quarter] = value - known
+
+
+def middle_gram_kernel(early_ref, *refs):
+    for quarter, value in enumerate(packed_gram(refs[:-1])[0]):
+        refs[-1][quarter] = early_ref[quarter] + value
 
 
 def gram_kernel(rest_count, early_ref, direction_ref, *refs):
@@ -512,12 +517,13 @@
     early_left, own_direction = call(
         functools.partial(early_gram_kernel, EARLY / len(rows)), (packed, direction), *rows[:EARLY]
     )
+    early_left = call(middle_gram_kernel, packed, early_left, *[rows[number] for number in (5,)])
     left, *parts = call(
         functools.partial(gram_kernel, rest_count),
         (packed,) + (message,) * 3,
         early_left,
         own_direction,
-        *rows[EARLY:],
+        *[rows[number] for number in (6, 7)],
     )
     total, directions, *rests = call(
         functools.partial(gather_kernel, rest_count, order),

time: 49.5 us -> 49.4 us (level)
    pallas_call x6 -> x7, Pallas kernels: 5.45 us -> 5.63 us  [call(): pl.pallas_call(kernel, out_shape=out_shape, in_specs=[vmem] * len(operand...]
  transfers between devices with their start and end apart: 20 -> 20, of which waited for: 15 -> 12; matrix products, arithmetic and copies ran while one was open for 0% -> 0% of each run, Pallas kernels for 4% -> 5%
where the time goes in v12:
time: 49.4 us; the launch traced here: 49.2 us
  starting transfers between devices  25.7 us (52%)
  waiting for transfers between devices  14.8 us (30%)
  Pallas kernels  7.42 us (15%)
  local copies, waits for them, and re-layouts  1.23 us (2%)
    ppermute x20, starting transfers between devices, swap(): lax.ppermute(array, AXES, permute)  25.7 us
    ppermute x20, waiting for transfers between devices, swap(): lax.ppermute(array, AXES, permute)  14.8 us
    pallas_call x7, Pallas kernels, call(): pl.pallas_call(kernel, out_shape=out_shape, in_specs=[vmem] * len(operand...  5.63 us
    pallas_call x2, Pallas kernels, new_weights(): pl.pallas_call(functools.partial(weights_kernel, rest_count, numbers), ou...  1.79 us
    unnamed x4, local copies, waits for them, and re-layouts  1.23 us
  transfers between devices with their start and end apart: 20, of which 12 were waited for; matrix products, arithmetic and copies ran while one was open for 0% of the time, Pallas kernels for 5%

profile of v12, /device:TPU:0, one launch (start us, length us, event | category | flops | bytes accessed | tf_op | source)
XLA Modules:
  0.0 49.2 jit_solution(11023293250706254802)
XLA Ops:
  0.0 1.2 %copy-done.1 = bf16[1,8,128,512]{3,2,1,0:T(8,128)(2,1)S(1)} copy-done((bf16[1,8,128,512]{3,2,1,0:T(8,128)(2,1)S(1)}, bf16[1,8,128,512]{3,2,1,0:T(8,128)(2,1)}, u32[]{:S(2)}) %copy-start.1) | copy-done | bytes 1048600
  1.3 2.5 %collective-permute-start = (bf16[128,512]{1,0:T(8,128)(2,1)S(1)}, bf16[128,512]{1,0:T(8,128)(2,1)S(1)}, u32[]{:S(2)}, u32[]{:S(2)}) collective-permute-start(bf16[128,512]{1,0:T(8,128)(2,1)S(1)} %get-tuple-element.33), channel_id=1, source_target_pairs={{0,5},{1,2},{2,7},{3,0},{4,1},{5,6},{6,3},{7,4},{8,13},{9,10},{10,... | collective-permute-start | bytes 393224 | tf_op jit(solution)/shard_map/ppermute | solution.py:501
  3.8 1.8 %collective-permute-start.2 = (bf16[128,512]{1,0:T(8,128)(2,1)S(1)}, bf16[128,512]{1,0:T(8,128)(2,1)S(1)}, u32[]{:S(2)}, u32[]{:S(2)}) collective-permute-start(bf16[128,512]{1,0:T(8,128)(2,1)S(1)} %get-tuple-element.35), channel_id=1, source_target_pairs={{0,9},{1,4},{2,11},{3,6},{4,13},{5,0},{6,15},{7,2},{8,1},{9,12},{1... | collective-permute-start | bytes 393224 | tf_op jit(solution)/shard_map/ppermute | solution.py:501
  5.6 1.5 %collective-permute-start.3 = (bf16[128,512]{1,0:T(8,128)(2,1)S(1)}, bf16[128,512]{1,0:T(8,128)(2,1)S(1)}, u32[]{:S(2)}, u32[]{:S(2)}) collective-permute-start(bf16[128,512]{1,0:T(8,128)(2,1)S(1)} %get-tuple-element.36), channel_id=1, source_target_pairs={{0,4},{1,3},{2,6},{3,1},{4,0},{5,7},{6,2},{7,5},{8,12},{9,11},{10,... | collective-permute-start | bytes 393224 | tf_op jit(solution)/shard_map/ppermute | solution.py:501
  7.1 0.5 %collective-permute-start.4 = (bf16[128,512]{1,0:T(8,128)(2,1)S(1)}, bf16[128,512]{1,0:T(8,128)(2,1)S(1)}, u32[]{:S(2)}, u32[]{:S(2)}) collective-permute-start(bf16[128,512]{1,0:T(8,128)(2,1)S(1)} %get-tuple-element.38), channel_id=1, source_target_pairs={{0,2},{1,9},{2,0},{3,11},{4,6},{5,13},{6,4},{7,15},{8,10},{9,1},{1... | collective-permute-start | bytes 393224 | tf_op jit(solution)/shard_map/ppermute | solution.py:501
  7.6 1.6 %collective-permute-start.5 = (bf16[128,512]{1,0:T(8,128)(2,1)S(1)}, bf16[128,512]{1,0:T(8,128)(2,1)S(1)}, u32[]{:S(2)}, u32[]{:S(2)}) collective-permute-start(bf16[128,512]{1,0:T(8,128)(2,1)S(1)} %get-tuple-element.40), channel_id=1, source_target_pairs={{0,8},{1,5},{2,10},{3,7},{4,12},{5,1},{6,14},{7,3},{8,0},{9,13},{1... | collective-permute-start | bytes 393224 | tf_op jit(solution)/shard_map/ppermute | solution.py:501
  9.2 1.3 %collective-permute-done.3.refs_4_.refs_7_ = bf16[128,512]{1,0:T(8,128)(2,1)S(1)} collective-permute-done((bf16[128,512]{1,0:T(8,128)(2,1)S(1)}, bf16[128,512]{1,0:T(8,128)(2,1)S(1)}, u32[]{:S(2)}, u32[]{:S(2)}) %collective-permute-start.3) | collective-permute-done | bytes 131104 | tf_op jit(solution)/shard_map/ppermute | solution.py:501
  10.6 0.9 %shard_map.29 = (f32[4,264,128]{2,1,0:T(8,128)S(1)}, bf16[16,512]{1,0:T(8,128)(2,1)S(1)}) custom-call(bf16[128,512]{1,0:T(8,128)(2,1)S(1)} %get-tuple-element.32.refs_0_.refs_3_, bf16[128,512]{1,0:T(8,128)(2,1)S(1)} %collective-permute-done.refs_1_.refs_4_, bf16[128,512]{1,0:T(8,128)(2,1)S(1)} %collective-permute-done.1.refs_2_.refs_5_, ...), custom_call_target="tpu_custom_call" | custom-call | tf_op jit(solution)/shard_map/pallas_call | solution.py:93
  11.5 0.6 %collective-permute-done.4.refs_0_.refs_8_ = bf16[128,512]{1,0:T(8,128)(2,1)S(1)} collective-permute-done((bf16[128,512]{1,0:T(8,128)(2,1)S(1)}, bf16[128,512]{1,0:T(8,128)(2,1)S(1)}, u32[]{:S(2)}, u32[]{:S(2)}) %collective-permute-start.4) | collective-permute-done | bytes 131104 | tf_op jit(solution)/shard_map/ppermute | solution.py:501
  12.4 0.5 collective-permute-done.5.refs_0_.refs_9_
  13.2 4.5 %collective-permute-start.7 = (bf16[272,128]{1,0:T(8,128)(2,1)S(1)}, bf16[272,128]{1,0:T(8,128)(2,1)S(1)}, u32[]{:S(2)}, u32[]{:S(2)}) collective-permute-start(bf16[272,128]{1,0:T(8,128)(2,1)S(1)} %get-tuple-element.43), channel_id=1, source_target_pairs={{0,22},{1,23},{2,20},{3,21},{4,18},{5,19},{6,16},{7,17},{8,30},{9,... | collective-permute-start | bytes 208904 | tf_op jit(solution)/shard_map/ppermute | solution.py:501
  17.7 1.5 %collective-permute-start.8 = (bf16[272,128]{1,0:T(8,128)(2,1)S(1)}, bf16[272,128]{1,0:T(8,128)(2,1)S(1)}, u32[]{:S(2)}, u32[]{:S(2)}) collective-permute-start(bf16[272,128]{1,0:T(8,128)(2,1)S(1)} %get-tuple-element.44), channel_id=1, source_target_pairs={{0,14},{1,15},{2,12},{3,13},{4,10},{5,11},{6,8},{7,9},{8,6},{9,7},... | collective-permute-start | bytes 208904 | tf_op jit(solution)/shard_map/ppermute | solution.py:501
  19.4 1.7 %collective-permute-done.7.refs_0_ = bf16[272,128]{1,0:T(8,128)(2,1)S(1)} collective-permute-done((bf16[272,128]{1,0:T(8,128)(2,1)S(1)}, bf16[272,128]{1,0:T(8,128)(2,1)S(1)}, u32[]{:S(2)}, u32[]{:S(2)}) %collective-permute-start.7) | collective-permute-done | bytes 69664 | tf_op jit(solution)/shard_map/ppermute | solution.py:501
  21.2 2.6 %collective-permute-done.8.refs_1_ = bf16[272,128]{1,0:T(8,128)(2,1)S(1)} collective-permute-done((bf16[272,128]{1,0:T(8,128)(2,1)S(1)}, bf16[272,128]{1,0:T(8,128)(2,1)S(1)}, u32[]{:S(2)}, u32[]{:S(2)}) %collective-permute-start.8) | collective-permute-done | bytes 69664 | tf_op jit(solution)/shard_map/ppermute | solution.py:501
  23.8 1.5 %collective-permute-done.9.refs_2_ = bf16[272,128]{1,0:T(8,128)(2,1)S(1)} collective-permute-done((bf16[272,128]{1,0:T(8,128)(2,1)S(1)}, bf16[272,128]{1,0:T(8,128)(2,1)S(1)}, u32[]{:S(2)}, u32[]{:S(2)}) %collective-permute-start.9) | collective-permute-done | bytes 69664 | tf_op jit(solution)/shard_map/ppermute | solution.py:501
  25.4 0.9 %collective-permute-start.10 = (bf16[272,128]{1,0:T(8,128)(2,1)S(1)}, bf16[272,128]{1,0:T(8,128)(2,1)S(1)}, u32[]{:S(2)}, u32[]{:S(2)}) collective-permute-start(bf16[272,128]{1,0:T(8,128)(2,1)S(1)} %get-tuple-element.48), channel_id=1, source_target_pairs={{0,22},{1,23},{2,20},{3,21},{4,18},{5,19},{6,16},{7,17},{8,30},{9,... | collective-permute-start | bytes 208904 | tf_op jit(solution)/shard_map/ppermute | solution.py:501
  26.3 3.0 %collective-permute-start.11 = (bf16[272,128]{1,0:T(8,128)(2,1)S(1)}, bf16[272,128]{1,0:T(8,128)(2,1)S(1)}, u32[]{:S(2)}, u32[]{:S(2)}) collective-permute-start(bf16[272,128]{1,0:T(8,128)(2,1)S(1)} %get-tuple-element.49), channel_id=1, source_target_pairs={{0,14},{1,15},{2,12},{3,13},{4,10},{5,11},{6,8},{7,9},{8,6},{9,7},... | collective-permute-start | bytes 208904 | tf_op jit(solution)/shard_map/ppermute | solution.py:501
  29.3 2.4 %collective-permute-start.12 = (bf16[272,128]{1,0:T(8,128)(2,1)S(1)}, bf16[272,128]{1,0:T(8,128)(2,1)S(1)}, u32[]{:S(2)}, u32[]{:S(2)}) collective-permute-start(bf16[272,128]{1,0:T(8,128)(2,1)S(1)} %get-tuple-element.50), channel_id=1, source_target_pairs={{0,24},{1,25},{2,26},{3,27},{4,28},{5,29},{6,30},{7,31},{8,16},{9,... | collective-permute-start | bytes 208904 | tf_op jit(solution)/shard_map/ppermute | solution.py:501
  32.0 2.2 %collective-permute-done.10.refs_0_ = bf16[272,128]{1,0:T(8,128)(2,1)S(1)} collective-permute-done((bf16[272,128]{1,0:T(8,128)(2,1)S(1)}, bf16[272,128]{1,0:T(8,128)(2,1)S(1)}, u32[]{:S(2)}, u32[]{:S(2)}) %collective-permute-start.10) | collective-permute-done | bytes 69664 | tf_op jit(solution)/shard_map/ppermute | solution.py:501
  34.2 1.2 %collective-permute-done.12.refs_2_ = bf16[272,128]{1,0:T(8,128)(2,1)S(1)} collective-permute-done((bf16[272,128]{1,0:T(8,128)(2,1)S(1)}, bf16[272,128]{1,0:T(8,128)(2,1)S(1)}, u32[]{:S(2)}, u32[]{:S(2)}) %collective-permute-start.12) | collective-permute-done | bytes 69664 | tf_op jit(solution)/shard_map/ppermute | solution.py:501
  35.4 3.6 %shard_map.34 = (bf16[128,512]{1,0:T(8,128)(2,1)S(1)}, bf16[128,512]{1,0:T(8,128)(2,1)S(1)}, bf16[128,512]{1,0:T(8,128)(2,1)S(1)}, bf16[128,512]{1,0:T(8,128)(2,...) custom-call(f32[4,264,128]{2,1,0:T(8,128)S(1)} %shard_map.33.base_re, ...), custom_call_target="tpu_custom_call" | custom-call | tf_op jit(solution)/shard_map/pallas_call | solution.py:93
  39.1 2.0 %collective-permute-start.18 = (bf16[128,512]{1,0:T(8,128)(2,1)S(1)}, bf16[128,512]{1,0:T(8,128)(2,1)S(1)}, u32[]{:S(2)}, u32[]{:S(2)}) collective-permute-start(bf16[128,512]{1,0:T(8,128)(2,1)S(1)} %get-tuple-element.57), channel_id=1, source_target_pairs={{9,0},{4,1},{11,2},{6,3},{13,4},{0,5},{15,6},{2,7},{1,8},{12,9},{3... | collective-permute-start | bytes 393224 | tf_op jit(solution)/shard_map/ppermute | solution.py:501
  41.1 0.8 %collective-permute-start.19 = (bf16[128,512]{1,0:T(8,128)(2,1)S(1)}, bf16[128,512]{1,0:T(8,128)(2,1)S(1)}, u32[]{:S(2)}, u32[]{:S(2)}) collective-permute-start(bf16[128,512]{1,0:T(8,128)(2,1)S(1)} %get-tuple-element.58), channel_id=1, source_target_pairs={{4,0},{3,1},{6,2},{1,3},{0,4},{7,5},{2,6},{5,7},{12,8},{11,9},{14,... | collective-permute-start | bytes 393224 | tf_op jit(solution)/shard_map/ppermute | solution.py:501
  41.9 1.2 %collective-permute-start.13 = (bf16[128,512]{1,0:T(8,128)(2,1)S(1)}, bf16[128,512]{1,0:T(8,128)(2,1)S(1)}, u32[]{:S(2)}, u32[]{:S(2)}) collective-permute-start(bf16[128,512]{1,0:T(8,128)(2,1)S(1)} %get-tuple-element.51), channel_id=1, source_target_pairs={{2,0},{9,1},{0,2},{11,3},{6,4},{13,5},{4,6},{15,7},{10,8},{1,9},{8... | collective-permute-start | bytes 393224 | tf_op jit(solution)/shard_map/ppermute | solution.py:501
  43.1 0.4 collective-permute-done.16.refs_1_
  43.4 0.4 collective-permute-start.14
  43.9 0.6 %collective-permute-done.17.refs_2_ = bf16[128,512]{1,0:T(8,128)(2,1)S(1)} collective-permute-done((bf16[128,512]{1,0:T(8,128)(2,1)S(1)}, bf16[128,512]{1,0:T(8,128)(2,1)S(1)}, u32[]{:S(2)}, u32[]{:S(2)}) %collective-permute-start.17) | collective-permute-done | bytes 131104 | tf_op jit(solution)/shard_map/ppermute | solution.py:501
  44.4 0.8 %collective-permute-start.15 = (bf16[128,512]{1,0:T(8,128)(2,1)S(1)}, bf16[128,512]{1,0:T(8,128)(2,1)S(1)}, u32[]{:S(2)}, u32[]{:S(2)}) collective-permute-start(bf16[128,512]{1,0:T(8,128)(2,1)S(1)} %get-tuple-element.53), channel_id=1, source_target_pairs={{1,0},{0,1},{3,2},{2,3},{5,4},{4,5},{7,6},{6,7},{9,8},{8,9},{11,10... | collective-permute-start | bytes 393224 | tf_op jit(solution)/shard_map/ppermute | solution.py:501
  45.3 1.0 %collective-permute-done.19.refs_4_ = bf16[128,512]{1,0:T(8,128)(2,1)S(1)} collective-permute-done((bf16[128,512]{1,0:T(8,128)(2,1)S(1)}, bf16[128,512]{1,0:T(8,128)(2,1)S(1)}, u32[]{:S(2)}, u32[]{:S(2)}) %collective-permute-start.19) | collective-permute-done | bytes 131104 | tf_op jit(solution)/shard_map/ppermute | solution.py:501
  46.2 1.0 %shard_map.35.refs_3_ = bf16[4,2,128,512]{3,2,1,0:T(8,128)(2,1)} custom-call(bf16[4,2,128,512]{3,2,1,0:T(8,128)(2,1)S(1)} %bitcast.3, bf16[128,512]{1,0:T(8,128)(2,1)S(1)} %get-tuple-element.54.refs_0_, bf16[128,512]{1,0:T(8,128)(2,1)S(1)} %collective-permute-done.16.refs_1_, bf16[128,512]{1,0:T(8,128)(2,1)S(1)} %collective-permute-done.17.refs_2_, ...), custom_call_target="tpu_custom_call" | custom-call | tf_op jit(solution)/shard_map/pallas_call | solution.py:464
  47.2 1.2 %collective-permute-done.14.refs_1_ = bf16[128,512]{1,0:T(8,128)(2,1)S(1)} collective-permute-done((bf16[128,512]{1,0:T(8,128)(2,1)S(1)}, bf16[128,512]{1,0:T(8,128)(2,1)S(1)}, u32[]{:S(2)}, u32[]{:S(2)}) %collective-permute-start.14) | collective-permute-done | bytes 131104 | tf_op jit(solution)/shard_map/ppermute | solution.py:501
  48.4 0.8 %shard_map.36 = bf16[4,2,128,512]{3,2,1,0:T(8,128)(2,1)} custom-call(bf16[4,2,128,512]{3,2,1,0:T(8,128)(2,1)S(1)} %bitcast.4, bf16[128,512]{1,0:T(8,128)(2,1)S(1)} %collective-permute-done.13.refs_0_, bf16[128,512]{1,0:T(8,128)(2,1)S(1)} %collective-permute-done.14.refs_1_, ...), custom_call_target="tpu_custom_call", output_to_operand_aliasing={{}: (4, {})} | custom-call | tf_op jit(solution)/shard_map/pallas_call | solution.py:464
  (21 shorter events, 1.6 us)
Async XLA Ops:
  0.0 1.2 %copy-start.1 = (bf16[1,8,128,512]{3,2,1,0:T(8,128)(2,1)S(1)}, bf16[1,8,128,512]{3,2,1,0:T(8,128)(2,1)}, u32[]{:S(2)}) copy-start(bf16[1,8,128,512]{3,2,1,0:T(8,128)(2,1)} %param.2) | copy-start | bytes 3145732
  1.3 6.3 %collective-permute-start = (bf16[128,512]{1,0:T(8,128)(2,1)S(1)}, bf16[128,512]{1,0:T(8,128)(2,1)S(1)}, u32[]{:S(2)}, u32[]{:S(2)}) collective-permute-start(bf16[128,512]{1,0:T(8,128)(2,1)S(1)} %get-tuple-element.33), channel_id=1, source_target_pairs={{0,5},{1,2},{2,7},{3,0},{4,1},{5,6},{6,3},{7,4},{8,13},{9,10},{10,... | collective-permute-start | bytes 393224 | tf_op jit(solution)/shard_map/ppermute | solution.py:501
  3.8 5.4 %collective-permute-start.1 = (bf16[128,512]{1,0:T(8,128)(2,1)S(1)}, bf16[128,512]{1,0:T(8,128)(2,1)S(1)}, u32[]{:S(2)}, u32[]{:S(2)}) collective-permute-start(bf16[128,512]{1,0:T(8,128)(2,1)S(1)} %get-tuple-element.34), channel_id=1, source_target_pairs={{0,3},{1,8},{2,1},{3,10},{4,7},{5,12},{6,5},{7,14},{8,11},{9,0},{1... | collective-permute-start | bytes 393224 | tf_op jit(solution)/shard_map/ppermute | solution.py:501
  3.8 5.4 %collective-permute-start.2 = (bf16[128,512]{1,0:T(8,128)(2,1)S(1)}, bf16[128,512]{1,0:T(8,128)(2,1)S(1)}, u32[]{:S(2)}, u32[]{:S(2)}) collective-permute-start(bf16[128,512]{1,0:T(8,128)(2,1)S(1)} %get-tuple-element.35), channel_id=1, source_target_pairs={{0,9},{1,4},{2,11},{3,6},{4,13},{5,0},{6,15},{7,2},{8,1},{9,12},{1... | collective-permute-start | bytes 393224 | tf_op jit(solution)/shard_map/ppermute | solution.py:501
  5.6 5.0 %collective-permute-start.3 = (bf16[128,512]{1,0:T(8,128)(2,1)S(1)}, bf16[128,512]{1,0:T(8,128)(2,1)S(1)}, u32[]{:S(2)}, u32[]{:S(2)}) collective-permute-start(bf16[128,512]{1,0:T(8,128)(2,1)S(1)} %get-tuple-element.36), channel_id=1, source_target_pairs={{0,4},{1,3},{2,6},{3,1},{4,0},{5,7},{6,2},{7,5},{8,12},{9,11},{10,... | collective-permute-start | bytes 393224 | tf_op jit(solution)/shard_map/ppermute | solution.py:501
  7.1 5.0 %collective-permute-start.4 = (bf16[128,512]{1,0:T(8,128)(2,1)S(1)}, bf16[128,512]{1,0:T(8,128)(2,1)S(1)}, u32[]{:S(2)}, u32[]{:S(2)}) collective-permute-start(bf16[128,512]{1,0:T(8,128)(2,1)S(1)} %get-tuple-element.38), channel_id=1, source_target_pairs={{0,2},{1,9},{2,0},{3,11},{4,6},{5,13},{6,4},{7,15},{8,10},{9,1},{1... | collective-permute-start | bytes 393224 | tf_op jit(solution)/shard_map/ppermute | solution.py:501
  7.6 5.2 %collective-permute-start.5 = (bf16[128,512]{1,0:T(8,128)(2,1)S(1)}, bf16[128,512]{1,0:T(8,128)(2,1)S(1)}, u32[]{:S(2)}, u32[]{:S(2)}) collective-permute-start(bf16[128,512]{1,0:T(8,128)(2,1)S(1)} %get-tuple-element.40), channel_id=1, source_target_pairs={{0,8},{1,5},{2,10},{3,7},{4,12},{5,1},{6,14},{7,3},{8,0},{9,13},{1... | collective-permute-start | bytes 393224 | tf_op jit(solution)/shard_map/ppermute | solution.py:501
  9.2 3.6 %collective-permute-start.6 = (bf16[128,512]{1,0:T(8,128)(2,1)S(1)}, bf16[128,512]{1,0:T(8,128)(2,1)S(1)}, u32[]{:S(2)}, u32[]{:S(2)}) collective-permute-start(bf16[128,512]{1,0:T(8,128)(2,1)S(1)} %get-tuple-element.41), channel_id=1, source_target_pairs={{0,1},{1,0},{2,3},{3,2},{4,5},{5,4},{6,7},{7,6},{8,9},{9,8},{10,11... | collective-permute-start | bytes 393224 | tf_op jit(solution)/shard_map/ppermute | solution.py:501
  13.2 8.0 %collective-permute-start.7 = (bf16[272,128]{1,0:T(8,128)(2,1)S(1)}, bf16[272,128]{1,0:T(8,128)(2,1)S(1)}, u32[]{:S(2)}, u32[]{:S(2)}) collective-permute-start(bf16[272,128]{1,0:T(8,128)(2,1)S(1)} %get-tuple-element.43), channel_id=1, source_target_pairs={{0,22},{1,23},{2,20},{3,21},{4,18},{5,19},{6,16},{7,17},{8,30},{9,... | collective-permute-start | bytes 208904 | tf_op jit(solution)/shard_map/ppermute | solution.py:501
  17.7 6.1 %collective-permute-start.8 = (bf16[272,128]{1,0:T(8,128)(2,1)S(1)}, bf16[272,128]{1,0:T(8,128)(2,1)S(1)}, u32[]{:S(2)}, u32[]{:S(2)}) collective-permute-start(bf16[272,128]{1,0:T(8,128)(2,1)S(1)} %get-tuple-element.44), channel_id=1, source_target_pairs={{0,14},{1,15},{2,12},{3,13},{4,10},{5,11},{6,8},{7,9},{8,6},{9,7},... | collective-permute-start | bytes 208904 | tf_op jit(solution)/shard_map/ppermute | solution.py:501
  19.2 6.1 %collective-permute-start.9 = (bf16[272,128]{1,0:T(8,128)(2,1)S(1)}, bf16[272,128]{1,0:T(8,128)(2,1)S(1)}, u32[]{:S(2)}, u32[]{:S(2)}) collective-permute-start(bf16[272,128]{1,0:T(8,128)(2,1)S(1)} %get-tuple-element.45), channel_id=1, source_target_pairs={{0,24},{1,25},{2,26},{3,27},{4,28},{5,29},{6,30},{7,31},{8,16},{9,... | collective-permute-start | bytes 208904 | tf_op jit(solution)/shard_map/ppermute | solution.py:501
  25.4 8.7 %collective-permute-start.10 = (bf16[272,128]{1,0:T(8,128)(2,1)S(1)}, bf16[272,128]{1,0:T(8,128)(2,1)S(1)}, u32[]{:S(2)}, u32[]{:S(2)}) collective-permute-start(bf16[272,128]{1,0:T(8,128)(2,1)S(1)} %get-tuple-element.48), channel_id=1, source_target_pairs={{0,22},{1,23},{2,20},{3,21},{4,18},{5,19},{6,16},{7,17},{8,30},{9,... | collective-permute-start | bytes 208904 | tf_op jit(solution)/shard_map/ppermute | solution.py:501
  26.3 7.9 %collective-permute-start.11 = (bf16[272,128]{1,0:T(8,128)(2,1)S(1)}, bf16[272,128]{1,0:T(8,128)(2,1)S(1)}, u32[]{:S(2)}, u32[]{:S(2)}) collective-permute-start(bf16[272,128]{1,0:T(8,128)(2,1)S(1)} %get-tuple-element.49), channel_id=1, source_target_pairs={{0,14},{1,15},{2,12},{3,13},{4,10},{5,11},{6,8},{7,9},{8,6},{9,7},... | collective-permute-start | bytes 208904 | tf_op jit(solution)/shard_map/ppermute | solution.py:501
  29.3 6.1 %collective-permute-start.12 = (bf16[272,128]{1,0:T(8,128)(2,1)S(1)}, bf16[272,128]{1,0:T(8,128)(2,1)S(1)}, u32[]{:S(2)}, u32[]{:S(2)}) collective-permute-start(bf16[272,128]{1,0:T(8,128)(2,1)S(1)} %get-tuple-element.50), channel_id=1, source_target_pairs={{0,24},{1,25},{2,26},{3,27},{4,28},{5,29},{6,30},{7,31},{8,16},{9,... | collective-permute-start | bytes 208904 | tf_op jit(solution)/shard_map/ppermute | solution.py:501
  32.0 14.3 %copy-start = (bf16[1,8,128,512]{3,2,1,0:T(8,128)(2,1)S(1)}, bf16[1,8,128,512]{3,2,1,0:T(8,128)(2,1)}, u32[]{:S(2)}) copy-start(bf16[1,8,128,512]{3,2,1,0:T(8,128)(2,1)} %param.3) | copy-start | bytes 3145732
  39.0 4.4 %collective-permute-start.16 = (bf16[128,512]{1,0:T(8,128)(2,1)S(1)}, bf16[128,512]{1,0:T(8,128)(2,1)S(1)}, u32[]{:S(2)}, u32[]{:S(2)}) collective-permute-start(bf16[128,512]{1,0:T(8,128)(2,1)S(1)} %get-tuple-element.55), channel_id=1, source_target_pairs={{5,0},{2,1},{7,2},{0,3},{1,4},{6,5},{3,6},{4,7},{13,8},{10,9},{15,... | collective-permute-start | bytes 393224 | tf_op jit(solution)/shard_map/ppermute | solution.py:501
  39.1 5.4 %collective-permute-start.17 = (bf16[128,512]{1,0:T(8,128)(2,1)S(1)}, bf16[128,512]{1,0:T(8,128)(2,1)S(1)}, u32[]{:S(2)}, u32[]{:S(2)}) collective-permute-start(bf16[128,512]{1,0:T(8,128)(2,1)S(1)} %get-tuple-element.56), channel_id=1, source_target_pairs={{3,0},{8,1},{1,2},{10,3},{7,4},{12,5},{5,6},{14,7},{11,8},{0,9},{9... | collective-permute-start | bytes 393224 | tf_op jit(solution)/shard_map/ppermute | solution.py:501
  39.1 6.1 %collective-permute-start.18 = (bf16[128,512]{1,0:T(8,128)(2,1)S(1)}, bf16[128,512]{1,0:T(8,128)(2,1)S(1)}, u32[]{:S(2)}, u32[]{:S(2)}) collective-permute-start(bf16[128,512]{1,0:T(8,128)(2,1)S(1)} %get-tuple-element.57), channel_id=1, source_target_pairs={{9,0},{4,1},{11,2},{6,3},{13,4},{0,5},{15,6},{2,7},{1,8},{12,9},{3... | collective-permute-start | bytes 393224 | tf_op jit(solution)/shard_map/ppermute | solution.py:501
  41.1 5.2 %collective-permute-start.19 = (bf16[128,512]{1,0:T(8,128)(2,1)S(1)}, bf16[128,512]{1,0:T(8,128)(2,1)S(1)}, u32[]{:S(2)}, u32[]{:S(2)}) collective-permute-start(bf16[128,512]{1,0:T(8,128)(2,1)S(1)} %get-tuple-element.58), channel_id=1, source_target_pairs={{4,0},{3,1},{6,2},{1,3},{0,4},{7,5},{2,6},{5,7},{12,8},{11,9},{14,... | collective-permute-start | bytes 393224 | tf_op jit(solution)/shard_map/ppermute | solution.py:501
  41.9 5.3 %collective-permute-start.13 = (bf16[128,512]{1,0:T(8,128)(2,1)S(1)}, bf16[128,512]{1,0:T(8,128)(2,1)S(1)}, u32[]{:S(2)}, u32[]{:S(2)}) collective-permute-start(bf16[128,512]{1,0:T(8,128)(2,1)S(1)} %get-tuple-element.51), channel_id=1, source_target_pairs={{2,0},{9,1},{0,2},{11,3},{6,4},{13,5},{4,6},{15,7},{10,8},{1,9},{8... | collective-permute-start | bytes 393224 | tf_op jit(solution)/shard_map/ppermute | solution.py:501
  43.4 5.0 %collective-permute-start.14 = (bf16[128,512]{1,0:T(8,128)(2,1)S(1)}, bf16[128,512]{1,0:T(8,128)(2,1)S(1)}, u32[]{:S(2)}, u32[]{:S(2)}) collective-permute-start(bf16[128,512]{1,0:T(8,128)(2,1)S(1)} %get-tuple-element.52), channel_id=1, source_target_pairs={{8,0},{5,1},{10,2},{7,3},{12,4},{1,5},{14,6},{3,7},{0,8},{13,9},{2... | collective-permute-start | bytes 393224 | tf_op jit(solution)/shard_map/ppermute | solution.py:501
  44.4 4.0 %collective-permute-start.15 = (bf16[128,512]{1,0:T(8,128)(2,1)S(1)}, bf16[128,512]{1,0:T(8,128)(2,1)S(1)}, u32[]{:S(2)}, u32[]{:S(2)}) collective-permute-start(bf16[128,512]{1,0:T(8,128)(2,1)S(1)} %get-tuple-element.53), channel_id=1, source_target_pairs={{1,0},{0,1},{3,2},{2,3},{5,4},{4,5},{7,6},{6,7},{9,8},{8,9},{11,10... | collective-permute-start | bytes 393224 | tf_op jit(solution)/shard_map/ppermute | solution.py:501

commit v13 on v11

--- a/solution.py
+++ b/solution.py
@@ -33,7 +33,7 @@
 
 def neighbour_steps():
     x, y, z = (0, 0, 1), (0, 1, 0), (1, 0, 0)
-    order = [(x, y), (z, x), (y, z)]
+    order = [(y, x), (x, z), (z, y)]
     return [tuple(flips_of(*way, pair=cross) for way in step) for cross in (1, 0) for step in order]
 
 

time: 49.5 us -> 49.4 us (level)
  waiting for transfers between devices: 15 us -> 14.5 us
    ppermute x20, waiting for transfers between devices: 15 us -> 14.5 us  [swap(): lax.ppermute(array, AXES, permute)]
  transfers between devices with their start and end apart: 20 -> 20, of which waited for: 15 -> 12; matrix products, arithmetic and copies ran while one was open for 0% -> 0% of each run, Pallas kernels for 4% -> 4%
where the time goes in v13:
time: 49.4 us; the launch traced here: 49.2 us
  starting transfers between devices  26.2 us (53%)
  waiting for transfers between devices  14.5 us (29%)
  Pallas kernels  7.24 us (15%)
  local copies, waits for them, and re-layouts  1.23 us (2%)
    ppermute x20, starting transfers between devices, swap(): lax.ppermute(array, AXES, permute)  26.2 us
    ppermute x20, waiting for transfers between devices, swap(): lax.ppermute(array, AXES, permute)  14.5 us
    pallas_call x6, Pallas kernels, call(): pl.pallas_call(kernel, out_shape=out_shape, in_specs=[vmem] * len(operand...  5.45 us
    pallas_call x2, Pallas kernels, new_weights(): pl.pallas_call(functools.partial(weights_kernel, rest_count, numbers), ou...  1.79 us
    unnamed x4, local copies, waits for them, and re-layouts  1.23 us
  transfers between devices with their start and end apart: 20, of which 12 were waited for; matrix products, arithmetic and copies ran while one was open for 0% of the time, Pallas kernels for 4%

profile of v13, /device:TPU:0, one launch (start us, length us, event | category | flops | bytes accessed | tf_op | source)
XLA Modules:
  0.0 49.2 jit_solution(14009300924502608637)
XLA Ops:
  0.0 1.2 %copy-done.1 = bf16[1,8,128,512]{3,2,1,0:T(8,128)(2,1)S(1)} copy-done((bf16[1,8,128,512]{3,2,1,0:T(8,128)(2,1)S(1)}, bf16[1,8,128,512]{3,2,1,0:T(8,128)(2,1)}, u32[]{:S(2)}) %copy-start.1) | copy-done | bytes 1048600
  1.3 2.5 %collective-permute-start = (bf16[128,512]{1,0:T(8,128)(2,1)S(1)}, bf16[128,512]{1,0:T(8,128)(2,1)S(1)}, u32[]{:S(2)}, u32[]{:S(2)}) collective-permute-start(bf16[128,512]{1,0:T(8,128)(2,1)S(1)} %get-tuple-element.33), channel_id=1, source_target_pairs={{0,5},{1,2},{2,7},{3,0},{4,1},{5,6},{6,3},{7,4},{8,13},{9,10},{10,... | collective-permute-start | bytes 393224 | tf_op jit(solution)/shard_map/ppermute | solution.py:496
  3.8 1.8 %collective-permute-start.2 = (bf16[128,512]{1,0:T(8,128)(2,1)S(1)}, bf16[128,512]{1,0:T(8,128)(2,1)S(1)}, u32[]{:S(2)}, u32[]{:S(2)}) collective-permute-start(bf16[128,512]{1,0:T(8,128)(2,1)S(1)} %get-tuple-element.35), channel_id=1, source_target_pairs={{0,9},{1,4},{2,11},{3,6},{4,13},{5,0},{6,15},{7,2},{8,1},{9,12},{1... | collective-permute-start | bytes 393224 | tf_op jit(solution)/shard_map/ppermute | solution.py:496
  5.6 1.5 %collective-permute-start.3 = (bf16[128,512]{1,0:T(8,128)(2,1)S(1)}, bf16[128,512]{1,0:T(8,128)(2,1)S(1)}, u32[]{:S(2)}, u32[]{:S(2)}) collective-permute-start(bf16[128,512]{1,0:T(8,128)(2,1)S(1)} %get-tuple-element.36), channel_id=1, source_target_pairs={{0,4},{1,3},{2,6},{3,1},{4,0},{5,7},{6,2},{7,5},{8,12},{9,11},{10,... | collective-permute-start | bytes 393224 | tf_op jit(solution)/shard_map/ppermute | solution.py:496
  7.1 0.5 %collective-permute-start.4 = (bf16[128,512]{1,0:T(8,128)(2,1)S(1)}, bf16[128,512]{1,0:T(8,128)(2,1)S(1)}, u32[]{:S(2)}, u32[]{:S(2)}) collective-permute-start(bf16[128,512]{1,0:T(8,128)(2,1)S(1)} %get-tuple-element.39), channel_id=1, source_target_pairs={{0,2},{1,9},{2,0},{3,11},{4,6},{5,13},{6,4},{7,15},{8,10},{9,1},{1... | collective-permute-start | bytes 393224 | tf_op jit(solution)/shard_map/ppermute | solution.py:496
  7.6 1.6 %collective-permute-start.5 = (bf16[128,512]{1,0:T(8,128)(2,1)S(1)}, bf16[128,512]{1,0:T(8,128)(2,1)S(1)}, u32[]{:S(2)}, u32[]{:S(2)}) collective-permute-start(bf16[128,512]{1,0:T(8,128)(2,1)S(1)} %get-tuple-element.40), channel_id=1, source_target_pairs={{0,8},{1,5},{2,10},{3,7},{4,12},{5,1},{6,14},{7,3},{8,0},{9,13},{1... | collective-permute-start | bytes 393224 | tf_op jit(solution)/shard_map/ppermute | solution.py:496
  9.2 1.3 %collective-permute-done.3.refs_4_.refs_7_ = bf16[128,512]{1,0:T(8,128)(2,1)S(1)} collective-permute-done((bf16[128,512]{1,0:T(8,128)(2,1)S(1)}, bf16[128,512]{1,0:T(8,128)(2,1)S(1)}, u32[]{:S(2)}, u32[]{:S(2)}) %collective-permute-start.3) | collective-permute-done | bytes 131104 | tf_op jit(solution)/shard_map/ppermute | solution.py:496
  10.6 0.9 %shard_map.29 = (f32[4,264,128]{2,1,0:T(8,128)S(1)}, bf16[16,512]{1,0:T(8,128)(2,1)S(1)}) custom-call(bf16[128,512]{1,0:T(8,128)(2,1)S(1)} %get-tuple-element.32.refs_0_.refs_3_, bf16[128,512]{1,0:T(8,128)(2,1)S(1)} %collective-permute-done.refs_1_.refs_4_, bf16[128,512]{1,0:T(8,128)(2,1)S(1)} %collective-permute-done.1.refs_2_.refs_5_, ...), custom_call_target="tpu_custom_call" | custom-call | tf_op jit(solution)/shard_map/pallas_call | solution.py:93
  11.5 0.6 %collective-permute-done.4.refs_0_.refs_8_ = bf16[128,512]{1,0:T(8,128)(2,1)S(1)} collective-permute-done((bf16[128,512]{1,0:T(8,128)(2,1)S(1)}, bf16[128,512]{1,0:T(8,128)(2,1)S(1)}, u32[]{:S(2)}, u32[]{:S(2)}) %collective-permute-start.4) | collective-permute-done | bytes 131104 | tf_op jit(solution)/shard_map/ppermute | solution.py:496
  12.1 0.8 %collective-permute-done.5.refs_1_.refs_9_ = bf16[128,512]{1,0:T(8,128)(2,1)S(1)} collective-permute-done((bf16[128,512]{1,0:T(8,128)(2,1)S(1)}, bf16[128,512]{1,0:T(8,128)(2,1)S(1)}, u32[]{:S(2)}, u32[]{:S(2)}) %collective-permute-start.5) | collective-permute-done | bytes 131104 | tf_op jit(solution)/shard_map/ppermute | solution.py:496
  12.8 0.5 shard_map.30
  13.3 4.5 %collective-permute-start.7 = (bf16[272,128]{1,0:T(8,128)(2,1)S(1)}, bf16[272,128]{1,0:T(8,128)(2,1)S(1)}, u32[]{:S(2)}, u32[]{:S(2)}) collective-permute-start(bf16[272,128]{1,0:T(8,128)(2,1)S(1)} %get-tuple-element.43), channel_id=1, source_target_pairs={{0,22},{1,23},{2,20},{3,21},{4,18},{5,19},{6,16},{7,17},{8,30},{9,... | collective-permute-start | bytes 208904 | tf_op jit(solution)/shard_map/ppermute | solution.py:496
  17.8 1.5 %collective-permute-start.8 = (bf16[272,128]{1,0:T(8,128)(2,1)S(1)}, bf16[272,128]{1,0:T(8,128)(2,1)S(1)}, u32[]{:S(2)}, u32[]{:S(2)}) collective-permute-start(bf16[272,128]{1,0:T(8,128)(2,1)S(1)} %get-tuple-element.44), channel_id=1, source_target_pairs={{0,14},{1,15},{2,12},{3,13},{4,10},{5,11},{6,8},{7,9},{8,6},{9,7},... | collective-permute-start | bytes 208904 | tf_op jit(solution)/shard_map/ppermute | solution.py:496
  19.6 1.7 %collective-permute-done.7.refs_0_ = bf16[272,128]{1,0:T(8,128)(2,1)S(1)} collective-permute-done((bf16[272,128]{1,0:T(8,128)(2,1)S(1)}, bf16[272,128]{1,0:T(8,128)(2,1)S(1)}, u32[]{:S(2)}, u32[]{:S(2)}) %collective-permute-start.7) | collective-permute-done | bytes 69664 | tf_op jit(solution)/shard_map/ppermute | solution.py:496
  21.3 2.6 %collective-permute-done.8.refs_1_ = bf16[272,128]{1,0:T(8,128)(2,1)S(1)} collective-permute-done((bf16[272,128]{1,0:T(8,128)(2,1)S(1)}, bf16[272,128]{1,0:T(8,128)(2,1)S(1)}, u32[]{:S(2)}, u32[]{:S(2)}) %collective-permute-start.8) | collective-permute-done | bytes 69664 | tf_op jit(solution)/shard_map/ppermute | solution.py:496
  23.9 1.5 %collective-permute-done.9.refs_2_ = bf16[272,128]{1,0:T(8,128)(2,1)S(1)} collective-permute-done((bf16[272,128]{1,0:T(8,128)(2,1)S(1)}, bf16[272,128]{1,0:T(8,128)(2,1)S(1)}, u32[]{:S(2)}, u32[]{:S(2)}) %collective-permute-start.9) | collective-permute-done | bytes 69664 | tf_op jit(solution)/shard_map/ppermute | solution.py:496
  25.5 0.6 %collective-permute-start.10 = (bf16[272,128]{1,0:T(8,128)(2,1)S(1)}, bf16[272,128]{1,0:T(8,128)(2,1)S(1)}, u32[]{:S(2)}, u32[]{:S(2)}) collective-permute-start(bf16[272,128]{1,0:T(8,128)(2,1)S(1)} %get-tuple-element.48), channel_id=1, source_target_pairs={{0,22},{1,23},{2,20},{3,21},{4,18},{5,19},{6,16},{7,17},{8,30},{9,... | collective-permute-start | bytes 208904 | tf_op jit(solution)/shard_map/ppermute | solution.py:496
  26.1 3.0 %collective-permute-start.11 = (bf16[272,128]{1,0:T(8,128)(2,1)S(1)}, bf16[272,128]{1,0:T(8,128)(2,1)S(1)}, u32[]{:S(2)}, u32[]{:S(2)}) collective-permute-start(bf16[272,128]{1,0:T(8,128)(2,1)S(1)} %get-tuple-element.49), channel_id=1, source_target_pairs={{0,14},{1,15},{2,12},{3,13},{4,10},{5,11},{6,8},{7,9},{8,6},{9,7},... | collective-permute-start | bytes 208904 | tf_op jit(solution)/shard_map/ppermute | solution.py:496
  29.2 2.6 %collective-permute-start.12 = (bf16[272,128]{1,0:T(8,128)(2,1)S(1)}, bf16[272,128]{1,0:T(8,128)(2,1)S(1)}, u32[]{:S(2)}, u32[]{:S(2)}) collective-permute-start(bf16[272,128]{1,0:T(8,128)(2,1)S(1)} %get-tuple-element.50), channel_id=1, source_target_pairs={{0,24},{1,25},{2,26},{3,27},{4,28},{5,29},{6,30},{7,31},{8,16},{9,... | collective-permute-start | bytes 208904 | tf_op jit(solution)/shard_map/ppermute | solution.py:496
  32.1 1.8 %collective-permute-done.10.refs_0_ = bf16[272,128]{1,0:T(8,128)(2,1)S(1)} collective-permute-done((bf16[272,128]{1,0:T(8,128)(2,1)S(1)}, bf16[272,128]{1,0:T(8,128)(2,1)S(1)}, u32[]{:S(2)}, u32[]{:S(2)}) %collective-permute-start.10) | collective-permute-done | bytes 69664 | tf_op jit(solution)/shard_map/ppermute | solution.py:496
  33.8 1.4 %collective-permute-done.12.refs_2_ = bf16[272,128]{1,0:T(8,128)(2,1)S(1)} collective-permute-done((bf16[272,128]{1,0:T(8,128)(2,1)S(1)}, bf16[272,128]{1,0:T(8,128)(2,1)S(1)}, u32[]{:S(2)}, u32[]{:S(2)}) %collective-permute-start.12) | collective-permute-done | bytes 69664 | tf_op jit(solution)/shard_map/ppermute | solution.py:496
  35.3 3.6 %shard_map.33 = (bf16[128,512]{1,0:T(8,128)(2,1)S(1)}, bf16[128,512]{1,0:T(8,128)(2,1)S(1)}, bf16[128,512]{1,0:T(8,128)(2,1)S(1)}, bf16[128,512]{1,0:T(8,128)(2,...) custom-call(f32[4,264,128]{2,1,0:T(8,128)S(1)} %shard_map.32.base_re, ...), custom_call_target="tpu_custom_call" | custom-call | tf_op jit(solution)/shard_map/pallas_call | solution.py:93
  39.0 2.2 %collective-permute-start.18 = (bf16[128,512]{1,0:T(8,128)(2,1)S(1)}, bf16[128,512]{1,0:T(8,128)(2,1)S(1)}, u32[]{:S(2)}, u32[]{:S(2)}) collective-permute-start(bf16[128,512]{1,0:T(8,128)(2,1)S(1)} %get-tuple-element.57), channel_id=1, source_target_pairs={{9,0},{4,1},{11,2},{6,3},{13,4},{0,5},{15,6},{2,7},{1,8},{12,9},{3... | collective-permute-start | bytes 393224 | tf_op jit(solution)/shard_map/ppermute | solution.py:496
  41.2 0.8 %collective-permute-start.19 = (bf16[128,512]{1,0:T(8,128)(2,1)S(1)}, bf16[128,512]{1,0:T(8,128)(2,1)S(1)}, u32[]{:S(2)}, u32[]{:S(2)}) collective-permute-start(bf16[128,512]{1,0:T(8,128)(2,1)S(1)} %get-tuple-element.58), channel_id=1, source_target_pairs={{4,0},{3,1},{6,2},{1,3},{0,4},{7,5},{2,6},{5,7},{12,8},{11,9},{14,... | collective-permute-start | bytes 393224 | tf_op jit(solution)/shard_map/ppermute | solution.py:496
  42.0 1.2 %collective-permute-start.13 = (bf16[128,512]{1,0:T(8,128)(2,1)S(1)}, bf16[128,512]{1,0:T(8,128)(2,1)S(1)}, u32[]{:S(2)}, u32[]{:S(2)}) collective-permute-start(bf16[128,512]{1,0:T(8,128)(2,1)S(1)} %get-tuple-element.51), channel_id=1, source_target_pairs={{2,0},{9,1},{0,2},{11,3},{6,4},{13,5},{4,6},{15,7},{10,8},{1,9},{8... | collective-permute-start | bytes 393224 | tf_op jit(solution)/shard_map/ppermute | solution.py:496
  43.3 0.6 %collective-permute-start.14 = (bf16[128,512]{1,0:T(8,128)(2,1)S(1)}, bf16[128,512]{1,0:T(8,128)(2,1)S(1)}, u32[]{:S(2)}, u32[]{:S(2)}) collective-permute-start(bf16[128,512]{1,0:T(8,128)(2,1)S(1)} %get-tuple-element.52), channel_id=1, source_target_pairs={{8,0},{5,1},{10,2},{7,3},{12,4},{1,5},{14,6},{3,7},{0,8},{13,9},{2... | collective-permute-start | bytes 393224 | tf_op jit(solution)/shard_map/ppermute | solution.py:496
  44.0 0.6 %collective-permute-done.17.refs_2_ = bf16[128,512]{1,0:T(8,128)(2,1)S(1)} collective-permute-done((bf16[128,512]{1,0:T(8,128)(2,1)S(1)}, bf16[128,512]{1,0:T(8,128)(2,1)S(1)}, u32[]{:S(2)}, u32[]{:S(2)}) %collective-permute-start.17) | collective-permute-done | bytes 131104 | tf_op jit(solution)/shard_map/ppermute | solution.py:496
  44.5 0.9 %collective-permute-start.15 = (bf16[128,512]{1,0:T(8,128)(2,1)S(1)}, bf16[128,512]{1,0:T(8,128)(2,1)S(1)}, u32[]{:S(2)}, u32[]{:S(2)}) collective-permute-start(bf16[128,512]{1,0:T(8,128)(2,1)S(1)} %get-tuple-element.53), channel_id=1, source_target_pairs={{1,0},{0,1},{3,2},{2,3},{5,4},{4,5},{7,6},{6,7},{9,8},{8,9},{11,10... | collective-permute-start | bytes 393224 | tf_op jit(solution)/shard_map/ppermute | solution.py:496
  45.4 0.9 %collective-permute-done.19.refs_4_ = bf16[128,512]{1,0:T(8,128)(2,1)S(1)} collective-permute-done((bf16[128,512]{1,0:T(8,128)(2,1)S(1)}, bf16[128,512]{1,0:T(8,128)(2,1)S(1)}, u32[]{:S(2)}, u32[]{:S(2)}) %collective-permute-start.19) | collective-permute-done | bytes 131104 | tf_op jit(solution)/shard_map/ppermute | solution.py:496
  46.3 1.0 %shard_map.34.refs_3_ = bf16[4,2,128,512]{3,2,1,0:T(8,128)(2,1)} custom-call(bf16[4,2,128,512]{3,2,1,0:T(8,128)(2,1)S(1)} %bitcast.3, bf16[128,512]{1,0:T(8,128)(2,1)S(1)} %get-tuple-element.54.refs_0_, bf16[128,512]{1,0:T(8,128)(2,1)S(1)} %collective-permute-done.16.refs_1_, bf16[128,512]{1,0:T(8,128)(2,1)S(1)} %collective-permute-done.17.refs_2_, ...), custom_call_target="tpu_custom_call" | custom-call | tf_op jit(solution)/shard_map/pallas_call | solution.py:459
  47.3 1.1 %collective-permute-done.14.refs_1_ = bf16[128,512]{1,0:T(8,128)(2,1)S(1)} collective-permute-done((bf16[128,512]{1,0:T(8,128)(2,1)S(1)}, bf16[128,512]{1,0:T(8,128)(2,1)S(1)}, u32[]{:S(2)}, u32[]{:S(2)}) %collective-permute-start.14) | collective-permute-done | bytes 131104 | tf_op jit(solution)/shard_map/ppermute | solution.py:496
  48.4 0.8 %shard_map.35 = bf16[4,2,128,512]{3,2,1,0:T(8,128)(2,1)} custom-call(bf16[4,2,128,512]{3,2,1,0:T(8,128)(2,1)S(1)} %bitcast.4, bf16[128,512]{1,0:T(8,128)(2,1)S(1)} %collective-permute-done.13.refs_0_, bf16[128,512]{1,0:T(8,128)(2,1)S(1)} %collective-permute-done.14.refs_1_, ...), custom_call_target="tpu_custom_call", output_to_operand_aliasing={{}: (4, {})} | custom-call | tf_op jit(solution)/shard_map/pallas_call | solution.py:459
  (20 shorter events, 1.1 us)
Async XLA Ops:
  0.0 1.2 %copy-start.1 = (bf16[1,8,128,512]{3,2,1,0:T(8,128)(2,1)S(1)}, bf16[1,8,128,512]{3,2,1,0:T(8,128)(2,1)}, u32[]{:S(2)}) copy-start(bf16[1,8,128,512]{3,2,1,0:T(8,128)(2,1)} %param.2) | copy-start | bytes 3145732
  1.3 6.3 %collective-permute-start = (bf16[128,512]{1,0:T(8,128)(2,1)S(1)}, bf16[128,512]{1,0:T(8,128)(2,1)S(1)}, u32[]{:S(2)}, u32[]{:S(2)}) collective-permute-start(bf16[128,512]{1,0:T(8,128)(2,1)S(1)} %get-tuple-element.33), channel_id=1, source_target_pairs={{0,5},{1,2},{2,7},{3,0},{4,1},{5,6},{6,3},{7,4},{8,13},{9,10},{10,... | collective-permute-start | bytes 393224 | tf_op jit(solution)/shard_map/ppermute | solution.py:496
  3.8 5.4 %collective-permute-start.1 = (bf16[128,512]{1,0:T(8,128)(2,1)S(1)}, bf16[128,512]{1,0:T(8,128)(2,1)S(1)}, u32[]{:S(2)}, u32[]{:S(2)}) collective-permute-start(bf16[128,512]{1,0:T(8,128)(2,1)S(1)} %get-tuple-element.34), channel_id=1, source_target_pairs={{0,3},{1,8},{2,1},{3,10},{4,7},{5,12},{6,5},{7,14},{8,11},{9,0},{1... | collective-permute-start | bytes 393224 | tf_op jit(solution)/shard_map/ppermute | solution.py:496
  3.8 5.4 %collective-permute-start.2 = (bf16[128,512]{1,0:T(8,128)(2,1)S(1)}, bf16[128,512]{1,0:T(8,128)(2,1)S(1)}, u32[]{:S(2)}, u32[]{:S(2)}) collective-permute-start(bf16[128,512]{1,0:T(8,128)(2,1)S(1)} %get-tuple-element.35), channel_id=1, source_target_pairs={{0,9},{1,4},{2,11},{3,6},{4,13},{5,0},{6,15},{7,2},{8,1},{9,12},{1... | collective-permute-start | bytes 393224 | tf_op jit(solution)/shard_map/ppermute | solution.py:496
  5.6 5.0 %collective-permute-start.3 = (bf16[128,512]{1,0:T(8,128)(2,1)S(1)}, bf16[128,512]{1,0:T(8,128)(2,1)S(1)}, u32[]{:S(2)}, u32[]{:S(2)}) collective-permute-start(bf16[128,512]{1,0:T(8,128)(2,1)S(1)} %get-tuple-element.36), channel_id=1, source_target_pairs={{0,4},{1,3},{2,6},{3,1},{4,0},{5,7},{6,2},{7,5},{8,12},{9,11},{10,... | collective-permute-start | bytes 393224 | tf_op jit(solution)/shard_map/ppermute | solution.py:496
  7.1 5.0 %collective-permute-start.4 = (bf16[128,512]{1,0:T(8,128)(2,1)S(1)}, bf16[128,512]{1,0:T(8,128)(2,1)S(1)}, u32[]{:S(2)}, u32[]{:S(2)}) collective-permute-start(bf16[128,512]{1,0:T(8,128)(2,1)S(1)} %get-tuple-element.39), channel_id=1, source_target_pairs={{0,2},{1,9},{2,0},{3,11},{4,6},{5,13},{6,4},{7,15},{8,10},{9,1},{1... | collective-permute-start | bytes 393224 | tf_op jit(solution)/shard_map/ppermute | solution.py:496
  7.6 5.2 %collective-permute-start.5 = (bf16[128,512]{1,0:T(8,128)(2,1)S(1)}, bf16[128,512]{1,0:T(8,128)(2,1)S(1)}, u32[]{:S(2)}, u32[]{:S(2)}) collective-permute-start(bf16[128,512]{1,0:T(8,128)(2,1)S(1)} %get-tuple-element.40), channel_id=1, source_target_pairs={{0,8},{1,5},{2,10},{3,7},{4,12},{5,1},{6,14},{7,3},{8,0},{9,13},{1... | collective-permute-start | bytes 393224 | tf_op jit(solution)/shard_map/ppermute | solution.py:496
  9.2 3.6 %collective-permute-start.6 = (bf16[128,512]{1,0:T(8,128)(2,1)S(1)}, bf16[128,512]{1,0:T(8,128)(2,1)S(1)}, u32[]{:S(2)}, u32[]{:S(2)}) collective-permute-start(bf16[128,512]{1,0:T(8,128)(2,1)S(1)} %get-tuple-element.41), channel_id=1, source_target_pairs={{0,1},{1,0},{2,3},{3,2},{4,5},{5,4},{6,7},{7,6},{8,9},{9,8},{10,11... | collective-permute-start | bytes 393224 | tf_op jit(solution)/shard_map/ppermute | solution.py:496
  13.3 8.0 %collective-permute-start.7 = (bf16[272,128]{1,0:T(8,128)(2,1)S(1)}, bf16[272,128]{1,0:T(8,128)(2,1)S(1)}, u32[]{:S(2)}, u32[]{:S(2)}) collective-permute-start(bf16[272,128]{1,0:T(8,128)(2,1)S(1)} %get-tuple-element.43), channel_id=1, source_target_pairs={{0,22},{1,23},{2,20},{3,21},{4,18},{5,19},{6,16},{7,17},{8,30},{9,... | collective-permute-start | bytes 208904 | tf_op jit(solution)/shard_map/ppermute | solution.py:496
  17.8 6.1 %collective-permute-start.8 = (bf16[272,128]{1,0:T(8,128)(2,1)S(1)}, bf16[272,128]{1,0:T(8,128)(2,1)S(1)}, u32[]{:S(2)}, u32[]{:S(2)}) collective-permute-start(bf16[272,128]{1,0:T(8,128)(2,1)S(1)} %get-tuple-element.44), channel_id=1, source_target_pairs={{0,14},{1,15},{2,12},{3,13},{4,10},{5,11},{6,8},{7,9},{8,6},{9,7},... | collective-permute-start | bytes 208904 | tf_op jit(solution)/shard_map/ppermute | solution.py:496
  19.3 6.1 %collective-permute-start.9 = (bf16[272,128]{1,0:T(8,128)(2,1)S(1)}, bf16[272,128]{1,0:T(8,128)(2,1)S(1)}, u32[]{:S(2)}, u32[]{:S(2)}) collective-permute-start(bf16[272,128]{1,0:T(8,128)(2,1)S(1)} %get-tuple-element.45), channel_id=1, source_target_pairs={{0,24},{1,25},{2,26},{3,27},{4,28},{5,29},{6,30},{7,31},{8,16},{9,... | collective-permute-start | bytes 208904 | tf_op jit(solution)/shard_map/ppermute | solution.py:496
  25.5 8.3 %collective-permute-start.10 = (bf16[272,128]{1,0:T(8,128)(2,1)S(1)}, bf16[272,128]{1,0:T(8,128)(2,1)S(1)}, u32[]{:S(2)}, u32[]{:S(2)}) collective-permute-start(bf16[272,128]{1,0:T(8,128)(2,1)S(1)} %get-tuple-element.48), channel_id=1, source_target_pairs={{0,22},{1,23},{2,20},{3,21},{4,18},{5,19},{6,16},{7,17},{8,30},{9,... | collective-permute-start | bytes 208904 | tf_op jit(solution)/shard_map/ppermute | solution.py:496
  26.1 7.7 %collective-permute-start.11 = (bf16[272,128]{1,0:T(8,128)(2,1)S(1)}, bf16[272,128]{1,0:T(8,128)(2,1)S(1)}, u32[]{:S(2)}, u32[]{:S(2)}) collective-permute-start(bf16[272,128]{1,0:T(8,128)(2,1)S(1)} %get-tuple-element.49), channel_id=1, source_target_pairs={{0,14},{1,15},{2,12},{3,13},{4,10},{5,11},{6,8},{7,9},{8,6},{9,7},... | collective-permute-start | bytes 208904 | tf_op jit(solution)/shard_map/ppermute | solution.py:496
  29.2 6.1 %collective-permute-start.12 = (bf16[272,128]{1,0:T(8,128)(2,1)S(1)}, bf16[272,128]{1,0:T(8,128)(2,1)S(1)}, u32[]{:S(2)}, u32[]{:S(2)}) collective-permute-start(bf16[272,128]{1,0:T(8,128)(2,1)S(1)} %get-tuple-element.50), channel_id=1, source_target_pairs={{0,24},{1,25},{2,26},{3,27},{4,28},{5,29},{6,30},{7,31},{8,16},{9,... | collective-permute-start | bytes 208904 | tf_op jit(solution)/shard_map/ppermute | solution.py:496
  32.1 14.3 %copy-start = (bf16[1,8,128,512]{3,2,1,0:T(8,128)(2,1)S(1)}, bf16[1,8,128,512]{3,2,1,0:T(8,128)(2,1)}, u32[]{:S(2)}) copy-start(bf16[1,8,128,512]{3,2,1,0:T(8,128)(2,1)} %param.3) | copy-start | bytes 3145732
  38.9 4.4 %collective-permute-start.16 = (bf16[128,512]{1,0:T(8,128)(2,1)S(1)}, bf16[128,512]{1,0:T(8,128)(2,1)S(1)}, u32[]{:S(2)}, u32[]{:S(2)}) collective-permute-start(bf16[128,512]{1,0:T(8,128)(2,1)S(1)} %get-tuple-element.55), channel_id=1, source_target_pairs={{5,0},{2,1},{7,2},{0,3},{1,4},{6,5},{3,6},{4,7},{13,8},{10,9},{15,... | collective-permute-start | bytes 393224 | tf_op jit(solution)/shard_map/ppermute | solution.py:496
  38.9 5.6 %collective-permute-start.17 = (bf16[128,512]{1,0:T(8,128)(2,1)S(1)}, bf16[128,512]{1,0:T(8,128)(2,1)S(1)}, u32[]{:S(2)}, u32[]{:S(2)}) collective-permute-start(bf16[128,512]{1,0:T(8,128)(2,1)S(1)} %get-tuple-element.56), channel_id=1, source_target_pairs={{3,0},{8,1},{1,2},{10,3},{7,4},{12,5},{5,6},{14,7},{11,8},{0,9},{9... | collective-permute-start | bytes 393224 | tf_op jit(solution)/shard_map/ppermute | solution.py:496
  39.0 6.4 %collective-permute-start.18 = (bf16[128,512]{1,0:T(8,128)(2,1)S(1)}, bf16[128,512]{1,0:T(8,128)(2,1)S(1)}, u32[]{:S(2)}, u32[]{:S(2)}) collective-permute-start(bf16[128,512]{1,0:T(8,128)(2,1)S(1)} %get-tuple-element.57), channel_id=1, source_target_pairs={{9,0},{4,1},{11,2},{6,3},{13,4},{0,5},{15,6},{2,7},{1,8},{12,9},{3... | collective-permute-start | bytes 393224 | tf_op jit(solution)/shard_map/ppermute | solution.py:496
  41.2 5.1 %collective-permute-start.19 = (bf16[128,512]{1,0:T(8,128)(2,1)S(1)}, bf16[128,512]{1,0:T(8,128)(2,1)S(1)}, u32[]{:S(2)}, u32[]{:S(2)}) collective-permute-start(bf16[128,512]{1,0:T(8,128)(2,1)S(1)} %get-tuple-element.58), channel_id=1, source_target_pairs={{4,0},{3,1},{6,2},{1,3},{0,4},{7,5},{2,6},{5,7},{12,8},{11,9},{14,... | collective-permute-start | bytes 393224 | tf_op jit(solution)/shard_map/ppermute | solution.py:496
  42.0 5.3 %collective-permute-start.13 = (bf16[128,512]{1,0:T(8,128)(2,1)S(1)}, bf16[128,512]{1,0:T(8,128)(2,1)S(1)}, u32[]{:S(2)}, u32[]{:S(2)}) collective-permute-start(bf16[128,512]{1,0:T(8,128)(2,1)S(1)} %get-tuple-element.51), channel_id=1, source_target_pairs={{2,0},{9,1},{0,2},{11,3},{6,4},{13,5},{4,6},{15,7},{10,8},{1,9},{8... | collective-permute-start | bytes 393224 | tf_op jit(solution)/shard_map/ppermute | solution.py:496
  43.3 5.1 %collective-permute-start.14 = (bf16[128,512]{1,0:T(8,128)(2,1)S(1)}, bf16[128,512]{1,0:T(8,128)(2,1)S(1)}, u32[]{:S(2)}, u32[]{:S(2)}) collective-permute-start(bf16[128,512]{1,0:T(8,128)(2,1)S(1)} %get-tuple-element.52), channel_id=1, source_target_pairs={{8,0},{5,1},{10,2},{7,3},{12,4},{1,5},{14,6},{3,7},{0,8},{13,9},{2... | collective-permute-start | bytes 393224 | tf_op jit(solution)/shard_map/ppermute | solution.py:496
  44.5 3.9 %collective-permute-start.15 = (bf16[128,512]{1,0:T(8,128)(2,1)S(1)}, bf16[128,512]{1,0:T(8,128)(2,1)S(1)}, u32[]{:S(2)}, u32[]{:S(2)}) collective-permute-start(bf16[128,512]{1,0:T(8,128)(2,1)S(1)} %get-tuple-element.53), channel_id=1, source_target_pairs={{1,0},{0,1},{3,2},{2,3},{5,4},{4,5},{7,6},{6,7},{9,8},{8,9},{11,10... | collective-permute-start | bytes 393224 | tf_op jit(solution)/shard_map/ppermute | solution.py:496
